TPU v7x, 256 devices: a whole 4x4x8 slice. The times are simulated.
256 devices in a mesh: trow: 16 (over x, y_lo, core), tcol: 16 (over y_hi, z).
Axes of the slice: x: 4, y: 4 (y_hi: 2, y_lo: 2; y = y_hi * 2 + y_lo), z: 8, core: 2. Of those that a mesh axis runs over, the one named last changes fastest.
Arguments:
- theta: float32 [25, 256, 4096], P(None, 'trow', 'tcol'), may hold values from -6 to 6
- salt: float32 [25, 256, 4096], P(None, 'trow', 'tcol'), may hold values from -6 to 6
- velocity_x: float32 [25, 256, 4096], P(None, 'trow', 'tcol'), may hold values from -0.5 to 0.5
- velocity_y: float32 [25, 256, 4096], P(None, 'trow', 'tcol'), may hold values from -0.5 to 0.5
- land_mask: int32 [25, 256, 4096], P(None, 'trow', 'tcol'), may hold values 0 or 1
- kappa: float32 [24, 256, 4096], P(None, 'trow', 'tcol'), may hold values from 0.02 to 5
- forcing: float32 [256, 4096], P('trow', 'tcol'), may hold values from -6 to 6
- bottom: int32 [256, 4096], P('trow', 'tcol'), may hold values from 0 to 25
- theta_cot: float32 [25, 256, 4096], P(None, 'trow', 'tcol'), may hold values from -6 to 6
- salt_cot: float32 [25, 256, 4096], P(None, 'trow', 'tcol'), may hold values from -6 to 6
- surface_cot: float32 [256, 4096], P('trow', 'tcol'), may hold values from -24 to 24
Outputs:
- theta_grad: float32 [25, 256, 4096], P(None, 'trow', 'tcol')
- salt_grad: float32 [25, 256, 4096], P(None, 'trow', 'tcol')
- kappa_grad: float32 [24, 256, 4096], P(None, 'trow', 'tcol')
- forcing_grad: float32 [256, 4096], P('trow', 'tcol')
All inputs are finite; a program needn't handle non-finite values. No bound on the sum of `land_mask` on one device may be relied on, other than what follows from the above.
Results may differ from a plain program's by a relative error of at most 0.0001.
Values sent between devices are 32-bit elements; how exact they have to be, the bound alone decides.
No kernel may reach another device: no remote copies, remote signals or barrier semaphores. Data moves between devices by JAX's collectives and lax.ppermute only.
A program may use at most 64 MiB of HBM per device.

v0:
```python
import functools

import jax
import jax.numpy as jnp
from jax import lax
from jax.sharding import Mesh
from jax.sharding import PartitionSpec as P

ITERS = 4
TROW_TCOL = ("trow_0", "trow_1", "trow_2", "tcol_0", "tcol_1")
TROW = ("trow_0", "trow_1", "trow_2")
TCOL = ("tcol_0", "tcol_1")


def with_halo(array, sides, width):
    edges = {}
    for axis, dim in sides:
        peers, length = (lax.axis_size(axis), array.shape[dim])
        up = [(i, (i + 1) % peers) for i in range(peers - 1)]
        last = lax.slice_in_dim(array, length - width, length, axis=dim)
        leading = lax.slice_in_dim(array, 0, width, axis=dim)
        edges[dim] = (
            lax.ppermute(last, axis, up),
            lax.ppermute(leading, axis, [(b, a) for a, b in up]),
        )
    done = []
    for _, dim in sides:
        low, high = edges[dim]
        around = [(width, width) if d in done else (0, 0) for d in range(array.ndim)]
        array = jnp.concatenate([jnp.pad(low, around), array, jnp.pad(high, around)], axis=dim)
        done.append(dim)
    return array


def over_axes(array, axes):
    return functools.reduce(lax.psum, axes, array)


def cut_along(array, start, count, axis_index):
    return lax.slice_in_dim(array, start, start + count, axis=axis_index)


def forward_change(padded_tracer, padded_velocity, padded_wet, axis_index, length):
    opened = (
        cut_along(padded_velocity, 1, length + 1, axis_index)
        * cut_along(padded_wet, 1, length + 1, axis_index)
        * cut_along(padded_wet, 2, length + 1, axis_index)
    )
    centre = cut_along(padded_tracer, 1, length + 1, axis_index) + cut_along(
        padded_tracer, 2, length + 1, axis_index
    )
    outer = cut_along(padded_tracer, 0, length + 1, axis_index) + cut_along(
        padded_tracer, 3, length + 1, axis_index
    )
    fluxes = opened * (7.0 * centre - outer) / 12.0
    return cut_along(fluxes, 1, length, axis_index) - cut_along(fluxes, 0, length, axis_index)


def adjoint_change(padded_lambda, padded_velocity, padded_wet, axis_index, length):
    opened = (
        cut_along(padded_velocity, 0, length + 3, axis_index)
        * cut_along(padded_wet, 0, length + 3, axis_index)
        * cut_along(padded_wet, 1, length + 3, axis_index)
    )
    faces = opened * (
        cut_along(padded_lambda, 0, length + 3, axis_index)
        - cut_along(padded_lambda, 1, length + 3, axis_index)
    )
    return (
        7.0 * (cut_along(faces, 2, length, axis_index) + cut_along(faces, 1, length, axis_index))
        - cut_along(faces, 3, length, axis_index)
        - cut_along(faces, 0, length, axis_index)
    ) / 12.0


def advect(padded_tracer, padded_ux, padded_uy, padded_wet, tracer):
    row_count = padded_tracer.shape[1] - 4
    col_count = padded_tracer.shape[2] - 4
    along_rows = forward_change(
        padded_tracer[:, :, 2:-2], padded_ux[:, :, 2:-2], padded_wet[:, :, 2:-2], 1, row_count
    )
    along_cols = forward_change(
        padded_tracer[:, 2:-2, :], padded_uy[:, 2:-2, :], padded_wet[:, 2:-2, :], 2, col_count
    )
    return tracer - along_rows - along_cols


def advect_adjoint(padded_lambda, padded_ux, padded_uy, padded_wet, lambda_field, wet):
    row_count = padded_lambda.shape[1] - 4
    col_count = padded_lambda.shape[2] - 4
    along_rows = adjoint_change(
        padded_lambda[:, :, 2:-2], padded_ux[:, :, 2:-2], padded_wet[:, :, 2:-2], 1, row_count
    )
    along_cols = adjoint_change(
        padded_lambda[:, 2:-2, :], padded_uy[:, 2:-2, :], padded_wet[:, 2:-2, :], 2, col_count
    )
    return lambda_field - wet * (along_rows + along_cols)


def factorize(couple, depth):
    inverses = []
    ratios = []
    for depth_index in range(depth):
        diagonal = jnp.ones_like(couple[0])
        if depth_index > 0:
            diagonal = (
                diagonal
                + couple[depth_index - 1]
                - couple[depth_index - 1] * ratios[depth_index - 1]
            )
        if depth_index < depth - 1:
            diagonal = diagonal + couple[depth_index]
        inverse = 1.0 / diagonal
        inverses.append(inverse)
        if depth_index < depth - 1:
            ratios.append(couple[depth_index] * inverse)
    return (inverses, ratios)


def solve_columns(inverses, ratios, couple, rhs):
    depth = rhs.shape[0]
    sweeps = []
    carried = rhs[0] * inverses[0]
    sweeps.append(carried)
    for depth_index in range(1, depth):
        carried = (rhs[depth_index] + couple[depth_index - 1] * carried) * inverses[depth_index]
        sweeps.append(carried)
    results = [sweeps[depth - 1]]
    for depth_index in range(depth - 2, -1, -1):
        results.append(sweeps[depth_index] + ratios[depth_index] * results[-1])
    return jnp.stack(results[::-1])


def surface_apply(field, diagonal):
    padded = with_halo(field, ((TROW, 0), (TCOL, 1)), 1)
    beside = padded[2:, 1:-1] + padded[:-2, 1:-1] + padded[1:-1, 2:] + padded[1:-1, :-2]
    return diagonal * field - beside


def paired_sums(residual, image):
    return (
        over_axes(jnp.sum(residual * residual), TROW_TCOL),
        over_axes(jnp.sum(residual * image), TROW_TCOL),
    )


def conjugate(target, diagonal):
    residual = target
    image = surface_apply(residual, diagonal)
    gamma_now, delta_now = paired_sums(residual, image)
    step_size = gamma_now / delta_now
    direction = residual
    along_image = image
    solution = step_size * direction
    residual = residual - step_size * along_image
    for iteration in range(1, ITERS):
        image = surface_apply(residual, diagonal)
        gamma_next, delta_now = paired_sums(residual, image)
        weight_ratio = gamma_next / gamma_now
        step_size = gamma_next / (delta_now - weight_ratio * gamma_next / step_size)
        direction = residual + weight_ratio * direction
        along_image = image + weight_ratio * along_image
        solution = solution + step_size * direction
        residual = residual - step_size * along_image
        gamma_now = gamma_next
    return solution


def forward_state(padded, theta, salt, forcing, wet, inverses, ratios, couple):
    theta_adv = advect(padded[0], padded[2], padded[3], padded[4], theta)
    salt_adv = advect(padded[1], padded[2], padded[3], padded[4], salt)
    source = jnp.concatenate([theta_adv[:1] + (forcing * wet[0])[None], theta_adv[1:]], axis=0)
    theta_mix = solve_columns(inverses, ratios, couple, source)
    salt_mix = solve_columns(inverses, ratios, couple, salt_adv)
    return (theta_mix, salt_mix)


def mixing_adjoint(zeta, wet, theta_cot, salt_cot, inverses, ratios, couple):
    theta_total = theta_cot + 0.2 * wet * zeta[None]
    salt_total = salt_cot - 0.15 * wet * zeta[None]
    theta_mu = solve_columns(inverses, ratios, couple, theta_total)
    salt_mu = solve_columns(inverses, ratios, couple, salt_total)
    return (theta_mu, salt_mu)


def shards(
    theta,
    salt,
    velocity_x,
    velocity_y,
    land_mask,
    kappa,
    forcing,
    bottom,
    theta_cot,
    salt_cot,
    surface_cot,
):
    depth = theta.shape[0]
    levels = lax.broadcasted_iota(jnp.int32, (depth, 1, 1), 0)
    wet = land_mask.astype(jnp.float32) * (levels < bottom[None]).astype(jnp.float32)
    couple = [
        kappa[depth_index] * wet[depth_index] * wet[depth_index + 1]
        for depth_index in range(depth - 1)
    ]
    inverses, ratios = factorize(couple, depth)
    diagonal = 4.2 + bottom.astype(jnp.float32) / depth
    stacked = jnp.stack([theta * wet, salt * wet, velocity_x, velocity_y, wet])
    padded = with_halo(stacked, ((TROW, 2), (TCOL, 3)), 2)
    theta_mix, salt_mix = forward_state(padded, theta, salt, forcing, wet, inverses, ratios, couple)
    zeta = conjugate(surface_cot, diagonal)
    theta_mu, salt_mu = mixing_adjoint(zeta, wet, theta_cot, salt_cot, inverses, ratios, couple)
    lambdas = with_halo(jnp.stack([theta_mu, salt_mu]), ((TROW, 2), (TCOL, 3)), 2)
    padded_theta_mu = lambdas[0]
    padded_salt_mu = lambdas[1]
    opened = wet[:-1] * wet[1:]
    kappa_grad = -opened * (
        (theta_mu[:-1] - theta_mu[1:]) * (theta_mix[:-1] - theta_mix[1:])
        + (salt_mu[:-1] - salt_mu[1:]) * (salt_mix[:-1] - salt_mix[1:])
    )
    forcing_grad = zeta + wet[0] * theta_mu[0]
    theta_grad = advect_adjoint(padded_theta_mu, padded[2], padded[3], padded[4], theta_mu, wet)
    salt_grad = advect_adjoint(padded_salt_mu, padded[2], padded[3], padded[4], salt_mu, wet)
    return (theta_grad, salt_grad, kappa_grad, forcing_grad)


def solution(mesh):
    split = Mesh(
        mesh.devices.reshape(4, 2, 2, 2, 8), ("trow_0", "trow_1", "trow_2", "tcol_0", "tcol_1")
    )
    return jax.shard_map(
        shards,
        mesh=split,
        in_specs=(
            P(None, TROW, TCOL),
            P(None, TROW, TCOL),
            P(None, TROW, TCOL),
            P(None, TROW, TCOL),
            P(None, TROW, TCOL),
            P(None, TROW, TCOL),
            P(TROW, TCOL),
            P(TROW, TCOL),
            P(None, TROW, TCOL),
            P(None, TROW, TCOL),
            P(TROW, TCOL),
        ),
        out_specs=(P(None, TROW, TCOL), P(None, TROW, TCOL), P(None, TROW, TCOL), P(TROW, TCOL)),
        check_vma=False,
    )
```

profile of v0, /device:TPU:1, one launch (start us, length us, event | category | flops | bytes accessed | tf_op | source)
XLA Modules:
  0.0 312.8 jit_solution(16002799444020555057)
XLA Ops:
  6.9 5.0 %collective-permute-start.16 = (f32[5,25,16,2]{1,2,3,0:T(8,128)}, f32[5,25,16,2]{1,2,3,0:T(8,128)}, u32[]{:S(2)}, u32[]{:S(2)}) collective-permute-start(f32[5,25,16,2]{1,2,3,0:T(8,128)} %copy.300), channel_id=1, source_target_pairs={{0,1},{1,2},{2,3},{3,4},{4,5},{5,6},{6,7},{7,8},{8,9},{9,10},{10,1... | collective-permute-start | bytes 48008 | tf_op jit(solution)/shard_map/ppermute | solution.py:23
  13.3 4.0 %collective-permute-start.3 = (f32[16,1]{1,0:T(8,128)S(1)}, f32[16,1]{1,0:T(8,128)S(1)}, u32[]{:S(2)}, u32[]{:S(2)}) collective-permute-start(f32[16,1]{1,0:T(8,128)S(1)} %get-tuple-element.513), channel_id=1, source_target_pairs={{0,1},{1,2},{2,3},{3,4},{4,5},{5,6},{6,7},{7,8},{8,9},{9,10},{10,1... | collective-permute-start | bytes 200 | tf_op jit(solution)/shard_map/ppermute | solution.py:23
  27.3 9.1 %all-reduce.19 = (f32[]{:T(128)}, f32[]{:T(128)}) all-reduce(f32[]{:T(128)} %get-tuple-element.15, f32[]{:T(128)} %get-tuple-element.14), channel_id=1, replica_groups=mesh['trow_0'=4,'trow_1'=2,'trow_2'=2,'tcol_0'=2,'tcol_1'=8] {'trow_0'}, use_global_device_ids=true, to_apply=%region_1.2 | all-reduce | flops 2 | bytes 16 | tf_op jit(solution)/shard_map/psum | solution.py:36
  36.4 4.4 %all-reduce.31 = (f32[]{:T(128)}, f32[]{:T(128)}) all-reduce(f32[]{:T(128)} %get-tuple-element.30, f32[]{:T(128)} %get-tuple-element.31), channel_id=1, replica_groups=mesh['trow_0'=4,'trow_1'=2,'trow_2'=2,'tcol_0'=2,'tcol_1'=8] {'trow_1'}, use_global_device_ids=true, to_apply=%region_2.3 | all-reduce | flops 2 | bytes 16 | tf_op jit(solution)/shard_map/psum | solution.py:36
  40.8 7.0 %all-reduce.27 = (f32[]{:T(128)}, f32[]{:T(128)}) all-reduce(f32[]{:T(128)} %get-tuple-element.54, f32[]{:T(128)} %get-tuple-element.55), channel_id=1, replica_groups=mesh['trow_0'=4,'trow_1'=2,'trow_2'=2,'tcol_0'=2,'tcol_1'=8] {'trow_2'}, use_global_device_ids=true, to_apply=%region_3.4 | all-reduce | flops 2 | bytes 16 | tf_op jit(solution)/shard_map/psum | solution.py:36
  47.8 8.1 %all-reduce.23 = (f32[]{:T(128)}, f32[]{:T(128)}) all-reduce(f32[]{:T(128)} %get-tuple-element.46, f32[]{:T(128)} %get-tuple-element.47), channel_id=1, replica_groups=mesh['trow_0'=4,'trow_1'=2,'trow_2'=2,'tcol_0'=2,'tcol_1'=8] {'tcol_0'}, use_global_device_ids=true, to_apply=%region_4.5 | all-reduce | flops 2 | bytes 16 | tf_op jit(solution)/shard_map/psum | solution.py:36
  55.9 16.1 %all-reduce.15 = (f32[]{:T(128)}, f32[]{:T(128)}) all-reduce(f32[]{:T(128)} %get-tuple-element.38, f32[]{:T(128)} %get-tuple-element.39), channel_id=1, replica_groups=mesh['trow_0'=4,'trow_1'=2,'trow_2'=2,'tcol_0'=2,'tcol_1'=8] {'tcol_1'}, use_global_device_ids=true, to_apply=%region_5.6 | all-reduce | flops 2 | bytes 16 | tf_op jit(solution)/shard_map/psum | solution.py:36
  73.4 7.1 %collective-permute-start.4 = (f32[1,256]{1,0:T(1,128)S(1)}, f32[1,256]{1,0:T(1,128)S(1)}, u32[]{:S(2)}, u32[]{:S(2)}) collective-permute-start(f32[1,256]{1,0:T(1,128)S(1)} %get-tuple-element.511), channel_id=1, source_target_pairs={{16,0},{32,16},{48,32},{64,48},{80,64},{96,80},{112,96},{128,112},... | collective-permute-start | bytes 3080 | tf_op jit(solution)/shard_map/ppermute | solution.py:24
  83.8 4.0 %collective-permute-start.7 = (f32[16,1]{1,0:T(8,128)S(1)}, f32[16,1]{1,0:T(8,128)S(1)}, u32[]{:S(2)}, u32[]{:S(2)}) collective-permute-start(f32[16,1]{1,0:T(8,128)S(1)} %get-tuple-element.509), channel_id=1, source_target_pairs={{0,1},{1,2},{2,3},{3,4},{4,5},{5,6},{6,7},{7,8},{8,9},{9,10},{10,1... | collective-permute-start | bytes 200 | tf_op jit(solution)/shard_map/ppermute | solution.py:23
  89.3 6.7 %all-reduce.18 = (f32[]{:T(128)}, f32[]{:T(128)}) all-reduce(f32[]{:T(128)} %get-tuple-element.13, f32[]{:T(128)} %get-tuple-element.12), channel_id=1, replica_groups=mesh['trow_0'=4,'trow_1'=2,'trow_2'=2,'tcol_0'=2,'tcol_1'=8] {'trow_0'}, use_global_device_ids=true, to_apply=%region_13.14 | all-reduce | flops 2 | bytes 16 | tf_op jit(solution)/shard_map/psum | solution.py:36
  96.0 4.5 %all-reduce.30 = (f32[]{:T(128)}, f32[]{:T(128)}) all-reduce(f32[]{:T(128)} %get-tuple-element.28, f32[]{:T(128)} %get-tuple-element.29), channel_id=1, replica_groups=mesh['trow_0'=4,'trow_1'=2,'trow_2'=2,'tcol_0'=2,'tcol_1'=8] {'trow_1'}, use_global_device_ids=true, to_apply=%region_14.15 | all-reduce | flops 2 | bytes 16 | tf_op jit(solution)/shard_map/psum | solution.py:36
  100.4 7.3 %all-reduce.26 = (f32[]{:T(128)}, f32[]{:T(128)}) all-reduce(f32[]{:T(128)} %get-tuple-element.52, f32[]{:T(128)} %get-tuple-element.53), channel_id=1, replica_groups=mesh['trow_0'=4,'trow_1'=2,'trow_2'=2,'tcol_0'=2,'tcol_1'=8] {'trow_2'}, use_global_device_ids=true, to_apply=%region_15.16 | all-reduce | flops 2 | bytes 16 | tf_op jit(solution)/shard_map/psum | solution.py:36
  107.7 9.3 %all-reduce.22 = (f32[]{:T(128)}, f32[]{:T(128)}) all-reduce(f32[]{:T(128)} %get-tuple-element.44, f32[]{:T(128)} %get-tuple-element.45), channel_id=1, replica_groups=mesh['trow_0'=4,'trow_1'=2,'trow_2'=2,'tcol_0'=2,'tcol_1'=8] {'tcol_0'}, use_global_device_ids=true, to_apply=%region_16.17 | all-reduce | flops 2 | bytes 16 | tf_op jit(solution)/shard_map/psum | solution.py:36
  117.0 11.4 %all-reduce.14 = (f32[]{:T(128)}, f32[]{:T(128)}) all-reduce(f32[]{:T(128)} %get-tuple-element.36, f32[]{:T(128)} %get-tuple-element.37), channel_id=1, replica_groups=mesh['trow_0'=4,'trow_1'=2,'trow_2'=2,'tcol_0'=2,'tcol_1'=8] {'tcol_1'}, use_global_device_ids=true, to_apply=%region_17.18 | all-reduce | flops 2 | bytes 16 | tf_op jit(solution)/shard_map/psum | solution.py:36
  133.0 6.9 %collective-permute-start.8 = (f32[1,256]{1,0:T(1,128)S(1)}, f32[1,256]{1,0:T(1,128)S(1)}, u32[]{:S(2)}, u32[]{:S(2)}) collective-permute-start(f32[1,256]{1,0:T(1,128)S(1)} %get-tuple-element.507), channel_id=1, source_target_pairs={{16,0},{32,16},{48,32},{64,48},{80,64},{96,80},{112,96},{128,112},... | collective-permute-start | bytes 3080 | tf_op jit(solution)/shard_map/ppermute | solution.py:24
  143.2 4.0 %collective-permute-start.11 = (f32[16,1]{1,0:T(8,128)S(1)}, f32[16,1]{1,0:T(8,128)S(1)}, u32[]{:S(2)}, u32[]{:S(2)}) collective-permute-start(f32[16,1]{1,0:T(8,128)S(1)} %get-tuple-element.505), channel_id=1, source_target_pairs={{0,1},{1,2},{2,3},{3,4},{4,5},{5,6},{6,7},{7,8},{8,9},{9,10},{10,1... | collective-permute-start | bytes 200 | tf_op jit(solution)/shard_map/ppermute | solution.py:23
  148.7 8.3 %all-reduce.17 = (f32[]{:T(128)}, f32[]{:T(128)}) all-reduce(f32[]{:T(128)} %get-tuple-element.11, f32[]{:T(128)} %get-tuple-element.10), channel_id=1, replica_groups=mesh['trow_0'=4,'trow_1'=2,'trow_2'=2,'tcol_0'=2,'tcol_1'=8] {'trow_0'}, use_global_device_ids=true, to_apply=%region_25.26 | all-reduce | flops 2 | bytes 16 | tf_op jit(solution)/shard_map/psum | solution.py:36
  157.0 4.4 %all-reduce.29 = (f32[]{:T(128)}, f32[]{:T(128)}) all-reduce(f32[]{:T(128)} %get-tuple-element.26, f32[]{:T(128)} %get-tuple-element.27), channel_id=1, replica_groups=mesh['trow_0'=4,'trow_1'=2,'trow_2'=2,'tcol_0'=2,'tcol_1'=8] {'trow_1'}, use_global_device_ids=true, to_apply=%region_26.27 | all-reduce | flops 2 | bytes 16 | tf_op jit(solution)/shard_map/psum | solution.py:36
  161.4 7.5 %all-reduce.25 = (f32[]{:T(128)}, f32[]{:T(128)}) all-reduce(f32[]{:T(128)} %get-tuple-element.50, f32[]{:T(128)} %get-tuple-element.51), channel_id=1, replica_groups=mesh['trow_0'=4,'trow_1'=2,'trow_2'=2,'tcol_0'=2,'tcol_1'=8] {'trow_2'}, use_global_device_ids=true, to_apply=%region_27.28 | all-reduce | flops 2 | bytes 16 | tf_op jit(solution)/shard_map/psum | solution.py:36
  168.9 11.2 %all-reduce.21 = (f32[]{:T(128)}, f32[]{:T(128)}) all-reduce(f32[]{:T(128)} %get-tuple-element.42, f32[]{:T(128)} %get-tuple-element.43), channel_id=1, replica_groups=mesh['trow_0'=4,'trow_1'=2,'trow_2'=2,'tcol_0'=2,'tcol_1'=8] {'tcol_0'}, use_global_device_ids=true, to_apply=%region_28.29 | all-reduce | flops 2 | bytes 16 | tf_op jit(solution)/shard_map/psum | solution.py:36
  180.1 11.3 %all-reduce.13 = (f32[]{:T(128)}, f32[]{:T(128)}) all-reduce(f32[]{:T(128)} %get-tuple-element.34, f32[]{:T(128)} %get-tuple-element.35), channel_id=1, replica_groups=mesh['trow_0'=4,'trow_1'=2,'trow_2'=2,'tcol_0'=2,'tcol_1'=8] {'tcol_1'}, use_global_device_ids=true, to_apply=%region_29.30 | all-reduce | flops 2 | bytes 16 | tf_op jit(solution)/shard_map/psum | solution.py:36
  195.5 6.9 %collective-permute-start.12 = (f32[1,256]{1,0:T(1,128)S(1)}, f32[1,256]{1,0:T(1,128)S(1)}, u32[]{:S(2)}, u32[]{:S(2)}) collective-permute-start(f32[1,256]{1,0:T(1,128)S(1)} %get-tuple-element.503), channel_id=1, source_target_pairs={{16,0},{32,16},{48,32},{64,48},{80,64},{96,80},{112,96},{128,112},... | collective-permute-start | bytes 3080 | tf_op jit(solution)/shard_map/ppermute | solution.py:24
  205.7 4.0 %collective-permute-start.15 = (f32[16,1]{1,0:T(8,128)S(1)}, f32[16,1]{1,0:T(8,128)S(1)}, u32[]{:S(2)}, u32[]{:S(2)}) collective-permute-start(f32[16,1]{1,0:T(8,128)S(1)} %get-tuple-element.501), channel_id=1, source_target_pairs={{0,1},{1,2},{2,3},{3,4},{4,5},{5,6},{6,7},{7,8},{8,9},{9,10},{10,1... | collective-permute-start | bytes 200 | tf_op jit(solution)/shard_map/ppermute | solution.py:23
  216.7 6.6 %all-reduce.16 = (f32[]{:T(128)}, f32[]{:T(128)}) all-reduce(f32[]{:T(128)} %get-tuple-element.9, f32[]{:T(128)} %get-tuple-element.8), channel_id=1, replica_groups=mesh['trow_0'=4,'trow_1'=2,'trow_2'=2,'tcol_0'=2,'tcol_1'=8] {'trow_0'}, use_global_device_ids=true, to_apply=%region_37.38 | all-reduce | flops 2 | bytes 16 | tf_op jit(solution)/shard_map/psum | solution.py:36
  223.4 4.4 %all-reduce.28 = (f32[]{:T(128)}, f32[]{:T(128)}) all-reduce(f32[]{:T(128)} %get-tuple-element.24, f32[]{:T(128)} %get-tuple-element.25), channel_id=1, replica_groups=mesh['trow_0'=4,'trow_1'=2,'trow_2'=2,'tcol_0'=2,'tcol_1'=8] {'trow_1'}, use_global_device_ids=true, to_apply=%region_38.39 | all-reduce | flops 2 | bytes 16 | tf_op jit(solution)/shard_map/psum | solution.py:36
  227.8 8.2 %all-reduce.24 = (f32[]{:T(128)}, f32[]{:T(128)}) all-reduce(f32[]{:T(128)} %get-tuple-element.48, f32[]{:T(128)} %get-tuple-element.49), channel_id=1, replica_groups=mesh['trow_0'=4,'trow_1'=2,'trow_2'=2,'tcol_0'=2,'tcol_1'=8] {'trow_2'}, use_global_device_ids=true, to_apply=%region_39.40 | all-reduce | flops 2 | bytes 16 | tf_op jit(solution)/shard_map/psum | solution.py:36
  235.9 11.5 %all-reduce.20 = (f32[]{:T(128)}, f32[]{:T(128)}) all-reduce(f32[]{:T(128)} %get-tuple-element.40, f32[]{:T(128)} %get-tuple-element.41), channel_id=1, replica_groups=mesh['trow_0'=4,'trow_1'=2,'trow_2'=2,'tcol_0'=2,'tcol_1'=8] {'tcol_0'}, use_global_device_ids=true, to_apply=%region_40.41 | all-reduce | flops 2 | bytes 16 | tf_op jit(solution)/shard_map/psum | solution.py:36
  247.5 11.5 %all-reduce.12 = (f32[]{:T(128)}, f32[]{:T(128)}) all-reduce(f32[]{:T(128)} %get-tuple-element.32, f32[]{:T(128)} %get-tuple-element.33), channel_id=1, replica_groups=mesh['trow_0'=4,'trow_1'=2,'trow_2'=2,'tcol_0'=2,'tcol_1'=8] {'tcol_1'}, use_global_device_ids=true, to_apply=%region_41.42 | all-reduce | flops 2 | bytes 16 | tf_op jit(solution)/shard_map/psum | solution.py:36
  269.9 4.5 %select_maximum_fusion = f32[5,25,20,260]{3,2,1,0:T(8,128)S(1)} fusion(f32[5,25,16,2]{3,2,1,0:T(8,128)} %copy.303, f32[5,25,16,2]{3,2,1,0:T(8,128)S(1)} %copy.301, f32[5,25,2,256]{3,2,1,0:T(2,128)} %collective-permute-done.18, f32[5,25,16,256]{3,2,1,0:T(8,128)S(1)} %constant_dynamic-update-slice_fusion.25, f32[5,25,2,256]{3,2,1,0:T(2,128)} %collective-permute-done.17), kind=kLoop, calls=%fused_computation | loop fusion | flops 5200000 | bytes 5192000 | tf_op jit(solution)/shard_map/concatenate | solution.py:30
  283.0 6.7 %collective-permute-start.21 = (f32[2,25,2,256]{3,2,1,0:T(2,128)S(1)}, f32[2,25,2,256]{3,2,1,0:T(2,128)S(1)}, u32[]{:S(2)}, u32[]{:S(2)}) collective-permute-start(f32[2,25,2,256]{3,2,1,0:T(2,128)S(1)} %get-tuple-element.340), channel_id=1, source_target_pairs={{0,16},{16,32},{32,48},{48,64},{64,80},{80,96},{96,112},{112,128},... | collective-permute-start | bytes 307208 | tf_op jit(solution)/shard_map/ppermute | solution.py:23
  297.3 6.5 %collective-permute-done.20 = f32[2,25,16,2]{3,2,1,0:T(8,128)S(1)} collective-permute-done((f32[2,25,16,2]{3,2,1,0:T(8,128)S(1)}, f32[2,25,16,2]{3,2,1,0:T(8,128)S(1)}, u32[]{:S(2)}, u32[]{:S(2)}) %collective-permute-start.20) | collective-permute-done | bytes 6432 | tf_op jit(solution)/shard_map/ppermute | solution.py:23
  303.7 4.1 %collective-permute-done.23 = f32[2,25,16,2]{3,2,1,0:T(8,128)S(1)} collective-permute-done((f32[2,25,16,2]{3,2,1,0:T(8,128)S(1)}, f32[2,25,16,2]{3,2,1,0:T(8,128)S(1)}, u32[]{:S(2)}, u32[]{:S(2)}) %collective-permute-start.23) | collective-permute-done | bytes 6432 | tf_op jit(solution)/shard_map/ppermute | solution.py:24
  (251 shorter events, 64.3 us)
Async XLA Ops:
  0.6 2.4 copy-start.8
  0.6 2.4 copy-start.9
  3.1 8.8 %copy-start.10 = (f32[16,256]{1,0:T(8,128)S(1)}, f32[16,256]{1,0:T(8,128)}, u32[]{:S(2)}) copy-start(f32[16,256]{1,0:T(8,128)} %param.21) | copy-start | bytes 49156
  4.5 22.1 %copy-start.7 = (s32[16,256]{1,0:T(8,128)S(1)}, s32[16,256]{1,0:T(8,128)}, u32[]{:S(2)}) copy-start(s32[16,256]{1,0:T(8,128)} %param.18) | copy-start | bytes 49156
  6.9 259.0 %collective-permute-start.16 = (f32[5,25,16,2]{1,2,3,0:T(8,128)}, f32[5,25,16,2]{1,2,3,0:T(8,128)}, u32[]{:S(2)}, u32[]{:S(2)}) collective-permute-start(f32[5,25,16,2]{1,2,3,0:T(8,128)} %copy.300), channel_id=1, source_target_pairs={{0,1},{1,2},{2,3},{3,4},{4,5},{5,6},{6,7},{7,8},{8,9},{9,10},{10,1... | collective-permute-start | bytes 48008 | tf_op jit(solution)/shard_map/ppermute | solution.py:23
  12.0 14.6 %collective-permute-start.2 = (f32[16,1]{1,0:T(8,128)S(1)}, f32[16,1]{1,0:T(8,128)S(1)}, u32[]{:S(2)}, u32[]{:S(2)}) collective-permute-start(f32[16,1]{1,0:T(8,128)S(1)} %get-tuple-element.512), channel_id=1, source_target_pairs={{1,0},{2,1},{3,2},{4,3},{5,4},{6,5},{7,6},{8,7},{9,8},{10,9},{11,1... | collective-permute-start | bytes 200 | tf_op jit(solution)/shard_map/ppermute | solution.py:24
  13.3 13.3 %collective-permute-start.3 = (f32[16,1]{1,0:T(8,128)S(1)}, f32[16,1]{1,0:T(8,128)S(1)}, u32[]{:S(2)}, u32[]{:S(2)}) collective-permute-start(f32[16,1]{1,0:T(8,128)S(1)} %get-tuple-element.513), channel_id=1, source_target_pairs={{0,1},{1,2},{2,3},{3,4},{4,5},{5,6},{6,7},{7,8},{8,9},{9,10},{10,1... | collective-permute-start | bytes 200 | tf_op jit(solution)/shard_map/ppermute | solution.py:23
  17.9 8.7 %collective-permute-start = (f32[1,256]{1,0:T(1,128)}, f32[1,256]{1,0:T(1,128)S(1)}, u32[]{:S(2)}, u32[]{:S(2)}) collective-permute-start(f32[1,256]{1,0:T(1,128)} %get-tuple-element.515), channel_id=1, source_target_pairs={{16,0},{32,16},{48,32},{64,48},{80,64},{96,80},{112,96},{128,112},... | collective-permute-start | bytes 3080 | tf_op jit(solution)/shard_map/ppermute | solution.py:24
  21.3 5.3 %collective-permute-start.1 = (f32[1,256]{1,0:T(1,128)}, f32[1,256]{1,0:T(1,128)S(1)}, u32[]{:S(2)}, u32[]{:S(2)}) collective-permute-start(f32[1,256]{1,0:T(1,128)} %get-tuple-element.514), channel_id=1, source_target_pairs={{0,16},{16,32},{32,48},{48,64},{64,80},{80,96},{96,112},{112,128},... | collective-permute-start | bytes 3080 | tf_op jit(solution)/shard_map/ppermute | solution.py:23
  26.6 238.4 %copy-start.5 = (f32[24,16,256]{2,1,0:T(8,128)S(1)}, f32[24,16,256]{2,1,0:T(8,128)}, u32[]{:S(2)}) copy-start(f32[24,16,256]{2,1,0:T(8,128)} %param.16) | copy-start | bytes 1179652
  73.4 15.2 %collective-permute-start.4 = (f32[1,256]{1,0:T(1,128)S(1)}, f32[1,256]{1,0:T(1,128)S(1)}, u32[]{:S(2)}, u32[]{:S(2)}) collective-permute-start(f32[1,256]{1,0:T(1,128)S(1)} %get-tuple-element.511), channel_id=1, source_target_pairs={{16,0},{32,16},{48,32},{64,48},{80,64},{96,80},{112,96},{128,112},... | collective-permute-start | bytes 3080 | tf_op jit(solution)/shard_map/ppermute | solution.py:24
  80.5 8.1 %collective-permute-start.5 = (f32[1,256]{1,0:T(1,128)S(1)}, f32[1,256]{1,0:T(1,128)S(1)}, u32[]{:S(2)}, u32[]{:S(2)}) collective-permute-start(f32[1,256]{1,0:T(1,128)S(1)} %get-tuple-element.510), channel_id=1, source_target_pairs={{0,16},{16,32},{32,48},{48,64},{64,80},{80,96},{96,112},{112,128},... | collective-permute-start | bytes 3080 | tf_op jit(solution)/shard_map/ppermute | solution.py:23
  82.5 5.3 %collective-permute-start.6 = (f32[16,1]{1,0:T(8,128)S(1)}, f32[16,1]{1,0:T(8,128)S(1)}, u32[]{:S(2)}, u32[]{:S(2)}) collective-permute-start(f32[16,1]{1,0:T(8,128)S(1)} %get-tuple-element.508), channel_id=1, source_target_pairs={{1,0},{2,1},{3,2},{4,3},{5,4},{6,5},{7,6},{8,7},{9,8},{10,9},{11,1... | collective-permute-start | bytes 200 | tf_op jit(solution)/shard_map/ppermute | solution.py:24
  83.8 4.8 %collective-permute-start.7 = (f32[16,1]{1,0:T(8,128)S(1)}, f32[16,1]{1,0:T(8,128)S(1)}, u32[]{:S(2)}, u32[]{:S(2)}) collective-permute-start(f32[16,1]{1,0:T(8,128)S(1)} %get-tuple-element.509), channel_id=1, source_target_pairs={{0,1},{1,2},{2,3},{3,4},{4,5},{5,6},{6,7},{7,8},{8,9},{9,10},{10,1... | collective-permute-start | bytes 200 | tf_op jit(solution)/shard_map/ppermute | solution.py:23
  133.0 15.0 %collective-permute-start.8 = (f32[1,256]{1,0:T(1,128)S(1)}, f32[1,256]{1,0:T(1,128)S(1)}, u32[]{:S(2)}, u32[]{:S(2)}) collective-permute-start(f32[1,256]{1,0:T(1,128)S(1)} %get-tuple-element.507), channel_id=1, source_target_pairs={{16,0},{32,16},{48,32},{64,48},{80,64},{96,80},{112,96},{128,112},... | collective-permute-start | bytes 3080 | tf_op jit(solution)/shard_map/ppermute | solution.py:24
  139.9 8.1 %collective-permute-start.9 = (f32[1,256]{1,0:T(1,128)S(1)}, f32[1,256]{1,0:T(1,128)S(1)}, u32[]{:S(2)}, u32[]{:S(2)}) collective-permute-start(f32[1,256]{1,0:T(1,128)S(1)} %get-tuple-element.506), channel_id=1, source_target_pairs={{0,16},{16,32},{32,48},{48,64},{64,80},{80,96},{96,112},{112,128},... | collective-permute-start | bytes 3080 | tf_op jit(solution)/shard_map/ppermute | solution.py:23
  141.9 5.3 %collective-permute-start.10 = (f32[16,1]{1,0:T(8,128)S(1)}, f32[16,1]{1,0:T(8,128)S(1)}, u32[]{:S(2)}, u32[]{:S(2)}) collective-permute-start(f32[16,1]{1,0:T(8,128)S(1)} %get-tuple-element.504), channel_id=1, source_target_pairs={{1,0},{2,1},{3,2},{4,3},{5,4},{6,5},{7,6},{8,7},{9,8},{10,9},{11,1... | collective-permute-start | bytes 200 | tf_op jit(solution)/shard_map/ppermute | solution.py:24
  143.2 4.8 %collective-permute-start.11 = (f32[16,1]{1,0:T(8,128)S(1)}, f32[16,1]{1,0:T(8,128)S(1)}, u32[]{:S(2)}, u32[]{:S(2)}) collective-permute-start(f32[16,1]{1,0:T(8,128)S(1)} %get-tuple-element.505), channel_id=1, source_target_pairs={{0,1},{1,2},{2,3},{3,4},{4,5},{5,6},{6,7},{7,8},{8,9},{9,10},{10,1... | collective-permute-start | bytes 200 | tf_op jit(solution)/shard_map/ppermute | solution.py:23
  195.5 18.1 %collective-permute-start.12 = (f32[1,256]{1,0:T(1,128)S(1)}, f32[1,256]{1,0:T(1,128)S(1)}, u32[]{:S(2)}, u32[]{:S(2)}) collective-permute-start(f32[1,256]{1,0:T(1,128)S(1)} %get-tuple-element.503), channel_id=1, source_target_pairs={{16,0},{32,16},{48,32},{64,48},{80,64},{96,80},{112,96},{128,112},... | collective-permute-start | bytes 3080 | tf_op jit(solution)/shard_map/ppermute | solution.py:24
  202.4 13.6 %collective-permute-start.13 = (f32[1,256]{1,0:T(1,128)S(1)}, f32[1,256]{1,0:T(1,128)S(1)}, u32[]{:S(2)}, u32[]{:S(2)}) collective-permute-start(f32[1,256]{1,0:T(1,128)S(1)} %get-tuple-element.502), channel_id=1, source_target_pairs={{0,16},{16,32},{32,48},{48,64},{64,80},{80,96},{96,112},{112,128},... | collective-permute-start | bytes 3080 | tf_op jit(solution)/shard_map/ppermute | solution.py:23
  204.4 5.3 %collective-permute-start.14 = (f32[16,1]{1,0:T(8,128)S(1)}, f32[16,1]{1,0:T(8,128)S(1)}, u32[]{:S(2)}, u32[]{:S(2)}) collective-permute-start(f32[16,1]{1,0:T(8,128)S(1)} %get-tuple-element.500), channel_id=1, source_target_pairs={{1,0},{2,1},{3,2},{4,3},{5,4},{6,5},{7,6},{8,7},{9,8},{10,9},{11,1... | collective-permute-start | bytes 200 | tf_op jit(solution)/shard_map/ppermute | solution.py:24
  205.7 5.3 %collective-permute-start.15 = (f32[16,1]{1,0:T(8,128)S(1)}, f32[16,1]{1,0:T(8,128)S(1)}, u32[]{:S(2)}, u32[]{:S(2)}) collective-permute-start(f32[16,1]{1,0:T(8,128)S(1)} %get-tuple-element.501), channel_id=1, source_target_pairs={{0,1},{1,2},{2,3},{3,4},{4,5},{5,6},{6,7},{7,8},{8,9},{9,10},{10,1... | collective-permute-start | bytes 200 | tf_op jit(solution)/shard_map/ppermute | solution.py:23
  209.7 57.7 %collective-permute-start.19 = (f32[5,25,16,2]{1,2,3,0:T(8,128)}, f32[5,25,16,2]{1,2,3,0:T(8,128)}, u32[]{:S(2)}, u32[]{:S(2)}) collective-permute-start(f32[5,25,16,2]{1,2,3,0:T(8,128)} %copy.302), channel_id=1, source_target_pairs={{1,0},{2,1},{3,2},{4,3},{5,4},{6,5},{7,6},{8,7},{9,8},{10,9},{11,1... | collective-permute-start | bytes 48008 | tf_op jit(solution)/shard_map/ppermute | solution.py:24
  211.0 58.9 %collective-permute-start.17 = (f32[5,25,2,256]{3,2,1,0:T(2,128)}, f32[5,25,2,256]{3,2,1,0:T(2,128)}, u32[]{:S(2)}, u32[]{:S(2)}) collective-permute-start(f32[5,25,2,256]{3,2,1,0:T(2,128)} %get-tuple-element.326), channel_id=1, source_target_pairs={{0,16},{16,32},{32,48},{48,64},{64,80},{80,96},{96,112},{112,128},... | collective-permute-start | bytes 768008 | tf_op jit(solution)/shard_map/ppermute | solution.py:23
  213.6 56.3 %collective-permute-start.18 = (f32[5,25,2,256]{3,2,1,0:T(2,128)}, f32[5,25,2,256]{3,2,1,0:T(2,128)}, u32[]{:S(2)}, u32[]{:S(2)}) collective-permute-start(f32[5,25,2,256]{3,2,1,0:T(2,128)} %get-tuple-element.327), channel_id=1, source_target_pairs={{16,0},{32,16},{48,32},{64,48},{80,64},{96,80},{112,96},{128,112},... | collective-permute-start | bytes 768008 | tf_op jit(solution)/shard_map/ppermute | solution.py:24
  276.6 1.6 copy-start.3
  276.6 1.6 copy-start.4
  278.8 1.0 copy-start.2
  283.0 24.8 %collective-permute-start.21 = (f32[2,25,2,256]{3,2,1,0:T(2,128)S(1)}, f32[2,25,2,256]{3,2,1,0:T(2,128)S(1)}, u32[]{:S(2)}, u32[]{:S(2)}) collective-permute-start(f32[2,25,2,256]{3,2,1,0:T(2,128)S(1)} %get-tuple-element.340), channel_id=1, source_target_pairs={{0,16},{16,32},{32,48},{48,64},{64,80},{80,96},{96,112},{112,128},... | collective-permute-start | bytes 307208 | tf_op jit(solution)/shard_map/ppermute | solution.py:23
  289.8 18.1 %collective-permute-start.22 = (f32[2,25,2,256]{3,2,1,0:T(2,128)S(1)}, f32[2,25,2,256]{3,2,1,0:T(2,128)S(1)}, u32[]{:S(2)}, u32[]{:S(2)}) collective-permute-start(f32[2,25,2,256]{3,2,1,0:T(2,128)S(1)} %get-tuple-element.341), channel_id=1, source_target_pairs={{16,0},{32,16},{48,32},{64,48},{80,64},{96,80},{112,96},{128,112},... | collective-permute-start | bytes 307208 | tf_op jit(solution)/shard_map/ppermute | solution.py:24
  291.7 12.0 %collective-permute-start.20 = (f32[2,25,16,2]{3,2,1,0:T(8,128)S(1)}, f32[2,25,16,2]{3,2,1,0:T(8,128)S(1)}, u32[]{:S(2)}, u32[]{:S(2)}) collective-permute-start(f32[2,25,16,2]{3,2,1,0:T(8,128)S(1)} %get-tuple-element.342), channel_id=1, source_target_pairs={{0,1},{1,2},{2,3},{3,4},{4,5},{5,6},{6,7},{7,8},{8,9},{9,10},{10,1... | collective-permute-start | bytes 19208 | tf_op jit(solution)/shard_map/ppermute | solution.py:23
  294.6 13.3 %collective-permute-start.23 = (f32[2,25,16,2]{3,2,1,0:T(8,128)S(1)}, f32[2,25,16,2]{3,2,1,0:T(8,128)S(1)}, u32[]{:S(2)}, u32[]{:S(2)}) collective-permute-start(f32[2,25,16,2]{3,2,1,0:T(8,128)S(1)} %get-tuple-element.343), channel_id=1, source_target_pairs={{1,0},{2,1},{3,2},{4,3},{5,4},{6,5},{7,6},{8,7},{9,8},{10,9},{11,1... | collective-permute-start | bytes 19208 | tf_op jit(solution)/shard_map/ppermute | solution.py:24
  (4 other events, 4.0 us)
where the time goes:
time: 316 us; the launch traced here: 313 us
  blocking collectives  169 us (53%)
  starting transfers between devices  78.6 us (25%)
  other arithmetic  24.1 us (8%)
  between operations  16.1 us (5%)
  local copies, waits for them, and re-layouts  13.1 us (4%)
  waiting for transfers between devices  12.1 us (4%)
    psum x20, blocking collectives, over_axes(): return functools.reduce(lax.psum, axes, array)  169 us
    ppermute x12, starting transfers between devices, with_halo(): lax.ppermute(last, axis, up)  42 us
    ppermute x12, starting transfers between devices, with_halo(): lax.ppermute(leading, axis, [(b, a) for a, b in up])  36.6 us
    ppermute x12, waiting for transfers between devices, with_halo(): lax.ppermute(last, axis, up)  8.02 us
  transfers between devices with their start and end apart: 24, of which 4 were waited for; matrix products, arithmetic and copies ran while one was open for 5% of the time, Pallas kernels for 0%

commit v1 on v0

v1 whole, which is shorter than its diff:
```python
import functools

import jax
import jax.numpy as jnp
from jax import lax
from jax.experimental import pallas as pl
from jax.experimental.pallas import tpu as pltpu
from jax.sharding import Mesh
from jax.sharding import PartitionSpec as P

TROW = ("trow_0", "trow_1", "trow_2")
TCOL = ("tcol_0", "tcol_1")
ALL = TROW + TCOL
CENTRE = 4.75
KRYLOV = 4
PAIRS = [(i, j) for i in range(KRYLOV) for j in range(i, KRYLOV)]
F32 = jnp.float32
VM = pl.BlockSpec(memory_space=pltpu.VMEM)
SM = pl.BlockSpec(memory_space=pltpu.SMEM)
PARAMS = pltpu.CompilerParams(vmem_limit_bytes=24 * 1024 * 1024)


def iota(shape, dim):
    return lax.broadcasted_iota(jnp.int32, shape, dim)


def two_sum(a, b):
    s = a + b
    t = s - a
    return s, (a - (s - t)) + (b - t)


def quick_two_sum(a, b):
    s = a + b
    return s, b - (s - a)


def halves(a):
    t = a * 4097.0
    high = t - (t - a)
    return high, a - high


def two_prod(a, b, a_parts, b_parts):
    p = a * b
    ah, al = a_parts
    bh, bl = b_parts
    return p, ((ah * bh - p) + ah * bl + al * bh) + al * bl


def df_add(a, b):
    s, e = two_sum(a[0], b[0])
    return quick_two_sum(s, e + (a[1] + b[1]))


def df_mul(a, b):
    p, e = two_prod(a[0], b[0], halves(a[0]), halves(b[0]))
    return quick_two_sum(p, e + (a[0] * b[1] + a[1] * b[0]))


def df_div(a, b):
    inverse = 1.0 / b[0]
    q1 = a[0] * inverse
    back = df_mul((q1, jnp.zeros_like(q1)), b)
    rest = df_add(a, (-back[0], -back[1]))
    return quick_two_sum(q1, rest[0] * inverse)


def edges_kernel(cot_ref, bottom_ref, rows_ref, cols_ref, corner_ref):
    cot = cot_ref[...]
    bottom = bottom_ref[...].astype(F32)
    rows_ref[0:8] = cot[8:16]
    rows_ref[8:16] = bottom[8:16]
    cols_ref[0:16] = cot[:, 128:256]
    cols_ref[16:32] = bottom[:, 128:256]
    corner_ref[0:8] = cot[8:16, 128:256]
    corner_ref[8:16] = bottom[8:16, 128:256]


def merge_rows(a, b, step):
    shape = a[0].shape
    first = (iota(shape, 0) & step) == 0

    def part(x, y):
        mixed = jnp.where(first, y, x)
        if step == 4:
            other = pltpu.roll(mixed, 4, 0)
        else:
            other = jnp.where(first, pltpu.roll(mixed, 8 - step, 0), pltpu.roll(mixed, step, 0))
        return jnp.where(first, x, y), other

    kept_high, other_high = part(a[0], b[0])
    kept_low, other_low = part(a[1], b[1])
    return df_add((kept_high, kept_low), (other_high, other_low))


def krylov_kernel(
    place_ref, cot_ref, bottom_ref, rows_ref, cols_ref, corner_ref, sums_ref, own_ref, up_ref, left_ref, diag_ref
):
    r = place_ref[0]
    c = place_ref[1]
    shape = (24, 384)
    row = iota(shape, 0)
    lane = iota(shape, 1)

    def window(main, at):
        top = jnp.concatenate([corner_ref[8 * at : 8 * at + 8], rows_ref[8 * at : 8 * at + 8]], axis=1)
        rest = jnp.concatenate([cols_ref[16 * at : 16 * at + 16], main], axis=1)
        return jnp.concatenate([top, rest], axis=0)

    inside = ((row >= 8) | (r > 0)) & ((lane >= 128) | (c > 0))
    start = jnp.where(inside, window(cot_ref[...], 0), 0.0)
    bottom = window(bottom_ref[...].astype(F32), 1)
    shifted = (4.2 + bottom / 25.0) - CENTRE

    def apply_shifted(v):
        below = jnp.where(row == 23, 0.0, pltpu.roll(v, 23, 0))
        right = jnp.where(lane == 383, 0.0, pltpu.roll(v, 383, 1))
        beside = below + pltpu.roll(v, 1, 0) + right + pltpu.roll(v, 1, 1)
        return jnp.where(inside, shifted * v - beside, 0.0)

    vectors = [start]
    images = []
    for step in range(KRYLOV):
        moved = apply_shifted(vectors[-1])
        images.append(moved + CENTRE * vectors[-1])
        if step == 0:
            vectors.append(moved * 0.25)
        elif step + 1 < KRYLOV:
            vectors.append(moved * 0.5 - vectors[-2])

    domain = (
        (row >= 4)
        & (row < jnp.where(r == 15, 24, 20))
        & (lane >= 124)
        & (lane < jnp.where(c == 15, 384, 380))
    )
    cut = [jnp.where(domain, v, 0.0) for v in vectors]
    cut_parts = [halves(v) for v in cut]
    image_parts = [halves(w) for w in images]

    def tile(x, at):
        i, j = divmod(at, 3)
        return x[8 * i : 8 * i + 8, 128 * j : 128 * j + 128]

    def dot(x, x_parts, y, y_parts):
        total = None
        for at in range(9):
            p, e = two_prod(
                tile(x, at),
                tile(y, at),
                [tile(h, at) for h in x_parts],
                [tile(h, at) for h in y_parts],
            )
            if total is None:
                total = (p, e)
            else:
                s, f = two_sum(total[0], p)
                total = (s, total[1] + (e + f))
        return total

    dots = [dot(cut[i], cut_parts[i], images[j], image_parts[j]) for i, j in PAIRS]
    start_parts = halves(start)
    dots += [dot(cut[i], cut_parts[i], start, start_parts) for i in range(KRYLOV)]
    zero = jnp.zeros((8, 128), F32)
    dots += [(zero, zero)] * (16 - len(dots))
    packed = []
    for base in (0, 8):
        group = dots[base : base + 8]
        for step in (4, 2, 1):
            group = [merge_rows(group[i], group[i + step], step) for i in range(step)]
        total = group[0]
        for step in (64, 32, 16, 8, 4, 2, 1):
            total = df_add(total, (pltpu.roll(total[0], step, 1), pltpu.roll(total[1], step, 1)))
        packed.append(total)
    small_row = iota((8, 128), 0)
    small_lane = iota((8, 128), 1)
    spread = zero
    for part in (0, 1):
        for base in (0, 1):
            chosen = jnp.zeros((8, 128), jnp.bool_)
            for i in range(KRYLOV):
                for j in range(KRYLOV + 1):
                    index = len(PAIRS) + i if j == KRYLOV else PAIRS.index((min(i, j), max(i, j)))
                    if index // 8 == base:
                        chosen = chosen | (
                            (small_row == index % 8) & (small_lane == 32 * part + 8 * i + j)
                        )
            spread = spread + jnp.where(chosen, packed[base][part], 0.0)
    line = jnp.sum(spread, axis=0, keepdims=True)
    sums_ref[...] = jnp.broadcast_to(line, (256, 128))

    for k, v in enumerate(vectors):
        own_ref[24 * k : 24 * k + 24] = v
        near = pltpu.roll(v[0:16], 12, 0)[0:8]
        up_ref[8 * k : 8 * k + 8] = near
        left_ref[24 * k : 24 * k + 24] = pltpu.roll(v[:, 0:256], 192, 1)[:, 0:128]
        diag_ref[8 * k : 8 * k + 8] = pltpu.roll(near[:, 0:256], 192, 1)[:, 0:128]


def columns_kernel(
    theta_ref,
    salt_ref,
    ux_ref,
    uy_ref,
    land_ref,
    kappa_ref,
    bottom_ref,
    tcot_ref,
    scot_ref,
    a_ref,
    c_ref,
    w_ref,
    inv_ref,
    ratio_ref,
    down_ref,
    up_ref,
    right_ref,
    left_ref,
):
    depth = theta_ref.shape[0]
    bottom = bottom_ref[...]

    def wet_at(k):
        return jnp.where(k < bottom, land_ref[k].astype(F32), 0.0)

    wet = wet_at(0)
    ratio = None
    couple_last = None
    state = None
    for k in range(depth):
        diagonal = jnp.ones((16, 256), F32)
        if k > 0:
            diagonal = diagonal + couple_last - couple_last * ratio
        if k < depth - 1:
            wet_next = wet_at(k + 1)
            couple = kappa_ref[k] * wet * wet_next
            diagonal = diagonal + couple
        inverse = 1.0 / diagonal
        rhs = (tcot_ref[k], scot_ref[k], wet)
        if k == 0:
            state = tuple(x * inverse for x in rhs)
        else:
            state = tuple((x + couple_last * s) * inverse for x, s in zip(rhs, state))
        a_ref[k], c_ref[k], w_ref[k] = state
        inv_ref[k] = inverse
        if k < depth - 1:
            ratio = couple * inverse
            ratio_ref[k] = ratio
            couple_last = couple
            wet = wet_next

    half = (8, 256)
    half_row = iota(half, 0)
    col = (16, 128)
    lane = iota(col, 1)

    def choose(parts, index, width):
        out = parts[-1]
        for n in range(len(parts) - 2, -1, -1):
            out = jnp.where(index < (n + 1) * width, parts[n], out)
        return out

    pending = None
    for k in range(depth - 1, -1, -1):
        wet = wet_at(k)
        if k < depth - 1:
            ratio = ratio_ref[k]
            state = tuple(x + ratio * s for x, s in zip((a_ref[k], c_ref[k], w_ref[k]), state))
            a_ref[k], c_ref[k], w_ref[k] = state
        fields = (theta_ref[k] * wet, salt_ref[k] * wet) + state
        ux = ux_ref[k]
        uy = uy_ref[k]
        low = [f[8:16] for f in fields]
        high = [f[0:8] for f in fields]
        down_ref[8 * k : 8 * k + 8] = choose(
            [pltpu.roll(low[n], (2 + 2 * n) % 8, 0) if n < 3 else low[n] for n in range(4)], half_row, 2
        )
        up_ref[8 * k : 8 * k + 8] = choose(
            [pltpu.roll(high[n], 2 * n, 0) if n else high[n] for n in range(4)], half_row, 2
        )
        flow = ux[8:16] * wet[8:16]
        flow_open = flow * pltpu.roll(wet[8:16], 7, 0)
        tail_down = choose(
            [pltpu.roll(low[4], 2, 0), jnp.where(half_row == 2, pltpu.roll(flow_open, 4, 0), pltpu.roll(flow, 4, 0))],
            half_row,
            2,
        )
        top_open = ux[0:8] * wet[0:8] * pltpu.roll(wet[0:8], 7, 0)
        tail_up = choose(
            [high[4], jnp.where(half_row == 2, pltpu.roll(top_open, 2, 0), pltpu.roll(wet[0:8], 3, 0))],
            half_row,
            2,
        )
        if k % 2:
            pending = (pltpu.roll(tail_down, 4, 0), pltpu.roll(tail_up, 4, 0))
        else:
            at = 8 * depth + 8 * (k // 2)
            if pending is None:
                pending = (tail_down, tail_up)
            down_ref[at : at + 8] = jnp.where(half_row < 4, tail_down, pending[0])
            up_ref[at : at + 8] = jnp.where(half_row < 4, tail_up, pending[1])
        last = [f[:, 128:256] for f in fields]
        first = [f[:, 0:128] for f in fields]
        edge_flow = uy[:, 128:256] * wet[:, 128:256]
        edge_open = edge_flow * pltpu.roll(wet[:, 128:256], 127, 1)
        last.append(jnp.where(lane == 126, edge_open, edge_flow))
        first_open = uy[:, 0:128] * wet[:, 0:128] * pltpu.roll(wet[:, 0:128], 127, 1)
        first.append(jnp.where(lane == 0, first_open, pltpu.roll(wet[:, 0:128], 1, 1)))
        right_ref[k] = choose(
            [pltpu.roll(last[n], 128 - 2 * n, 1) if n else last[n] for n in range(5, -1, -1)], lane - 116, 2
        )
        left_ref[k] = choose([pltpu.roll(first[n], 2 * n, 1) if n else first[n] for n in range(6)], lane, 2)


def final_kernel(
    place_ref,
    sums_ref,
    own_ref,
    from_below_ref,
    from_right_ref,
    from_corner_ref,
    theta_ref,
    salt_ref,
    ux_ref,
    uy_ref,
    land_ref,
    kappa_ref,
    forcing_ref,
    bottom_ref,
    a_ref,
    c_ref,
    w_ref,
    inv_ref,
    ratio_ref,
    above_ref,
    below_ref,
    west_ref,
    east_ref,
    theta_grad_ref,
    salt_grad_ref,
    kappa_grad_ref,
    forcing_grad_ref,
    theta_sweep_ref,
    salt_sweep_ref,
):
    depth = theta_ref.shape[0]
    r = place_ref[0]
    c = place_ref[1]
    has_up = jnp.where(r > 0, 1.0, 0.0)
    has_down = jnp.where(r < 15, 1.0, 0.0)
    has_left = jnp.where(c > 0, 1.0, 0.0)
    has_right = jnp.where(c < 15, 1.0, 0.0)

    small = (8, 128)
    small_row = iota(small, 0)
    total = (sums_ref[0:8], jnp.zeros(small, F32))
    for at in range(1, 32):
        s, e = two_sum(total[0], sums_ref[8 * at : 8 * at + 8])
        total = (s, total[1] + e)
    for step in (4, 2, 1):
        s, e = two_sum(total[0], pltpu.roll(total[0], step, 0))
        total = (s, (total[1] + pltpu.roll(total[1], step, 0)) + e)
    low = total[1] + pltpu.roll(total[0] + total[1], 96, 1)
    total = quick_two_sum(total[0], low)

    def as_rows(x):
        out = x
        for i in range(1, KRYLOV):
            out = jnp.where(small_row == i, pltpu.roll(x, 128 - 8 * i, 1), out)
        return out

    system = (as_rows(total[0]), as_rows(total[1]))

    def row_of(x, k):
        return jnp.broadcast_to(x[k : k + 1, :], small)

    def lane_of(x, k):
        return jnp.broadcast_to(x[:, k : k + 1], small)

    keep = []
    weights = []
    scales = [lane_of(row_of(system[0], k), k) for k in range(KRYLOV)]
    for k in range(KRYLOV):
        across = (row_of(system[0], k), row_of(system[1], k))
        pivot = (lane_of(across[0], k), lane_of(across[1], k))
        fine = pivot[0] > 1e-13 * scales[k]
        keep.append(fine)
        pivot = (jnp.where(fine, pivot[0], 1.0), jnp.where(fine, pivot[1], 0.0))
        factor = df_div((lane_of(system[0], k), lane_of(system[1], k)), pivot)
        used = fine & (small_row != k)
        factor = (jnp.where(used, factor[0], 0.0), jnp.where(used, factor[1], 0.0))
        product = df_mul(factor, across)
        system = df_add(system, (-product[0], -product[1]))
    for k in range(KRYLOV):
        pivot = lane_of(row_of(system[0], k), k)
        value = lane_of(row_of(system[0], k), KRYLOV)
        value = jnp.where(keep[k], value / jnp.where(keep[k], pivot, 1.0), 0.0)
        weights.append(value[0:1, 0:1])

    def combined(ref, rows):
        out = weights[0] * ref[0:rows]
        for k in range(1, KRYLOV):
            out = out + weights[k] * ref[rows * k : rows * k + rows]
        return out

    def rows_joined(upper, lower):
        turned = pltpu.roll(lower, 4, 0)
        row8 = iota(turned.shape, 0)
        middle = jnp.where((row8 >= 5) & (r < 15), turned, upper[16:24])
        return jnp.concatenate([upper[0:16], middle, turned * has_down], axis=0)

    joined = rows_joined(combined(own_ref, 24), combined(from_below_ref, 8))
    beside = pltpu.roll(rows_joined(combined(from_right_ref, 24), combined(from_corner_ref, 8)), 64, 1)
    lane_wide = iota((32, 128), 1)
    ending = jnp.where((lane_wide >= 125) & (c < 15), beside, joined[:, 256:384])
    surface = jnp.concatenate([joined[:, 128:256], ending], axis=1)
    zeta = surface[8:24]
    zeta_up = (surface[7:8], surface[6:7])
    zeta_down = (surface[24:25], surface[25:26])
    zeta_left = (joined[8:24, 127:128], joined[8:24, 126:127])
    zeta_right = (beside[8:24, 0:1] * has_right, beside[8:24, 1:2] * has_right)

    bottom = bottom_ref[...]
    shape = (16, 256)
    row = iota(shape, 0)
    lane = iota(shape, 1)
    first_row = row == 0
    last_row = row == 15
    first_lane = lane == 0
    last_lane = lane == 255

    def before(q, edge, axis):
        return jnp.where(first_row if axis == 0 else first_lane, edge, pltpu.roll(q, 1, axis))

    def after(q, edge, axis):
        return jnp.where(
            last_row if axis == 0 else last_lane, edge, pltpu.roll(q, shape[axis] - 1, axis)
        )

    def start_of(q, axis):
        return q[0:1, :] if axis == 0 else q[:, 0:1]

    def end_of(q, axis):
        return q[15:16, :] if axis == 0 else q[:, 255:256]

    def wet_at(k):
        return jnp.where(k < bottom, land_ref[k].astype(F32), 0.0)

    def row_edges(k, f):
        if f < 4:
            at = 8 * k + 2 * f
        else:
            at = 8 * depth + 8 * (k // 2) + 4 * (k % 2) + 2 * (f - 4)
        up = (above_ref[at + 1 : at + 2] * has_up, above_ref[at : at + 1] * has_up)
        down = (below_ref[at : at + 1] * has_down, below_ref[at + 1 : at + 2] * has_down)
        return up, down

    def col_edges(k, f):
        at = 126 - 2 * f
        left = (west_ref[k, :, at + 1 : at + 2] * has_left, west_ref[k, :, at : at + 1] * has_left)
        at = 2 * f
        right = (east_ref[k, :, at : at + 1] * has_right, east_ref[k, :, at + 1 : at + 2] * has_right)
        return left, right

    def edges(k, f, axis):
        return row_edges(k, f) if axis == 0 else col_edges(k, f)

    def open_faces(k, wet, axis):
        velocity = (ux_ref if axis == 0 else uy_ref)[k]
        (flow, outer), (far, wet_next) = edges(k, 5, axis)
        scale = 1.0 / 12.0
        main = velocity * wet * after(wet, wet_next, axis) * scale
        low = (flow * start_of(wet, axis) * scale, outer * scale)
        return main, low, far * scale

    def spread_of(k, q, f, faces, axis):
        main, low, _ = faces
        (q1, q2), (q3, q4) = edges(k, f, axis)
        pair = q + after(q, q3, axis)
        pair_low = q1 + start_of(q, axis)
        flux = main * (8.0 * pair - before(pair, pair_low, axis) - after(pair, q3 + q4, axis))
        flux_low = low[0] * (8.0 * pair_low - (q1 + q2) - start_of(pair, axis))
        return flux - before(flux, flux_low, axis)

    def gathered(m, m_low, m_high, faces, axis):
        main, low, far = faces
        h = main * (m - after(m, m_high[0], axis))
        h1 = low[0] * (m_low[0] - start_of(m, axis))
        h2 = low[1] * (m_low[1] - m_low[0])
        h3 = far * (m_high[0] - m_high[1])
        pair = h + before(h, h1, axis)
        return 8.0 * pair - before(pair, h1 + h2, axis) - after(pair, h3 + end_of(h, axis), axis)

    theta_state = None
    salt_state = None
    couple_last = None
    wet = wet_at(0)
    for k in range(depth):
        x_faces = open_faces(k, wet, 0)
        y_faces = open_faces(k, wet, 1)
        advected = []
        for f, ref in ((0, theta_ref), (1, salt_ref)):
            q = ref[k]
            masked = q * wet
            advected.append(q - spread_of(k, masked, f, x_faces, 0) - spread_of(k, masked, f, y_faces, 1))
        if k == 0:
            advected[0] = advected[0] + forcing_ref[...] * wet
        inverse = inv_ref[k]
        if k == 0:
            theta_state = advected[0] * inverse
            salt_state = advected[1] * inverse
        else:
            theta_state = (advected[0] + couple_last * theta_state) * inverse
            salt_state = (advected[1] + couple_last * salt_state) * inverse
        theta_sweep_ref[k] = theta_state
        salt_sweep_ref[k] = salt_state
        if k < depth - 1:
            wet_next = wet_at(k + 1)
            couple_last = kappa_ref[k] * wet * wet_next
            wet = wet_next

    weight = (0.2, -0.15)
    mu_later = None
    wet_later = None
    for k in range(depth - 1, -1, -1):
        wet = wet_at(k)
        w = w_ref[k]
        w_edges = (row_edges(k, 4), col_edges(k, 4))
        mu = (a_ref[k] + 0.2 * zeta * w, c_ref[k] - 0.15 * zeta * w)
        if k < depth - 1:
            ratio = ratio_ref[k]
            theta_new = theta_sweep_ref[k] + ratio * theta_state
            salt_new = salt_sweep_ref[k] + ratio * salt_state
            kappa_grad_ref[k] = -(wet * wet_later) * (
                (mu[0] - mu_later[0]) * (theta_new - theta_state)
                + (mu[1] - mu_later[1]) * (salt_new - salt_state)
            )
            theta_state = theta_new
            salt_state = salt_new
        faces = (open_faces(k, wet, 0), open_faces(k, wet, 1))
        for n, ref in ((0, theta_grad_ref), (1, salt_grad_ref)):
            total = None
            for axis in (0, 1):
                low, high = edges(k, 2 + n, axis)
                w_low, w_high = w_edges[axis]
                z_low, z_high = (zeta_up, zeta_down) if axis == 0 else (zeta_left, zeta_right)
                m_low = tuple(low[i] + weight[n] * z_low[i] * w_low[i] for i in (0, 1))
                m_high = tuple(high[i] + weight[n] * z_high[i] * w_high[i] for i in (0, 1))
                part = gathered(mu[n], m_low, m_high, faces[axis], axis)
                total = part if total is None else total + part
            ref[k] = mu[n] - wet * total
        if k == 0:
            forcing_grad_ref[...] = zeta + wet * mu[0]
        mu_later = mu
        wet_later = wet


def call(kernel, outs, args, scalars=0, scratch=()):
    return pl.pallas_call(
        kernel,
        out_shape=[jax.ShapeDtypeStruct(s, F32) for s in outs],
        in_specs=[SM] * scalars + [VM] * (len(args) - scalars),
        out_specs=[VM] * len(outs),
        scratch_shapes=[pltpu.VMEM(s, F32) for s in scratch],
        compiler_params=PARAMS,
    )(*args)


def around(count, step):
    return [(i, (i + step) % count) for i in range(count)]


def across(step):
    return [
        (16 * i + j, 16 * ((i + step) % 16) + (j + step) % 16) for i in range(16) for j in range(16)
    ]


def shards(
    theta,
    salt,
    velocity_x,
    velocity_y,
    land_mask,
    kappa,
    forcing,
    bottom,
    theta_cot,
    salt_cot,
    surface_cot,
):
    depth = theta.shape[0]
    whole = theta.shape
    place = jnp.stack([lax.axis_index(TROW), lax.axis_index(TCOL)]).astype(jnp.int32)
    rows, cols, corner = call(
        edges_kernel, [(16, 256), (32, 128), (16, 128)], (surface_cot, bottom)
    )
    rows = lax.ppermute(rows, TROW, around(16, 1))
    cols = lax.ppermute(cols, TCOL, around(16, 1))
    corner = lax.ppermute(corner, ALL, across(1))
    lines = 8 * depth + 8 * ((depth + 1) // 2)
    a, c, w, inv, ratio, down, up, right, left = call(
        columns_kernel,
        [whole] * 4 + [kappa.shape] + [(lines, 256)] * 2 + [(depth, 16, 128)] * 2,
        (theta, salt, velocity_x, velocity_y, land_mask, kappa, bottom, theta_cot, salt_cot),
    )
    above = lax.ppermute(down, TROW, around(16, 1))
    below = lax.ppermute(up, TROW, around(16, -1))
    west = lax.ppermute(right, TCOL, around(16, 1))
    east = lax.ppermute(left, TCOL, around(16, -1))
    sums, own, near, side, tip = call(
        krylov_kernel,
        [(256, 128), (96, 384), (32, 384), (96, 128), (32, 128)],
        (place, surface_cot, bottom, rows, cols, corner),
        scalars=1,
    )
    near = lax.ppermute(near, TROW, around(16, -1))
    side = lax.ppermute(side, TCOL, around(16, -1))
    tip = lax.ppermute(tip, ALL, across(-1))
    sums = lax.all_to_all(sums, ALL, 0, 0, tiled=True)
    return tuple(
        call(
            final_kernel,
            [whole, whole, kappa.shape, forcing.shape],
            (place, sums, own, near, side, tip, theta, salt, velocity_x, velocity_y, land_mask, kappa)
            + (forcing, bottom, a, c, w, inv, ratio, above, below, west, east),
            scalars=1,
            scratch=[whole, whole],
        )
    )


def solution(mesh):
    split = Mesh(mesh.devices.reshape(4, 2, 2, 2, 8), ALL)
    block = P(None, TROW, TCOL)
    flat = P(TROW, TCOL)
    return jax.shard_map(
        shards,
        mesh=split,
        in_specs=(block,) * 6 + (flat, flat, block, block, flat),
        out_specs=(block, block, block, flat),
        check_vma=False,
    )
```

time: 316 us -> 119 us (0.38)
  blocking collectives: 169 us -> 0 us
  Pallas kernels: 0 us -> 45.5 us
  starting transfers between devices: 78.6 us -> 37.4 us
  other arithmetic: 24.1 us -> 0.07 us
  between operations: 16.1 us -> 0.82 us
  local copies, waits for them, and re-layouts: 13.1 us -> 27.2 us
  waiting for transfers between devices: 12.1 us -> 6.5 us
    psum x20 -> x0, blocking collectives: 169 us -> none  [over_axes(): return functools.reduce(lax.psum, axes, array)]
    ppermute x24 -> x10, starting transfers between devices: 78.6 us -> 23.7 us  [the longest x1 5.8 us: shards(): side = lax.ppermute(side, TCOL, around(16, -1))]
    pallas_call x0 -> x4, Pallas kernels: none -> 45.5 us  [call(): pl.pallas_call(kernel, out_shape=[jax.ShapeDtypeStruct(s, F32) for s in o...]
    unnamed x160 -> x86, local copies, waits for them, and re-layouts: 1.81 us -> 27.2 us
    all_to_all x0 -> x1, starting transfers between devices: none -> 13.7 us  [shards(): sums = lax.all_to_all(sums, ALL, 0, 0, tiled=True)]
    slice x12 -> x0, local copies, waits for them, and re-layouts: 6.84 us -> none  [the longest x7 5.33 us: with_halo(): last = lax.slice_in_dim(array, length - width, length, axis=dim)]
    ppermute x24 -> x10, waiting for transfers between devices: 12.1 us -> 6.5 us  [the longest x1 2.52 us: shards(): near = lax.ppermute(near, TROW, around(16, -1))]
    concatenate x2 -> x0, other arithmetic: 5.6 us -> none  [with_halo(): jnp.concatenate([jnp.pad(low, around), array, jnp.pad(high, around)], axi...]
  transfers between devices with their start and end apart: 24 -> 11, of which waited for: 4 -> 3; matrix products, arithmetic and copies ran while one was open for 5% -> 0% of each run, Pallas kernels for 0% -> 4%
where the time goes in v1:
time: 119 us; the launch traced here: 117 us
  Pallas kernels  45.5 us (38%)
  starting transfers between devices  37.4 us (31%)
  local copies, waits for them, and re-layouts  27.2 us (23%)
  waiting for transfers between devices  6.5 us (5%)
    pallas_call x4, Pallas kernels, call(): pl.pallas_call(kernel, out_shape=[jax.ShapeDtypeStruct(s, F32) for s in o...  45.5 us
    unnamed x86, local copies, waits for them, and re-layouts  27.2 us
    all_to_all x1, starting transfers between devices, shards(): sums = lax.all_to_all(sums, ALL, 0, 0, tiled=True)  13.7 us
    ppermute x1, starting transfers between devices, shards(): side = lax.ppermute(side, TCOL, around(16, -1))  5.8 us
    ppermute x1, starting transfers between devices, shards(): east = lax.ppermute(left, TCOL, around(16, -1))  5.45 us
    ppermute x1, starting transfers between devices, shards(): corner = lax.ppermute(corner, ALL, across(1))  4.04 us
    ppermute x1, waiting for transfers between devices, shards(): near = lax.ppermute(near, TROW, around(16, -1))  2.52 us
    ppermute x1, waiting for transfers between devices, shards(): tip = lax.ppermute(tip, ALL, across(-1))  2.46 us
  transfers between devices with their start and end apart: 11, of which 3 were waited for; matrix products, arithmetic and copies ran while one was open for 0% of the time, Pallas kernels for 4%

profile of v1, /device:TPU:1, one launch (start us, length us, event | category | flops | bytes accessed | tf_op | source)
XLA Modules:
  0.0 117.5 jit_solution(12478147082387537987)
XLA Ops:
  2.1 4.0 %collective-permute-start.2 = (f32[16,128]{1,0:T(8,128)S(1)}, f32[16,128]{1,0:T(8,128)S(1)}, u32[]{:S(2)}, u32[]{:S(2)}) collective-permute-start(f32[16,128]{1,0:T(8,128)S(1)} %get-tuple-element.23), channel_id=1, source_target_pairs={{0,17},{1,18},{2,19},{3,20},{4,21},{5,22},{6,23},{7,24},{8,25},{9,... | collective-permute-start | bytes 24584 | tf_op jit(solution)/shard_map/ppermute | solution.py:601
  6.1 1.6 %collective-permute-start.1 = (f32[32,128]{1,0:T(8,128)S(1)}, f32[32,128]{1,0:T(8,128)S(1)}, u32[]{:S(2)}, u32[]{:S(2)}) collective-permute-start(f32[32,128]{1,0:T(8,128)S(1)} %get-tuple-element.22), channel_id=1, source_target_pairs={{0,1},{1,2},{2,3},{3,4},{4,5},{5,6},{6,7},{7,8},{8,9},{9,10},{10,1... | collective-permute-start | bytes 49160 | tf_op jit(solution)/shard_map/ppermute | solution.py:600
  7.8 1.0 copy-done
  8.8 1.0 copy-done.2
  9.8 1.0 copy-done.4
  10.8 1.0 copy-done.6
  11.8 1.0 copy-done.8
  12.8 1.0 copy-done.10
  13.8 1.0 copy-done.12
  14.8 1.0 copy-done.13
  15.8 2.8 %shard_map.140 = (f32[25,16,256]{2,1,0:T(8,128)S(1)}, f32[25,16,256]{2,1,0:T(8,128)S(1)}, f32[25,16,256]{2,1,0:T(8,128)S(1)}, f32[25,16,256]{2,1,0:T(8,128)S(1)}...) custom-call(f32[25,16,256]{2,1,0:T(8,128)S(1)} %copy-done, ...), custom_call_target="tpu_custom_call" | custom-call | tf_op jit(solution)/shard_map/pallas_call | solution.py:560
  18.6 0.7 copy-done.14
  19.3 0.7 copy-done.16
  22.2 1.8 %collective-permute-start.6 = (f32[304,256]{1,0:T(8,128)}, f32[304,256]{1,0:T(8,128)}, u32[]{:S(2)}, u32[]{:S(2)}) collective-permute-start(f32[304,256]{1,0:T(8,128)} %get-tuple-element.34), channel_id=1, source_target_pairs={{0,16},{16,32},{32,48},{48,64},{64,80},{80,96},{96,112},{112,128},... | collective-permute-start | bytes 933896 | tf_op jit(solution)/shard_map/ppermute | solution.py:608
  24.1 1.6 %shard_map.139 = (f32[256,128]{1,0:T(8,128)S(1)}, f32[96,384]{1,0:T(8,128)S(1)}, f32[32,384]{1,0:T(8,128)S(1)}, f32[96,128]{1,0:T(8,128)S(1)}, f32[32,128]{1,0:T(8,128)S(1)}) custom-call(s32[2]{0:T(128)S(1)} %pad_add_fusion.place_ref, f32[16,256]{1,0:T(8,128)S(1)} %copy-done.28, s32[16,256]{1,0:T(8,128)S(1)} %copy-done.21, ...), custom_call_target="tpu_custom_call" | custom-call | tf_op jit(solution)/shard_map/pallas_call | solution.py:560
  28.2 13.7 %all-to-all-start = ((f32[256,1,128]{2,1,0:T(1,128)}), f32[256,1,128]{2,1,0:T(1,128)S(1)}, u32[]{:S(2)}, u32[]{:S(2)}) async-start(f32[256,1,128]{2,1,0:T(1,128)} %bitcast.7), calls=%async_computation | async-start | bytes 262144 | tf_op jit(solution)/shard_map/all_to_all | solution.py:621
  41.9 1.6 %collective-permute-start.8 = (f32[25,16,128]{2,1,0:T(8,128)}, f32[25,16,128]{2,1,0:T(8,128)S(1)}, u32[]{:S(2)}, u32[]{:S(2)}) collective-permute-start(f32[25,16,128]{2,1,0:T(8,128)} %copy-done.39), channel_id=1, source_target_pairs={{0,1},{1,2},{2,3},{3,4},{4,5},{5,6},{6,7},{7,8},{8,9},{9,10},{10,1... | collective-permute-start | bytes 614408 | tf_op jit(solution)/shard_map/ppermute | solution.py:610
  43.5 5.5 %collective-permute-start.9 = (f32[25,16,128]{2,1,0:T(8,128)}, f32[25,16,128]{2,1,0:T(8,128)S(1)}, u32[]{:S(2)}, u32[]{:S(2)}) collective-permute-start(f32[25,16,128]{2,1,0:T(8,128)} %copy-done.38), channel_id=1, source_target_pairs={{0,15},{1,0},{2,1},{3,2},{4,3},{5,4},{6,5},{7,6},{8,7},{9,8},{10,9... | collective-permute-start | bytes 614408 | tf_op jit(solution)/shard_map/ppermute | solution.py:611
  49.0 2.2 %collective-permute-start.5 = (f32[32,128]{1,0:T(8,128)}, f32[32,128]{1,0:T(8,128)S(1)}, u32[]{:S(2)}, u32[]{:S(2)}) collective-permute-start(f32[32,128]{1,0:T(8,128)} %copy-done.42), channel_id=1, source_target_pairs={{0,255},{1,240},{2,241},{3,242},{4,243},{5,244},{6,245},{7,246},{8... | collective-permute-start | bytes 49160 | tf_op jit(solution)/shard_map/ppermute | solution.py:620
  51.2 2.5 %collective-permute-done.5.from_corner_ref = f32[32,128]{1,0:T(8,128)S(1)} collective-permute-done((f32[32,128]{1,0:T(8,128)}, f32[32,128]{1,0:T(8,128)S(1)}, u32[]{:S(2)}, u32[]{:S(2)}) %collective-permute-start.5) | collective-permute-done | bytes 16416 | tf_op jit(solution)/shard_map/ppermute | solution.py:620
  54.2 1.2 %collective-permute-start.3 = (f32[32,384]{1,0:T(8,128)}, f32[32,384]{1,0:T(8,128)S(1)}, u32[]{:S(2)}, u32[]{:S(2)}) collective-permute-start(f32[32,384]{1,0:T(8,128)} %copy-done.41), channel_id=1, source_target_pairs={{0,240},{16,0},{32,16},{48,32},{64,48},{80,64},{96,80},{112,96},{1... | collective-permute-start | bytes 147464 | tf_op jit(solution)/shard_map/ppermute | solution.py:618
  55.4 2.5 %collective-permute-done.3.from_below_ref = f32[32,384]{1,0:T(8,128)S(1)} collective-permute-done((f32[32,384]{1,0:T(8,128)}, f32[32,384]{1,0:T(8,128)S(1)}, u32[]{:S(2)}, u32[]{:S(2)}) %collective-permute-start.3) | collective-permute-done | bytes 49184 | tf_op jit(solution)/shard_map/ppermute | solution.py:618
  58.6 5.8 %collective-permute-start.4 = (f32[96,128]{1,0:T(8,128)}, f32[96,128]{1,0:T(8,128)S(1)}, u32[]{:S(2)}, u32[]{:S(2)}) collective-permute-start(f32[96,128]{1,0:T(8,128)} %copy-done.40), channel_id=1, source_target_pairs={{0,15},{1,0},{2,1},{3,2},{4,3},{5,4},{6,5},{7,6},{8,7},{9,8},{10,9... | collective-permute-start | bytes 147464 | tf_op jit(solution)/shard_map/ppermute | solution.py:619
  64.4 1.5 %collective-permute-done.4.from_right_ref = f32[96,128]{1,0:T(8,128)S(1)} collective-permute-done((f32[96,128]{1,0:T(8,128)}, f32[96,128]{1,0:T(8,128)S(1)}, u32[]{:S(2)}, u32[]{:S(2)}) %collective-permute-start.4) | collective-permute-done | bytes 49184 | tf_op jit(solution)/shard_map/ppermute | solution.py:619
  68.5 1.0 copy-done.15
  69.5 1.0 copy-done.17
  70.5 1.0 copy-done.19
  71.5 0.9 copy-done.23
  72.4 0.9 copy-done.25
  73.3 0.8 copy-done.30
  74.1 0.8 copy-done.32
  76.4 41.1 %shard_map.141 = (f32[25,16,256]{2,1,0:T(8,128)}, f32[25,16,256]{2,1,0:T(8,128)}, f32[24,16,256]{2,1,0:T(8,128)}, f32[16,256]{1,0:T(8,128)}) custom-call(s32[2]{0:T(128)S(1)} %copy-done.37, f32[256,128]{1,0:T(8,128)S(1)} %bitcast.6, f32[96,384]{1,0:T(8,128)S(1)} %get-tuple-element.25.own_ref, f32[32,384]{1,0:T(8,128)S(1)} %copy-done.30, ...), custom_call_target="tpu_custom_call" | custom-call | tf_op jit(solution)/shard_map/pallas_call | solution.py:560
  (81 shorter events, 11.3 us)
Async XLA Ops:
  2.1 5.7 %copy-start.21 = (s32[16,256]{1,0:T(8,128)S(1)}, s32[16,256]{1,0:T(8,128)}, u32[]{:S(2)}) copy-start(s32[16,256]{1,0:T(8,128)} %bottom_ref.7) | copy-start | bytes 49156
  2.1 22.0 %collective-permute-start.2 = (f32[16,128]{1,0:T(8,128)S(1)}, f32[16,128]{1,0:T(8,128)S(1)}, u32[]{:S(2)}, u32[]{:S(2)}) collective-permute-start(f32[16,128]{1,0:T(8,128)S(1)} %get-tuple-element.23), channel_id=1, source_target_pairs={{0,17},{1,18},{2,19},{3,20},{4,21},{5,22},{6,23},{7,24},{8,25},{9,... | collective-permute-start | bytes 24584 | tf_op jit(solution)/shard_map/ppermute | solution.py:601
  6.1 18.0 %collective-permute-start = (f32[16,256]{1,0:T(8,128)S(1)}, f32[16,256]{1,0:T(8,128)S(1)}, u32[]{:S(2)}, u32[]{:S(2)}) collective-permute-start(f32[16,256]{1,0:T(8,128)S(1)} %get-tuple-element.21), channel_id=1, source_target_pairs={{0,16},{16,32},{32,48},{48,64},{64,80},{80,96},{96,112},{112,128},... | collective-permute-start | bytes 49160 | tf_op jit(solution)/shard_map/ppermute | solution.py:599
  6.1 18.0 %collective-permute-start.1 = (f32[32,128]{1,0:T(8,128)S(1)}, f32[32,128]{1,0:T(8,128)S(1)}, u32[]{:S(2)}, u32[]{:S(2)}) collective-permute-start(f32[32,128]{1,0:T(8,128)S(1)} %get-tuple-element.22), channel_id=1, source_target_pairs={{0,1},{1,2},{2,3},{3,4},{4,5},{5,6},{6,7},{7,8},{8,9},{9,10},{10,1... | collective-permute-start | bytes 49160 | tf_op jit(solution)/shard_map/ppermute | solution.py:600
  7.8 1.0 copy-start
  8.8 1.0 copy-start.2
  9.8 1.0 copy-start.4
  10.8 1.0 copy-start.6
  11.8 1.0 copy-start.8
  12.8 1.0 copy-start.10
  13.8 1.0 copy-start.12
  14.8 1.0 copy-start.13
  15.8 8.3 %copy-start.28 = (f32[16,256]{1,0:T(8,128)S(1)}, f32[16,256]{1,0:T(8,128)}, u32[]{:S(2)}) copy-start(f32[16,256]{1,0:T(8,128)} %cot_ref.3) | copy-start | bytes 49156
  15.8 52.1 %copy-start.3 = (f32[25,16,256]{2,1,0:T(8,128)S(1)}, f32[25,16,256]{2,1,0:T(8,128)}, u32[]{:S(2)}) copy-start(f32[25,16,256]{2,1,0:T(8,128)} %salt_ref.3) | copy-start | bytes 1228804
  15.8 52.1 %copy-start.5 = (f32[25,16,256]{2,1,0:T(8,128)S(1)}, f32[25,16,256]{2,1,0:T(8,128)}, u32[]{:S(2)}) copy-start(f32[25,16,256]{2,1,0:T(8,128)} %ux_ref.3) | copy-start | bytes 1228804
  15.8 52.1 %copy-start.7 = (f32[25,16,256]{2,1,0:T(8,128)S(1)}, f32[25,16,256]{2,1,0:T(8,128)}, u32[]{:S(2)}) copy-start(f32[25,16,256]{2,1,0:T(8,128)} %uy_ref.3) | copy-start | bytes 1228804
  15.8 52.1 %copy-start.9 = (s32[25,16,256]{2,1,0:T(8,128)S(1)}, s32[25,16,256]{2,1,0:T(8,128)}, u32[]{:S(2)}) copy-start(s32[25,16,256]{2,1,0:T(8,128)} %land_ref.3) | copy-start | bytes 1228804
  15.8 52.1 %copy-start.11 = (f32[24,16,256]{2,1,0:T(8,128)S(1)}, f32[24,16,256]{2,1,0:T(8,128)}, u32[]{:S(2)}) copy-start(f32[24,16,256]{2,1,0:T(8,128)} %kappa_ref.3) | copy-start | bytes 1179652
  21.5 46.4 %copy-start.1 = (f32[25,16,256]{2,1,0:T(8,128)S(1)}, f32[25,16,256]{2,1,0:T(8,128)}, u32[]{:S(2)}) copy-start(f32[25,16,256]{2,1,0:T(8,128)} %theta_ref.3) | copy-start | bytes 1228804
  22.2 45.7 %collective-permute-start.6 = (f32[304,256]{1,0:T(8,128)}, f32[304,256]{1,0:T(8,128)}, u32[]{:S(2)}, u32[]{:S(2)}) collective-permute-start(f32[304,256]{1,0:T(8,128)} %get-tuple-element.34), channel_id=1, source_target_pairs={{0,16},{16,32},{32,48},{48,64},{64,80},{80,96},{96,112},{112,128},... | collective-permute-start | bytes 933896 | tf_op jit(solution)/shard_map/ppermute | solution.py:608
  24.0 43.9 %collective-permute-start.7 = (f32[304,256]{1,0:T(8,128)}, f32[304,256]{1,0:T(8,128)}, u32[]{:S(2)}, u32[]{:S(2)}) collective-permute-start(f32[304,256]{1,0:T(8,128)} %get-tuple-element.35), channel_id=1, source_target_pairs={{0,240},{16,0},{32,16},{48,32},{64,48},{80,64},{96,80},{112,96},{1... | collective-permute-start | bytes 933896 | tf_op jit(solution)/shard_map/ppermute | solution.py:609
  24.1 1.7 %copy-start.36 = (s32[2]{0:T(128)}, s32[2]{0:T(128)S(1)}, u32[]{:S(2)}) copy-start(s32[2]{0:T(128)S(1)} %pad_add_fusion.place_ref) | copy-start | bytes 28
  28.2 39.7 %all-to-all-start = ((f32[256,1,128]{2,1,0:T(1,128)}), f32[256,1,128]{2,1,0:T(1,128)S(1)}, u32[]{:S(2)}, u32[]{:S(2)}) async-start(f32[256,1,128]{2,1,0:T(1,128)} %bitcast.7), calls=%async_computation | async-start | bytes 262144 | tf_op jit(solution)/shard_map/all_to_all | solution.py:621
  41.9 24.5 %collective-permute-start.8 = (f32[25,16,128]{2,1,0:T(8,128)}, f32[25,16,128]{2,1,0:T(8,128)S(1)}, u32[]{:S(2)}, u32[]{:S(2)}) collective-permute-start(f32[25,16,128]{2,1,0:T(8,128)} %copy-done.39), channel_id=1, source_target_pairs={{0,1},{1,2},{2,3},{3,4},{4,5},{5,6},{6,7},{7,8},{8,9},{9,10},{10,1... | collective-permute-start | bytes 614408 | tf_op jit(solution)/shard_map/ppermute | solution.py:610
  43.5 23.7 %collective-permute-start.9 = (f32[25,16,128]{2,1,0:T(8,128)}, f32[25,16,128]{2,1,0:T(8,128)S(1)}, u32[]{:S(2)}, u32[]{:S(2)}) collective-permute-start(f32[25,16,128]{2,1,0:T(8,128)} %copy-done.38), channel_id=1, source_target_pairs={{0,15},{1,0},{2,1},{3,2},{4,3},{5,4},{6,5},{7,6},{8,7},{9,8},{10,9... | collective-permute-start | bytes 614408 | tf_op jit(solution)/shard_map/ppermute | solution.py:611
  49.0 4.6 %collective-permute-start.5 = (f32[32,128]{1,0:T(8,128)}, f32[32,128]{1,0:T(8,128)S(1)}, u32[]{:S(2)}, u32[]{:S(2)}) collective-permute-start(f32[32,128]{1,0:T(8,128)} %copy-done.42), channel_id=1, source_target_pairs={{0,255},{1,240},{2,241},{3,242},{4,243},{5,244},{6,245},{7,246},{8... | collective-permute-start | bytes 49160 | tf_op jit(solution)/shard_map/ppermute | solution.py:620
  54.2 3.7 %collective-permute-start.3 = (f32[32,384]{1,0:T(8,128)}, f32[32,384]{1,0:T(8,128)S(1)}, u32[]{:S(2)}, u32[]{:S(2)}) collective-permute-start(f32[32,384]{1,0:T(8,128)} %copy-done.41), channel_id=1, source_target_pairs={{0,240},{16,0},{32,16},{48,32},{64,48},{80,64},{96,80},{112,96},{1... | collective-permute-start | bytes 147464 | tf_op jit(solution)/shard_map/ppermute | solution.py:618
  58.6 7.3 %collective-permute-start.4 = (f32[96,128]{1,0:T(8,128)}, f32[96,128]{1,0:T(8,128)S(1)}, u32[]{:S(2)}, u32[]{:S(2)}) collective-permute-start(f32[96,128]{1,0:T(8,128)} %copy-done.40), channel_id=1, source_target_pairs={{0,15},{1,0},{2,1},{3,2},{4,3},{5,4},{6,5},{7,6},{8,7},{9,8},{10,9... | collective-permute-start | bytes 147464 | tf_op jit(solution)/shard_map/ppermute | solution.py:619
  68.5 1.0 copy-start.15
  69.5 1.0 copy-start.17
  70.5 1.0 copy-start.19
  71.5 0.9 copy-start.23
  (22 other events, 15.3 us)

commit v2 on v1

v2 whole, which is shorter than its diff:
```python
import functools

import jax
import jax.numpy as jnp
from jax import lax
from jax.experimental import pallas as pl
from jax.experimental.pallas import tpu as pltpu
from jax.sharding import Mesh
from jax.sharding import PartitionSpec as P

TROW = ("trow_0", "trow_1", "trow_2")
TCOL = ("tcol_0", "tcol_1")
ALL = TROW + TCOL
CENTRE = 4.75
KRYLOV = 4
PAIRS = [(i, j) for i in range(KRYLOV) for j in range(i, KRYLOV)]
F32 = jnp.float32
VM = pl.BlockSpec(memory_space=pltpu.VMEM)
SM = pl.BlockSpec(memory_space=pltpu.SMEM)
HB = pl.BlockSpec(memory_space=pltpu.HBM)
PARAMS = pltpu.CompilerParams(vmem_limit_bytes=24 * 1024 * 1024)


def iota(shape, dim):
    return lax.broadcasted_iota(jnp.int32, shape, dim)


def two_sum(a, b):
    s = a + b
    t = s - a
    return s, (a - (s - t)) + (b - t)


def quick_two_sum(a, b):
    s = a + b
    return s, b - (s - a)


def halves(a):
    t = a * 4097.0
    high = t - (t - a)
    return high, a - high


def two_prod(a, b, a_parts, b_parts):
    p = a * b
    ah, al = a_parts
    bh, bl = b_parts
    return p, ((ah * bh - p) + ah * bl + al * bh) + al * bl


def df_add(a, b):
    s, e = two_sum(a[0], b[0])
    return quick_two_sum(s, e + (a[1] + b[1]))


def df_mul(a, b):
    p, e = two_prod(a[0], b[0], halves(a[0]), halves(b[0]))
    return quick_two_sum(p, e + (a[0] * b[1] + a[1] * b[0]))


def df_div(a, b):
    inverse = 1.0 / b[0]
    q1 = a[0] * inverse
    back = df_mul((q1, jnp.zeros_like(q1)), b)
    rest = df_add(a, (-back[0], -back[1]))
    return quick_two_sum(q1, rest[0] * inverse)


class Loaded:
    def __init__(self, source, ref, sem):
        self.ref = ref
        self.copy = pltpu.make_async_copy(source, ref, sem)
        self.copy.start()
        self.waited = False

    def get(self):
        if not self.waited:
            self.copy.wait()
            self.waited = True
        return self.ref


class Stored:
    def __init__(self, target, ref, take_sem, pending):
        self.target, self.ref, self.take_sem, self.pending = target, ref, take_sem, pending

    def send(self, start=None, count=None):
        source, target = self.ref, self.target
        if start is not None:
            source, target = source.at[pl.ds(start, count)], target.at[pl.ds(start, count)]
        copy = pltpu.make_async_copy(source, target, self.take_sem())
        copy.start()
        self.pending.append(copy)


def staged(kernel, args, outs, place=None, scratch=(), sends=None, aliases=None, views=None):
    views = views or {}
    aliases = aliases or {}
    aliased = [args[i] for i in aliases]
    loaded_args = [a for i, a in enumerate(args) if i not in aliases]
    smem = [] if place is None else [place]
    n_in, n_alias, n_out = len(loaded_args), len(aliased), len(outs)
    sends = sends or n_out
    staging = [pltpu.VMEM(a.shape, a.dtype) for a in loaded_args]
    for n, shape in enumerate(outs):
        held = (views[n][1],) + tuple(shape[1:]) if n in views else shape
        staging.append(pltpu.VMEM(held, F32))

    def body(*refs):
        refs = list(refs)
        places = [refs.pop(0) for _ in smem]
        sources = [refs.pop(0) for _ in range(n_in)]
        for _ in range(n_alias):
            refs.pop(0)
        targets = [refs.pop(0) for _ in range(n_out)]
        buffers = [refs.pop(0) for _ in range(n_in)]
        holds = [refs.pop(0) for _ in range(n_out)]
        in_sems, out_sems = refs.pop(-2), refs.pop(-1)
        ins = [Loaded(s, b, in_sems.at[n]) for n, (s, b) in enumerate(zip(sources, buffers))]
        pending = []
        given = []
        for n in range(n_out):
            target = targets[n].at[pl.ds(*views[n])] if n in views else targets[n]
            given.append(Stored(target, holds[n], lambda: out_sems.at[len(pending)], pending))
        kernel(ins, given, *places, *refs)
        for x in ins:
            x.get()
        for copy in pending:
            copy.wait()

    return pl.pallas_call(
        body,
        out_shape=[jax.ShapeDtypeStruct(s, F32) for s in outs],
        in_specs=[SM] * len(smem) + [HB] * (n_in + n_alias),
        out_specs=[HB] * n_out,
        input_output_aliases={len(smem) + n_in + i: out for i, out in enumerate(aliases.values())},
        scratch_shapes=staging
        + [pltpu.VMEM(s, F32) for s in scratch]
        + [pltpu.SemaphoreType.DMA((n_in,)), pltpu.SemaphoreType.DMA((sends,))],
        compiler_params=PARAMS,
    )(*smem, *loaded_args, *aliased)


def edges_kernel(ins, outs):
    cot_ref, bottom_ref = [x.get() for x in ins]
    rows_ref, cols_ref, corner_ref = [x.ref for x in outs]
    cot = cot_ref[...]
    bottom = bottom_ref[...].astype(F32)
    rows_ref[0:8] = cot[8:16]
    rows_ref[8:16] = bottom[8:16]
    cols_ref[0:16] = cot[:, 128:256]
    cols_ref[16:32] = bottom[:, 128:256]
    corner_ref[0:8] = cot[8:16, 128:256]
    corner_ref[8:16] = bottom[8:16, 128:256]
    for out in outs:
        out.send()


def merge_rows(a, b, step):
    shape = a[0].shape
    first = (iota(shape, 0) & step) == 0

    def part(x, y):
        mixed = jnp.where(first, y, x)
        if step == 4:
            other = pltpu.roll(mixed, 4, 0)
        else:
            other = jnp.where(first, pltpu.roll(mixed, 8 - step, 0), pltpu.roll(mixed, step, 0))
        return jnp.where(first, x, y), other

    kept_high, other_high = part(a[0], b[0])
    kept_low, other_low = part(a[1], b[1])
    return df_add((kept_high, kept_low), (other_high, other_low))


def krylov_kernel(ins, outs, place_ref):
    cot_ref, bottom_ref, rows_ref, cols_ref, corner_ref = [x.get() for x in ins]
    up_out, left_out, sums_out, own_out, diag_out = outs
    sums_ref, own_ref, up_ref, left_ref, diag_ref = [
        x.ref for x in (sums_out, own_out, up_out, left_out, diag_out)
    ]
    r = place_ref[0]
    c = place_ref[1]
    shape = (24, 384)
    row = iota(shape, 0)
    lane = iota(shape, 1)

    def window(main, at):
        top = jnp.concatenate([corner_ref[8 * at : 8 * at + 8], rows_ref[8 * at : 8 * at + 8]], axis=1)
        rest = jnp.concatenate([cols_ref[16 * at : 16 * at + 16], main], axis=1)
        return jnp.concatenate([top, rest], axis=0)

    inside = ((row >= 8) | (r > 0)) & ((lane >= 128) | (c > 0))
    start = jnp.where(inside, window(cot_ref[...], 0), 0.0)
    bottom = window(bottom_ref[...].astype(F32), 1)
    shifted = (4.2 + bottom / 25.0) - CENTRE

    def apply_shifted(v):
        below = jnp.where(row == 23, 0.0, pltpu.roll(v, 23, 0))
        right = jnp.where(lane == 383, 0.0, pltpu.roll(v, 383, 1))
        beside = below + pltpu.roll(v, 1, 0) + right + pltpu.roll(v, 1, 1)
        return jnp.where(inside, shifted * v - beside, 0.0)

    vectors = [start]
    images = []
    for step in range(KRYLOV):
        moved = apply_shifted(vectors[-1])
        images.append(moved + CENTRE * vectors[-1])
        if step == 0:
            vectors.append(moved * 0.25)
        elif step + 1 < KRYLOV:
            vectors.append(moved * 0.5 - vectors[-2])

    for k, v in enumerate(vectors):
        own_ref[24 * k : 24 * k + 24] = v
        near = pltpu.roll(v[0:16], 12, 0)[0:8]
        up_ref[8 * k : 8 * k + 8] = near[:, 128:384]
        up_ref[32 + 8 * (k // 2) : 40 + 8 * (k // 2), 128 * (k % 2) : 128 * (k % 2) + 128] = near[:, 0:128]
        beside = pltpu.roll(v[:, 0:256], 192, 1)[:, 0:128]
        for n in range(3):
            at = 3 * k + n
            left_ref[at // 2, 8 * (at % 2) : 8 * (at % 2) + 8] = beside[8 * n : 8 * n + 8]
        diag_ref[8 * k : 8 * k + 8] = pltpu.roll(near[:, 0:256], 192, 1)[:, 0:128]
    for out in (up_out, left_out, diag_out, own_out):
        out.send()

    domain = (
        (row >= 4)
        & (row < jnp.where(r == 15, 24, 20))
        & (lane >= 124)
        & (lane < jnp.where(c == 15, 384, 380))
    )
    cut = [jnp.where(domain, v, 0.0) for v in vectors]
    cut_parts = [halves(v) for v in cut]
    image_parts = [halves(w) for w in images]

    def tile(x, at):
        i, j = divmod(at, 3)
        return x[8 * i : 8 * i + 8, 128 * j : 128 * j + 128]

    def dot(x, x_parts, y, y_parts):
        total = None
        for at in range(9):
            p, e = two_prod(
                tile(x, at),
                tile(y, at),
                [tile(h, at) for h in x_parts],
                [tile(h, at) for h in y_parts],
            )
            if total is None:
                total = (p, e)
            else:
                s, f = two_sum(total[0], p)
                total = (s, total[1] + (e + f))
        return total

    dots = [dot(cut[i], cut_parts[i], images[j], image_parts[j]) for i, j in PAIRS]
    start_parts = halves(start)
    dots += [dot(cut[i], cut_parts[i], start, start_parts) for i in range(KRYLOV)]
    zero = jnp.zeros((8, 128), F32)
    dots += [(zero, zero)] * (16 - len(dots))
    packed = []
    for base in (0, 8):
        group = dots[base : base + 8]
        for step in (4, 2, 1):
            group = [merge_rows(group[i], group[i + step], step) for i in range(step)]
        total = group[0]
        for step in (64, 32, 16, 8, 4, 2, 1):
            total = df_add(total, (pltpu.roll(total[0], step, 1), pltpu.roll(total[1], step, 1)))
        packed.append(total)
    small_row = iota((8, 128), 0)
    small_lane = iota((8, 128), 1)
    spread = zero
    for part in (0, 1):
        for base in (0, 1):
            chosen = jnp.zeros((8, 128), jnp.bool_)
            for i in range(KRYLOV):
                for j in range(KRYLOV + 1):
                    index = len(PAIRS) + i if j == KRYLOV else PAIRS.index((min(i, j), max(i, j)))
                    if index // 8 == base:
                        chosen = chosen | (
                            (small_row == index % 8) & (small_lane == 32 * part + 8 * i + j)
                        )
            spread = spread + jnp.where(chosen, packed[base][part], 0.0)
    line = jnp.sum(spread, axis=0, keepdims=True)
    sums_ref[...] = jnp.broadcast_to(line, (256, 128))

    sums_out.send()


ROW_TURNS = (0, 4, 2, 6)
FIELDS = 6


def packed_rows(parts, from_above):
    row = iota((8, 256), 0)
    order = (2, 1, 3, 0) if from_above else (0, 2, 1, 3)
    turned = [pltpu.roll(p, t, 0) if t else p for p, t in zip(parts, ROW_TURNS)]
    out = turned[order[3]]
    for n in (2, 1, 0):
        out = jnp.where(row < 2 * n + 2, turned[order[n]], out)
    return out


def packed_cols(parts):
    group = (iota((16, 128), 1) + 2) & 127
    out = pltpu.roll(parts[-1], 4 * (len(parts) - 1), 1)
    for f in range(len(parts) - 2, -1, -1):
        out = jnp.where(group < 4 * f + 4, pltpu.roll(parts[f], 4 * f, 1) if f else parts[f], out)
    return out


def columns_kernel(ins, outs):
    depth = ins[0].ref.shape[0]
    land_in, kappa_in, bottom_in, tcot_in, scot_in, theta_in, salt_in, ux_in, uy_in = ins
    a_out, c_out, w_out, inv_out, ratio_out, down_out, up_out, right_out, left_out = outs
    a_ref, c_ref, w_ref, inv_ref, ratio_ref, down_ref, up_ref, right_ref, left_ref = [x.ref for x in outs]
    bottom = bottom_in.get()[...]
    land_ref = land_in.get()
    kappa_ref = kappa_in.get()
    tcot_ref = tcot_in.get()
    scot_ref = scot_in.get()

    def wet_at(k):
        return jnp.where(k < bottom, land_ref[k].astype(F32), 0.0)

    wet = wet_at(0)
    ratio = None
    couple_last = None
    state = None
    for k in range(depth):
        diagonal = jnp.ones((16, 256), F32)
        if k > 0:
            diagonal = diagonal + couple_last - couple_last * ratio
        if k < depth - 1:
            wet_next = wet_at(k + 1)
            couple = kappa_ref[k] * wet * wet_next
            diagonal = diagonal + couple
        inverse = 1.0 / diagonal
        rhs = (tcot_ref[k], scot_ref[k], wet)
        if k == 0:
            state = tuple(x * inverse for x in rhs)
        else:
            state = tuple((x + couple_last * s) * inverse for x, s in zip(rhs, state))
        a_ref[k], c_ref[k], w_ref[k] = state
        inv_ref[k] = inverse
        if k < depth - 1:
            ratio = couple * inverse
            ratio_ref[k] = ratio
            couple_last = couple
            wet = wet_next
    inv_out.send()
    ratio_out.send()
    theta_ref = theta_in.get()
    salt_ref = salt_in.get()
    ux_ref = ux_in.get()
    uy_ref = uy_in.get()
    row8 = iota((8, 256), 0)
    lane = iota((16, 128), 1)
    tails = {}
    for k in range(depth - 1, -1, -1):
        wet = wet_at(k)
        if k < depth - 1:
            ratio = ratio_ref[k]
            state = tuple(x + ratio * s for x, s in zip((a_ref[k], c_ref[k], w_ref[k]), state))
            a_ref[k], c_ref[k], w_ref[k] = state
        fields = (theta_ref[k] * wet, salt_ref[k] * wet) + state
        down_ref[8 * k : 8 * k + 8] = packed_rows([f[8:16] for f in fields[:4]], True)
        up_ref[8 * k : 8 * k + 8] = packed_rows([f[0:8] for f in fields[:4]], False)
        flow = ux_ref[k] * wet
        open_low = flow[8:16] * pltpu.roll(wet[8:16], 7, 0)
        open_high = flow[0:8] * pltpu.roll(wet[0:8], 7, 0)
        face_low = jnp.where(row8 == 6, open_low, flow[8:16])
        face_high = jnp.where(row8 == 0, open_high, pltpu.roll(wet[0:8], 1, 0))
        tails[k] = ((state[2][8:16], face_low), (state[2][0:8], face_high))
        if k % 2 == 0:
            later = tails.pop(k + 1, tails[k])
            this = tails.pop(k)
            at = 8 * depth + 4 * k
            down_ref[at : at + 8] = packed_rows(this[0] + later[0], True)
            up_ref[at : at + 8] = packed_rows(this[1] + later[1], False)
        flow = uy_ref[k] * wet
        open_last = flow[:, 128:256] * pltpu.roll(wet[:, 128:256], 127, 1)
        open_first = flow[:, 0:128] * pltpu.roll(wet[:, 0:128], 127, 1)
        last = [f[:, 128:256] for f in fields] + [jnp.where(lane == 126, open_last, flow[:, 128:256])]
        first = [f[:, 0:128] for f in fields] + [
            jnp.where(lane == 0, open_first, pltpu.roll(wet[:, 0:128], 1, 1))
        ]
        right_ref[k] = packed_cols(last)
        left_ref[k] = packed_cols(first)
    for out in (down_out, right_out, up_out, left_out, a_out, c_out, w_out):
        out.send()


def final_kernel(ins, outs, place_ref, theta_sweep_ref, salt_sweep_ref, x_open_ref, y_open_ref):
    (
        sums_in,
        own_in,
        corner_in,
        land_in,
        bottom_in,
        above_in,
        below_in,
        west_in,
        east_in,
        ux_in,
        uy_in,
        theta_in,
        salt_in,
        forcing_in,
        kappa_in,
        inv_in,
        ratio_in,
        w_in,
        a_in,
        c_in,
    ) = ins
    theta_out, salt_out, kappa_out, forcing_out = outs
    theta_grad_ref, salt_grad_ref, kappa_grad_ref, forcing_grad_ref = [x.ref for x in outs]
    depth = theta_in.ref.shape[0]
    lines = 8 * depth + 8 * ((depth + 1) // 2)
    r = place_ref[0]
    c = place_ref[1]
    has_up = jnp.where(r > 0, 1.0, 0.0)
    has_down = jnp.where(r < 15, 1.0, 0.0)
    has_left = jnp.where(c > 0, 1.0, 0.0)
    has_right = jnp.where(c < 15, 1.0, 0.0)
    row8 = iota((8, 256), 0)
    lane16 = iota((16, 128), 1)
    bottom = bottom_in.get()[...]
    land_ref = land_in.get()
    sums_ref, own_ref, from_corner_ref, above_ref, below_ref, west_ref, east_ref = [
        x.get() for x in (sums_in, own_in, corner_in, above_in, below_in, west_in, east_in)
    ]
    from_right_ref = [east_ref[depth + n] for n in range(6)]

    def near_of(k):
        at = lines + 8 * k
        side = lines + 32 + 8 * (k // 2)
        start = 128 * (k % 2)
        return jnp.concatenate([below_ref[side : side + 8, start : start + 128], below_ref[at : at + 8]], axis=1)

    from_right = jnp.concatenate(from_right_ref, axis=0)

    small = (8, 128)
    small_row = iota(small, 0)
    total = (sums_ref[0:8], jnp.zeros(small, F32))
    for at in range(1, 32):
        s, e = two_sum(total[0], sums_ref[8 * at : 8 * at + 8])
        total = (s, total[1] + e)
    for step in (4, 2, 1):
        s, e = two_sum(total[0], pltpu.roll(total[0], step, 0))
        total = (s, (total[1] + pltpu.roll(total[1], step, 0)) + e)
    low = total[1] + pltpu.roll(total[0] + total[1], 96, 1)
    total = quick_two_sum(total[0], low)

    def as_rows(x):
        out = x
        for i in range(1, KRYLOV):
            out = jnp.where(small_row == i, pltpu.roll(x, 128 - 8 * i, 1), out)
        return out

    system = (as_rows(total[0]), as_rows(total[1]))

    def row_of(x, k):
        return jnp.broadcast_to(x[k : k + 1, :], small)

    def lane_of(x, k):
        return jnp.broadcast_to(x[:, k : k + 1], small)

    keep = []
    weights = []
    scales = [lane_of(row_of(system[0], k), k) for k in range(KRYLOV)]
    for k in range(KRYLOV):
        across = (row_of(system[0], k), row_of(system[1], k))
        pivot = (lane_of(across[0], k), lane_of(across[1], k))
        fine = pivot[0] > 1e-13 * scales[k]
        keep.append(fine)
        pivot = (jnp.where(fine, pivot[0], 1.0), jnp.where(fine, pivot[1], 0.0))
        factor = df_div((lane_of(system[0], k), lane_of(system[1], k)), pivot)
        used = fine & (small_row != k)
        factor = (jnp.where(used, factor[0], 0.0), jnp.where(used, factor[1], 0.0))
        product = df_mul(factor, across)
        system = df_add(system, (-product[0], -product[1]))
    for k in range(KRYLOV):
        pivot = lane_of(row_of(system[0], k), k)
        value = lane_of(row_of(system[0], k), KRYLOV)
        value = jnp.where(keep[k], value / jnp.where(keep[k], pivot, 1.0), 0.0)
        weights.append(value[0:1, 0:1])

    def combined(ref, rows):
        out = weights[0] * ref[0:rows]
        for k in range(1, KRYLOV):
            out = out + weights[k] * ref[rows * k : rows * k + rows]
        return out

    def rows_joined(upper, lower):
        turned = pltpu.roll(lower, 4, 0)
        row8 = iota(turned.shape, 0)
        middle = jnp.where((row8 >= 5) & (r < 15), turned, upper[16:24])
        return jnp.concatenate([upper[0:16], middle, turned * has_down], axis=0)

    near = weights[0] * near_of(0)
    for k in range(1, KRYLOV):
        near = near + weights[k] * near_of(k)
    joined = rows_joined(combined(own_ref, 24), near)
    beside = pltpu.roll(rows_joined(combined(from_right, 24), combined(from_corner_ref, 8)), 64, 1)
    lane_wide = iota((32, 128), 1)
    ending = jnp.where((lane_wide >= 125) & (c < 15), beside, joined[:, 256:384])
    surface = jnp.concatenate([joined[:, 128:256], ending], axis=1)
    zeta = surface[8:24]

    zeta_rows = jnp.where(row8 < 4, surface[24:32], surface[0:8])
    zeta_cols = jnp.where(lane16 < 64, beside[8:24], joined[8:24, 0:128])

    def wet_at(k):
        return jnp.where(k < bottom, land_ref[k].astype(F32), 0.0)

    above_rows = (row8 & 2) != 0
    row_flag = jnp.where(above_rows, has_up, has_down)
    row_flag_turned = jnp.where(above_rows, has_down, has_up)
    west_lanes = (lane16 & 2) != 0
    lane_flag = jnp.where(west_lanes, has_left, has_right)

    def row_pair(at, second):
        above = above_ref[at : at + 8]
        below = below_ref[at : at + 8]
        if second:
            return jnp.where(above_rows, below, above) * row_flag_turned
        return jnp.where(above_rows, above, below) * row_flag

    def turned_rows(pair, f):
        turn = (8 - ROW_TURNS[f]) % 8
        return pltpu.roll(pair, turn, 0) if turn else pair

    def tail_pair(k):
        return row_pair(8 * depth + 8 * (k // 2), k % 2 == 1)

    def tail_rows(k, f):
        return turned_rows(tail_pair(k), f + 2 * (k % 2))

    def col_pair(k):
        return jnp.where(west_lanes, west_ref[k], east_ref[k]) * lane_flag

    def turned_cols(pair, f):
        return pltpu.roll(pair, 128 - 4 * f, 1) if f else pair

    def next_of(x, axis):
        return pltpu.roll(x, x.shape[axis] - 1, axis)

    def last_of(x, axis):
        return pltpu.roll(x, 1, axis)

    def main_of(x):
        return x[0:16, 0:256]

    def spread_of(q, edge, faces, axis):
        wide = jnp.concatenate([q, edge], axis=axis)
        pair = wide + next_of(wide, axis)
        flux = faces * (8.0 * pair - last_of(pair, axis) - next_of(pair, axis))
        return main_of(flux - last_of(flux, axis))

    def gathered(m, edge, faces, axis):
        wide = jnp.concatenate([m, edge], axis=axis)
        h = faces * (wide - next_of(wide, axis))
        pair = h + last_of(h, axis)
        return main_of(8.0 * pair - last_of(pair, axis) - next_of(pair, axis))

    scale = 1.0 / 12.0
    ux_ref, uy_ref, theta_ref, salt_ref, forcing_ref, kappa_ref, inv_ref = [
        x.get() for x in (ux_in, uy_in, theta_in, salt_in, forcing_in, kappa_in, inv_in)
    ]
    couple_last = None
    state = None
    wet = wet_at(0)
    for k in range(depth):
        faces = tail_rows(k, 1)
        wide = jnp.concatenate([wet, pltpu.roll(faces, 7, 0)], axis=0)
        later = next_of(wide, 0)
        x_open = jnp.concatenate(
            [ux_ref[k] * wet * later[0:16], jnp.where(row8 == 7, faces * later[16:24], faces)], axis=0
        )
        x_open = x_open * scale
        columns = col_pair(k)
        faces = turned_cols(columns, 5)
        wide = jnp.concatenate([wet, pltpu.roll(faces, 127, 1)], axis=1)
        later = next_of(wide, 1)
        y_open = jnp.concatenate(
            [uy_ref[k] * wet * later[:, 0:256], jnp.where(lane16 == 127, faces * later[:, 256:384], faces)], axis=1
        )
        y_open = y_open * scale
        x_open_ref[k] = x_open
        y_open_ref[k] = y_open
        rows = row_pair(8 * k, False)
        advected = []
        for f, ref in ((0, theta_ref), (1, salt_ref)):
            q = ref[k]
            masked = q * wet
            along_rows = spread_of(masked, turned_rows(rows, f), x_open, 0)
            along_cols = spread_of(masked, turned_cols(columns, f), y_open, 1)
            advected.append(q - along_rows - along_cols)
        if k == 0:
            advected[0] = advected[0] + forcing_ref[...] * wet
        inverse = inv_ref[k]
        if k == 0:
            state = tuple(x * inverse for x in advected)
        else:
            state = tuple((x + couple_last * s) * inverse for x, s in zip(advected, state))
        theta_sweep_ref[k], salt_sweep_ref[k] = state
        if k < depth - 1:
            wet_next = wet_at(k + 1)
            couple_last = kappa_ref[k] * wet * wet_next
            wet = wet_next

    ratio_ref, w_ref, a_ref, c_ref = [x.get() for x in (ratio_in, w_in, a_in, c_in)]
    share = (0.2, -0.15)
    mu_later = None
    wet_later = None
    for k in range(depth - 1, -1, -1):
        wet = wet_at(k)
        rise = zeta * w_ref[k]
        mu = (a_ref[k] + share[0] * rise, c_ref[k] + share[1] * rise)
        if k < depth - 1:
            ratio = ratio_ref[k]
            new = (theta_sweep_ref[k] + ratio * state[0], salt_sweep_ref[k] + ratio * state[1])
            kappa_grad_ref[k] = -(wet * wet_later) * (
                (mu[0] - mu_later[0]) * (new[0] - state[0]) + (mu[1] - mu_later[1]) * (new[1] - state[1])
            )
            state = new
        rows = row_pair(8 * k, True)
        columns = col_pair(k)
        row_rise = zeta_rows * tail_rows(k, 0)
        col_rise = zeta_cols * turned_cols(columns, 4)
        x_open = x_open_ref[k]
        y_open = y_open_ref[k]
        for n, ref in ((0, theta_grad_ref), (1, salt_grad_ref)):
            row_edge = turned_rows(rows, 2 + n) + share[n] * row_rise
            col_edge = turned_cols(columns, 2 + n) + share[n] * col_rise
            total = gathered(mu[n], row_edge, x_open, 0) + gathered(mu[n], col_edge, y_open, 1)
            ref[k] = mu[n] - wet * total
        if k == 0:
            forcing_grad_ref[...] = zeta + wet * mu[0]
        mu_later = mu
        wet_later = wet
        if k % 5 == 0:
            theta_out.send(k, 5)
            salt_out.send(k, 5)
            kappa_out.send(k, min(5, depth - 1 - k))
    forcing_out.send()


def around(count, step):
    return [(i, (i + step) % count) for i in range(count)]


def across(step):
    return [
        (16 * i + j, 16 * ((i + step) % 16) + (j + step) % 16) for i in range(16) for j in range(16)
    ]


def shards(
    theta,
    salt,
    velocity_x,
    velocity_y,
    land_mask,
    kappa,
    forcing,
    bottom,
    theta_cot,
    salt_cot,
    surface_cot,
):
    depth = theta.shape[0]
    whole = theta.shape
    place = jnp.stack([lax.axis_index(TROW), lax.axis_index(TCOL)]).astype(jnp.int32)
    rows, cols, corner = staged(edges_kernel, (surface_cot, bottom), [(16, 256), (32, 128), (16, 128)])
    rows = lax.ppermute(rows, TROW, around(16, 1))
    cols = lax.ppermute(cols, TCOL, around(16, 1))
    corner = lax.ppermute(corner, ALL, across(1))
    lines = 8 * depth + 8 * ((depth + 1) // 2)
    columns = (depth, 16, 128)
    extra_lines, extra_cols = 48, 6
    a, c, w, inv, ratio, down, up, right, left = staged(
        columns_kernel,
        (land_mask, kappa, bottom, theta_cot, salt_cot, theta, salt, velocity_x, velocity_y),
        [whole] * 4 + [kappa.shape, (lines, 256), (lines + extra_lines, 256), columns, (depth + extra_cols, 16, 128)],
        views={6: (0, lines), 8: (0, depth)},
    )
    above = lax.ppermute(down, TROW, around(16, 1))
    west = lax.ppermute(right, TCOL, around(16, 1))
    up, left, sums, own, tip = staged(
        krylov_kernel,
        (surface_cot, bottom, rows, cols, corner, up, left),
        [up.shape, left.shape, (256, 128), (96, 384), (32, 128)],
        place=place,
        aliases={5: 0, 6: 1},
        views={0: (lines, extra_lines), 1: (depth, extra_cols)},
    )
    below = lax.ppermute(up, TROW, around(16, -1))
    east = lax.ppermute(left, TCOL, around(16, -1))
    tip = lax.ppermute(tip, ALL, across(-1))
    sums = lax.all_to_all(sums, ALL, 0, 0, tiled=True)
    return tuple(
        staged(
            final_kernel,
            (sums, own, tip, land_mask, bottom, above, below, west, east, velocity_x, velocity_y, theta, salt)
            + (forcing, kappa, inv, ratio, w, a, c),
            [whole, whole, kappa.shape, forcing.shape],
            place=place,
            scratch=[whole, whole, (depth, 24, 256), (depth, 16, 384)],
            sends=16,
        )
    )


def solution(mesh):
    split = Mesh(mesh.devices.reshape(4, 2, 2, 2, 8), ALL)
    block = P(None, TROW, TCOL)
    flat = P(TROW, TCOL)
    return jax.shard_map(
        shards,
        mesh=split,
        in_specs=(block,) * 6 + (flat, flat, block, block, flat),
        out_specs=(block, block, block, flat),
        check_vma=False,
    )
```

time: 119 us -> 96.7 us (0.81)
  Pallas kernels: 45.5 us -> 34.6 us
  local copies, waits for them, and re-layouts: 27.2 us -> 23.1 us
  starting transfers between devices: 37.4 us -> 33.6 us
  waiting for transfers between devices: 6.5 us -> 3.42 us
    pallas_call x4, Pallas kernels: 45.5 us -> 34.6 us  [staged(): pl.pallas_call(body, out_shape=[jax.ShapeDtypeStruct(s, F32) for s in out...]
    ppermute x2 -> x0, starting transfers between devices: 7 us -> none  [the longest x1 5.8 us: shards(): side = lax.ppermute(side, TCOL, around(16, -1))]
    unnamed x86 -> x74, local copies, waits for them, and re-layouts: 27.2 us -> 23.1 us
    ppermute x2 -> x0, waiting for transfers between devices: 4.01 us -> none  [the longest x1 2.52 us: shards(): near = lax.ppermute(near, TROW, around(16, -1))]
    ppermute x1, starting transfers between devices: 2.18 us -> 5.88 us  [shards(): tip = lax.ppermute(tip, ALL, across(-1))]
    ppermute x1, waiting for transfers between devices: 0.01 us -> 2.32 us  [shards(): west = lax.ppermute(right, TCOL, around(16, 1))]
    ppermute x1, starting transfers between devices: 1.58 us -> 0.01 us  [shards(): west = lax.ppermute(right, TCOL, around(16, 1))]
    ppermute x1, starting transfers between devices: 5.45 us -> 6.95 us  [shards(): east = lax.ppermute(left, TCOL, around(16, -1))]
  transfers between devices with their start and end apart: 11 -> 9, of which waited for: 3 -> 2; matrix products, arithmetic and copies ran while one was open for 0% -> 0% of each run, Pallas kernels for 4% -> 6%
where the time goes in v2:
time: 96.7 us; the launch traced here: 95.8 us
  Pallas kernels  34.6 us (36%)
  starting transfers between devices  33.6 us (35%)
  local copies, waits for them, and re-layouts  23.1 us (24%)
  waiting for transfers between devices  3.42 us (4%)
  between operations  1.01 us (1%)
    pallas_call x4, Pallas kernels, staged(): pl.pallas_call(body, out_shape=[jax.ShapeDtypeStruct(s, F32) for s in out...  34.6 us
    unnamed x74, local copies, waits for them, and re-layouts  23.1 us
    all_to_all x1, starting transfers between devices, shards(): sums = lax.all_to_all(sums, ALL, 0, 0, tiled=True)  13.2 us
    ppermute x1, starting transfers between devices, shards(): east = lax.ppermute(left, TCOL, around(16, -1))  6.95 us
    ppermute x1, starting transfers between devices, shards(): tip = lax.ppermute(tip, ALL, across(-1))  5.88 us
    ppermute x1, starting transfers between devices, shards(): corner = lax.ppermute(corner, ALL, across(1))  4.12 us
    ppermute x1, waiting for transfers between devices, shards(): west = lax.ppermute(right, TCOL, around(16, 1))  2.32 us
  transfers between devices with their start and end apart: 9, of which 2 were waited for; matrix products, arithmetic and copies ran while one was open for 0% of the time, Pallas kernels for 6%

profile of v2, /device:TPU:1, one launch (start us, length us, event | category | flops | bytes accessed | tf_op | source)
XLA Modules:
  0.0 95.8 jit_solution(6752675283373020930)
XLA Ops:
  0.6 0.7 copy-done.20
  1.4 0.7 copy-done.28
  2.2 4.1 %collective-permute-start.2 = (f32[16,128]{1,0:T(8,128)S(1)}, f32[16,128]{1,0:T(8,128)S(1)}, u32[]{:S(2)}, u32[]{:S(2)}) collective-permute-start(f32[16,128]{1,0:T(8,128)S(1)} %get-tuple-element.23), channel_id=1, source_target_pairs={{0,17},{1,18},{2,19},{3,20},{4,21},{5,22},{6,23},{7,24},{8,25},{9,... | collective-permute-start | bytes 24584 | tf_op jit(solution)/shard_map/ppermute | solution.py:682
  6.3 1.6 %collective-permute-start.1 = (f32[32,128]{1,0:T(8,128)S(1)}, f32[32,128]{1,0:T(8,128)S(1)}, u32[]{:S(2)}, u32[]{:S(2)}) collective-permute-start(f32[32,128]{1,0:T(8,128)S(1)} %get-tuple-element.22), channel_id=1, source_target_pairs={{0,1},{1,2},{2,3},{3,4},{4,5},{5,6},{6,7},{7,8},{8,9},{9,10},{10,1... | collective-permute-start | bytes 49160 | tf_op jit(solution)/shard_map/ppermute | solution.py:681
  8.7 1.0 %copy-done = s32[25,16,256]{2,1,0:T(8,128)S(1)} copy-done((s32[25,16,256]{2,1,0:T(8,128)S(1)}, s32[25,16,256]{2,1,0:T(8,128)}, u32[]{:S(2)}) %copy-start) | copy-done | bytes 409624
  9.7 1.0 %copy-done.2 = f32[25,16,256]{2,1,0:T(8,128)S(1)} copy-done((f32[25,16,256]{2,1,0:T(8,128)S(1)}, f32[25,16,256]{2,1,0:T(8,128)}, u32[]{:S(2)}) %copy-start.2) | copy-done | bytes 409624
  10.7 1.0 %copy-done.4 = f32[25,16,256]{2,1,0:T(8,128)S(1)} copy-done((f32[25,16,256]{2,1,0:T(8,128)S(1)}, f32[25,16,256]{2,1,0:T(8,128)}, u32[]{:S(2)}) %copy-start.4) | copy-done | bytes 409624
  11.7 1.0 %copy-done.6 = f32[25,16,256]{2,1,0:T(8,128)S(1)} copy-done((f32[25,16,256]{2,1,0:T(8,128)S(1)}, f32[25,16,256]{2,1,0:T(8,128)}, u32[]{:S(2)}) %copy-start.6) | copy-done | bytes 409624
  12.7 1.0 %copy-done.8 = f32[25,16,256]{2,1,0:T(8,128)S(1)} copy-done((f32[25,16,256]{2,1,0:T(8,128)S(1)}, f32[25,16,256]{2,1,0:T(8,128)}, u32[]{:S(2)}) %copy-start.8) | copy-done | bytes 409624
  13.7 1.0 %copy-done.10 = f32[24,16,256]{2,1,0:T(8,128)S(1)} copy-done((f32[24,16,256]{2,1,0:T(8,128)S(1)}, f32[24,16,256]{2,1,0:T(8,128)}, u32[]{:S(2)}) %copy-start.10) | copy-done | bytes 393240
  14.7 1.0 %copy-done.12 = f32[25,16,256]{2,1,0:T(8,128)S(1)} copy-done((f32[25,16,256]{2,1,0:T(8,128)S(1)}, f32[25,16,256]{2,1,0:T(8,128)}, u32[]{:S(2)}) %copy-start.12) | copy-done | bytes 409624
  15.7 1.0 %copy-done.13 = f32[25,16,256]{2,1,0:T(8,128)S(1)} copy-done((f32[25,16,256]{2,1,0:T(8,128)S(1)}, f32[25,16,256]{2,1,0:T(8,128)}, u32[]{:S(2)}) %copy-start.13) | copy-done | bytes 409624
  16.7 5.9 %shard_map.139 = (f32[25,16,256]{2,1,0:T(8,128)S(1)}, f32[25,16,256]{2,1,0:T(8,128)S(1)}, f32[25,16,256]{2,1,0:T(8,128)S(1)}, f32[25,16,256]{2,1,0:T(8,128)S(1)}...) custom-call(s32[25,16,256]{2,1,0:T(8,128)S(1)} %copy-done, ...), custom_call_target="tpu_custom_call" | custom-call | tf_op jit(solution)/shard_map/pallas_call | solution.py:132
  22.6 0.7 copy-done.14
  23.3 0.7 copy-done.16
  24.1 0.7 copy-done.18
  24.9 2.5 %shard_map.140 = (f32[352,256]{1,0:T(8,128)}, f32[31,16,128]{2,1,0:T(8,128)S(1)}, f32[256,128]{1,0:T(8,128)S(1)}, f32[96,384]{1,0:T(8,128)S(1)}, f32[32,128]{1,0:T(8,128)S(1)}) custom-call(s32[2]{0:T(128)S(1)} %pad_add_fusion.refs_0_, f32[16,256]{1,0:T(8,128)S(1)} %copy-done.29, ...), custom_call_target="tpu_custom_call", output_to_operand_aliasing={{0}: (6, {}), {1}: (7, {})} | custom-call | tf_op jit(solution)/shard_map/pallas_call | solution.py:132
  29.3 0.8 collective-permute-start.5
  30.1 1.0 %collective-permute-start.4 = (f32[304,256]{1,0:T(8,128)}, f32[304,256]{1,0:T(8,128)}, u32[]{:S(2)}, u32[]{:S(2)}) collective-permute-start(f32[304,256]{1,0:T(8,128)} %get-tuple-element.29), channel_id=1, source_target_pairs={{0,16},{16,32},{32,48},{48,64},{64,80},{80,96},{96,112},{112,128},... | collective-permute-start | bytes 933896 | tf_op jit(solution)/shard_map/ppermute | solution.py:692
  31.1 13.2 %all-to-all-start = ((f32[256,1,128]{2,1,0:T(1,128)}), f32[256,1,128]{2,1,0:T(1,128)S(1)}, u32[]{:S(2)}, u32[]{:S(2)}) async-start(f32[256,1,128]{2,1,0:T(1,128)} %bitcast.7), calls=%async_computation | async-start | bytes 262144 | tf_op jit(solution)/shard_map/all_to_all | solution.py:705
  44.3 6.9 %collective-permute-start.7 = (f32[31,16,128]{2,1,0:T(8,128)}, f32[31,16,128]{2,1,0:T(8,128)S(1)}, u32[]{:S(2)}, u32[]{:S(2)}) collective-permute-start(f32[31,16,128]{2,1,0:T(8,128)} %copy-done.24), channel_id=1, source_target_pairs={{0,15},{1,0},{2,1},{3,2},{4,3},{5,4},{6,5},{7,6},{8,7},{9,8},{10,9... | collective-permute-start | bytes 761864 | tf_op jit(solution)/shard_map/ppermute | solution.py:703
  51.3 5.9 %collective-permute-start.3 = (f32[32,128]{1,0:T(8,128)}, f32[32,128]{1,0:T(8,128)S(1)}, u32[]{:S(2)}, u32[]{:S(2)}) collective-permute-start(f32[32,128]{1,0:T(8,128)} %copy-done.36), channel_id=1, source_target_pairs={{0,255},{1,240},{2,241},{3,242},{4,243},{5,244},{6,245},{7,246},{8... | collective-permute-start | bytes 49160 | tf_op jit(solution)/shard_map/ppermute | solution.py:704
  57.1 1.1 %collective-permute-done.3.refs_3_ = f32[32,128]{1,0:T(8,128)S(1)} collective-permute-done((f32[32,128]{1,0:T(8,128)}, f32[32,128]{1,0:T(8,128)S(1)}, u32[]{:S(2)}, u32[]{:S(2)}) %collective-permute-start.3) | collective-permute-done | bytes 16416 | tf_op jit(solution)/shard_map/ppermute | solution.py:704
  58.8 2.3 %collective-permute-done.6.refs_8_ = f32[25,16,128]{2,1,0:T(8,128)S(1)} collective-permute-done((f32[25,16,128]{2,1,0:T(8,128)}, f32[25,16,128]{2,1,0:T(8,128)S(1)}, u32[]{:S(2)}, u32[]{:S(2)}) %collective-permute-start.6) | collective-permute-done | bytes 204832 | tf_op jit(solution)/shard_map/ppermute | solution.py:693
  63.2 1.0 %copy-done.15 = f32[25,16,256]{2,1,0:T(8,128)S(1)} copy-done((f32[25,16,256]{2,1,0:T(8,128)S(1)}, f32[25,16,256]{2,1,0:T(8,128)}, u32[]{:S(2)}) %copy-start.15) | copy-done | bytes 409624
  64.2 1.0 %copy-done.17 = f32[25,16,256]{2,1,0:T(8,128)S(1)} copy-done((f32[25,16,256]{2,1,0:T(8,128)S(1)}, f32[25,16,256]{2,1,0:T(8,128)}, u32[]{:S(2)}) %copy-start.17) | copy-done | bytes 409624
  65.2 1.0 %copy-done.19 = f32[24,16,256]{2,1,0:T(8,128)S(1)} copy-done((f32[24,16,256]{2,1,0:T(8,128)S(1)}, f32[24,16,256]{2,1,0:T(8,128)}, u32[]{:S(2)}) %copy-start.19) | copy-done | bytes 393240
  66.2 0.9 copy-done.23
  67.1 0.9 copy-done.26
  68.0 0.7 copy-done.30
  68.8 0.7 copy-done.32
  69.5 26.1 %shard_map.141 = (f32[25,16,256]{2,1,0:T(8,128)}, f32[25,16,256]{2,1,0:T(8,128)}, f32[24,16,256]{2,1,0:T(8,128)}, f32[16,256]{1,0:T(8,128)}) custom-call(s32[2]{0:T(128)S(1)} %copy-done.34, f32[256,128]{1,0:T(8,128)S(1)} %bitcast.6, f32[96,384]{1,0:T(8,128)S(1)} %get-tuple-element.27.refs_2_, f32[32,128]{1,0:T(8,128)S(1)} %copy-done.32, ...), custom_call_target="tpu_custom_call" | custom-call | tf_op jit(solution)/shard_map/pallas_call | solution.py:132
  (65 shorter events, 5.4 us)
Async XLA Ops:
  2.2 22.6 %collective-permute-start.2 = (f32[16,128]{1,0:T(8,128)S(1)}, f32[16,128]{1,0:T(8,128)S(1)}, u32[]{:S(2)}, u32[]{:S(2)}) collective-permute-start(f32[16,128]{1,0:T(8,128)S(1)} %get-tuple-element.23), channel_id=1, source_target_pairs={{0,17},{1,18},{2,19},{3,20},{4,21},{5,22},{6,23},{7,24},{8,25},{9,... | collective-permute-start | bytes 24584 | tf_op jit(solution)/shard_map/ppermute | solution.py:682
  6.3 18.5 %collective-permute-start = (f32[16,256]{1,0:T(8,128)S(1)}, f32[16,256]{1,0:T(8,128)S(1)}, u32[]{:S(2)}, u32[]{:S(2)}) collective-permute-start(f32[16,256]{1,0:T(8,128)S(1)} %get-tuple-element.21), channel_id=1, source_target_pairs={{0,16},{16,32},{32,48},{48,64},{64,80},{80,96},{96,112},{112,128},... | collective-permute-start | bytes 49160 | tf_op jit(solution)/shard_map/ppermute | solution.py:680
  6.3 18.5 %collective-permute-start.1 = (f32[32,128]{1,0:T(8,128)S(1)}, f32[32,128]{1,0:T(8,128)S(1)}, u32[]{:S(2)}, u32[]{:S(2)}) collective-permute-start(f32[32,128]{1,0:T(8,128)S(1)} %get-tuple-element.22), channel_id=1, source_target_pairs={{0,1},{1,2},{2,3},{3,4},{4,5},{5,6},{6,7},{7,8},{8,9},{9,10},{10,1... | collective-permute-start | bytes 49160 | tf_op jit(solution)/shard_map/ppermute | solution.py:681
  8.7 1.0 %copy-start = (s32[25,16,256]{2,1,0:T(8,128)S(1)}, s32[25,16,256]{2,1,0:T(8,128)}, u32[]{:S(2)}) copy-start(s32[25,16,256]{2,1,0:T(8,128)} %refs_4_.3) | copy-start | bytes 1228804
  9.7 1.0 %copy-start.2 = (f32[25,16,256]{2,1,0:T(8,128)S(1)}, f32[25,16,256]{2,1,0:T(8,128)}, u32[]{:S(2)}) copy-start(f32[25,16,256]{2,1,0:T(8,128)} %refs_12_.1) | copy-start | bytes 1228804
  10.7 1.0 %copy-start.4 = (f32[25,16,256]{2,1,0:T(8,128)S(1)}, f32[25,16,256]{2,1,0:T(8,128)}, u32[]{:S(2)}) copy-start(f32[25,16,256]{2,1,0:T(8,128)} %refs_13_.1) | copy-start | bytes 1228804
  11.7 1.0 %copy-start.6 = (f32[25,16,256]{2,1,0:T(8,128)S(1)}, f32[25,16,256]{2,1,0:T(8,128)}, u32[]{:S(2)}) copy-start(f32[25,16,256]{2,1,0:T(8,128)} %refs_10_.1) | copy-start | bytes 1228804
  12.7 1.0 %copy-start.8 = (f32[25,16,256]{2,1,0:T(8,128)S(1)}, f32[25,16,256]{2,1,0:T(8,128)}, u32[]{:S(2)}) copy-start(f32[25,16,256]{2,1,0:T(8,128)} %refs_11_.1) | copy-start | bytes 1228804
  13.7 1.0 %copy-start.10 = (f32[24,16,256]{2,1,0:T(8,128)S(1)}, f32[24,16,256]{2,1,0:T(8,128)}, u32[]{:S(2)}) copy-start(f32[24,16,256]{2,1,0:T(8,128)} %refs_15_.1) | copy-start | bytes 1179652
  14.7 1.0 %copy-start.12 = (f32[25,16,256]{2,1,0:T(8,128)S(1)}, f32[25,16,256]{2,1,0:T(8,128)}, u32[]{:S(2)}) copy-start(f32[25,16,256]{2,1,0:T(8,128)} %refs_3_.1) | copy-start | bytes 1228804
  15.7 1.0 %copy-start.13 = (f32[25,16,256]{2,1,0:T(8,128)S(1)}, f32[25,16,256]{2,1,0:T(8,128)}, u32[]{:S(2)}) copy-start(f32[25,16,256]{2,1,0:T(8,128)} %refs_4_.2) | copy-start | bytes 1228804
  16.7 8.2 %copy-start.33 = (s32[2]{0:T(128)}, s32[2]{0:T(128)S(1)}, u32[]{:S(2)}) copy-start(s32[2]{0:T(128)S(1)} %pad_add_fusion.refs_0_) | copy-start | bytes 28
  16.7 8.2 %copy-start.29 = (f32[16,256]{1,0:T(8,128)S(1)}, f32[16,256]{1,0:T(8,128)}, u32[]{:S(2)}) copy-start(f32[16,256]{1,0:T(8,128)} %refs_1_.5) | copy-start | bytes 49156
  16.7 45.9 %copy-start.5 = (f32[25,16,256]{2,1,0:T(8,128)S(1)}, f32[25,16,256]{2,1,0:T(8,128)}, u32[]{:S(2)}) copy-start(f32[25,16,256]{2,1,0:T(8,128)} %refs_13_.1) | copy-start | bytes 1228804
  16.7 45.9 %copy-start.7 = (f32[25,16,256]{2,1,0:T(8,128)S(1)}, f32[25,16,256]{2,1,0:T(8,128)}, u32[]{:S(2)}) copy-start(f32[25,16,256]{2,1,0:T(8,128)} %refs_10_.1) | copy-start | bytes 1228804
  16.7 45.9 %copy-start.9 = (f32[25,16,256]{2,1,0:T(8,128)S(1)}, f32[25,16,256]{2,1,0:T(8,128)}, u32[]{:S(2)}) copy-start(f32[25,16,256]{2,1,0:T(8,128)} %refs_11_.1) | copy-start | bytes 1228804
  16.7 45.9 %copy-start.11 = (f32[24,16,256]{2,1,0:T(8,128)S(1)}, f32[24,16,256]{2,1,0:T(8,128)}, u32[]{:S(2)}) copy-start(f32[24,16,256]{2,1,0:T(8,128)} %refs_15_.1) | copy-start | bytes 1179652
  22.6 0.8 copy-start.14
  24.8 2.5 %copy-start.35 = (f32[25,16,128]{2,1,0:T(8,128)}, f32[25,16,128]{2,1,0:T(8,128)S(1)}, u32[]{:S(2)}) copy-start(f32[25,16,128]{2,1,0:T(8,128)S(1)} %get-tuple-element.31) | copy-start | bytes 614404
  24.9 37.7 %copy-start.1 = (s32[25,16,256]{2,1,0:T(8,128)S(1)}, s32[25,16,256]{2,1,0:T(8,128)}, u32[]{:S(2)}) copy-start(s32[25,16,256]{2,1,0:T(8,128)} %refs_4_.3) | copy-start | bytes 1228804
  24.9 37.7 %copy-start.3 = (f32[25,16,256]{2,1,0:T(8,128)S(1)}, f32[25,16,256]{2,1,0:T(8,128)}, u32[]{:S(2)}) copy-start(f32[25,16,256]{2,1,0:T(8,128)} %refs_12_.1) | copy-start | bytes 1228804
  29.3 33.2 %collective-permute-start.5 = (f32[352,256]{1,0:T(8,128)}, f32[352,256]{1,0:T(8,128)}, u32[]{:S(2)}, u32[]{:S(2)}) collective-permute-start(f32[352,256]{1,0:T(8,128)} %get-tuple-element.30), channel_id=1, source_target_pairs={{0,240},{16,0},{32,16},{48,32},{64,48},{80,64},{96,80},{112,96},{1... | collective-permute-start | bytes 1081352 | tf_op jit(solution)/shard_map/ppermute | solution.py:702
  30.1 32.4 %collective-permute-start.4 = (f32[304,256]{1,0:T(8,128)}, f32[304,256]{1,0:T(8,128)}, u32[]{:S(2)}, u32[]{:S(2)}) collective-permute-start(f32[304,256]{1,0:T(8,128)} %get-tuple-element.29), channel_id=1, source_target_pairs={{0,16},{16,32},{32,48},{48,64},{64,80},{80,96},{96,112},{112,128},... | collective-permute-start | bytes 933896 | tf_op jit(solution)/shard_map/ppermute | solution.py:692
  31.1 31.4 %all-to-all-start = ((f32[256,1,128]{2,1,0:T(1,128)}), f32[256,1,128]{2,1,0:T(1,128)S(1)}, u32[]{:S(2)}, u32[]{:S(2)}) async-start(f32[256,1,128]{2,1,0:T(1,128)} %bitcast.7), calls=%async_computation | async-start | bytes 262144 | tf_op jit(solution)/shard_map/all_to_all | solution.py:705
  44.3 17.5 %collective-permute-start.7 = (f32[31,16,128]{2,1,0:T(8,128)}, f32[31,16,128]{2,1,0:T(8,128)S(1)}, u32[]{:S(2)}, u32[]{:S(2)}) collective-permute-start(f32[31,16,128]{2,1,0:T(8,128)} %copy-done.24), channel_id=1, source_target_pairs={{0,15},{1,0},{2,1},{3,2},{4,3},{5,4},{6,5},{7,6},{8,7},{9,8},{10,9... | collective-permute-start | bytes 761864 | tf_op jit(solution)/shard_map/ppermute | solution.py:703
  51.3 9.9 %collective-permute-start.6 = (f32[25,16,128]{2,1,0:T(8,128)}, f32[25,16,128]{2,1,0:T(8,128)S(1)}, u32[]{:S(2)}, u32[]{:S(2)}) collective-permute-start(f32[25,16,128]{2,1,0:T(8,128)} %copy-done.35), channel_id=1, source_target_pairs={{0,1},{1,2},{2,3},{3,4},{4,5},{5,6},{6,7},{7,8},{8,9},{9,10},{10,1... | collective-permute-start | bytes 614408 | tf_op jit(solution)/shard_map/ppermute | solution.py:693
  51.3 7.0 %collective-permute-start.3 = (f32[32,128]{1,0:T(8,128)}, f32[32,128]{1,0:T(8,128)S(1)}, u32[]{:S(2)}, u32[]{:S(2)}) collective-permute-start(f32[32,128]{1,0:T(8,128)} %copy-done.36), channel_id=1, source_target_pairs={{0,255},{1,240},{2,241},{3,242},{4,243},{5,244},{6,245},{7,246},{8... | collective-permute-start | bytes 49160 | tf_op jit(solution)/shard_map/ppermute | solution.py:704
  63.2 1.0 %copy-start.15 = (f32[25,16,256]{2,1,0:T(8,128)S(1)}, f32[25,16,256]{2,1,0:T(8,128)}, u32[]{:S(2)}) copy-start(f32[25,16,256]{2,1,0:T(8,128)} %copy-done.14) | copy-start | bytes 1228804
  64.2 1.0 %copy-start.17 = (f32[25,16,256]{2,1,0:T(8,128)S(1)}, f32[25,16,256]{2,1,0:T(8,128)}, u32[]{:S(2)}) copy-start(f32[25,16,256]{2,1,0:T(8,128)} %copy-done.16) | copy-start | bytes 1228804
  65.2 1.0 %copy-start.19 = (f32[24,16,256]{2,1,0:T(8,128)S(1)}, f32[24,16,256]{2,1,0:T(8,128)}, u32[]{:S(2)}) copy-start(f32[24,16,256]{2,1,0:T(8,128)} %copy-done.18) | copy-start | bytes 1179652
  66.2 0.9 copy-start.23
  67.1 0.9 copy-start.26
  (14 other events, 9.6 us)

commit v3 on v2

--- a/solution.py
+++ b/solution.py
@@ -1,7 +1,8 @@
-import functools
+import math
 
 import jax
 import jax.numpy as jnp
+import numpy as np
 from jax import lax
 from jax.experimental import pallas as pl
 from jax.experimental.pallas import tpu as pltpu
@@ -18,7 +19,7 @@
 VM = pl.BlockSpec(memory_space=pltpu.VMEM)
 SM = pl.BlockSpec(memory_space=pltpu.SMEM)
 HB = pl.BlockSpec(memory_space=pltpu.HBM)
-PARAMS = pltpu.CompilerParams(vmem_limit_bytes=24 * 1024 * 1024)
+PARAMS = pltpu.CompilerParams(vmem_limit_bytes=58 * 1024 * 1024)
 
 
 def iota(shape, dim):
@@ -94,24 +95,21 @@
         self.pending.append(copy)
 
 
-def staged(kernel, args, outs, place=None, scratch=(), sends=None, aliases=None, views=None):
-    views = views or {}
-    aliases = aliases or {}
-    aliased = [args[i] for i in aliases]
-    loaded_args = [a for i, a in enumerate(args) if i not in aliases]
+def staged(kernel, args, outs, place=None, scratch=(), sends=None, after=(), flops=0):
     smem = [] if place is None else [place]
-    n_in, n_alias, n_out = len(loaded_args), len(aliased), len(outs)
+    cuts = [a[1:] if isinstance(a, tuple) else None for a in args]
+    args = [a[0] if isinstance(a, tuple) else a for a in args]
+    n_in, n_out = len(args), len(outs)
     sends = sends or n_out
-    staging = [pltpu.VMEM(a.shape, a.dtype) for a in loaded_args]
-    for n, shape in enumerate(outs):
-        held = (views[n][1],) + tuple(shape[1:]) if n in views else shape
-        staging.append(pltpu.VMEM(held, F32))
+    staging = [pltpu.VMEM(a.shape if cut is None else (cut[1],) + a.shape[1:], a.dtype) for a, cut in zip(args, cuts)]
+    staging += [pltpu.VMEM(s, F32) for s in outs]
 
     def body(*refs):
         refs = list(refs)
         places = [refs.pop(0) for _ in smem]
         sources = [refs.pop(0) for _ in range(n_in)]
-        for _ in range(n_alias):
+        sources = [s if cut is None else s.at[pl.ds(*cut)] for s, cut in zip(sources, cuts)]
+        for _ in after:
             refs.pop(0)
         targets = [refs.pop(0) for _ in range(n_out)]
         buffers = [refs.pop(0) for _ in range(n_in)]
@@ -121,8 +119,7 @@
         pending = []
         given = []
         for n in range(n_out):
-            target = targets[n].at[pl.ds(*views[n])] if n in views else targets[n]
-            given.append(Stored(target, holds[n], lambda: out_sems.at[len(pending)], pending))
+            given.append(Stored(targets[n], holds[n], lambda: out_sems.at[len(pending)], pending))
         kernel(ins, given, *places, *refs)
         for x in ins:
             x.get()
@@ -132,29 +129,16 @@
     return pl.pallas_call(
         body,
         out_shape=[jax.ShapeDtypeStruct(s, F32) for s in outs],
-        in_specs=[SM] * len(smem) + [HB] * (n_in + n_alias),
+        in_specs=[SM] * len(smem) + [HB] * (n_in + len(after)),
         out_specs=[HB] * n_out,
-        input_output_aliases={len(smem) + n_in + i: out for i, out in enumerate(aliases.values())},
         scratch_shapes=staging
-        + [pltpu.VMEM(s, F32) for s in scratch]
+        + [pltpu.VMEM(s, t) for s, t in scratch]
         + [pltpu.SemaphoreType.DMA((n_in,)), pltpu.SemaphoreType.DMA((sends,))],
+        cost_estimate=pl.CostEstimate(
+            flops=flops, bytes_accessed=4 * (sum(a.size for a in args) + sum(map(math.prod, outs))), transcendentals=0
+        ),
         compiler_params=PARAMS,
-    )(*smem, *loaded_args, *aliased)
-
-
-def edges_kernel(ins, outs):
-    cot_ref, bottom_ref = [x.get() for x in ins]
-    rows_ref, cols_ref, corner_ref = [x.ref for x in outs]
-    cot = cot_ref[...]
-    bottom = bottom_ref[...].astype(F32)
-    rows_ref[0:8] = cot[8:16]
-    rows_ref[8:16] = bottom[8:16]
-    cols_ref[0:16] = cot[:, 128:256]
-    cols_ref[16:32] = bottom[:, 128:256]
-    corner_ref[0:8] = cot[8:16, 128:256]
-    corner_ref[8:16] = bottom[8:16, 128:256]
-    for out in outs:
-        out.send()
+    )(*smem, *args, *after)
 
 
 def merge_rows(a, b, step):
@@ -176,10 +160,8 @@
 
 def krylov_kernel(ins, outs, place_ref):
     cot_ref, bottom_ref, rows_ref, cols_ref, corner_ref = [x.get() for x in ins]
-    up_out, left_out, sums_out, own_out, diag_out = outs
-    sums_ref, own_ref, up_ref, left_ref, diag_ref = [
-        x.ref for x in (sums_out, own_out, up_out, left_out, diag_out)
-    ]
+    up_out, left_out, own_out, diag_out = outs
+    own_ref, up_ref, left_ref, diag_ref = [x.ref for x in (own_out, up_out, left_out, diag_out)]
     r = place_ref[0]
     c = place_ref[1]
     shape = (24, 384)
@@ -188,7 +170,7 @@
 
     def window(main, at):
         top = jnp.concatenate([corner_ref[8 * at : 8 * at + 8], rows_ref[8 * at : 8 * at + 8]], axis=1)
-        rest = jnp.concatenate([cols_ref[16 * at : 16 * at + 16], main], axis=1)
+        rest = jnp.concatenate([cols_ref[at], main], axis=1)
         return jnp.concatenate([top, rest], axis=0)
 
     inside = ((row >= 8) | (r > 0)) & ((lane >= 128) | (c > 0))
@@ -214,17 +196,27 @@
 
     for k, v in enumerate(vectors):
         own_ref[24 * k : 24 * k + 24] = v
+        own_ref[24 * (KRYLOV + k) : 24 * (KRYLOV + k) + 24] = images[k]
         near = pltpu.roll(v[0:16], 12, 0)[0:8]
-        up_ref[8 * k : 8 * k + 8] = near[:, 128:384]
-        up_ref[32 + 8 * (k // 2) : 40 + 8 * (k // 2), 128 * (k % 2) : 128 * (k % 2) + 128] = near[:, 0:128]
-        beside = pltpu.roll(v[:, 0:256], 192, 1)[:, 0:128]
-        for n in range(3):
-            at = 3 * k + n
-            left_ref[at // 2, 8 * (at % 2) : 8 * (at % 2) + 8] = beside[8 * n : 8 * n + 8]
+        up_ref[8 * k : 8 * k + 8] = near
+        left_ref[24 * k : 24 * k + 24] = pltpu.roll(v[:, 0:256], 192, 1)[:, 0:128]
         diag_ref[8 * k : 8 * k + 8] = pltpu.roll(near[:, 0:256], 192, 1)[:, 0:128]
     for out in (up_out, left_out, diag_out, own_out):
         out.send()
 
+
+def products_kernel(ins, outs, place_ref):
+    own_ref = ins[0].get()
+    sums_out = outs[0]
+    sums_ref = sums_out.ref
+    r = place_ref[0]
+    c = place_ref[1]
+    shape = (24, 384)
+    row = iota(shape, 0)
+    lane = iota(shape, 1)
+    vectors = [own_ref[24 * k : 24 * k + 24] for k in range(KRYLOV)]
+    images = [own_ref[24 * k : 24 * k + 24] for k in range(KRYLOV, 2 * KRYLOV)]
+    start = vectors[0]
     domain = (
         (row >= 4)
         & (row < jnp.where(r == 15, 24, 20))
@@ -313,10 +305,16 @@
 
 def columns_kernel(ins, outs):
     depth = ins[0].ref.shape[0]
-    land_in, kappa_in, bottom_in, tcot_in, scot_in, theta_in, salt_in, ux_in, uy_in = ins
-    a_out, c_out, w_out, inv_out, ratio_out, down_out, up_out, right_out, left_out = outs
-    a_ref, c_ref, w_ref, inv_ref, ratio_ref, down_ref, up_ref, right_ref, left_ref = [x.ref for x in outs]
+    land_in, kappa_in, bottom_in, tcot_in, scot_in, theta_in, salt_in, ux_in, uy_in, surface_in = ins
+    a_out, c_out, w_out, inv_out, ratio_out, down_out, up_out, right_out, left_out, corner_out = outs
+    a_ref, c_ref, w_ref, inv_ref, ratio_ref, down_ref, up_ref, right_ref, left_ref, corner_ref = [x.ref for x in outs]
     bottom = bottom_in.get()[...]
+    lines = 8 * depth + 8 * ((depth + 1) // 2)
+    for n, field in enumerate((surface_in.get()[...], bottom.astype(F32))):
+        down_ref[lines + 8 * n : lines + 8 * n + 8] = field[8:16]
+        right_ref[depth + n] = field[:, 128:256]
+        corner_ref[8 * n : 8 * n + 8] = field[8:16, 128:256]
+    corner_out.send()
     land_ref = land_in.get()
     kappa_ref = kappa_in.get()
     tcot_ref = tcot_in.get()
@@ -393,11 +391,74 @@
         out.send()
 
 
-def final_kernel(ins, outs, place_ref, theta_sweep_ref, salt_sweep_ref, x_open_ref, y_open_ref):
+SCALE = 1.0 / 12.0
+BF16 = jnp.bfloat16
+
+
+class Edges:
+    def __init__(self, place_ref, depth, above, below, west, east):
+        r = place_ref[0]
+        c = place_ref[1]
+        self.depth, self.above, self.below, self.west, self.east = depth, above, below, west, east
+        self.row8 = iota((8, 256), 0)
+        self.lane16 = iota((16, 128), 1)
+        has_up = jnp.where(r > 0, 1.0, 0.0)
+        has_down = jnp.where(r < 15, 1.0, 0.0)
+        has_left = jnp.where(c > 0, 1.0, 0.0)
+        has_right = jnp.where(c < 15, 1.0, 0.0)
+        self.above_rows = (self.row8 & 2) != 0
+        self.row_flags = (
+            jnp.where(self.above_rows, has_up, has_down),
+            jnp.where(self.above_rows, has_down, has_up),
+        )
+        self.west_lanes = (self.lane16 & 2) != 0
+        self.lane_flag = jnp.where(self.west_lanes, has_left, has_right)
+
+    def row_pair(self, at, second):
+        above = self.above[at : at + 8]
+        below = self.below[at : at + 8]
+        if second:
+            return jnp.where(self.above_rows, below, above) * self.row_flags[1]
+        return jnp.where(self.above_rows, above, below) * self.row_flags[0]
+
+    def turned_rows(self, pair, f):
+        turn = (8 - ROW_TURNS[f]) % 8
+        return pltpu.roll(pair, turn, 0) if turn else pair
+
+    def tail_rows(self, k, f):
+        pair = self.row_pair(8 * self.depth + 8 * (k // 2), k % 2 == 1)
+        return self.turned_rows(pair, f + 2 * (k % 2))
+
+    def col_pair(self, k):
+        return jnp.where(self.west_lanes, self.west[k], self.east[k]) * self.lane_flag
+
+    def turned_cols(self, pair, f):
+        return pltpu.roll(pair, 128 - 4 * f, 1) if f else pair
+
+
+def next_of(x, axis):
+    return pltpu.roll(x, x.shape[axis] - 1, axis)
+
+
+def last_of(x, axis):
+    return pltpu.roll(x, 1, axis)
+
+
+def two_parts(x):
+    high = x.astype(BF16)
+    return jnp.concatenate([high, (x - high.astype(F32)).astype(BF16)], axis=1)
+
+
+def stencil(offsets, columns):
+    out = np.zeros((384, columns), np.float32)
+    for j in range(columns):
+        for offset, value in offsets:
+            out[(j + offset) % 384, j] += value
+    return jnp.asarray(np.concatenate([out, out]), BF16)
+
+
+def forward_kernel(ins, outs, place_ref, parts_ref, filtered_ref, theta_sweep_ref, salt_sweep_ref):
     (
-        sums_in,
-        own_in,
-        corner_in,
         land_in,
         bottom_in,
         above_in,
@@ -408,40 +469,125 @@
         uy_in,
         theta_in,
         salt_in,
+        filter_in,
         forcing_in,
         kappa_in,
         inv_in,
         ratio_in,
+    ) = ins
+    x_out, y_out, theta_out, salt_out = outs
+    x_open_ref, y_open_ref, theta_drop_ref, salt_drop_ref = [x.ref for x in outs]
+    depth = theta_in.ref.shape[0]
+    bottom = bottom_in.get()[...]
+    land_ref = land_in.get()
+    edges = Edges(place_ref, depth, *[x.get() for x in (above_in, below_in, west_in, east_in)])
+    row8, lane16 = edges.row8, edges.lane16
+    ux_ref, uy_ref, theta_ref, salt_ref = [x.get() for x in (ux_in, uy_in, theta_in, salt_in)]
+
+    def wet_at(k):
+        return jnp.where(k < bottom, land_ref[k].astype(F32), 0.0)
+
+    for k in range(depth):
+        wet = wet_at(k)
+        faces = edges.tail_rows(k, 1)
+        wide = jnp.concatenate([wet, pltpu.roll(faces, 7, 0)], axis=0)
+        later = next_of(wide, 0)
+        x_open = jnp.concatenate(
+            [ux_ref[k] * wet * later[0:16], jnp.where(row8 == 7, faces * later[16:24], faces)], axis=0
+        )
+        x_open_ref[k] = x_open * SCALE
+        columns = edges.col_pair(k)
+        faces = edges.turned_cols(columns, 5)
+        wide = jnp.concatenate([wet, pltpu.roll(faces, 127, 1)], axis=1)
+        later = next_of(wide, 1)
+        y_open = jnp.concatenate(
+            [uy_ref[k] * wet * later[:, 0:256], jnp.where(lane16 == 127, faces * later[:, 256:384], faces)], axis=1
+        )
+        y_open_ref[k] = y_open * SCALE
+        for f, ref in ((0, theta_ref), (1, salt_ref)):
+            wide = jnp.concatenate([ref[k] * wet, edges.turned_cols(columns, f)], axis=1)
+            at = 16 * (depth * f + k)
+            parts_ref[at : at + 16] = two_parts(wide)
+    x_out.send()
+    y_out.send()
+    filtered_ref[...] = jnp.dot(parts_ref[...], filter_in.get()[...], preferred_element_type=F32)
+    forcing_ref, kappa_ref, inv_ref, ratio_ref = [x.get() for x in (forcing_in, kappa_in, inv_in, ratio_in)]
+
+    couple_last = None
+    state = None
+    wet = wet_at(0)
+    for k in range(depth):
+        rows = edges.row_pair(8 * k, False)
+        x_open = x_open_ref[k]
+        y_open = y_open_ref[k]
+        advected = []
+        for f, ref in ((0, theta_ref), (1, salt_ref)):
+            q = ref[k]
+            wide = jnp.concatenate([q * wet, edges.turned_rows(rows, f)], axis=0)
+            pair = wide + next_of(wide, 0)
+            flux = x_open * (8.0 * pair - last_of(pair, 0) - next_of(pair, 0))
+            change = (flux - last_of(flux, 0))[0:16]
+            at = 16 * (depth * f + k)
+            flux = y_open * filtered_ref[at : at + 16]
+            change = change + (flux - last_of(flux, 1))[:, 0:256]
+            advected.append(q - change)
+        if k == 0:
+            advected[0] = advected[0] + forcing_ref[...] * wet
+        inverse = inv_ref[k]
+        if k == 0:
+            state = tuple(x * inverse for x in advected)
+        else:
+            state = tuple((x + couple_last * s) * inverse for x, s in zip(advected, state))
+        theta_sweep_ref[k], salt_sweep_ref[k] = state
+        if k < depth - 1:
+            wet_next = wet_at(k + 1)
+            couple_last = kappa_ref[k] * wet * wet_next
+            wet = wet_next
+    wet_later = wet
+    for k in range(depth - 2, -1, -1):
+        wet = wet_at(k)
+        ratio = ratio_ref[k]
+        new = (theta_sweep_ref[k] + ratio * state[0], salt_sweep_ref[k] + ratio * state[1])
+        opened = wet * wet_later
+        theta_drop_ref[k] = opened * (state[0] - new[0])
+        salt_drop_ref[k] = opened * (state[1] - new[1])
+        state = new
+        wet_later = wet
+    theta_out.send()
+    salt_out.send()
+
+
+def backward_kernel(ins, outs, place_ref, parts_ref, filtered_ref):
+    (
+        sums_in,
+        own_in,
+        near_in,
+        side_in,
+        corner_in,
+        land_in,
+        bottom_in,
+        above_in,
+        below_in,
+        west_in,
+        east_in,
         w_in,
         a_in,
         c_in,
+        theta_drop_in,
+        salt_drop_in,
+        x_open_in,
+        y_open_in,
+        filter_in,
     ) = ins
     theta_out, salt_out, kappa_out, forcing_out = outs
     theta_grad_ref, salt_grad_ref, kappa_grad_ref, forcing_grad_ref = [x.ref for x in outs]
-    depth = theta_in.ref.shape[0]
-    lines = 8 * depth + 8 * ((depth + 1) // 2)
+    depth = w_in.ref.shape[0]
     r = place_ref[0]
     c = place_ref[1]
-    has_up = jnp.where(r > 0, 1.0, 0.0)
     has_down = jnp.where(r < 15, 1.0, 0.0)
-    has_left = jnp.where(c > 0, 1.0, 0.0)
-    has_right = jnp.where(c < 15, 1.0, 0.0)
-    row8 = iota((8, 256), 0)
-    lane16 = iota((16, 128), 1)
-    bottom = bottom_in.get()[...]
-    land_ref = land_in.get()
-    sums_ref, own_ref, from_corner_ref, above_ref, below_ref, west_ref, east_ref = [
-        x.get() for x in (sums_in, own_in, corner_in, above_in, below_in, west_in, east_in)
+    sums_ref, own_ref, from_below_ref, from_right_ref, from_corner_ref = [
+        x.get() for x in (sums_in, own_in, near_in, side_in, corner_in)
     ]
-    from_right_ref = [east_ref[depth + n] for n in range(6)]
-
-    def near_of(k):
-        at = lines + 8 * k
-        side = lines + 32 + 8 * (k // 2)
-        start = 128 * (k % 2)
-        return jnp.concatenate([below_ref[side : side + 8, start : start + 128], below_ref[at : at + 8]], axis=1)
-
-    from_right = jnp.concatenate(from_right_ref, axis=0)
 
     small = (8, 128)
     small_row = iota(small, 0)
@@ -501,153 +647,60 @@
         middle = jnp.where((row8 >= 5) & (r < 15), turned, upper[16:24])
         return jnp.concatenate([upper[0:16], middle, turned * has_down], axis=0)
 
-    near = weights[0] * near_of(0)
-    for k in range(1, KRYLOV):
-        near = near + weights[k] * near_of(k)
-    joined = rows_joined(combined(own_ref, 24), near)
-    beside = pltpu.roll(rows_joined(combined(from_right, 24), combined(from_corner_ref, 8)), 64, 1)
+    joined = rows_joined(combined(own_ref, 24), combined(from_below_ref, 8))
+    beside = pltpu.roll(rows_joined(combined(from_right_ref, 24), combined(from_corner_ref, 8)), 64, 1)
     lane_wide = iota((32, 128), 1)
     ending = jnp.where((lane_wide >= 125) & (c < 15), beside, joined[:, 256:384])
     surface = jnp.concatenate([joined[:, 128:256], ending], axis=1)
     zeta = surface[8:24]
 
-    zeta_rows = jnp.where(row8 < 4, surface[24:32], surface[0:8])
-    zeta_cols = jnp.where(lane16 < 64, beside[8:24], joined[8:24, 0:128])
+    bottom = bottom_in.get()[...]
+    land_ref = land_in.get()
+    edges = Edges(place_ref, depth, *[x.get() for x in (above_in, below_in, west_in, east_in)])
+    zeta_rows = jnp.where(edges.row8 < 4, surface[24:32], surface[0:8])
+    zeta_cols = jnp.where(edges.lane16 < 64, beside[8:24], joined[8:24, 0:128])
 
     def wet_at(k):
         return jnp.where(k < bottom, land_ref[k].astype(F32), 0.0)
 
-    above_rows = (row8 & 2) != 0
-    row_flag = jnp.where(above_rows, has_up, has_down)
-    row_flag_turned = jnp.where(above_rows, has_down, has_up)
-    west_lanes = (lane16 & 2) != 0
-    lane_flag = jnp.where(west_lanes, has_left, has_right)
-
-    def row_pair(at, second):
-        above = above_ref[at : at + 8]
-        below = below_ref[at : at + 8]
-        if second:
-            return jnp.where(above_rows, below, above) * row_flag_turned
-        return jnp.where(above_rows, above, below) * row_flag
-
-    def turned_rows(pair, f):
-        turn = (8 - ROW_TURNS[f]) % 8
-        return pltpu.roll(pair, turn, 0) if turn else pair
-
-    def tail_pair(k):
-        return row_pair(8 * depth + 8 * (k // 2), k % 2 == 1)
-
-    def tail_rows(k, f):
-        return turned_rows(tail_pair(k), f + 2 * (k % 2))
-
-    def col_pair(k):
-        return jnp.where(west_lanes, west_ref[k], east_ref[k]) * lane_flag
-
-    def turned_cols(pair, f):
-        return pltpu.roll(pair, 128 - 4 * f, 1) if f else pair
-
-    def next_of(x, axis):
-        return pltpu.roll(x, x.shape[axis] - 1, axis)
-
-    def last_of(x, axis):
-        return pltpu.roll(x, 1, axis)
-
-    def main_of(x):
-        return x[0:16, 0:256]
-
-    def spread_of(q, edge, faces, axis):
-        wide = jnp.concatenate([q, edge], axis=axis)
-        pair = wide + next_of(wide, axis)
-        flux = faces * (8.0 * pair - last_of(pair, axis) - next_of(pair, axis))
-        return main_of(flux - last_of(flux, axis))
-
-    def gathered(m, edge, faces, axis):
-        wide = jnp.concatenate([m, edge], axis=axis)
-        h = faces * (wide - next_of(wide, axis))
-        pair = h + last_of(h, axis)
-        return main_of(8.0 * pair - last_of(pair, axis) - next_of(pair, axis))
-
-    scale = 1.0 / 12.0
-    ux_ref, uy_ref, theta_ref, salt_ref, forcing_ref, kappa_ref, inv_ref = [
-        x.get() for x in (ux_in, uy_in, theta_in, salt_in, forcing_in, kappa_in, inv_in)
+    w_ref, a_ref, c_ref, theta_drop_ref, salt_drop_ref, x_open_ref, y_open_ref = [
+        x.get() for x in (w_in, a_in, c_in, theta_drop_in, salt_drop_in, x_open_in, y_open_in)
     ]
-    couple_last = None
-    state = None
-    wet = wet_at(0)
-    for k in range(depth):
-        faces = tail_rows(k, 1)
-        wide = jnp.concatenate([wet, pltpu.roll(faces, 7, 0)], axis=0)
-        later = next_of(wide, 0)
-        x_open = jnp.concatenate(
-            [ux_ref[k] * wet * later[0:16], jnp.where(row8 == 7, faces * later[16:24], faces)], axis=0
-        )
-        x_open = x_open * scale
-        columns = col_pair(k)
-        faces = turned_cols(columns, 5)
-        wide = jnp.concatenate([wet, pltpu.roll(faces, 127, 1)], axis=1)
-        later = next_of(wide, 1)
-        y_open = jnp.concatenate(
-            [uy_ref[k] * wet * later[:, 0:256], jnp.where(lane16 == 127, faces * later[:, 256:384], faces)], axis=1
-        )
-        y_open = y_open * scale
-        x_open_ref[k] = x_open
-        y_open_ref[k] = y_open
-        rows = row_pair(8 * k, False)
-        advected = []
-        for f, ref in ((0, theta_ref), (1, salt_ref)):
-            q = ref[k]
-            masked = q * wet
-            along_rows = spread_of(masked, turned_rows(rows, f), x_open, 0)
-            along_cols = spread_of(masked, turned_cols(columns, f), y_open, 1)
-            advected.append(q - along_rows - along_cols)
-        if k == 0:
-            advected[0] = advected[0] + forcing_ref[...] * wet
-        inverse = inv_ref[k]
-        if k == 0:
-            state = tuple(x * inverse for x in advected)
-        else:
-            state = tuple((x + couple_last * s) * inverse for x, s in zip(advected, state))
-        theta_sweep_ref[k], salt_sweep_ref[k] = state
-        if k < depth - 1:
-            wet_next = wet_at(k + 1)
-            couple_last = kappa_ref[k] * wet * wet_next
-            wet = wet_next
-
-    ratio_ref, w_ref, a_ref, c_ref = [x.get() for x in (ratio_in, w_in, a_in, c_in)]
     share = (0.2, -0.15)
     mu_later = None
-    wet_later = None
     for k in range(depth - 1, -1, -1):
         wet = wet_at(k)
         rise = zeta * w_ref[k]
         mu = (a_ref[k] + share[0] * rise, c_ref[k] + share[1] * rise)
         if k < depth - 1:
-            ratio = ratio_ref[k]
-            new = (theta_sweep_ref[k] + ratio * state[0], salt_sweep_ref[k] + ratio * state[1])
-            kappa_grad_ref[k] = -(wet * wet_later) * (
-                (mu[0] - mu_later[0]) * (new[0] - state[0]) + (mu[1] - mu_later[1]) * (new[1] - state[1])
-            )
-            state = new
-        rows = row_pair(8 * k, True)
-        columns = col_pair(k)
-        row_rise = zeta_rows * tail_rows(k, 0)
-        col_rise = zeta_cols * turned_cols(columns, 4)
+            kappa_grad_ref[k] = theta_drop_ref[k] * (mu[0] - mu_later[0]) + salt_drop_ref[k] * (mu[1] - mu_later[1])
+        rows = edges.row_pair(8 * k, True)
+        columns = edges.col_pair(k)
+        row_rise = zeta_rows * edges.tail_rows(k, 0)
+        col_rise = zeta_cols * edges.turned_cols(columns, 4)
         x_open = x_open_ref[k]
         y_open = y_open_ref[k]
         for n, ref in ((0, theta_grad_ref), (1, salt_grad_ref)):
-            row_edge = turned_rows(rows, 2 + n) + share[n] * row_rise
-            col_edge = turned_cols(columns, 2 + n) + share[n] * col_rise
-            total = gathered(mu[n], row_edge, x_open, 0) + gathered(mu[n], col_edge, y_open, 1)
-            ref[k] = mu[n] - wet * total
+            wide = jnp.concatenate([mu[n], edges.turned_cols(columns, 2 + n) + share[n] * col_rise], axis=1)
+            at = 16 * (depth * n + k)
+            parts_ref[at : at + 16] = two_parts(y_open * (wide - next_of(wide, 1)))
+            wide = jnp.concatenate([mu[n], edges.turned_rows(rows, 2 + n) + share[n] * row_rise], axis=0)
+            h = x_open * (wide - next_of(wide, 0))
+            pair = h + last_of(h, 0)
+            change = (8.0 * pair - last_of(pair, 0) - next_of(pair, 0))[0:16]
+            ref[k] = mu[n] - wet * change
         if k == 0:
             forcing_grad_ref[...] = zeta + wet * mu[0]
         mu_later = mu
-        wet_later = wet
-        if k % 5 == 0:
-            theta_out.send(k, 5)
-            salt_out.send(k, 5)
-            kappa_out.send(k, min(5, depth - 1 - k))
+    kappa_out.send()
     forcing_out.send()
+    filtered_ref[...] = jnp.dot(parts_ref[...], filter_in.get()[...], preferred_element_type=F32)
+    for n, ref, out in ((0, theta_grad_ref, theta_out), (1, salt_grad_ref, salt_out)):
+        for k in range(depth):
+            at = 16 * (depth * n + k)
+            ref[k] = ref[k] - wet_at(k) * filtered_ref[at : at + 16]
+            if k % 5 == 4:
+                out.send(k - 4, 5)
 
 
 def around(count, step):
@@ -676,42 +729,50 @@
     depth = theta.shape[0]
     whole = theta.shape
     place = jnp.stack([lax.axis_index(TROW), lax.axis_index(TCOL)]).astype(jnp.int32)
-    rows, cols, corner = staged(edges_kernel, (surface_cot, bottom), [(16, 256), (32, 128), (16, 128)])
-    rows = lax.ppermute(rows, TROW, around(16, 1))
-    cols = lax.ppermute(cols, TCOL, around(16, 1))
-    corner = lax.ppermute(corner, ALL, across(1))
     lines = 8 * depth + 8 * ((depth + 1) // 2)
     columns = (depth, 16, 128)
-    extra_lines, extra_cols = 48, 6
-    a, c, w, inv, ratio, down, up, right, left = staged(
+    a, c, w, inv, ratio, down, up, right, left, corner = staged(
         columns_kernel,
-        (land_mask, kappa, bottom, theta_cot, salt_cot, theta, salt, velocity_x, velocity_y),
-        [whole] * 4 + [kappa.shape, (lines, 256), (lines + extra_lines, 256), columns, (depth + extra_cols, 16, 128)],
-        views={6: (0, lines), 8: (0, depth)},
+        (land_mask, kappa, bottom, theta_cot, salt_cot, theta, salt, velocity_x, velocity_y, surface_cot),
+        [whole] * 4
+        + [kappa.shape, (lines + 16, 256), (lines, 256), (depth + 2, 16, 128), columns, (16, 128)],
+        flops=100 * theta.size,
     )
     above = lax.ppermute(down, TROW, around(16, 1))
     west = lax.ppermute(right, TCOL, around(16, 1))
-    up, left, sums, own, tip = staged(
-        krylov_kernel,
-        (surface_cot, bottom, rows, cols, corner, up, left),
-        [up.shape, left.shape, (256, 128), (96, 384), (32, 128)],
-        place=place,
-        aliases={5: 0, 6: 1},
-        views={0: (lines, extra_lines), 1: (depth, extra_cols)},
-    )
+    corner = lax.ppermute(corner, ALL, across(1))
     below = lax.ppermute(up, TROW, around(16, -1))
     east = lax.ppermute(left, TCOL, around(16, -1))
+    near, side, own, tip = staged(
+        krylov_kernel,
+        (surface_cot, bottom, (above, lines, 16), (west, depth, 2), corner),
+        [(32, 384), (96, 128), (192, 384), (32, 128)],
+        place=place,
+    )
+    near = lax.ppermute(near, TROW, around(16, -1))
+    side = lax.ppermute(side, TCOL, around(16, -1))
     tip = lax.ppermute(tip, ALL, across(-1))
+    x_open, y_open, theta_drop, salt_drop = staged(
+        forward_kernel,
+        (land_mask, bottom, above, below, west, east, velocity_x, velocity_y, theta, salt)
+        + (stencil(((-1, -1), (0, 7), (1, 7), (2, -1)), 384), forcing, kappa, inv, ratio),
+        [(depth, 24, 256), (depth, 16, 384), kappa.shape, kappa.shape],
+        place=place,
+        after=(own,),
+        flops=200 * theta.size,
+        scratch=[((32 * depth, 768), BF16), ((32 * depth, 384), F32), (whole, F32), (whole, F32)],
+    )
+    (sums,) = staged(products_kernel, (own,), [(256, 128)], place=place, after=(theta_drop, near, side, tip))
     sums = lax.all_to_all(sums, ALL, 0, 0, tiled=True)
     return tuple(
         staged(
-            final_kernel,
-            (sums, own, tip, land_mask, bottom, above, below, west, east, velocity_x, velocity_y, theta, salt)
-            + (forcing, kappa, inv, ratio, w, a, c),
+            backward_kernel,
+            (sums, own, near, side, tip, land_mask, bottom, above, below, west, east, w, a, c)
+            + (theta_drop, salt_drop, x_open, y_open, stencil(((-2, -1), (-1, 7), (0, 7), (1, -1)), 256)),
             [whole, whole, kappa.shape, forcing.shape],
             place=place,
-            scratch=[whole, whole, (depth, 24, 256), (depth, 16, 384)],
-            sends=16,
+            scratch=[((32 * depth, 768), BF16), ((32 * depth, 256), F32)],
+            sends=12,
         )
     )
 

time: 96.7 us -> 75.6 us (0.78)
  blocking collectives: 0 us -> 22.7 us
  local copies, waits for them, and re-layouts: 23.1 us -> 2.83 us
  starting transfers between devices: 33.6 us -> 15.8 us
  Pallas kernels: 34.6 us -> 25.7 us
  waiting for transfers between devices: 3.42 us -> 6.6 us
    all_to_all x0 -> x1, blocking collectives: none -> 22.7 us  [shards(): sums = lax.all_to_all(sums, ALL, 0, 0, tiled=True)]
    unnamed x74 -> x18, local copies, waits for them, and re-layouts: 23.1 us -> 2.83 us
    all_to_all x1 -> x0, starting transfers between devices: 13.2 us -> none  [shards(): sums = lax.all_to_all(sums, ALL, 0, 0, tiled=True)]
    pallas_call x4 -> x5, Pallas kernels: 34.6 us -> 25.7 us  [staged(): pl.pallas_call(body, out_shape=[jax.ShapeDtypeStruct(s, F32) for s in out...]
    ppermute x1, waiting for transfers between devices: 0.01 us -> 6.58 us  [shards(): corner = lax.ppermute(corner, ALL, across(1))]
    ppermute x1, starting transfers between devices: 5.88 us -> 0.56 us  [shards(): tip = lax.ppermute(tip, ALL, across(-1))]
    ppermute x1, starting transfers between devices: 4.12 us -> 0.01 us  [shards(): corner = lax.ppermute(corner, ALL, across(1))]
    ppermute x2, starting transfers between devices: 1.64 us -> 4.61 us  [the longest x1 4.6 us: shards(): near = lax.ppermute(near, TROW, around(16, -1))]
  transfers between devices with their start and end apart: 9 -> 8, of which waited for: 2 -> 1; matrix products, arithmetic and copies ran while one was open for 0% -> 1% of each run, Pallas kernels for 6% -> 13%
where the time goes in v3:
time: 75.6 us; the launch traced here: 75.2 us
  Pallas kernels  25.7 us (34%)
  blocking collectives  22.7 us (30%)
  starting transfers between devices  15.8 us (21%)
  waiting for transfers between devices  6.6 us (9%)
  local copies, waits for them, and re-layouts  2.83 us (4%)
  between operations  0.91 us (1%)
    pallas_call x5, Pallas kernels, staged(): pl.pallas_call(body, out_shape=[jax.ShapeDtypeStruct(s, F32) for s in out...  25.7 us
    all_to_all x1, blocking collectives, shards(): sums = lax.all_to_all(sums, ALL, 0, 0, tiled=True)  22.7 us
    ppermute x1, waiting for transfers between devices, shards(): corner = lax.ppermute(corner, ALL, across(1))  6.58 us
    ppermute x1, starting transfers between devices, shards(): east = lax.ppermute(left, TCOL, around(16, -1))  6.28 us
    ppermute x1, starting transfers between devices, shards(): near = lax.ppermute(near, TROW, around(16, -1))  4.6 us
    unnamed x18, local copies, waits for them, and re-layouts  2.83 us
    ppermute x1, starting transfers between devices, shards(): above = lax.ppermute(down, TROW, around(16, 1))  2.76 us
  transfers between devices with their start and end apart: 8, of which 1 were waited for; matrix products, arithmetic and copies ran while one was open for 1% of the time, Pallas kernels for 13%

profile of v3, /device:TPU:1, one launch (start us, length us, event | category | flops | bytes accessed | tf_op | source)
XLA Modules:
  0.0 75.2 jit_solution(18382639644459710696)
XLA Ops:
  0.6 5.6 %shard_map.156 = (f32[25,16,256]{2,1,0:T(8,128)}, f32[25,16,256]{2,1,0:T(8,128)}, f32[25,16,256]{2,1,0:T(8,128)}, f32[25,16,256]{2,1,0:T(8,128)}, f32[24,16,256]...) custom-call(s32[25,16,256]{2,1,0:T(8,128)} %refs_6_.3, ...), custom_call_target="tpu_custom_call" | custom-call | flops 10240000 | bytes 6397952 | tf_op jit(solution)/shard_map/pallas_call | solution.py:129
  6.2 0.0 copy-start.8
  6.2 2.8 %collective-permute-start = (f32[320,256]{1,0:T(8,128)}, f32[320,256]{1,0:T(8,128)S(1)}, u32[]{:S(2)}, u32[]{:S(2)}) collective-permute-start(f32[320,256]{1,0:T(8,128)} %get-tuple-element.22), channel_id=1, source_target_pairs={{0,16},{16,32},{32,48},{48,64},{64,80},{80,96},{96,112},{112,128},... | collective-permute-start | bytes 983048 | tf_op jit(solution)/shard_map/ppermute | solution.py:741
  9.0 0.6 collective-permute-start.3
  9.6 1.0 %collective-permute-start.1 = (f32[27,16,128]{2,1,0:T(8,128)}, f32[27,16,128]{2,1,0:T(8,128)S(1)}, u32[]{:S(2)}, u32[]{:S(2)}) collective-permute-start(f32[27,16,128]{2,1,0:T(8,128)} %get-tuple-element.23), channel_id=1, source_target_pairs={{0,1},{1,2},{2,3},{3,4},{4,5},{5,6},{6,7},{7,8},{8,9},{9,10},{10,1... | collective-permute-start | bytes 663560 | tf_op jit(solution)/shard_map/ppermute | solution.py:742
  10.6 6.3 %collective-permute-start.4 = (f32[25,16,128]{2,1,0:T(8,128)}, f32[25,16,128]{2,1,0:T(8,128)S(1)}, u32[]{:S(2)}, u32[]{:S(2)}) collective-permute-start(f32[25,16,128]{2,1,0:T(8,128)} %get-tuple-element.27), channel_id=1, source_target_pairs={{0,15},{1,0},{2,1},{3,2},{4,3},{5,4},{6,5},{7,6},{8,7},{9,8},{10,9... | collective-permute-start | bytes 614408 | tf_op jit(solution)/shard_map/ppermute | solution.py:745
  16.9 0.0 collective-permute-start.2
  16.9 0.6 pad_add_fusion.refs_0_
  17.5 6.6 %collective-permute-done.2.refs_5_ = f32[16,128]{1,0:T(8,128)S(1)} collective-permute-done((f32[16,128]{1,0:T(8,128)S(1)}, f32[16,128]{1,0:T(8,128)S(1)}, u32[]{:S(2)}, u32[]{:S(2)}) %collective-permute-start.2) | collective-permute-done | bytes 8224 | tf_op jit(solution)/shard_map/ppermute | solution.py:743
  24.1 0.0 collective-permute-done.1.refs_4_.refs_5_.refs_10_
  24.1 0.0 collective-permute-done.refs_3_.refs_8_
  24.1 0.6 copy-done.7
  24.7 0.1 copy-done.1
  24.8 0.7 copy-done
  25.5 2.6 %shard_map.157 = (f32[32,384]{1,0:T(8,128)}, f32[96,128]{1,0:T(8,128)}, f32[192,384]{1,0:T(8,128)}, f32[32,128]{1,0:T(8,128)}) custom-call(s32[2]{0:T(128)} %pad_add_fusion.refs_0_, f32[16,256]{1,0:T(8,128)} %refs_1_.4, s32[16,256]{1,0:T(8,128)} %refs_7_.5, f32[320,256]{1,0:T(8,128)} %copy-done, f32[27,16,128]{2,1,0:T(8,128)} %copy-done.1, f32[16,128]{1,0:T(8,128)} %copy-done.7), custom_call_target="tpu_custom_call" | custom-call | bytes 999424 | tf_op jit(solution)/shard_map/pallas_call | solution.py:129
  28.1 4.6 %collective-permute-start.5 = (f32[32,384]{1,0:T(8,128)}, f32[32,384]{1,0:T(8,128)S(1)}, u32[]{:S(2)}, u32[]{:S(2)}) collective-permute-start(f32[32,384]{1,0:T(8,128)} %get-tuple-element.31), channel_id=1, source_target_pairs={{0,240},{16,0},{32,16},{48,32},{64,48},{80,64},{96,80},{112,96},{1... | collective-permute-start | bytes 147464 | tf_op jit(solution)/shard_map/ppermute | solution.py:752
  32.7 0.0 collective-permute-start.6
  32.7 0.6 collective-permute-start.7
  33.3 0.0 collective-permute-done.4.refs_6_.refs_11_
  33.3 0.0 collective-permute-done.3.refs_4_.refs_9_
  33.3 0.7 copy-done.3
  34.0 0.1 copy-done.2
  34.1 6.9 %shard_map.158 = (f32[25,24,256]{2,1,0:T(8,128)}, f32[25,16,384]{2,1,0:T(8,128)}, f32[24,16,256]{2,1,0:T(8,128)}, f32[24,16,256]{2,1,0:T(8,128)}) custom-call(s32[2]{0:T(128)} %pad_add_fusion.refs_0_, s32[25,16,256]{2,1,0:T(8,128)} %refs_6_.3, s32[16,256]{1,0:T(8,128)} %refs_7_.5, f32[320,256]{1,0:T(8,128)} %copy-done, f32[304,256]{1,0:T(8,128)} %copy-done.2, ...), custom_call_target="tpu_custom_call" | custom-call | flops 20480000 | bytes 7536640 | tf_op jit(solution)/shard_map/pallas_call | solution.py:129
  41.0 0.0 collective-permute-done.7.refs_5_
  41.0 0.0 collective-permute-done.5.refs_3_
  41.1 0.0 collective-permute-done.6.refs_4_
  41.1 0.5 copy-done.6
  41.6 0.0 copy-done.4
  41.7 0.0 copy-done.5
  41.7 3.2 %shard_map.159 = f32[256,128]{1,0:T(8,128)} custom-call(s32[2]{0:T(128)} %pad_add_fusion.refs_0_, f32[192,384]{1,0:T(8,128)} %get-tuple-element.25.refs_16_.refs_1_.refs_2_, f32[24,16,256]{2,1,0:T(8,128)} %get-tuple-element.30.refs_2_.refs_15_, f32[32,384]{1,0:T(8,128)} %copy-done.4, f32[96,128]{1,0:T(8,128)} %copy-done.5, f32[32,128]{1,0:T(8,128)} %copy-done.6), custom_call_target="tpu_custom_call" | custom-call | bytes 425984 | tf_op jit(solution)/shard_map/pallas_call | solution.py:129
  44.9 22.7 %all_to_all.11 = f32[256,1,128]{2,1,0:T(1,128)} all-to-all(f32[256,1,128]{2,1,0:T(1,128)} %bitcast.7), channel_id=1, replica_groups=mesh['trow_0'=4,'trow_1'=2,'trow_2'=2,'tcol_0'=2,'tcol_1'=8] {'trow_0','..., dimensions={0} | all-to-all | bytes 262144 | tf_op jit(solution)/shard_map/all_to_all | solution.py:766
  67.6 7.5 %shard_map.160 = (f32[25,16,256]{2,1,0:T(8,128)}, f32[25,16,256]{2,1,0:T(8,128)}, f32[24,16,256]{2,1,0:T(8,128)}, f32[16,256]{1,0:T(8,128)}) custom-call(s32[2]{0:T(128)} %pad_add_fusion.refs_0_, f32[256,128]{1,0:T(8,128)} %bitcast.6, f32[192,384]{1,0:T(8,128)} %get-tuple-element.25.refs_16_.refs_1_.refs_2_, f32[32,384]{1,0:T(8,128)} %copy-done.4, ...), custom_call_target="tpu_custom_call" | custom-call | bytes 7290880 | tf_op jit(solution)/shard_map/pallas_call | solution.py:129
  (9 shorter events, 0.0 us)
Async XLA Ops:
  6.2 10.7 %copy-start.8 = (f32[16,128]{1,0:T(8,128)S(1)}, f32[16,128]{1,0:T(8,128)}, u32[]{:S(2)}) copy-start(f32[16,128]{1,0:T(8,128)} %get-tuple-element.24) | copy-start | bytes 24580
  6.2 17.9 %collective-permute-start = (f32[320,256]{1,0:T(8,128)}, f32[320,256]{1,0:T(8,128)S(1)}, u32[]{:S(2)}, u32[]{:S(2)}) collective-permute-start(f32[320,256]{1,0:T(8,128)} %get-tuple-element.22), channel_id=1, source_target_pairs={{0,16},{16,32},{32,48},{48,64},{64,80},{80,96},{96,112},{112,128},... | collective-permute-start | bytes 983048 | tf_op jit(solution)/shard_map/ppermute | solution.py:741
  9.0 24.3 %collective-permute-start.3 = (f32[304,256]{1,0:T(8,128)}, f32[304,256]{1,0:T(8,128)S(1)}, u32[]{:S(2)}, u32[]{:S(2)}) collective-permute-start(f32[304,256]{1,0:T(8,128)} %get-tuple-element.26), channel_id=1, source_target_pairs={{0,240},{16,0},{32,16},{48,32},{64,48},{80,64},{96,80},{112,96},{1... | collective-permute-start | bytes 933896 | tf_op jit(solution)/shard_map/ppermute | solution.py:744
  9.6 14.5 %collective-permute-start.1 = (f32[27,16,128]{2,1,0:T(8,128)}, f32[27,16,128]{2,1,0:T(8,128)S(1)}, u32[]{:S(2)}, u32[]{:S(2)}) collective-permute-start(f32[27,16,128]{2,1,0:T(8,128)} %get-tuple-element.23), channel_id=1, source_target_pairs={{0,1},{1,2},{2,3},{3,4},{4,5},{5,6},{6,7},{7,8},{8,9},{9,10},{10,1... | collective-permute-start | bytes 663560 | tf_op jit(solution)/shard_map/ppermute | solution.py:742
  10.6 22.7 %collective-permute-start.4 = (f32[25,16,128]{2,1,0:T(8,128)}, f32[25,16,128]{2,1,0:T(8,128)S(1)}, u32[]{:S(2)}, u32[]{:S(2)}) collective-permute-start(f32[25,16,128]{2,1,0:T(8,128)} %get-tuple-element.27), channel_id=1, source_target_pairs={{0,15},{1,0},{2,1},{3,2},{4,3},{5,4},{6,5},{7,6},{8,7},{9,8},{10,9... | collective-permute-start | bytes 614408 | tf_op jit(solution)/shard_map/ppermute | solution.py:745
  16.9 7.2 %collective-permute-start.2 = (f32[16,128]{1,0:T(8,128)S(1)}, f32[16,128]{1,0:T(8,128)S(1)}, u32[]{:S(2)}, u32[]{:S(2)}) collective-permute-start(f32[16,128]{1,0:T(8,128)S(1)} %copy-done.8), channel_id=1, source_target_pairs={{0,17},{1,18},{2,19},{3,20},{4,21},{5,22},{6,23},{7,24},{8,25},{9,... | collective-permute-start | bytes 24584 | tf_op jit(solution)/shard_map/ppermute | solution.py:743
  24.1 0.6 copy-start.7
  24.1 0.7 copy-start.1
  24.8 0.7 copy-start
  28.1 12.9 %collective-permute-start.5 = (f32[32,384]{1,0:T(8,128)}, f32[32,384]{1,0:T(8,128)S(1)}, u32[]{:S(2)}, u32[]{:S(2)}) collective-permute-start(f32[32,384]{1,0:T(8,128)} %get-tuple-element.31), channel_id=1, source_target_pairs={{0,240},{16,0},{32,16},{48,32},{64,48},{80,64},{96,80},{112,96},{1... | collective-permute-start | bytes 147464 | tf_op jit(solution)/shard_map/ppermute | solution.py:752
  32.7 8.3 %collective-permute-start.6 = (f32[96,128]{1,0:T(8,128)}, f32[96,128]{1,0:T(8,128)S(1)}, u32[]{:S(2)}, u32[]{:S(2)}) collective-permute-start(f32[96,128]{1,0:T(8,128)} %get-tuple-element.32), channel_id=1, source_target_pairs={{0,15},{1,0},{2,1},{3,2},{4,3},{5,4},{6,5},{7,6},{8,7},{9,8},{10,9... | collective-permute-start | bytes 147464 | tf_op jit(solution)/shard_map/ppermute | solution.py:753
  32.7 8.3 %collective-permute-start.7 = (f32[32,128]{1,0:T(8,128)}, f32[32,128]{1,0:T(8,128)S(1)}, u32[]{:S(2)}, u32[]{:S(2)}) collective-permute-start(f32[32,128]{1,0:T(8,128)} %get-tuple-element.33), channel_id=1, source_target_pairs={{0,255},{1,240},{2,241},{3,242},{4,243},{5,244},{6,245},{7,246},{8... | collective-permute-start | bytes 49160 | tf_op jit(solution)/shard_map/ppermute | solution.py:754
  33.3 0.7 copy-start.3
  33.3 0.8 %copy-start.2 = (f32[304,256]{1,0:T(8,128)}, f32[304,256]{1,0:T(8,128)S(1)}, u32[]{:S(2)}) copy-start(f32[304,256]{1,0:T(8,128)S(1)} %collective-permute-done.3.refs_4_.refs_9_) | copy-start | bytes 933892
  41.0 0.6 copy-start.6
  41.1 0.6 copy-start.4
  41.1 0.6 copy-start.5

commit v4 on v3

--- a/solution.py
+++ b/solution.py
@@ -160,8 +160,8 @@
 
 def krylov_kernel(ins, outs, place_ref):
     cot_ref, bottom_ref, rows_ref, cols_ref, corner_ref = [x.get() for x in ins]
-    up_out, left_out, own_out, diag_out = outs
-    own_ref, up_ref, left_ref, diag_ref = [x.ref for x in (own_out, up_out, left_out, diag_out)]
+    up_out, left_out, own_out, diag_out, sums_out = outs
+    up_ref, left_ref, own_ref, diag_ref, sums_ref = [x.ref for x in outs]
     r = place_ref[0]
     c = place_ref[1]
     shape = (24, 384)
@@ -170,7 +170,8 @@
 
     def window(main, at):
         top = jnp.concatenate([corner_ref[8 * at : 8 * at + 8], rows_ref[8 * at : 8 * at + 8]], axis=1)
-        rest = jnp.concatenate([cols_ref[at], main], axis=1)
+        side = jnp.where(iota((16, 128), 1) >= 120, pltpu.roll(cols_ref[at], 2, 1), 0.0)
+        rest = jnp.concatenate([side, main], axis=1)
         return jnp.concatenate([top, rest], axis=0)
 
     inside = ((row >= 8) | (r > 0)) & ((lane >= 128) | (c > 0))
@@ -196,7 +197,6 @@
 
     for k, v in enumerate(vectors):
         own_ref[24 * k : 24 * k + 24] = v
-        own_ref[24 * (KRYLOV + k) : 24 * (KRYLOV + k) + 24] = images[k]
         near = pltpu.roll(v[0:16], 12, 0)[0:8]
         up_ref[8 * k : 8 * k + 8] = near
         left_ref[24 * k : 24 * k + 24] = pltpu.roll(v[:, 0:256], 192, 1)[:, 0:128]
@@ -204,19 +204,6 @@
     for out in (up_out, left_out, diag_out, own_out):
         out.send()
 
-
-def products_kernel(ins, outs, place_ref):
-    own_ref = ins[0].get()
-    sums_out = outs[0]
-    sums_ref = sums_out.ref
-    r = place_ref[0]
-    c = place_ref[1]
-    shape = (24, 384)
-    row = iota(shape, 0)
-    lane = iota(shape, 1)
-    vectors = [own_ref[24 * k : 24 * k + 24] for k in range(KRYLOV)]
-    images = [own_ref[24 * k : 24 * k + 24] for k in range(KRYLOV, 2 * KRYLOV)]
-    start = vectors[0]
     domain = (
         (row >= 4)
         & (row < jnp.where(r == 15, 24, 20))
@@ -283,6 +270,7 @@
 
 ROW_TURNS = (0, 4, 2, 6)
 FIELDS = 6
+LEVELS = 5
 
 
 def packed_rows(parts, from_above):
@@ -295,11 +283,11 @@
     return out
 
 
-def packed_cols(parts):
+def packed_cols(parts, spare):
     group = (iota((16, 128), 1) + 2) & 127
-    out = pltpu.roll(parts[-1], 4 * (len(parts) - 1), 1)
-    for f in range(len(parts) - 2, -1, -1):
-        out = jnp.where(group < 4 * f + 4, pltpu.roll(parts[f], 4 * f, 1) if f else parts[f], out)
+    out = spare
+    for m in range(len(parts) - 1, -1, -1):
+        out = jnp.where(group < 4 * m + 4, pltpu.roll(parts[m], 4 * m, 1) if m else parts[m], out)
     return out
 
 
@@ -310,9 +298,10 @@
     a_ref, c_ref, w_ref, inv_ref, ratio_ref, down_ref, up_ref, right_ref, left_ref, corner_ref = [x.ref for x in outs]
     bottom = bottom_in.get()[...]
     lines = 8 * depth + 8 * ((depth + 1) // 2)
+    spare = []
     for n, field in enumerate((surface_in.get()[...], bottom.astype(F32))):
         down_ref[lines + 8 * n : lines + 8 * n + 8] = field[8:16]
-        right_ref[depth + n] = field[:, 128:256]
+        spare.append(pltpu.roll(field[:, 128:256], 126, 1))
         corner_ref[8 * n : 8 * n + 8] = field[8:16, 128:256]
     corner_out.send()
     land_ref = land_in.get()
@@ -357,6 +346,7 @@
     row8 = iota((8, 256), 0)
     lane = iota((16, 128), 1)
     tails = {}
+    last_parts, first_parts = [], []
     for k in range(depth - 1, -1, -1):
         wet = wet_at(k)
         if k < depth - 1:
@@ -385,8 +375,14 @@
         first = [f[:, 0:128] for f in fields] + [
             jnp.where(lane == 0, open_first, pltpu.roll(wet[:, 0:128], 1, 1))
         ]
-        right_ref[k] = packed_cols(last)
-        left_ref[k] = packed_cols(first)
+        last_parts = last + last_parts
+        first_parts = first + first_parts
+        if k % LEVELS == 0:
+            g = k // LEVELS
+            filler = spare[g % 2]
+            right_ref[g] = packed_cols(last_parts, filler)
+            left_ref[g] = packed_cols(first_parts, filler)
+            last_parts, first_parts = [], []
     for out in (down_out, right_out, up_out, left_out, a_out, c_out, w_out):
         out.send()
 
@@ -429,11 +425,11 @@
         pair = self.row_pair(8 * self.depth + 8 * (k // 2), k % 2 == 1)
         return self.turned_rows(pair, f + 2 * (k % 2))
 
-    def col_pair(self, k):
-        return jnp.where(self.west_lanes, self.west[k], self.east[k]) * self.lane_flag
-
-    def turned_cols(self, pair, f):
-        return pltpu.roll(pair, 128 - 4 * f, 1) if f else pair
+    def cols(self, k, f):
+        g = k // LEVELS
+        pair = jnp.where(self.west_lanes, self.west[g], self.east[g]) * self.lane_flag
+        turn = 4 * (FIELDS * (k % LEVELS) + f)
+        return pltpu.roll(pair, 128 - turn, 1) if turn else pair
 
 
 def next_of(x, axis):
@@ -496,8 +492,7 @@
             [ux_ref[k] * wet * later[0:16], jnp.where(row8 == 7, faces * later[16:24], faces)], axis=0
         )
         x_open_ref[k] = x_open * SCALE
-        columns = edges.col_pair(k)
-        faces = edges.turned_cols(columns, 5)
+        faces = edges.cols(k, 5)
         wide = jnp.concatenate([wet, pltpu.roll(faces, 127, 1)], axis=1)
         later = next_of(wide, 1)
         y_open = jnp.concatenate(
@@ -505,7 +500,7 @@
         )
         y_open_ref[k] = y_open * SCALE
         for f, ref in ((0, theta_ref), (1, salt_ref)):
-            wide = jnp.concatenate([ref[k] * wet, edges.turned_cols(columns, f)], axis=1)
+            wide = jnp.concatenate([ref[k] * wet, edges.cols(k, f)], axis=1)
             at = 16 * (depth * f + k)
             parts_ref[at : at + 16] = two_parts(wide)
     x_out.send()
@@ -675,13 +670,12 @@
         if k < depth - 1:
             kappa_grad_ref[k] = theta_drop_ref[k] * (mu[0] - mu_later[0]) + salt_drop_ref[k] * (mu[1] - mu_later[1])
         rows = edges.row_pair(8 * k, True)
-        columns = edges.col_pair(k)
         row_rise = zeta_rows * edges.tail_rows(k, 0)
-        col_rise = zeta_cols * edges.turned_cols(columns, 4)
+        col_rise = zeta_cols * edges.cols(k, 4)
         x_open = x_open_ref[k]
         y_open = y_open_ref[k]
         for n, ref in ((0, theta_grad_ref), (1, salt_grad_ref)):
-            wide = jnp.concatenate([mu[n], edges.turned_cols(columns, 2 + n) + share[n] * col_rise], axis=1)
+            wide = jnp.concatenate([mu[n], edges.cols(k, 2 + n) + share[n] * col_rise], axis=1)
             at = 16 * (depth * n + k)
             parts_ref[at : at + 16] = two_parts(y_open * (wide - next_of(wide, 1)))
             wide = jnp.concatenate([mu[n], edges.turned_rows(rows, 2 + n) + share[n] * row_rise], axis=0)
@@ -730,12 +724,12 @@
     whole = theta.shape
     place = jnp.stack([lax.axis_index(TROW), lax.axis_index(TCOL)]).astype(jnp.int32)
     lines = 8 * depth + 8 * ((depth + 1) // 2)
-    columns = (depth, 16, 128)
+    columns = (depth // LEVELS, 16, 128)
     a, c, w, inv, ratio, down, up, right, left, corner = staged(
         columns_kernel,
         (land_mask, kappa, bottom, theta_cot, salt_cot, theta, salt, velocity_x, velocity_y, surface_cot),
         [whole] * 4
-        + [kappa.shape, (lines + 16, 256), (lines, 256), (depth + 2, 16, 128), columns, (16, 128)],
+        + [kappa.shape, (lines + 16, 256), (lines, 256), columns, columns, (16, 128)],
         flops=100 * theta.size,
     )
     above = lax.ppermute(down, TROW, around(16, 1))
@@ -743,10 +737,10 @@
     corner = lax.ppermute(corner, ALL, across(1))
     below = lax.ppermute(up, TROW, around(16, -1))
     east = lax.ppermute(left, TCOL, around(16, -1))
-    near, side, own, tip = staged(
+    near, side, own, tip, sums = staged(
         krylov_kernel,
-        (surface_cot, bottom, (above, lines, 16), (west, depth, 2), corner),
-        [(32, 384), (96, 128), (192, 384), (32, 128)],
+        (surface_cot, bottom, (above, lines, 16), (west, 0, 2), corner),
+        [(32, 384), (96, 128), (96, 384), (32, 128), (256, 128)],
         place=place,
     )
     near = lax.ppermute(near, TROW, around(16, -1))
@@ -758,11 +752,9 @@
         + (stencil(((-1, -1), (0, 7), (1, 7), (2, -1)), 384), forcing, kappa, inv, ratio),
         [(depth, 24, 256), (depth, 16, 384), kappa.shape, kappa.shape],
         place=place,
-        after=(own,),
         flops=200 * theta.size,
         scratch=[((32 * depth, 768), BF16), ((32 * depth, 384), F32), (whole, F32), (whole, F32)],
     )
-    (sums,) = staged(products_kernel, (own,), [(256, 128)], place=place, after=(theta_drop, near, side, tip))
     sums = lax.all_to_all(sums, ALL, 0, 0, tiled=True)
     return tuple(
         staged(

time: 75.6 us -> 63.3 us (0.84)
  blocking collectives: 22.7 us -> 0 us
  starting transfers between devices: 15.8 us -> 31.2 us
  Pallas kernels: 25.7 us -> 22.3 us
  waiting for transfers between devices: 6.6 us -> 5.15 us
    all_to_all x1 -> x0, blocking collectives: 22.7 us -> none  [shards(): sums = lax.all_to_all(sums, ALL, 0, 0, tiled=True)]
    all_to_all x0 -> x1, starting transfers between devices: none -> 11.7 us  [shards(): sums = lax.all_to_all(sums, ALL, 0, 0, tiled=True)]
    ppermute x1, starting transfers between devices: 6.28 us -> 0.91 us  [shards(): east = lax.ppermute(left, TCOL, around(16, -1))]
    ppermute x1, starting transfers between devices: 0.01 us -> 5.09 us  [shards(): side = lax.ppermute(side, TCOL, around(16, -1))]
    ppermute x1, starting transfers between devices: 0.56 us -> 4.51 us  [shards(): tip = lax.ppermute(tip, ALL, across(-1))]
    pallas_call x5 -> x4, Pallas kernels: 25.7 us -> 22.3 us  [staged(): pl.pallas_call(body, out_shape=[jax.ShapeDtypeStruct(s, F32) for s in out...]
    ppermute x1, waiting for transfers between devices: 6.58 us -> 3.99 us  [shards(): corner = lax.ppermute(corner, ALL, across(1))]
    ppermute x1, starting transfers between devices: 4.6 us -> 2.22 us  [shards(): near = lax.ppermute(near, TROW, around(16, -1))]
  transfers between devices with their start and end apart: 8 -> 9, of which waited for: 1 -> 2; matrix products, arithmetic and copies ran while one was open for 1% -> 1% of each run, Pallas kernels for 13% -> 17%
where the time goes in v4:
time: 63.3 us; the launch traced here: 62.9 us
  starting transfers between devices  31.2 us (49%)
  Pallas kernels  22.3 us (35%)
  waiting for transfers between devices  5.15 us (8%)
  local copies, waits for them, and re-layouts  2.71 us (4%)
  between operations  0.95 us (2%)
    pallas_call x4, Pallas kernels, staged(): pl.pallas_call(body, out_shape=[jax.ShapeDtypeStruct(s, F32) for s in out...  22.3 us
    all_to_all x1, starting transfers between devices, shards(): sums = lax.all_to_all(sums, ALL, 0, 0, tiled=True)  11.7 us
    ppermute x1, starting transfers between devices, shards(): side = lax.ppermute(side, TCOL, around(16, -1))  5.09 us
    ppermute x1, starting transfers between devices, shards(): tip = lax.ppermute(tip, ALL, across(-1))  4.51 us
    ppermute x1, waiting for transfers between devices, shards(): corner = lax.ppermute(corner, ALL, across(1))  3.99 us
    ppermute x1, starting transfers between devices, shards(): above = lax.ppermute(down, TROW, around(16, 1))  2.76 us
    unnamed x26, local copies, waits for them, and re-layouts  2.71 us
    ppermute x1, starting transfers between devices, shards(): near = lax.ppermute(near, TROW, around(16, -1))  2.22 us
  transfers between devices with their start and end apart: 9, of which 2 were waited for; matrix products, arithmetic and copies ran while one was open for 1% of the time, Pallas kernels for 17%

profile of v4, /device:TPU:1, one launch (start us, length us, event | category | flops | bytes accessed | tf_op | source)
XLA Modules:
  0.0 62.9 jit_solution(1505396188538621249)
XLA Ops:
  0.6 4.5 %shard_map.156 = (f32[25,16,256]{2,1,0:T(8,128)}, f32[25,16,256]{2,1,0:T(8,128)}, f32[25,16,256]{2,1,0:T(8,128)}, f32[25,16,256]{2,1,0:T(8,128)}, f32[24,16,256]...) custom-call(s32[25,16,256]{2,1,0:T(8,128)} %refs_6_.3, ...), custom_call_target="tpu_custom_call" | custom-call | flops 10240000 | bytes 6053888 | tf_op jit(solution)/shard_map/pallas_call | solution.py:129
  5.1 2.8 %collective-permute-start = (f32[320,256]{1,0:T(8,128)}, f32[320,256]{1,0:T(8,128)S(1)}, u32[]{:S(2)}, u32[]{:S(2)}) collective-permute-start(f32[320,256]{1,0:T(8,128)} %get-tuple-element.23), channel_id=1, source_target_pairs={{0,16},{16,32},{32,48},{48,64},{64,80},{80,96},{96,112},{112,128},... | collective-permute-start | bytes 983048 | tf_op jit(solution)/shard_map/ppermute | solution.py:735
  7.9 1.4 %collective-permute-start.2 = (f32[16,128]{1,0:T(8,128)}, f32[16,128]{1,0:T(8,128)S(1)}, u32[]{:S(2)}, u32[]{:S(2)}) collective-permute-start(f32[16,128]{1,0:T(8,128)} %get-tuple-element.25), channel_id=1, source_target_pairs={{0,17},{1,18},{2,19},{3,20},{4,21},{5,22},{6,23},{7,24},{8,25},{9,... | collective-permute-start | bytes 24584 | tf_op jit(solution)/shard_map/ppermute | solution.py:737
  9.3 1.6 %collective-permute-start.1 = (f32[5,16,128]{2,1,0:T(8,128)}, f32[5,16,128]{2,1,0:T(8,128)S(1)}, u32[]{:S(2)}, u32[]{:S(2)}) collective-permute-start(f32[5,16,128]{2,1,0:T(8,128)} %get-tuple-element.24), channel_id=1, source_target_pairs={{0,1},{1,2},{2,3},{3,4},{4,5},{5,6},{6,7},{7,8},{8,9},{9,10},{10,1... | collective-permute-start | bytes 122888 | tf_op jit(solution)/shard_map/ppermute | solution.py:736
  11.0 0.9 %collective-permute-start.6 = (f32[304,256]{1,0:T(8,128)}, f32[304,256]{1,0:T(8,128)S(1)}, u32[]{:S(2)}, u32[]{:S(2)}) collective-permute-start(f32[304,256]{1,0:T(8,128)} %get-tuple-element.31), channel_id=1, source_target_pairs={{0,240},{16,0},{32,16},{48,32},{64,48},{80,64},{96,80},{112,96},{1... | collective-permute-start | bytes 933896 | tf_op jit(solution)/shard_map/ppermute | solution.py:738
  11.8 0.6 pad_add_fusion.refs_0_
  12.4 4.0 %collective-permute-done.2.refs_5_ = f32[16,128]{1,0:T(8,128)S(1)} collective-permute-done((f32[16,128]{1,0:T(8,128)}, f32[16,128]{1,0:T(8,128)S(1)}, u32[]{:S(2)}, u32[]{:S(2)}) %collective-permute-start.2) | collective-permute-done | bytes 8224 | tf_op jit(solution)/shard_map/ppermute | solution.py:737
  16.4 1.1 %collective-permute-done.1.refs_4_.refs_5_.refs_10_ = f32[5,16,128]{2,1,0:T(8,128)S(1)} collective-permute-done((f32[5,16,128]{2,1,0:T(8,128)}, f32[5,16,128]{2,1,0:T(8,128)S(1)}, u32[]{:S(2)}, u32[]{:S(2)}) %collective-permute-start.1) | collective-permute-done | bytes 40992 | tf_op jit(solution)/shard_map/ppermute | solution.py:736
  17.6 0.0 collective-permute-done.refs_3_.refs_8_
  17.6 0.6 copy-done.3
  18.2 0.7 %copy-done = f32[320,256]{1,0:T(8,128)} copy-done((f32[320,256]{1,0:T(8,128)}, f32[320,256]{1,0:T(8,128)S(1)}, u32[]{:S(2)}) %copy-start) | copy-done | bytes 327704
  18.9 3.3 %shard_map.157 = (f32[32,384]{1,0:T(8,128)}, f32[96,128]{1,0:T(8,128)}, f32[96,384]{1,0:T(8,128)}, f32[32,128]{1,0:T(8,128)}, f32[256,128]{1,0:T(8,128)}) custom-call(s32[2]{0:T(128)} %pad_add_fusion.refs_0_, f32[16,256]{1,0:T(8,128)} %refs_1_.4, s32[16,256]{1,0:T(8,128)} %refs_7_.5, f32[320,256]{1,0:T(8,128)} %copy-done, f32[5,16,128]{2,1,0:T(8,128)} %copy-done.3, ...), custom_call_target="tpu_custom_call" | custom-call | bytes 802816 | tf_op jit(solution)/shard_map/pallas_call | solution.py:129
  22.3 0.0 copy-start.12
  22.3 11.7 %all-to-all-start = ((f32[256,1,128]{2,1,0:T(1,128)}), f32[256,1,128]{2,1,0:T(1,128)S(1)}, u32[]{:S(2)}, u32[]{:S(2)}) async-start(f32[256,1,128]{2,1,0:T(1,128)} %bitcast.7), calls=%async_computation | async-start | bytes 262144 | tf_op jit(solution)/shard_map/all_to_all | solution.py:758
  34.0 2.2 %collective-permute-start.3 = (f32[32,384]{1,0:T(8,128)S(1)}, f32[32,384]{1,0:T(8,128)S(1)}, u32[]{:S(2)}, u32[]{:S(2)}) collective-permute-start(f32[32,384]{1,0:T(8,128)S(1)} %copy-done.10), channel_id=1, source_target_pairs={{0,240},{16,0},{32,16},{48,32},{64,48},{80,64},{96,80},{112,96},{1... | collective-permute-start | bytes 147464 | tf_op jit(solution)/shard_map/ppermute | solution.py:746
  36.3 5.1 %collective-permute-start.4 = (f32[96,128]{1,0:T(8,128)S(1)}, f32[96,128]{1,0:T(8,128)S(1)}, u32[]{:S(2)}, u32[]{:S(2)}) collective-permute-start(f32[96,128]{1,0:T(8,128)S(1)} %copy-done.9), channel_id=1, source_target_pairs={{0,15},{1,0},{2,1},{3,2},{4,3},{5,4},{6,5},{7,6},{8,7},{9,8},{10,9... | collective-permute-start | bytes 147464 | tf_op jit(solution)/shard_map/ppermute | solution.py:747
  41.3 0.9 %collective-permute-start.7 = (f32[5,16,128]{2,1,0:T(8,128)S(1)}, f32[5,16,128]{2,1,0:T(8,128)S(1)}, u32[]{:S(2)}, u32[]{:S(2)}) collective-permute-start(f32[5,16,128]{2,1,0:T(8,128)S(1)} %copy-done.11), channel_id=1, source_target_pairs={{0,15},{1,0},{2,1},{3,2},{4,3},{5,4},{6,5},{7,6},{8,7},{9,8},{10,9... | collective-permute-start | bytes 122888 | tf_op jit(solution)/shard_map/ppermute | solution.py:739
  42.3 4.5 %collective-permute-start.5 = (f32[32,128]{1,0:T(8,128)S(1)}, f32[32,128]{1,0:T(8,128)S(1)}, u32[]{:S(2)}, u32[]{:S(2)}) collective-permute-start(f32[32,128]{1,0:T(8,128)S(1)} %copy-done.12), channel_id=1, source_target_pairs={{0,255},{1,240},{2,241},{3,242},{4,243},{5,244},{6,245},{7,246},{8... | collective-permute-start | bytes 49160 | tf_op jit(solution)/shard_map/ppermute | solution.py:748
  46.8 0.0 collective-permute-done.7.refs_6_.refs_11_
  46.8 0.0 collective-permute-done.6.refs_4_.refs_9_
  46.8 0.6 copy-done.4
  47.4 0.1 copy-done.1
  47.5 7.2 %shard_map.158 = (f32[25,24,256]{2,1,0:T(8,128)}, f32[25,16,384]{2,1,0:T(8,128)}, f32[24,16,256]{2,1,0:T(8,128)}, f32[24,16,256]{2,1,0:T(8,128)}) custom-call(s32[2]{0:T(128)} %pad_add_fusion.refs_0_, s32[25,16,256]{2,1,0:T(8,128)} %refs_6_.3, s32[16,256]{1,0:T(8,128)} %refs_7_.5, f32[320,256]{1,0:T(8,128)} %copy-done, f32[304,256]{1,0:T(8,128)} %copy-done.1, ...), custom_call_target="tpu_custom_call" | custom-call | flops 20480000 | bytes 7192576 | tf_op jit(solution)/shard_map/pallas_call | solution.py:129
  54.7 0.0 collective-permute-done.5.refs_5_
  54.7 0.0 collective-permute-done.3.refs_3_
  54.7 0.0 collective-permute-done.4.refs_4_
  54.7 0.0 all-to-all-done
  54.8 0.5 copy-done.7
  55.3 0.0 copy-done.5
  55.3 0.0 copy-done.6
  55.4 0.1 copy-done.2
  55.4 7.4 %shard_map.159 = (f32[25,16,256]{2,1,0:T(8,128)}, f32[25,16,256]{2,1,0:T(8,128)}, f32[24,16,256]{2,1,0:T(8,128)}, f32[16,256]{1,0:T(8,128)}) custom-call(s32[2]{0:T(128)} %pad_add_fusion.refs_0_, f32[256,128]{1,0:T(8,128)} %bitcast.6, f32[96,384]{1,0:T(8,128)} %get-tuple-element.27.refs_2_, f32[32,384]{1,0:T(8,128)} %copy-done.5, f32[96,128]{1,0:T(8,128)} %copy-done.6, ...), custom_call_target="tpu_custom_call" | custom-call | bytes 6799360 | tf_op jit(solution)/shard_map/pallas_call | solution.py:129
  (17 shorter events, 0.0 us)
Async XLA Ops:
  5.1 12.5 %collective-permute-start = (f32[320,256]{1,0:T(8,128)}, f32[320,256]{1,0:T(8,128)S(1)}, u32[]{:S(2)}, u32[]{:S(2)}) collective-permute-start(f32[320,256]{1,0:T(8,128)} %get-tuple-element.23), channel_id=1, source_target_pairs={{0,16},{16,32},{32,48},{48,64},{64,80},{80,96},{96,112},{112,128},... | collective-permute-start | bytes 983048 | tf_op jit(solution)/shard_map/ppermute | solution.py:735
  7.9 8.5 %collective-permute-start.2 = (f32[16,128]{1,0:T(8,128)}, f32[16,128]{1,0:T(8,128)S(1)}, u32[]{:S(2)}, u32[]{:S(2)}) collective-permute-start(f32[16,128]{1,0:T(8,128)} %get-tuple-element.25), channel_id=1, source_target_pairs={{0,17},{1,18},{2,19},{3,20},{4,21},{5,22},{6,23},{7,24},{8,25},{9,... | collective-permute-start | bytes 24584 | tf_op jit(solution)/shard_map/ppermute | solution.py:737
  9.3 8.3 %collective-permute-start.1 = (f32[5,16,128]{2,1,0:T(8,128)}, f32[5,16,128]{2,1,0:T(8,128)S(1)}, u32[]{:S(2)}, u32[]{:S(2)}) collective-permute-start(f32[5,16,128]{2,1,0:T(8,128)} %get-tuple-element.24), channel_id=1, source_target_pairs={{0,1},{1,2},{2,3},{3,4},{4,5},{5,6},{6,7},{7,8},{8,9},{9,10},{10,1... | collective-permute-start | bytes 122888 | tf_op jit(solution)/shard_map/ppermute | solution.py:736
  11.0 35.8 %collective-permute-start.6 = (f32[304,256]{1,0:T(8,128)}, f32[304,256]{1,0:T(8,128)S(1)}, u32[]{:S(2)}, u32[]{:S(2)}) collective-permute-start(f32[304,256]{1,0:T(8,128)} %get-tuple-element.31), channel_id=1, source_target_pairs={{0,240},{16,0},{32,16},{48,32},{64,48},{80,64},{96,80},{112,96},{1... | collective-permute-start | bytes 933896 | tf_op jit(solution)/shard_map/ppermute | solution.py:738
  16.4 1.2 %copy-start.8 = (f32[16,128]{1,0:T(8,128)}, f32[16,128]{1,0:T(8,128)S(1)}, u32[]{:S(2)}) copy-start(f32[16,128]{1,0:T(8,128)S(1)} %collective-permute-done.2.refs_5_) | copy-start | bytes 24580
  17.6 0.6 copy-start.3
  18.2 0.7 %copy-start = (f32[320,256]{1,0:T(8,128)}, f32[320,256]{1,0:T(8,128)S(1)}, u32[]{:S(2)}) copy-start(f32[320,256]{1,0:T(8,128)S(1)} %collective-permute-done.refs_3_.refs_8_) | copy-start | bytes 983044
  22.2 11.8 %copy-start.10 = (f32[32,384]{1,0:T(8,128)S(1)}, f32[32,384]{1,0:T(8,128)}, u32[]{:S(2)}) copy-start(f32[32,384]{1,0:T(8,128)} %get-tuple-element.28) | copy-start | bytes 147460
  22.2 14.0 %copy-start.9 = (f32[96,128]{1,0:T(8,128)S(1)}, f32[96,128]{1,0:T(8,128)}, u32[]{:S(2)}) copy-start(f32[96,128]{1,0:T(8,128)} %get-tuple-element.29) | copy-start | bytes 147460
  22.2 19.1 %copy-start.11 = (f32[5,16,128]{2,1,0:T(8,128)S(1)}, f32[5,16,128]{2,1,0:T(8,128)}, u32[]{:S(2)}) copy-start(f32[5,16,128]{2,1,0:T(8,128)} %get-tuple-element.32) | copy-start | bytes 122884
  22.3 20.0 %copy-start.12 = (f32[32,128]{1,0:T(8,128)S(1)}, f32[32,128]{1,0:T(8,128)}, u32[]{:S(2)}) copy-start(f32[32,128]{1,0:T(8,128)} %get-tuple-element.30) | copy-start | bytes 49156
  22.3 32.5 %all-to-all-start = ((f32[256,1,128]{2,1,0:T(1,128)}), f32[256,1,128]{2,1,0:T(1,128)S(1)}, u32[]{:S(2)}, u32[]{:S(2)}) async-start(f32[256,1,128]{2,1,0:T(1,128)} %bitcast.7), calls=%async_computation | async-start | bytes 262144 | tf_op jit(solution)/shard_map/all_to_all | solution.py:758
  34.0 20.7 %collective-permute-start.3 = (f32[32,384]{1,0:T(8,128)S(1)}, f32[32,384]{1,0:T(8,128)S(1)}, u32[]{:S(2)}, u32[]{:S(2)}) collective-permute-start(f32[32,384]{1,0:T(8,128)S(1)} %copy-done.10), channel_id=1, source_target_pairs={{0,240},{16,0},{32,16},{48,32},{64,48},{80,64},{96,80},{112,96},{1... | collective-permute-start | bytes 147464 | tf_op jit(solution)/shard_map/ppermute | solution.py:746
  36.3 18.5 %collective-permute-start.4 = (f32[96,128]{1,0:T(8,128)S(1)}, f32[96,128]{1,0:T(8,128)S(1)}, u32[]{:S(2)}, u32[]{:S(2)}) collective-permute-start(f32[96,128]{1,0:T(8,128)S(1)} %copy-done.9), channel_id=1, source_target_pairs={{0,15},{1,0},{2,1},{3,2},{4,3},{5,4},{6,5},{7,6},{8,7},{9,8},{10,9... | collective-permute-start | bytes 147464 | tf_op jit(solution)/shard_map/ppermute | solution.py:747
  41.3 5.4 %collective-permute-start.7 = (f32[5,16,128]{2,1,0:T(8,128)S(1)}, f32[5,16,128]{2,1,0:T(8,128)S(1)}, u32[]{:S(2)}, u32[]{:S(2)}) collective-permute-start(f32[5,16,128]{2,1,0:T(8,128)S(1)} %copy-done.11), channel_id=1, source_target_pairs={{0,15},{1,0},{2,1},{3,2},{4,3},{5,4},{6,5},{7,6},{8,7},{9,8},{10,9... | collective-permute-start | bytes 122888 | tf_op jit(solution)/shard_map/ppermute | solution.py:739
  42.3 12.4 %collective-permute-start.5 = (f32[32,128]{1,0:T(8,128)S(1)}, f32[32,128]{1,0:T(8,128)S(1)}, u32[]{:S(2)}, u32[]{:S(2)}) collective-permute-start(f32[32,128]{1,0:T(8,128)S(1)} %copy-done.12), channel_id=1, source_target_pairs={{0,255},{1,240},{2,241},{3,242},{4,243},{5,244},{6,245},{7,246},{8... | collective-permute-start | bytes 49160 | tf_op jit(solution)/shard_map/ppermute | solution.py:748
  46.8 0.6 copy-start.4
  46.8 0.7 %copy-start.1 = (f32[304,256]{1,0:T(8,128)}, f32[304,256]{1,0:T(8,128)S(1)}, u32[]{:S(2)}) copy-start(f32[304,256]{1,0:T(8,128)S(1)} %collective-permute-done.6.refs_4_.refs_9_) | copy-start | bytes 933892
  54.7 0.6 copy-start.7
  54.7 0.6 copy-start.5
  54.7 0.6 copy-start.6
  54.8 0.7 %copy-start.2 = (f32[256,1,128]{2,1,0:T(1,128)}, f32[256,1,128]{2,1,0:T(1,128)S(1)}, u32[]{:S(2)}) copy-start(f32[256,1,128]{2,1,0:T(1,128)S(1)} %all-to-all-done) | copy-start | bytes 393220

commit v5 on v4

--- a/solution.py
+++ b/solution.py
@@ -69,16 +69,28 @@
 
 
 class Loaded:
-    def __init__(self, source, ref, sem):
+    def __init__(self, source, ref, parts, take_sem):
         self.ref = ref
-        self.copy = pltpu.make_async_copy(source, ref, sem)
-        self.copy.start()
-        self.waited = False
+        self.copies = []
+        for part in parts:
+            if part is None:
+                self.copies.append(pltpu.make_async_copy(source, ref, take_sem()))
+            else:
+                self.copies.append(pltpu.make_async_copy(source.at[pl.ds(*part)], ref.at[pl.ds(*part)], take_sem()))
+
+    def start(self, n):
+        if n < len(self.copies):
+            self.copies[n].start()
+            self.waiting = list(self.copies)
+
+    def first(self):
+        if len(self.waiting) == len(self.copies):
+            self.waiting.pop(0).wait()
+        return self.ref
 
     def get(self):
-        if not self.waited:
-            self.copy.wait()
-            self.waited = True
+        while self.waiting:
+            self.waiting.pop(0).wait()
         return self.ref
 
 
@@ -95,8 +107,15 @@
         self.pending.append(copy)
 
 
-def staged(kernel, args, outs, place=None, scratch=(), sends=None, after=(), flops=0):
+def staged(kernel, args, outs, place=None, scratch=(), sends=None, after=(), flops=0, lead=None):
     smem = [] if place is None else [place]
+
+    def parts_of(shape):
+        if lead is None or len(shape) < 3 or shape[0] < 24:
+            return [None]
+        start, stop = lead[0], min(lead[0] + lead[1], shape[0])
+        return [(start, stop - start), (0, start) if start else (stop, shape[0] - stop)]
+
     cuts = [a[1:] if isinstance(a, tuple) else None for a in args]
     args = [a[0] if isinstance(a, tuple) else a for a in args]
     n_in, n_out = len(args), len(outs)
@@ -115,7 +134,11 @@
         buffers = [refs.pop(0) for _ in range(n_in)]
         holds = [refs.pop(0) for _ in range(n_out)]
         in_sems, out_sems = refs.pop(-2), refs.pop(-1)
-        ins = [Loaded(s, b, in_sems.at[n]) for n, (s, b) in enumerate(zip(sources, buffers))]
+        numbers = iter(range(2 * n_in))
+        ins = [Loaded(s, b, parts_of(b.shape), lambda: in_sems.at[next(numbers)]) for s, b in zip(sources, buffers)]
+        for n in (0, 1):
+            for x in ins:
+                x.start(n)
         pending = []
         given = []
         for n in range(n_out):
@@ -133,7 +156,7 @@
         out_specs=[HB] * n_out,
         scratch_shapes=staging
         + [pltpu.VMEM(s, t) for s, t in scratch]
-        + [pltpu.SemaphoreType.DMA((n_in,)), pltpu.SemaphoreType.DMA((sends,))],
+        + [pltpu.SemaphoreType.DMA((2 * n_in,)), pltpu.SemaphoreType.DMA((sends,))],
         cost_estimate=pl.CostEstimate(
             flops=flops, bytes_accessed=4 * (sum(a.size for a in args) + sum(map(math.prod, outs))), transcendentals=0
         ),
@@ -304,10 +327,8 @@
         spare.append(pltpu.roll(field[:, 128:256], 126, 1))
         corner_ref[8 * n : 8 * n + 8] = field[8:16, 128:256]
     corner_out.send()
-    land_ref = land_in.get()
-    kappa_ref = kappa_in.get()
-    tcot_ref = tcot_in.get()
-    scot_ref = scot_in.get()
+    early = (land_in, kappa_in, tcot_in, scot_in)
+    land_ref, kappa_ref, tcot_ref, scot_ref = [x.first() for x in early]
 
     def wet_at(k):
         return jnp.where(k < bottom, land_ref[k].astype(F32), 0.0)
@@ -317,6 +338,9 @@
     couple_last = None
     state = None
     for k in range(depth):
+        if k == LEVELS - 1:
+            for x in early:
+                x.get()
         diagonal = jnp.ones((16, 256), F32)
         if k > 0:
             diagonal = diagonal + couple_last - couple_last * ratio
@@ -383,7 +407,9 @@
             right_ref[g] = packed_cols(last_parts, filler)
             left_ref[g] = packed_cols(first_parts, filler)
             last_parts, first_parts = [], []
-    for out in (down_out, right_out, up_out, left_out, a_out, c_out, w_out):
+            for out in (a_out, c_out, w_out):
+                out.send(k, LEVELS)
+    for out in (down_out, right_out, up_out, left_out):
         out.send()
 
 
@@ -475,15 +501,19 @@
     x_open_ref, y_open_ref, theta_drop_ref, salt_drop_ref = [x.ref for x in outs]
     depth = theta_in.ref.shape[0]
     bottom = bottom_in.get()[...]
-    land_ref = land_in.get()
+    land_ref = land_in.first()
     edges = Edges(place_ref, depth, *[x.get() for x in (above_in, below_in, west_in, east_in)])
     row8, lane16 = edges.row8, edges.lane16
-    ux_ref, uy_ref, theta_ref, salt_ref = [x.get() for x in (ux_in, uy_in, theta_in, salt_in)]
+    early = (ux_in, uy_in, theta_in, salt_in, land_in)
+    ux_ref, uy_ref, theta_ref, salt_ref, _ = [x.first() for x in early]
 
     def wet_at(k):
         return jnp.where(k < bottom, land_ref[k].astype(F32), 0.0)
 
     for k in range(depth):
+        if k == LEVELS:
+            for x in early:
+                x.get()
         wet = wet_at(k)
         faces = edges.tail_rows(k, 1)
         wide = jnp.concatenate([wet, pltpu.roll(faces, 7, 0)], axis=0)
@@ -548,8 +578,9 @@
         salt_drop_ref[k] = opened * (state[1] - new[1])
         state = new
         wet_later = wet
-    theta_out.send()
-    salt_out.send()
+        if k % LEVELS == 0:
+            theta_out.send(k, min(LEVELS, depth - 1 - k))
+            salt_out.send(k, min(LEVELS, depth - 1 - k))
 
 
 def backward_kernel(ins, outs, place_ref, parts_ref, filtered_ref):
@@ -650,7 +681,7 @@
     zeta = surface[8:24]
 
     bottom = bottom_in.get()[...]
-    land_ref = land_in.get()
+    land_ref = land_in.first()
     edges = Edges(place_ref, depth, *[x.get() for x in (above_in, below_in, west_in, east_in)])
     zeta_rows = jnp.where(edges.row8 < 4, surface[24:32], surface[0:8])
     zeta_cols = jnp.where(edges.lane16 < 64, beside[8:24], joined[8:24, 0:128])
@@ -658,12 +689,14 @@
     def wet_at(k):
         return jnp.where(k < bottom, land_ref[k].astype(F32), 0.0)
 
-    w_ref, a_ref, c_ref, theta_drop_ref, salt_drop_ref, x_open_ref, y_open_ref = [
-        x.get() for x in (w_in, a_in, c_in, theta_drop_in, salt_drop_in, x_open_in, y_open_in)
-    ]
+    early = (w_in, a_in, c_in, theta_drop_in, salt_drop_in, x_open_in, y_open_in, land_in)
+    w_ref, a_ref, c_ref, theta_drop_ref, salt_drop_ref, x_open_ref, y_open_ref, _ = [x.first() for x in early]
     share = (0.2, -0.15)
     mu_later = None
     for k in range(depth - 1, -1, -1):
+        if k == depth - LEVELS - 1:
+            for x in early:
+                x.get()
         wet = wet_at(k)
         rise = zeta * w_ref[k]
         mu = (a_ref[k] + share[0] * rise, c_ref[k] + share[1] * rise)
@@ -731,6 +764,8 @@
         [whole] * 4
         + [kappa.shape, (lines + 16, 256), (lines, 256), columns, columns, (16, 128)],
         flops=100 * theta.size,
+        lead=(0, LEVELS),
+        sends=32,
     )
     above = lax.ppermute(down, TROW, around(16, 1))
     west = lax.ppermute(right, TCOL, around(16, 1))
@@ -742,6 +777,7 @@
         (surface_cot, bottom, (above, lines, 16), (west, 0, 2), corner),
         [(32, 384), (96, 128), (96, 384), (32, 128), (256, 128)],
         place=place,
+        after=(below, east),
     )
     near = lax.ppermute(near, TROW, around(16, -1))
     side = lax.ppermute(side, TCOL, around(16, -1))
@@ -753,6 +789,8 @@
         [(depth, 24, 256), (depth, 16, 384), kappa.shape, kappa.shape],
         place=place,
         flops=200 * theta.size,
+        lead=(0, LEVELS),
+        sends=16,
         scratch=[((32 * depth, 768), BF16), ((32 * depth, 384), F32), (whole, F32), (whole, F32)],
     )
     sums = lax.all_to_all(sums, ALL, 0, 0, tiled=True)
@@ -765,6 +803,7 @@
             place=place,
             scratch=[((32 * depth, 768), BF16), ((32 * depth, 256), F32)],
             sends=12,
+            lead=(depth - LEVELS, LEVELS),
         )
     )
 

time: 63.3 us -> 63 us (level)
  starting transfers between devices: 31.2 us -> 33.3 us
  waiting for transfers between devices: 5.15 us -> 3.85 us
    ppermute x1, starting transfers between devices: 0.91 us -> 3.44 us  [shards(): east = lax.ppermute(left, TCOL, around(16, -1))]
    ppermute x1, waiting for transfers between devices: 1.15 us -> 0.01 us  [shards(): west = lax.ppermute(right, TCOL, around(16, 1))]
    ppermute x1, starting transfers between devices: 1.44 us -> 2.46 us  [shards(): corner = lax.ppermute(corner, ALL, across(1))]
    all_to_all x1, starting transfers between devices: 11.7 us -> 10.8 us  [shards(): sums = lax.all_to_all(sums, ALL, 0, 0, tiled=True)]
    unnamed x26 -> x24, local copies, waits for them, and re-layouts: 2.71 us -> 2.1 us
  transfers between devices with their start and end apart: 9 -> 9, of which waited for: 2 -> 1; matrix products, arithmetic and copies ran while one was open for 1% -> 1% of each run, Pallas kernels for 17% -> 11%
where the time goes in v5:
time: 63 us; the launch traced here: 62.7 us
  starting transfers between devices  33.3 us (53%)
  Pallas kernels  21.9 us (35%)
  waiting for transfers between devices  3.85 us (6%)
  local copies, waits for them, and re-layouts  2.1 us (3%)
  between operations  0.97 us (2%)
    pallas_call x4, Pallas kernels, staged(): pl.pallas_call(body, out_shape=[jax.ShapeDtypeStruct(s, F32) for s in out...  21.9 us
    all_to_all x1, starting transfers between devices, shards(): sums = lax.all_to_all(sums, ALL, 0, 0, tiled=True)  10.8 us
    ppermute x1, starting transfers between devices, shards(): side = lax.ppermute(side, TCOL, around(16, -1))  5.09 us
    ppermute x1, starting transfers between devices, shards(): tip = lax.ppermute(tip, ALL, across(-1))  4.23 us
    ppermute x1, waiting for transfers between devices, shards(): corner = lax.ppermute(corner, ALL, across(1))  3.83 us
    ppermute x1, starting transfers between devices, shards(): east = lax.ppermute(left, TCOL, around(16, -1))  3.44 us
    ppermute x1, starting transfers between devices, shards(): above = lax.ppermute(down, TROW, around(16, 1))  2.76 us
    ppermute x1, starting transfers between devices, shards(): corner = lax.ppermute(corner, ALL, across(1))  2.46 us
  transfers between devices with their start and end apart: 9, of which 1 were waited for; matrix products, arithmetic and copies ran while one was open for 1% of the time, Pallas kernels for 11%

profile of v5, /device:TPU:1, one launch (start us, length us, event | category | flops | bytes accessed | tf_op | source)
XLA Modules:
  0.0 62.7 jit_solution(8007008753203627657)
XLA Ops:
  0.6 4.6 %shard_map.156 = (f32[25,16,256]{2,1,0:T(8,128)}, f32[25,16,256]{2,1,0:T(8,128)}, f32[25,16,256]{2,1,0:T(8,128)}, f32[25,16,256]{2,1,0:T(8,128)}, f32[24,16,256]...) custom-call(s32[25,16,256]{2,1,0:T(8,128)} %refs_6_.3, ...), custom_call_target="tpu_custom_call" | custom-call | flops 10240000 | bytes 6053888 | tf_op jit(solution)/shard_map/pallas_call | solution.py:152
  5.2 2.8 %collective-permute-start = (f32[320,256]{1,0:T(8,128)}, f32[320,256]{1,0:T(8,128)S(1)}, u32[]{:S(2)}, u32[]{:S(2)}) collective-permute-start(f32[320,256]{1,0:T(8,128)} %get-tuple-element.23), channel_id=1, source_target_pairs={{0,16},{16,32},{32,48},{48,64},{64,80},{80,96},{96,112},{112,128},... | collective-permute-start | bytes 983048 | tf_op jit(solution)/shard_map/ppermute | solution.py:770
  8.0 0.6 %collective-permute-start.3 = (f32[304,256]{1,0:T(8,128)}, f32[304,256]{1,0:T(8,128)S(1)}, u32[]{:S(2)}, u32[]{:S(2)}) collective-permute-start(f32[304,256]{1,0:T(8,128)} %get-tuple-element.26), channel_id=1, source_target_pairs={{0,240},{16,0},{32,16},{48,32},{64,48},{80,64},{96,80},{112,96},{1... | collective-permute-start | bytes 933896 | tf_op jit(solution)/shard_map/ppermute | solution.py:773
  8.6 2.5 %collective-permute-start.2 = (f32[16,128]{1,0:T(8,128)}, f32[16,128]{1,0:T(8,128)S(1)}, u32[]{:S(2)}, u32[]{:S(2)}) collective-permute-start(f32[16,128]{1,0:T(8,128)} %get-tuple-element.25), channel_id=1, source_target_pairs={{0,17},{1,18},{2,19},{3,20},{4,21},{5,22},{6,23},{7,24},{8,25},{9,... | collective-permute-start | bytes 24584 | tf_op jit(solution)/shard_map/ppermute | solution.py:772
  11.1 1.6 %collective-permute-start.1 = (f32[5,16,128]{2,1,0:T(8,128)}, f32[5,16,128]{2,1,0:T(8,128)S(1)}, u32[]{:S(2)}, u32[]{:S(2)}) collective-permute-start(f32[5,16,128]{2,1,0:T(8,128)} %get-tuple-element.24), channel_id=1, source_target_pairs={{0,1},{1,2},{2,3},{3,4},{4,5},{5,6},{6,7},{7,8},{8,9},{9,10},{10,1... | collective-permute-start | bytes 122888 | tf_op jit(solution)/shard_map/ppermute | solution.py:771
  12.7 3.4 %collective-permute-start.4 = (f32[5,16,128]{2,1,0:T(8,128)}, f32[5,16,128]{2,1,0:T(8,128)S(1)}, u32[]{:S(2)}, u32[]{:S(2)}) collective-permute-start(f32[5,16,128]{2,1,0:T(8,128)} %get-tuple-element.27), channel_id=1, source_target_pairs={{0,15},{1,0},{2,1},{3,2},{4,3},{5,4},{6,5},{7,6},{8,7},{9,8},{10,9... | collective-permute-start | bytes 122888 | tf_op jit(solution)/shard_map/ppermute | solution.py:774
  16.2 0.6 pad_add_fusion.refs_0_
  16.8 3.8 %collective-permute-done.2.refs_5_ = f32[16,128]{1,0:T(8,128)S(1)} collective-permute-done((f32[16,128]{1,0:T(8,128)}, f32[16,128]{1,0:T(8,128)S(1)}, u32[]{:S(2)}, u32[]{:S(2)}) %collective-permute-start.2) | collective-permute-done | bytes 8224 | tf_op jit(solution)/shard_map/ppermute | solution.py:772
  20.6 0.0 collective-permute-done.1.refs_4_.refs_5_.refs_10_
  20.6 0.0 collective-permute-done.4.refs_7_.refs_6_.refs_11_
  20.6 0.0 collective-permute-done.3.refs_6_.refs_4_.refs_9_
  20.6 0.0 collective-permute-done.refs_3_.refs_8_
  20.7 0.5 copy-done.8
  21.2 0.0 copy-done.3
  21.2 0.0 copy-done.4
  21.2 0.1 copy-done.1
  21.4 0.7 %copy-done = f32[320,256]{1,0:T(8,128)} copy-done((f32[320,256]{1,0:T(8,128)}, f32[320,256]{1,0:T(8,128)S(1)}, u32[]{:S(2)}) %copy-start) | copy-done | bytes 327704
  22.1 3.4 %shard_map.157 = (f32[32,384]{1,0:T(8,128)}, f32[96,128]{1,0:T(8,128)}, f32[96,384]{1,0:T(8,128)}, f32[32,128]{1,0:T(8,128)}, f32[256,128]{1,0:T(8,128)}) custom-call(s32[2]{0:T(128)} %pad_add_fusion.refs_0_, f32[16,256]{1,0:T(8,128)} %refs_1_.4, s32[16,256]{1,0:T(8,128)} %refs_7_.5, f32[320,256]{1,0:T(8,128)} %copy-done, f32[5,16,128]{2,1,0:T(8,128)} %copy-done.3, ...), custom_call_target="tpu_custom_call" | custom-call | bytes 802816 | tf_op jit(solution)/shard_map/pallas_call | solution.py:152
  25.5 0.0 copy-start.11
  25.5 10.8 %all-to-all-start = ((f32[256,1,128]{2,1,0:T(1,128)}), f32[256,1,128]{2,1,0:T(1,128)S(1)}, u32[]{:S(2)}, u32[]{:S(2)}) async-start(f32[256,1,128]{2,1,0:T(1,128)} %bitcast.7), calls=%async_computation | async-start | bytes 262144 | tf_op jit(solution)/shard_map/all_to_all | solution.py:796
  36.3 2.2 %collective-permute-start.5 = (f32[32,384]{1,0:T(8,128)S(1)}, f32[32,384]{1,0:T(8,128)S(1)}, u32[]{:S(2)}, u32[]{:S(2)}) collective-permute-start(f32[32,384]{1,0:T(8,128)S(1)} %copy-done.10), channel_id=1, source_target_pairs={{0,240},{16,0},{32,16},{48,32},{64,48},{80,64},{96,80},{112,96},{1... | collective-permute-start | bytes 147464 | tf_op jit(solution)/shard_map/ppermute | solution.py:782
  38.5 5.1 %collective-permute-start.6 = (f32[96,128]{1,0:T(8,128)S(1)}, f32[96,128]{1,0:T(8,128)S(1)}, u32[]{:S(2)}, u32[]{:S(2)}) collective-permute-start(f32[96,128]{1,0:T(8,128)S(1)} %copy-done.9), channel_id=1, source_target_pairs={{0,15},{1,0},{2,1},{3,2},{4,3},{5,4},{6,5},{7,6},{8,7},{9,8},{10,9... | collective-permute-start | bytes 147464 | tf_op jit(solution)/shard_map/ppermute | solution.py:783
  43.6 4.2 %collective-permute-start.7 = (f32[32,128]{1,0:T(8,128)S(1)}, f32[32,128]{1,0:T(8,128)S(1)}, u32[]{:S(2)}, u32[]{:S(2)}) collective-permute-start(f32[32,128]{1,0:T(8,128)S(1)} %copy-done.11), channel_id=1, source_target_pairs={{0,255},{1,240},{2,241},{3,242},{4,243},{5,244},{6,245},{7,246},{8... | collective-permute-start | bytes 49160 | tf_op jit(solution)/shard_map/ppermute | solution.py:784
  47.8 7.0 %shard_map.158 = (f32[25,24,256]{2,1,0:T(8,128)}, f32[25,16,384]{2,1,0:T(8,128)}, f32[24,16,256]{2,1,0:T(8,128)}, f32[24,16,256]{2,1,0:T(8,128)}) custom-call(s32[2]{0:T(128)} %pad_add_fusion.refs_0_, s32[25,16,256]{2,1,0:T(8,128)} %refs_6_.3, s32[16,256]{1,0:T(8,128)} %refs_7_.5, f32[320,256]{1,0:T(8,128)} %copy-done, f32[304,256]{1,0:T(8,128)} %copy-done.1, ...), custom_call_target="tpu_custom_call" | custom-call | flops 20480000 | bytes 7192576 | tf_op jit(solution)/shard_map/pallas_call | solution.py:152
  54.8 0.0 collective-permute-done.7.refs_5_
  54.9 0.0 collective-permute-done.5.refs_3_
  54.9 0.0 collective-permute-done.6.refs_4_
  54.9 0.5 copy-done.7
  55.5 0.0 copy-done.5
  55.5 0.0 copy-done.6
  55.5 0.1 copy-done.2
  55.6 6.9 %shard_map.159 = (f32[25,16,256]{2,1,0:T(8,128)}, f32[25,16,256]{2,1,0:T(8,128)}, f32[24,16,256]{2,1,0:T(8,128)}, f32[16,256]{1,0:T(8,128)}) custom-call(s32[2]{0:T(128)} %pad_add_fusion.refs_0_, f32[256,128]{1,0:T(8,128)} %bitcast.6, f32[96,384]{1,0:T(8,128)} %get-tuple-element.29.refs_2_, f32[32,384]{1,0:T(8,128)} %copy-done.5, f32[96,128]{1,0:T(8,128)} %copy-done.6, ...), custom_call_target="tpu_custom_call" | custom-call | bytes 6799360 | tf_op jit(solution)/shard_map/pallas_call | solution.py:152
  (15 shorter events, 0.0 us)
Async XLA Ops:
  5.2 15.4 %collective-permute-start = (f32[320,256]{1,0:T(8,128)}, f32[320,256]{1,0:T(8,128)S(1)}, u32[]{:S(2)}, u32[]{:S(2)}) collective-permute-start(f32[320,256]{1,0:T(8,128)} %get-tuple-element.23), channel_id=1, source_target_pairs={{0,16},{16,32},{32,48},{48,64},{64,80},{80,96},{96,112},{112,128},... | collective-permute-start | bytes 983048 | tf_op jit(solution)/shard_map/ppermute | solution.py:770
  8.0 12.6 %collective-permute-start.3 = (f32[304,256]{1,0:T(8,128)}, f32[304,256]{1,0:T(8,128)S(1)}, u32[]{:S(2)}, u32[]{:S(2)}) collective-permute-start(f32[304,256]{1,0:T(8,128)} %get-tuple-element.26), channel_id=1, source_target_pairs={{0,240},{16,0},{32,16},{48,32},{64,48},{80,64},{96,80},{112,96},{1... | collective-permute-start | bytes 933896 | tf_op jit(solution)/shard_map/ppermute | solution.py:773
  8.6 12.0 %collective-permute-start.2 = (f32[16,128]{1,0:T(8,128)}, f32[16,128]{1,0:T(8,128)S(1)}, u32[]{:S(2)}, u32[]{:S(2)}) collective-permute-start(f32[16,128]{1,0:T(8,128)} %get-tuple-element.25), channel_id=1, source_target_pairs={{0,17},{1,18},{2,19},{3,20},{4,21},{5,22},{6,23},{7,24},{8,25},{9,... | collective-permute-start | bytes 24584 | tf_op jit(solution)/shard_map/ppermute | solution.py:772
  11.1 9.5 %collective-permute-start.1 = (f32[5,16,128]{2,1,0:T(8,128)}, f32[5,16,128]{2,1,0:T(8,128)S(1)}, u32[]{:S(2)}, u32[]{:S(2)}) collective-permute-start(f32[5,16,128]{2,1,0:T(8,128)} %get-tuple-element.24), channel_id=1, source_target_pairs={{0,1},{1,2},{2,3},{3,4},{4,5},{5,6},{6,7},{7,8},{8,9},{9,10},{10,1... | collective-permute-start | bytes 122888 | tf_op jit(solution)/shard_map/ppermute | solution.py:771
  12.7 7.9 %collective-permute-start.4 = (f32[5,16,128]{2,1,0:T(8,128)}, f32[5,16,128]{2,1,0:T(8,128)S(1)}, u32[]{:S(2)}, u32[]{:S(2)}) collective-permute-start(f32[5,16,128]{2,1,0:T(8,128)} %get-tuple-element.27), channel_id=1, source_target_pairs={{0,15},{1,0},{2,1},{3,2},{4,3},{5,4},{6,5},{7,6},{8,7},{9,8},{10,9... | collective-permute-start | bytes 122888 | tf_op jit(solution)/shard_map/ppermute | solution.py:774
  20.6 0.6 copy-start.8
  20.6 0.6 copy-start.3
  20.6 0.6 %copy-start.4 = (f32[5,16,128]{2,1,0:T(8,128)}, f32[5,16,128]{2,1,0:T(8,128)S(1)}, u32[]{:S(2)}) copy-start(f32[5,16,128]{2,1,0:T(8,128)S(1)} %collective-permute-done.4.refs_7_.refs_6_.refs_11_) | copy-start | bytes 122884
  20.6 0.7 %copy-start.1 = (f32[304,256]{1,0:T(8,128)}, f32[304,256]{1,0:T(8,128)S(1)}, u32[]{:S(2)}) copy-start(f32[304,256]{1,0:T(8,128)S(1)} %collective-permute-done.3.refs_6_.refs_4_.refs_9_) | copy-start | bytes 933892
  21.4 0.7 %copy-start = (f32[320,256]{1,0:T(8,128)}, f32[320,256]{1,0:T(8,128)S(1)}, u32[]{:S(2)}) copy-start(f32[320,256]{1,0:T(8,128)S(1)} %collective-permute-done.refs_3_.refs_8_) | copy-start | bytes 983044
  25.5 10.8 %copy-start.10 = (f32[32,384]{1,0:T(8,128)S(1)}, f32[32,384]{1,0:T(8,128)}, u32[]{:S(2)}) copy-start(f32[32,384]{1,0:T(8,128)} %get-tuple-element.30) | copy-start | bytes 147460
  25.5 13.1 %copy-start.9 = (f32[96,128]{1,0:T(8,128)S(1)}, f32[96,128]{1,0:T(8,128)}, u32[]{:S(2)}) copy-start(f32[96,128]{1,0:T(8,128)} %get-tuple-element.31) | copy-start | bytes 147460
  25.5 18.1 %copy-start.11 = (f32[32,128]{1,0:T(8,128)S(1)}, f32[32,128]{1,0:T(8,128)}, u32[]{:S(2)}) copy-start(f32[32,128]{1,0:T(8,128)} %get-tuple-element.32) | copy-start | bytes 49156
  25.5 29.4 %all-to-all-start = ((f32[256,1,128]{2,1,0:T(1,128)}), f32[256,1,128]{2,1,0:T(1,128)S(1)}, u32[]{:S(2)}, u32[]{:S(2)}) async-start(f32[256,1,128]{2,1,0:T(1,128)} %bitcast.7), calls=%async_computation | async-start | bytes 262144 | tf_op jit(solution)/shard_map/all_to_all | solution.py:796
  36.3 18.6 %collective-permute-start.5 = (f32[32,384]{1,0:T(8,128)S(1)}, f32[32,384]{1,0:T(8,128)S(1)}, u32[]{:S(2)}, u32[]{:S(2)}) collective-permute-start(f32[32,384]{1,0:T(8,128)S(1)} %copy-done.10), channel_id=1, source_target_pairs={{0,240},{16,0},{32,16},{48,32},{64,48},{80,64},{96,80},{112,96},{1... | collective-permute-start | bytes 147464 | tf_op jit(solution)/shard_map/ppermute | solution.py:782
  38.5 16.4 %collective-permute-start.6 = (f32[96,128]{1,0:T(8,128)S(1)}, f32[96,128]{1,0:T(8,128)S(1)}, u32[]{:S(2)}, u32[]{:S(2)}) collective-permute-start(f32[96,128]{1,0:T(8,128)S(1)} %copy-done.9), channel_id=1, source_target_pairs={{0,15},{1,0},{2,1},{3,2},{4,3},{5,4},{6,5},{7,6},{8,7},{9,8},{10,9... | collective-permute-start | bytes 147464 | tf_op jit(solution)/shard_map/ppermute | solution.py:783
  43.6 11.2 %collective-permute-start.7 = (f32[32,128]{1,0:T(8,128)S(1)}, f32[32,128]{1,0:T(8,128)S(1)}, u32[]{:S(2)}, u32[]{:S(2)}) collective-permute-start(f32[32,128]{1,0:T(8,128)S(1)} %copy-done.11), channel_id=1, source_target_pairs={{0,255},{1,240},{2,241},{3,242},{4,243},{5,244},{6,245},{7,246},{8... | collective-permute-start | bytes 49160 | tf_op jit(solution)/shard_map/ppermute | solution.py:784
  54.9 0.6 copy-start.7
  54.9 0.6 copy-start.5
  54.9 0.6 copy-start.6
  54.9 0.7 %copy-start.2 = (f32[256,1,128]{2,1,0:T(1,128)}, f32[256,1,128]{2,1,0:T(1,128)S(1)}, u32[]{:S(2)}) copy-start(f32[256,1,128]{2,1,0:T(1,128)S(1)} %all-to-all-done) | copy-start | bytes 393220

commit v6 on v5

--- a/solution.py
+++ b/solution.py
@@ -164,6 +164,22 @@
     )(*smem, *args, *after)
 
 
+def corners_kernel(ins, outs, place_ref):
+    fields = (ins[0].get()[...], ins[1].get()[...].astype(F32))
+    main_a, main_b, cross_a, cross_b = [x.ref for x in outs]
+    odd_row = (place_ref[0] & 1) == 1
+    for n, field in enumerate(fields):
+        at = slice(8 * n, 8 * n + 8)
+        top_left, top_right = field[0:8, 0:128], field[0:8, 128:256]
+        bottom_left, bottom_right = field[8:16, 0:128], field[8:16, 128:256]
+        main_a[at] = jnp.where(odd_row, top_left, bottom_right)
+        main_b[at] = jnp.where(odd_row, bottom_right, top_left)
+        cross_a[at] = jnp.where(odd_row, top_right, bottom_left)
+        cross_b[at] = jnp.where(odd_row, bottom_left, top_right)
+    for out in outs:
+        out.send()
+
+
 def merge_rows(a, b, step):
     shape = a[0].shape
     first = (iota(shape, 0) & step) == 0
@@ -182,30 +198,48 @@
 
 
 def krylov_kernel(ins, outs, place_ref):
-    cot_ref, bottom_ref, rows_ref, cols_ref, corner_ref = [x.get() for x in ins]
-    up_out, left_out, own_out, diag_out, sums_out = outs
-    up_ref, left_ref, own_ref, diag_ref, sums_ref = [x.ref for x in outs]
+    cot_in, bottom_in, rows_a_in, rows_b_in, cols_a_in, cols_b_in = ins[:6]
+    own_out, sums_out = outs
+    own_ref, sums_ref = own_out.ref, sums_out.ref
     r = place_ref[0]
     c = place_ref[1]
-    shape = (24, 384)
+    odd_row = (r & 1) == 1
+    odd_col = (c & 1) == 1
+    shape = (32, 384)
     row = iota(shape, 0)
     lane = iota(shape, 1)
-
-    def window(main, at):
-        top = jnp.concatenate([corner_ref[8 * at : 8 * at + 8], rows_ref[8 * at : 8 * at + 8]], axis=1)
-        side = jnp.where(iota((16, 128), 1) >= 120, pltpu.roll(cols_ref[at], 2, 1), 0.0)
-        rest = jnp.concatenate([side, main], axis=1)
-        return jnp.concatenate([top, rest], axis=0)
-
-    inside = ((row >= 8) | (r > 0)) & ((lane >= 128) | (c > 0))
-    start = jnp.where(inside, window(cot_ref[...], 0), 0.0)
-    bottom = window(bottom_ref[...].astype(F32), 1)
+    edge = iota((16, 128), 1)
+    inside = ((row >= 8) | (r > 0)) & ((row < 24) | (r < 15))
+    inside = inside & ((lane < 256) | ((lane < 264) & (c < 15)) | ((lane >= 376) & (c > 0)))
+    rows_a, rows_b, cols_a, cols_b = [x.get() for x in (rows_a_in, rows_b_in, cols_a_in, cols_b_in)]
+    main_a, main_b, cross_a, cross_b = [x.get() for x in ins[6:]]
+
+    def window(main, n):
+        at = slice(8 * n, 8 * n + 8)
+        above = jnp.where(odd_row, rows_a[at], rows_b[at])
+        below = jnp.where(odd_row, rows_b[at], rows_a[at])
+        west = jnp.where(odd_col, cols_a[n], cols_b[n])
+        east = jnp.where(odd_col, cols_b[n], cols_a[n])
+        up_left = jnp.where(odd_row, main_a[at], main_b[at])
+        down_right = jnp.where(odd_row, main_b[at], main_a[at])
+        up_right = jnp.where(odd_row, cross_a[at], cross_b[at])
+        down_left = jnp.where(odd_row, cross_b[at], cross_a[at])
+        sides = jnp.where(edge < 64, pltpu.roll(east, 10, 1), pltpu.roll(west, 2, 1))
+        return jnp.concatenate(
+            [
+                jnp.concatenate([above, jnp.where(edge[0:8] < 64, up_right, up_left)], axis=1),
+                jnp.concatenate([main, sides], axis=1),
+                jnp.concatenate([below, jnp.where(edge[0:8] < 64, down_right, down_left)], axis=1),
+            ],
+            axis=0,
+        )
+
+    start = jnp.where(inside, window(cot_in.get()[...], 0), 0.0)
+    bottom = window(bottom_in.get()[...].astype(F32), 1)
     shifted = (4.2 + bottom / 25.0) - CENTRE
 
     def apply_shifted(v):
-        below = jnp.where(row == 23, 0.0, pltpu.roll(v, 23, 0))
-        right = jnp.where(lane == 383, 0.0, pltpu.roll(v, 383, 1))
-        beside = below + pltpu.roll(v, 1, 0) + right + pltpu.roll(v, 1, 1)
+        beside = pltpu.roll(v, 31, 0) + pltpu.roll(v, 1, 0) + pltpu.roll(v, 383, 1) + pltpu.roll(v, 1, 1)
         return jnp.where(inside, shifted * v - beside, 0.0)
 
     vectors = [start]
@@ -219,31 +253,21 @@
             vectors.append(moved * 0.5 - vectors[-2])
 
     for k, v in enumerate(vectors):
-        own_ref[24 * k : 24 * k + 24] = v
-        near = pltpu.roll(v[0:16], 12, 0)[0:8]
-        up_ref[8 * k : 8 * k + 8] = near
-        left_ref[24 * k : 24 * k + 24] = pltpu.roll(v[:, 0:256], 192, 1)[:, 0:128]
-        diag_ref[8 * k : 8 * k + 8] = pltpu.roll(near[:, 0:256], 192, 1)[:, 0:128]
-    for out in (up_out, left_out, diag_out, own_out):
-        out.send()
-
-    domain = (
-        (row >= 4)
-        & (row < jnp.where(r == 15, 24, 20))
-        & (lane >= 124)
-        & (lane < jnp.where(c == 15, 384, 380))
-    )
-    cut = [jnp.where(domain, v, 0.0) for v in vectors]
+        own_ref[32 * k : 32 * k + 32] = v
+    own_out.send()
+
+    cut = [v[8:24, 0:256] for v in vectors]
+    images = [w[8:24, 0:256] for w in images]
     cut_parts = [halves(v) for v in cut]
     image_parts = [halves(w) for w in images]
 
     def tile(x, at):
-        i, j = divmod(at, 3)
+        i, j = divmod(at, 2)
         return x[8 * i : 8 * i + 8, 128 * j : 128 * j + 128]
 
     def dot(x, x_parts, y, y_parts):
         total = None
-        for at in range(9):
+        for at in range(4):
             p, e = two_prod(
                 tile(x, at),
                 tile(y, at),
@@ -258,8 +282,7 @@
         return total
 
     dots = [dot(cut[i], cut_parts[i], images[j], image_parts[j]) for i, j in PAIRS]
-    start_parts = halves(start)
-    dots += [dot(cut[i], cut_parts[i], start, start_parts) for i in range(KRYLOV)]
+    dots += [dot(cut[i], cut_parts[i], cut[0], cut_parts[0]) for i in range(KRYLOV)]
     zero = jnp.zeros((8, 128), F32)
     dots += [(zero, zero)] * (16 - len(dots))
     packed = []
@@ -314,19 +337,28 @@
     return out
 
 
-def columns_kernel(ins, outs):
+def columns_kernel(ins, outs, place_ref):
     depth = ins[0].ref.shape[0]
     land_in, kappa_in, bottom_in, tcot_in, scot_in, theta_in, salt_in, ux_in, uy_in, surface_in = ins
-    a_out, c_out, w_out, inv_out, ratio_out, down_out, up_out, right_out, left_out, corner_out = outs
-    a_ref, c_ref, w_ref, inv_ref, ratio_ref, down_ref, up_ref, right_ref, left_ref, corner_ref = [x.ref for x in outs]
+    a_out, c_out, w_out, inv_out, ratio_out, rows_a_out, rows_b_out, cols_a_out, cols_b_out = outs
+    a_ref, c_ref, w_ref, inv_ref, ratio_ref, rows_a_ref, rows_b_ref, cols_a_ref, cols_b_ref = [x.ref for x in outs]
+    odd_row = (place_ref[0] & 1) == 1
+    odd_col = (place_ref[1] & 1) == 1
+
+    def put_rows(at, down, up):
+        rows_a_ref[at : at + 8] = jnp.where(odd_row, up, down)
+        rows_b_ref[at : at + 8] = jnp.where(odd_row, down, up)
+
+    def put_cols(g, right, left):
+        cols_a_ref[g] = jnp.where(odd_col, left, right)
+        cols_b_ref[g] = jnp.where(odd_col, right, left)
+
     bottom = bottom_in.get()[...]
     lines = 8 * depth + 8 * ((depth + 1) // 2)
     spare = []
     for n, field in enumerate((surface_in.get()[...], bottom.astype(F32))):
-        down_ref[lines + 8 * n : lines + 8 * n + 8] = field[8:16]
-        spare.append(pltpu.roll(field[:, 128:256], 126, 1))
-        corner_ref[8 * n : 8 * n + 8] = field[8:16, 128:256]
-    corner_out.send()
+        put_rows(lines + 8 * n, field[8:16], field[0:8])
+        spare.append((pltpu.roll(field[:, 128:256], 126, 1), pltpu.roll(field[:, 0:128], 118, 1)))
     early = (land_in, kappa_in, tcot_in, scot_in)
     land_ref, kappa_ref, tcot_ref, scot_ref = [x.first() for x in early]
 
@@ -378,8 +410,11 @@
             state = tuple(x + ratio * s for x, s in zip((a_ref[k], c_ref[k], w_ref[k]), state))
             a_ref[k], c_ref[k], w_ref[k] = state
         fields = (theta_ref[k] * wet, salt_ref[k] * wet) + state
-        down_ref[8 * k : 8 * k + 8] = packed_rows([f[8:16] for f in fields[:4]], True)
-        up_ref[8 * k : 8 * k + 8] = packed_rows([f[0:8] for f in fields[:4]], False)
+        put_rows(
+            8 * k,
+            packed_rows([f[8:16] for f in fields[:4]], True),
+            packed_rows([f[0:8] for f in fields[:4]], False),
+        )
         flow = ux_ref[k] * wet
         open_low = flow[8:16] * pltpu.roll(wet[8:16], 7, 0)
         open_high = flow[0:8] * pltpu.roll(wet[0:8], 7, 0)
@@ -389,9 +424,7 @@
         if k % 2 == 0:
             later = tails.pop(k + 1, tails[k])
             this = tails.pop(k)
-            at = 8 * depth + 4 * k
-            down_ref[at : at + 8] = packed_rows(this[0] + later[0], True)
-            up_ref[at : at + 8] = packed_rows(this[1] + later[1], False)
+            put_rows(8 * depth + 4 * k, packed_rows(this[0] + later[0], True), packed_rows(this[1] + later[1], False))
         flow = uy_ref[k] * wet
         open_last = flow[:, 128:256] * pltpu.roll(wet[:, 128:256], 127, 1)
         open_first = flow[:, 0:128] * pltpu.roll(wet[:, 0:128], 127, 1)
@@ -403,13 +436,11 @@
         first_parts = first + first_parts
         if k % LEVELS == 0:
             g = k // LEVELS
-            filler = spare[g % 2]
-            right_ref[g] = packed_cols(last_parts, filler)
-            left_ref[g] = packed_cols(first_parts, filler)
+            put_cols(g, packed_cols(last_parts, spare[g % 2][0]), packed_cols(first_parts, spare[g % 2][1]))
             last_parts, first_parts = [], []
             for out in (a_out, c_out, w_out):
                 out.send(k, LEVELS)
-    for out in (down_out, right_out, up_out, left_out):
+    for out in (rows_a_out, rows_b_out, cols_a_out, cols_b_out):
         out.send()
 
 
@@ -418,30 +449,30 @@
 
 
 class Edges:
-    def __init__(self, place_ref, depth, above, below, west, east):
+    def __init__(self, place_ref, depth, rows_a, rows_b, cols_a, cols_b):
         r = place_ref[0]
         c = place_ref[1]
-        self.depth, self.above, self.below, self.west, self.east = depth, above, below, west, east
+        self.depth, self.rows_a, self.rows_b, self.cols_a, self.cols_b = depth, rows_a, rows_b, cols_a, cols_b
         self.row8 = iota((8, 256), 0)
         self.lane16 = iota((16, 128), 1)
         has_up = jnp.where(r > 0, 1.0, 0.0)
         has_down = jnp.where(r < 15, 1.0, 0.0)
         has_left = jnp.where(c > 0, 1.0, 0.0)
         has_right = jnp.where(c < 15, 1.0, 0.0)
-        self.above_rows = (self.row8 & 2) != 0
+        above_rows = (self.row8 >> 1) & 1
         self.row_flags = (
-            jnp.where(self.above_rows, has_up, has_down),
-            jnp.where(self.above_rows, has_down, has_up),
+            jnp.where(above_rows == 1, has_up, has_down),
+            jnp.where(above_rows == 1, has_down, has_up),
         )
-        self.west_lanes = (self.lane16 & 2) != 0
-        self.lane_flag = jnp.where(self.west_lanes, has_left, has_right)
+        self.rows_from_a = (above_rows == (r & 1), above_rows != (r & 1))
+        west_lanes = (self.lane16 >> 1) & 1
+        self.lane_flag = jnp.where(west_lanes == 1, has_left, has_right)
+        self.cols_from_a = west_lanes == (c & 1)
 
     def row_pair(self, at, second):
-        above = self.above[at : at + 8]
-        below = self.below[at : at + 8]
-        if second:
-            return jnp.where(self.above_rows, below, above) * self.row_flags[1]
-        return jnp.where(self.above_rows, above, below) * self.row_flags[0]
+        n = 1 if second else 0
+        pair = jnp.where(self.rows_from_a[n], self.rows_a[at : at + 8], self.rows_b[at : at + 8])
+        return pair * self.row_flags[n]
 
     def turned_rows(self, pair, f):
         turn = (8 - ROW_TURNS[f]) % 8
@@ -453,7 +484,7 @@
 
     def cols(self, k, f):
         g = k // LEVELS
-        pair = jnp.where(self.west_lanes, self.west[g], self.east[g]) * self.lane_flag
+        pair = jnp.where(self.cols_from_a, self.cols_a[g], self.cols_b[g]) * self.lane_flag
         turn = 4 * (FIELDS * (k % LEVELS) + f)
         return pltpu.roll(pair, 128 - turn, 1) if turn else pair
 
@@ -483,10 +514,10 @@
     (
         land_in,
         bottom_in,
-        above_in,
-        below_in,
-        west_in,
-        east_in,
+        rows_a_in,
+        rows_b_in,
+        cols_a_in,
+        cols_b_in,
         ux_in,
         uy_in,
         theta_in,
@@ -502,7 +533,7 @@
     depth = theta_in.ref.shape[0]
     bottom = bottom_in.get()[...]
     land_ref = land_in.first()
-    edges = Edges(place_ref, depth, *[x.get() for x in (above_in, below_in, west_in, east_in)])
+    edges = Edges(place_ref, depth, *[x.get() for x in (rows_a_in, rows_b_in, cols_a_in, cols_b_in)])
     row8, lane16 = edges.row8, edges.lane16
     early = (ux_in, uy_in, theta_in, salt_in, land_in)
     ux_ref, uy_ref, theta_ref, salt_ref, _ = [x.first() for x in early]
@@ -587,15 +618,12 @@
     (
         sums_in,
         own_in,
-        near_in,
-        side_in,
-        corner_in,
         land_in,
         bottom_in,
-        above_in,
-        below_in,
-        west_in,
-        east_in,
+        rows_a_in,
+        rows_b_in,
+        cols_a_in,
+        cols_b_in,
         w_in,
         a_in,
         c_in,
@@ -608,12 +636,8 @@
     theta_out, salt_out, kappa_out, forcing_out = outs
     theta_grad_ref, salt_grad_ref, kappa_grad_ref, forcing_grad_ref = [x.ref for x in outs]
     depth = w_in.ref.shape[0]
-    r = place_ref[0]
-    c = place_ref[1]
-    has_down = jnp.where(r < 15, 1.0, 0.0)
-    sums_ref, own_ref, from_below_ref, from_right_ref, from_corner_ref = [
-        x.get() for x in (sums_in, own_in, near_in, side_in, corner_in)
-    ]
+    sums_ref = sums_in.get()
+    own_ref = own_in.get()
 
     small = (8, 128)
     small_row = iota(small, 0)
@@ -667,24 +691,13 @@
             out = out + weights[k] * ref[rows * k : rows * k + rows]
         return out
 
-    def rows_joined(upper, lower):
-        turned = pltpu.roll(lower, 4, 0)
-        row8 = iota(turned.shape, 0)
-        middle = jnp.where((row8 >= 5) & (r < 15), turned, upper[16:24])
-        return jnp.concatenate([upper[0:16], middle, turned * has_down], axis=0)
-
-    joined = rows_joined(combined(own_ref, 24), combined(from_below_ref, 8))
-    beside = pltpu.roll(rows_joined(combined(from_right_ref, 24), combined(from_corner_ref, 8)), 64, 1)
-    lane_wide = iota((32, 128), 1)
-    ending = jnp.where((lane_wide >= 125) & (c < 15), beside, joined[:, 256:384])
-    surface = jnp.concatenate([joined[:, 128:256], ending], axis=1)
-    zeta = surface[8:24]
-
+    surface = combined(own_ref, 32)
+    zeta = surface[8:24, 0:256]
     bottom = bottom_in.get()[...]
     land_ref = land_in.first()
-    edges = Edges(place_ref, depth, *[x.get() for x in (above_in, below_in, west_in, east_in)])
-    zeta_rows = jnp.where(edges.row8 < 4, surface[24:32], surface[0:8])
-    zeta_cols = jnp.where(edges.lane16 < 64, beside[8:24], joined[8:24, 0:128])
+    edges = Edges(place_ref, depth, *[x.get() for x in (rows_a_in, rows_b_in, cols_a_in, cols_b_in)])
+    zeta_rows = jnp.where(edges.row8 < 4, surface[24:32, 0:256], surface[0:8, 0:256])
+    zeta_cols = surface[8:24, 256:384]
 
     def wet_at(k):
         return jnp.where(k < bottom, land_ref[k].astype(F32), 0.0)
@@ -730,14 +743,23 @@
                 out.send(k - 4, 5)
 
 
-def around(count, step):
-    return [(i, (i + step) % count) for i in range(count)]
-
-
-def across(step):
-    return [
-        (16 * i + j, 16 * ((i + step) % 16) + (j + step) % 16) for i in range(16) for j in range(16)
-    ]
+def swaps(first):
+    out = []
+    for i in range(16):
+        j = i + 1 if (i - first) % 2 == 0 else i - 1
+        out.append((i, j if 0 <= j < 16 else i))
+    return out
+
+
+def corner_swaps(first, side):
+    out = []
+    for i in range(16):
+        for j in range(16):
+            step = 1 if (i - first) % 2 == 0 else -1
+            row, col = i + step, j + side * step
+            there = 0 <= row < 16 and 0 <= col < 16
+            out.append((16 * i + j, 16 * row + col if there else 16 * i + j))
+    return out
 
 
 def shards(
@@ -758,33 +780,34 @@
     place = jnp.stack([lax.axis_index(TROW), lax.axis_index(TCOL)]).astype(jnp.int32)
     lines = 8 * depth + 8 * ((depth + 1) // 2)
     columns = (depth // LEVELS, 16, 128)
-    a, c, w, inv, ratio, down, up, right, left, corner = staged(
+    corners = staged(corners_kernel, (surface_cot, bottom), [(16, 128)] * 4, place=place)
+    corners = [
+        lax.ppermute(x, ALL, corner_swaps(first, side))
+        for x, (first, side) in zip(corners, ((0, 1), (1, 1), (0, -1), (1, -1)))
+    ]
+    a, c, w, inv, ratio, rows_a, rows_b, cols_a, cols_b = staged(
         columns_kernel,
         (land_mask, kappa, bottom, theta_cot, salt_cot, theta, salt, velocity_x, velocity_y, surface_cot),
-        [whole] * 4
-        + [kappa.shape, (lines + 16, 256), (lines, 256), columns, columns, (16, 128)],
+        [whole] * 4 + [kappa.shape, (lines + 16, 256), (lines + 16, 256), columns, columns],
+        place=place,
         flops=100 * theta.size,
         lead=(0, LEVELS),
         sends=32,
     )
-    above = lax.ppermute(down, TROW, around(16, 1))
-    west = lax.ppermute(right, TCOL, around(16, 1))
-    corner = lax.ppermute(corner, ALL, across(1))
-    below = lax.ppermute(up, TROW, around(16, -1))
-    east = lax.ppermute(left, TCOL, around(16, -1))
-    near, side, own, tip, sums = staged(
+    rows_a, rows_b, cols_a, cols_b, *corners = lax.optimization_barrier((rows_a, rows_b, cols_a, cols_b, *corners))
+    rows_a = lax.ppermute(rows_a, TROW, swaps(0))
+    rows_b = lax.ppermute(rows_b, TROW, swaps(1))
+    cols_a = lax.ppermute(cols_a, TCOL, swaps(0))
+    cols_b = lax.ppermute(cols_b, TCOL, swaps(1))
+    own, sums = staged(
         krylov_kernel,
-        (surface_cot, bottom, (above, lines, 16), (west, 0, 2), corner),
-        [(32, 384), (96, 128), (96, 384), (32, 128), (256, 128)],
+        (surface_cot, bottom, (rows_a, lines, 16), (rows_b, lines, 16), (cols_a, 0, 2), (cols_b, 0, 2), *corners),
+        [(128, 384), (256, 128)],
         place=place,
-        after=(below, east),
     )
-    near = lax.ppermute(near, TROW, around(16, -1))
-    side = lax.ppermute(side, TCOL, around(16, -1))
-    tip = lax.ppermute(tip, ALL, across(-1))
     x_open, y_open, theta_drop, salt_drop = staged(
         forward_kernel,
-        (land_mask, bottom, above, below, west, east, velocity_x, velocity_y, theta, salt)
+        (land_mask, bottom, rows_a, rows_b, cols_a, cols_b, velocity_x, velocity_y, theta, salt)
         + (stencil(((-1, -1), (0, 7), (1, 7), (2, -1)), 384), forcing, kappa, inv, ratio),
         [(depth, 24, 256), (depth, 16, 384), kappa.shape, kappa.shape],
         place=place,
@@ -797,7 +820,7 @@
     return tuple(
         staged(
             backward_kernel,
-            (sums, own, near, side, tip, land_mask, bottom, above, below, west, east, w, a, c)
+            (sums, own, land_mask, bottom, rows_a, rows_b, cols_a, cols_b, w, a, c)
             + (theta_drop, salt_drop, x_open, y_open, stencil(((-2, -1), (-1, 7), (0, 7), (1, -1)), 256)),
             [whole, whole, kappa.shape, forcing.shape],
             place=place,

time: 63 us -> 75.5 us (1.20)
  waiting for transfers between devices: 3.85 us -> 9.32 us
  starting transfers between devices: 33.3 us -> 38.2 us
  Pallas kernels: 21.9 us -> 24.6 us
    all_to_all x1, waiting for transfers between devices: 0.01 us -> 5.87 us  [shards(): sums = lax.all_to_all(sums, ALL, 0, 0, tiled=True)]
    all_to_all x1, starting transfers between devices: 10.8 us -> 15.7 us  [shards(): sums = lax.all_to_all(sums, ALL, 0, 0, tiled=True)]
    pallas_call x4 -> x5, Pallas kernels: 21.9 us -> 24.6 us  [staged(): pl.pallas_call(body, out_shape=[jax.ShapeDtypeStruct(s, F32) for s in out...]
    unnamed x24 -> x18, local copies, waits for them, and re-layouts: 2.1 us -> 1.39 us
  transfers between devices with their start and end apart: 9 -> 9, of which waited for: 1 -> 3; matrix products, arithmetic and copies ran while one was open for 1% -> 0% of each run, Pallas kernels for 11% -> 16%
where the time goes in v6:
time: 75.5 us; the launch traced here: 74.9 us
  starting transfers between devices  38.2 us (51%)
  Pallas kernels  24.6 us (33%)
  waiting for transfers between devices  9.32 us (12%)
  local copies, waits for them, and re-layouts  1.39 us (2%)
  between operations  0.83 us (1%)
    pallas_call x5, Pallas kernels, staged(): pl.pallas_call(body, out_shape=[jax.ShapeDtypeStruct(s, F32) for s in out...  24.6 us
    all_to_all x1, starting transfers between devices, shards(): sums = lax.all_to_all(sums, ALL, 0, 0, tiled=True)  15.7 us
    ppermute x4, starting transfers between devices, shards(): lax.ppermute(x, ALL, corner_swaps(first, side))  12.5 us
    all_to_all x1, waiting for transfers between devices, shards(): sums = lax.all_to_all(sums, ALL, 0, 0, tiled=True)  5.87 us
    ppermute x1, starting transfers between devices, shards(): rows_b = lax.ppermute(rows_b, TROW, swaps(1))  5.59 us
    ppermute x1, waiting for transfers between devices, shards(): rows_b = lax.ppermute(rows_b, TROW, swaps(1))  3.26 us
    ppermute x1, starting transfers between devices, shards(): cols_a = lax.ppermute(cols_a, TCOL, swaps(0))  2.93 us
  transfers between devices with their start and end apart: 9, of which 3 were waited for; matrix products, arithmetic and copies ran while one was open for 0% of the time, Pallas kernels for 16%

profile of v6, /device:TPU:1, one launch (start us, length us, event | category | flops | bytes accessed | tf_op | source)
XLA Modules:
  0.0 74.9 jit_solution(4310743965747311206)
XLA Ops:
  0.6 0.6 pad_add_fusion.refs_0_
  1.2 2.1 %shard_map.157 = (f32[16,128]{1,0:T(8,128)}, f32[16,128]{1,0:T(8,128)}, f32[16,128]{1,0:T(8,128)}, f32[16,128]{1,0:T(8,128)}) custom-call(s32[2]{0:T(128)} %pad_add_fusion.refs_0_, f32[16,256]{1,0:T(8,128)} %refs_1_.6, s32[16,256]{1,0:T(8,128)} %refs_4_.3), custom_call_target="tpu_custom_call" | custom-call | bytes 65536 | tf_op jit(solution)/shard_map/pallas_call | solution.py:152
  3.3 1.4 %collective-permute-start = (f32[16,128]{1,0:T(8,128)}, f32[16,128]{1,0:T(8,128)S(1)}, u32[]{:S(2)}, u32[]{:S(2)}) collective-permute-start(f32[16,128]{1,0:T(8,128)} %get-tuple-element.35), channel_id=1, source_target_pairs={{0,17},{1,18},{2,19},{3,20},{4,21},{5,22},{6,23},{7,24},{8,25},{9,... | collective-permute-start | bytes 24584 | tf_op jit(solution)/shard_map/ppermute | solution.py:785
  4.6 7.9 %collective-permute-start.1 = (f32[16,128]{1,0:T(8,128)}, f32[16,128]{1,0:T(8,128)S(1)}, u32[]{:S(2)}, u32[]{:S(2)}) collective-permute-start(f32[16,128]{1,0:T(8,128)} %get-tuple-element.36), channel_id=1, source_target_pairs={{0,0},{1,1},{2,2},{3,3},{4,4},{5,5},{6,6},{7,7},{8,8},{9,9},{10,10... | collective-permute-start | bytes 24584 | tf_op jit(solution)/shard_map/ppermute | solution.py:785
  12.5 1.9 %collective-permute-start.2 = (f32[16,128]{1,0:T(8,128)}, f32[16,128]{1,0:T(8,128)S(1)}, u32[]{:S(2)}, u32[]{:S(2)}) collective-permute-start(f32[16,128]{1,0:T(8,128)} %get-tuple-element.37), channel_id=1, source_target_pairs={{0,0},{1,16},{2,17},{3,18},{4,19},{5,20},{6,21},{7,22},{8,23},{9,2... | collective-permute-start | bytes 24584 | tf_op jit(solution)/shard_map/ppermute | solution.py:785
  14.4 1.4 %collective-permute-start.3 = (f32[16,128]{1,0:T(8,128)}, f32[16,128]{1,0:T(8,128)S(1)}, u32[]{:S(2)}, u32[]{:S(2)}) collective-permute-start(f32[16,128]{1,0:T(8,128)} %get-tuple-element.38), channel_id=1, source_target_pairs={{0,0},{1,1},{2,2},{3,3},{4,4},{5,5},{6,6},{7,7},{8,8},{9,9},{10,10... | collective-permute-start | bytes 24584 | tf_op jit(solution)/shard_map/ppermute | solution.py:785
  15.8 5.3 %shard_map.156 = (f32[25,16,256]{2,1,0:T(8,128)}, f32[25,16,256]{2,1,0:T(8,128)}, f32[25,16,256]{2,1,0:T(8,128)}, f32[25,16,256]{2,1,0:T(8,128)}, f32[24,16,256]...) custom-call(s32[2]{0:T(128)} %pad_add_fusion.refs_0_, ...), custom_call_target="tpu_custom_call" | custom-call | flops 10240000 | bytes 6062080 | tf_op jit(solution)/shard_map/pallas_call | solution.py:152
  21.1 0.0 collective-permute-done.refs_7_
  21.1 0.0 copy-start.5
  21.1 0.0 collective-permute-done.1.refs_8_
  21.1 0.0 collective-permute-done.2.refs_9_
  21.1 0.0 collective-permute-done.3.refs_10_
  21.1 0.0 copy-start.8
  21.1 0.1 collective-permute-start.4
  21.2 5.6 %collective-permute-start.5 = (f32[320,256]{1,0:T(8,128)}, f32[320,256]{1,0:T(8,128)S(1)}, u32[]{:S(2)}, u32[]{:S(2)}) collective-permute-start(f32[320,256]{1,0:T(8,128)} %get-tuple-element.40), channel_id=1, source_target_pairs={{0,0},{16,32},{32,16},{48,64},{64,48},{80,96},{96,80},{112,128},{1... | collective-permute-start | bytes 983048 | tf_op jit(solution)/shard_map/ppermute | solution.py:799
  26.8 2.9 %collective-permute-start.6 = (f32[5,16,128]{2,1,0:T(8,128)}, f32[5,16,128]{2,1,0:T(8,128)S(1)}, u32[]{:S(2)}, u32[]{:S(2)}) collective-permute-start(f32[5,16,128]{2,1,0:T(8,128)} %get-tuple-element.41), channel_id=1, source_target_pairs={{0,1},{1,0},{2,3},{3,2},{4,5},{5,4},{6,7},{7,6},{8,9},{9,8},{10,11... | collective-permute-start | bytes 122888 | tf_op jit(solution)/shard_map/ppermute | solution.py:800
  29.8 1.4 %collective-permute-start.7 = (f32[5,16,128]{2,1,0:T(8,128)}, f32[5,16,128]{2,1,0:T(8,128)S(1)}, u32[]{:S(2)}, u32[]{:S(2)}) collective-permute-start(f32[5,16,128]{2,1,0:T(8,128)} %get-tuple-element.42), channel_id=1, source_target_pairs={{0,0},{1,2},{2,1},{3,4},{4,3},{5,6},{6,5},{7,8},{8,7},{9,10},{10,9... | collective-permute-start | bytes 122888 | tf_op jit(solution)/shard_map/ppermute | solution.py:801
  31.2 0.2 collective-permute-done.6.refs_5_.refs_7_
  31.4 0.0 collective-permute-done.7.refs_6_.refs_8_
  31.4 0.0 collective-permute-done.4.refs_3_.refs_5_
  31.4 3.3 %collective-permute-done.5.refs_4_.refs_6_ = f32[320,256]{1,0:T(8,128)S(1)} collective-permute-done((f32[320,256]{1,0:T(8,128)}, f32[320,256]{1,0:T(8,128)S(1)}, u32[]{:S(2)}, u32[]{:S(2)}) %collective-permute-start.5) | collective-permute-done | bytes 327712 | tf_op jit(solution)/shard_map/ppermute | solution.py:799
  34.7 0.0 copy-done.5
  34.7 0.0 copy-done.3
  34.7 0.0 copy-done.4
  34.7 0.0 copy-done
  34.7 0.7 copy-done.1
  35.4 3.4 %shard_map.158 = (f32[128,384]{1,0:T(8,128)}, f32[256,128]{1,0:T(8,128)}) custom-call(s32[2]{0:T(128)} %pad_add_fusion.refs_0_, f32[16,256]{1,0:T(8,128)} %refs_1_.6, s32[16,256]{1,0:T(8,128)} %refs_4_.3, f32[320,256]{1,0:T(8,128)} %copy-done, f32[320,256]{1,0:T(8,128)} %copy-done.1, f32[5,16,128]{2,1,0:T(8,128)} %copy-done.3, f32[5,16,128]{2,1,0:T(8,128)} %copy-done.4, ...), custom_call_target="tpu_custom_call" | custom-call | bytes 1130496 | tf_op jit(solution)/shard_map/pallas_call | solution.py:152
  38.8 15.7 %all-to-all-start = ((f32[256,1,128]{2,1,0:T(1,128)}), f32[256,1,128]{2,1,0:T(1,128)S(1)}, u32[]{:S(2)}, u32[]{:S(2)}) async-start(f32[256,1,128]{2,1,0:T(1,128)} %bitcast.7), calls=%async_computation | async-start | bytes 262144 | tf_op jit(solution)/shard_map/all_to_all | solution.py:819
  54.5 7.0 %shard_map.159 = (f32[25,24,256]{2,1,0:T(8,128)}, f32[25,16,384]{2,1,0:T(8,128)}, f32[24,16,256]{2,1,0:T(8,128)}, f32[24,16,256]{2,1,0:T(8,128)}) custom-call(s32[2]{0:T(128)} %pad_add_fusion.refs_0_, s32[25,16,256]{2,1,0:T(8,128)} %refs_3_.3, s32[16,256]{1,0:T(8,128)} %refs_4_.3, f32[320,256]{1,0:T(8,128)} %copy-done, f32[320,256]{1,0:T(8,128)} %copy-done.1, ...), custom_call_target="tpu_custom_call" | custom-call | flops 20480000 | bytes 7208960 | tf_op jit(solution)/shard_map/pallas_call | solution.py:152
  61.5 5.9 %all-to-all-done = f32[256,1,128]{2,1,0:T(1,128)S(1)} async-done(((f32[256,1,128]{2,1,0:T(1,128)}), f32[256,1,128]{2,1,0:T(1,128)S(1)}, u32[]{:S(2)}, u32[]{:S(2)}) %all-to-all-start) | async-done | bytes 131104 | tf_op jit(solution)/shard_map/all_to_all | solution.py:819
  67.4 0.6 copy-done.2
  68.0 6.9 %shard_map.160 = (f32[25,16,256]{2,1,0:T(8,128)}, f32[25,16,256]{2,1,0:T(8,128)}, f32[24,16,256]{2,1,0:T(8,128)}, f32[16,256]{1,0:T(8,128)}) custom-call(s32[2]{0:T(128)} %pad_add_fusion.refs_0_, f32[256,128]{1,0:T(8,128)} %bitcast.6, f32[128,384]{1,0:T(8,128)} %get-tuple-element.48.refs_2_, s32[25,16,256]{2,1,0:T(8,128)} %refs_3_.3, s32[16,256]{1,0:T(8,128)} %refs_4_.3, ...), custom_call_target="tpu_custom_call" | custom-call | bytes 6750208 | tf_op jit(solution)/shard_map/pallas_call | solution.py:152
  (10 shorter events, 0.0 us)
Async XLA Ops:
  3.3 17.8 %collective-permute-start = (f32[16,128]{1,0:T(8,128)}, f32[16,128]{1,0:T(8,128)S(1)}, u32[]{:S(2)}, u32[]{:S(2)}) collective-permute-start(f32[16,128]{1,0:T(8,128)} %get-tuple-element.35), channel_id=1, source_target_pairs={{0,17},{1,18},{2,19},{3,20},{4,21},{5,22},{6,23},{7,24},{8,25},{9,... | collective-permute-start | bytes 24584 | tf_op jit(solution)/shard_map/ppermute | solution.py:785
  4.6 16.4 %collective-permute-start.1 = (f32[16,128]{1,0:T(8,128)}, f32[16,128]{1,0:T(8,128)S(1)}, u32[]{:S(2)}, u32[]{:S(2)}) collective-permute-start(f32[16,128]{1,0:T(8,128)} %get-tuple-element.36), channel_id=1, source_target_pairs={{0,0},{1,1},{2,2},{3,3},{4,4},{5,5},{6,6},{7,7},{8,8},{9,9},{10,10... | collective-permute-start | bytes 24584 | tf_op jit(solution)/shard_map/ppermute | solution.py:785
  12.5 8.6 %collective-permute-start.2 = (f32[16,128]{1,0:T(8,128)}, f32[16,128]{1,0:T(8,128)S(1)}, u32[]{:S(2)}, u32[]{:S(2)}) collective-permute-start(f32[16,128]{1,0:T(8,128)} %get-tuple-element.37), channel_id=1, source_target_pairs={{0,0},{1,16},{2,17},{3,18},{4,19},{5,20},{6,21},{7,22},{8,23},{9,2... | collective-permute-start | bytes 24584 | tf_op jit(solution)/shard_map/ppermute | solution.py:785
  14.4 6.7 %collective-permute-start.3 = (f32[16,128]{1,0:T(8,128)}, f32[16,128]{1,0:T(8,128)S(1)}, u32[]{:S(2)}, u32[]{:S(2)}) collective-permute-start(f32[16,128]{1,0:T(8,128)} %get-tuple-element.38), channel_id=1, source_target_pairs={{0,0},{1,1},{2,2},{3,3},{4,4},{5,5},{6,6},{7,7},{8,8},{9,9},{10,10... | collective-permute-start | bytes 24584 | tf_op jit(solution)/shard_map/ppermute | solution.py:785
  21.1 13.6 %copy-start.5 = (f32[16,128]{1,0:T(8,128)}, f32[16,128]{1,0:T(8,128)S(1)}, u32[]{:S(2)}) copy-start(f32[16,128]{1,0:T(8,128)S(1)} %collective-permute-done.refs_7_) | copy-start | bytes 24580
  21.1 13.6 %copy-start.6 = (f32[16,128]{1,0:T(8,128)}, f32[16,128]{1,0:T(8,128)S(1)}, u32[]{:S(2)}) copy-start(f32[16,128]{1,0:T(8,128)S(1)} %collective-permute-done.1.refs_8_) | copy-start | bytes 24580
  21.1 13.6 %copy-start.7 = (f32[16,128]{1,0:T(8,128)}, f32[16,128]{1,0:T(8,128)S(1)}, u32[]{:S(2)}) copy-start(f32[16,128]{1,0:T(8,128)S(1)} %collective-permute-done.2.refs_9_) | copy-start | bytes 24580
  21.1 13.5 %copy-start.8 = (f32[16,128]{1,0:T(8,128)}, f32[16,128]{1,0:T(8,128)S(1)}, u32[]{:S(2)}) copy-start(f32[16,128]{1,0:T(8,128)S(1)} %collective-permute-done.3.refs_10_) | copy-start | bytes 24580
  21.1 10.2 %collective-permute-start.4 = (f32[320,256]{1,0:T(8,128)}, f32[320,256]{1,0:T(8,128)S(1)}, u32[]{:S(2)}, u32[]{:S(2)}) collective-permute-start(f32[320,256]{1,0:T(8,128)} %get-tuple-element.39), channel_id=1, source_target_pairs={{0,16},{16,0},{32,48},{48,32},{64,80},{80,64},{96,112},{112,96},{1... | collective-permute-start | bytes 983048 | tf_op jit(solution)/shard_map/ppermute | solution.py:798
  21.2 13.4 %collective-permute-start.5 = (f32[320,256]{1,0:T(8,128)}, f32[320,256]{1,0:T(8,128)S(1)}, u32[]{:S(2)}, u32[]{:S(2)}) collective-permute-start(f32[320,256]{1,0:T(8,128)} %get-tuple-element.40), channel_id=1, source_target_pairs={{0,0},{16,32},{32,16},{48,64},{64,48},{80,96},{96,80},{112,128},{1... | collective-permute-start | bytes 983048 | tf_op jit(solution)/shard_map/ppermute | solution.py:799
  26.8 4.5 %collective-permute-start.6 = (f32[5,16,128]{2,1,0:T(8,128)}, f32[5,16,128]{2,1,0:T(8,128)S(1)}, u32[]{:S(2)}, u32[]{:S(2)}) collective-permute-start(f32[5,16,128]{2,1,0:T(8,128)} %get-tuple-element.41), channel_id=1, source_target_pairs={{0,1},{1,0},{2,3},{3,2},{4,5},{5,4},{6,7},{7,6},{8,9},{9,8},{10,11... | collective-permute-start | bytes 122888 | tf_op jit(solution)/shard_map/ppermute | solution.py:800
  29.8 1.6 %collective-permute-start.7 = (f32[5,16,128]{2,1,0:T(8,128)}, f32[5,16,128]{2,1,0:T(8,128)S(1)}, u32[]{:S(2)}, u32[]{:S(2)}) collective-permute-start(f32[5,16,128]{2,1,0:T(8,128)} %get-tuple-element.42), channel_id=1, source_target_pairs={{0,0},{1,2},{2,1},{3,4},{4,3},{5,6},{6,5},{7,8},{8,7},{9,10},{10,9... | collective-permute-start | bytes 122888 | tf_op jit(solution)/shard_map/ppermute | solution.py:801
  31.4 3.3 %copy-start.3 = (f32[5,16,128]{2,1,0:T(8,128)}, f32[5,16,128]{2,1,0:T(8,128)S(1)}, u32[]{:S(2)}) copy-start(f32[5,16,128]{2,1,0:T(8,128)S(1)} %collective-permute-done.6.refs_5_.refs_7_) | copy-start | bytes 122884
  31.4 3.3 %copy-start.4 = (f32[5,16,128]{2,1,0:T(8,128)}, f32[5,16,128]{2,1,0:T(8,128)S(1)}, u32[]{:S(2)}) copy-start(f32[5,16,128]{2,1,0:T(8,128)S(1)} %collective-permute-done.7.refs_6_.refs_8_) | copy-start | bytes 122884
  31.4 3.3 %copy-start = (f32[320,256]{1,0:T(8,128)}, f32[320,256]{1,0:T(8,128)S(1)}, u32[]{:S(2)}) copy-start(f32[320,256]{1,0:T(8,128)S(1)} %collective-permute-done.4.refs_3_.refs_5_) | copy-start | bytes 983044
  34.7 0.7 copy-start.1
  38.8 28.5 %all-to-all-start = ((f32[256,1,128]{2,1,0:T(1,128)}), f32[256,1,128]{2,1,0:T(1,128)S(1)}, u32[]{:S(2)}, u32[]{:S(2)}) async-start(f32[256,1,128]{2,1,0:T(1,128)} %bitcast.7), calls=%async_computation | async-start | bytes 262144 | tf_op jit(solution)/shard_map/all_to_all | solution.py:819
  67.4 0.6 copy-start.2

commit v7 on v6

--- a/solution.py
+++ b/solution.py
@@ -107,7 +107,7 @@
         self.pending.append(copy)
 
 
-def staged(kernel, args, outs, place=None, scratch=(), sends=None, after=(), flops=0, lead=None):
+def staged(kernel, args, outs, place=None, scratch=(), sends=None, after=(), flops=0, lead=None, into=None):
     smem = [] if place is None else [place]
 
     def parts_of(shape):
@@ -121,14 +121,16 @@
     n_in, n_out = len(args), len(outs)
     sends = sends or n_out
     staging = [pltpu.VMEM(a.shape if cut is None else (cut[1],) + a.shape[1:], a.dtype) for a, cut in zip(args, cuts)]
-    staging += [pltpu.VMEM(s, F32) for s in outs]
+    held = outs if into is None else [(count,) + tuple(x.shape[1:]) for x, (start, count) in into]
+    staging += [pltpu.VMEM(s, F32) for s in held]
+    over = [] if into is None else [x for x, _ in into]
 
     def body(*refs):
         refs = list(refs)
         places = [refs.pop(0) for _ in smem]
         sources = [refs.pop(0) for _ in range(n_in)]
         sources = [s if cut is None else s.at[pl.ds(*cut)] for s, cut in zip(sources, cuts)]
-        for _ in after:
+        for _ in (*after, *over):
             refs.pop(0)
         targets = [refs.pop(0) for _ in range(n_out)]
         buffers = [refs.pop(0) for _ in range(n_in)]
@@ -142,7 +144,8 @@
         pending = []
         given = []
         for n in range(n_out):
-            given.append(Stored(targets[n], holds[n], lambda: out_sems.at[len(pending)], pending))
+            target = targets[n] if into is None else targets[n].at[pl.ds(*into[n][1])]
+            given.append(Stored(target, holds[n], lambda: out_sems.at[len(pending)], pending))
         kernel(ins, given, *places, *refs)
         for x in ins:
             x.get()
@@ -152,8 +155,9 @@
     return pl.pallas_call(
         body,
         out_shape=[jax.ShapeDtypeStruct(s, F32) for s in outs],
-        in_specs=[SM] * len(smem) + [HB] * (n_in + len(after)),
+        in_specs=[SM] * len(smem) + [HB] * (n_in + len(after) + len(over)),
         out_specs=[HB] * n_out,
+        input_output_aliases={len(smem) + n_in + len(after) + n: n for n in range(len(over))},
         scratch_shapes=staging
         + [pltpu.VMEM(s, t) for s, t in scratch]
         + [pltpu.SemaphoreType.DMA((2 * n_in,)), pltpu.SemaphoreType.DMA((sends,))],
@@ -161,21 +165,24 @@
             flops=flops, bytes_accessed=4 * (sum(a.size for a in args) + sum(map(math.prod, outs))), transcendentals=0
         ),
         compiler_params=PARAMS,
-    )(*smem, *args, *after)
-
-
-def corners_kernel(ins, outs, place_ref):
-    fields = (ins[0].get()[...], ins[1].get()[...].astype(F32))
-    main_a, main_b, cross_a, cross_b = [x.ref for x in outs]
+    )(*smem, *args, *after, *over)
+
+
+def sides_of(cols_a, cols_b, n, odd_col):
+    west = jnp.where(odd_col, cols_a[n], cols_b[n])
+    east = jnp.where(odd_col, cols_b[n], cols_a[n])
+    return jnp.where(iota((16, 128), 1) < 64, pltpu.roll(east, 10, 1), pltpu.roll(west, 2, 1))
+
+
+def ends_kernel(ins, outs, place_ref):
+    cols_a, cols_b = [x.get() for x in ins]
     odd_row = (place_ref[0] & 1) == 1
-    for n, field in enumerate(fields):
-        at = slice(8 * n, 8 * n + 8)
-        top_left, top_right = field[0:8, 0:128], field[0:8, 128:256]
-        bottom_left, bottom_right = field[8:16, 0:128], field[8:16, 128:256]
-        main_a[at] = jnp.where(odd_row, top_left, bottom_right)
-        main_b[at] = jnp.where(odd_row, bottom_right, top_left)
-        cross_a[at] = jnp.where(odd_row, top_right, bottom_left)
-        cross_b[at] = jnp.where(odd_row, bottom_left, top_right)
+    odd_col = (place_ref[1] & 1) == 1
+    for n in (0, 1):
+        sides = sides_of(cols_a, cols_b, n, odd_col)
+        lanes = slice(128 * n, 128 * n + 128)
+        outs[0].ref[:, lanes] = jnp.where(odd_row, sides[0:8], sides[8:16])
+        outs[1].ref[:, lanes] = jnp.where(odd_row, sides[8:16], sides[0:8])
     for out in outs:
         out.send()
 
@@ -198,7 +205,7 @@
 
 
 def krylov_kernel(ins, outs, place_ref):
-    cot_in, bottom_in, rows_a_in, rows_b_in, cols_a_in, cols_b_in = ins[:6]
+    cot_in, bottom_in, rows_a_in, rows_b_in, cols_a_in, cols_b_in = ins
     own_out, sums_out = outs
     own_ref, sums_ref = own_out.ref, sums_out.ref
     r = place_ref[0]
@@ -208,28 +215,22 @@
     shape = (32, 384)
     row = iota(shape, 0)
     lane = iota(shape, 1)
-    edge = iota((16, 128), 1)
     inside = ((row >= 8) | (r > 0)) & ((row < 24) | (r < 15))
     inside = inside & ((lane < 256) | ((lane < 264) & (c < 15)) | ((lane >= 376) & (c > 0)))
     rows_a, rows_b, cols_a, cols_b = [x.get() for x in (rows_a_in, rows_b_in, cols_a_in, cols_b_in)]
-    main_a, main_b, cross_a, cross_b = [x.get() for x in ins[6:]]
 
     def window(main, n):
         at = slice(8 * n, 8 * n + 8)
         above = jnp.where(odd_row, rows_a[at], rows_b[at])
         below = jnp.where(odd_row, rows_b[at], rows_a[at])
-        west = jnp.where(odd_col, cols_a[n], cols_b[n])
-        east = jnp.where(odd_col, cols_b[n], cols_a[n])
-        up_left = jnp.where(odd_row, main_a[at], main_b[at])
-        down_right = jnp.where(odd_row, main_b[at], main_a[at])
-        up_right = jnp.where(odd_row, cross_a[at], cross_b[at])
-        down_left = jnp.where(odd_row, cross_b[at], cross_a[at])
-        sides = jnp.where(edge < 64, pltpu.roll(east, 10, 1), pltpu.roll(west, 2, 1))
+        lanes = slice(128 * n, 128 * n + 128)
+        above_ends = jnp.where(odd_row, rows_a[16:24, lanes], rows_b[16:24, lanes])
+        below_ends = jnp.where(odd_row, rows_b[16:24, lanes], rows_a[16:24, lanes])
         return jnp.concatenate(
             [
-                jnp.concatenate([above, jnp.where(edge[0:8] < 64, up_right, up_left)], axis=1),
-                jnp.concatenate([main, sides], axis=1),
-                jnp.concatenate([below, jnp.where(edge[0:8] < 64, down_right, down_left)], axis=1),
+                jnp.concatenate([above, above_ends], axis=1),
+                jnp.concatenate([main, sides_of(cols_a, cols_b, n, odd_col)], axis=1),
+                jnp.concatenate([below, below_ends], axis=1),
             ],
             axis=0,
         )
@@ -440,8 +441,10 @@
             last_parts, first_parts = [], []
             for out in (a_out, c_out, w_out):
                 out.send(k, LEVELS)
-    for out in (rows_a_out, rows_b_out, cols_a_out, cols_b_out):
-        out.send()
+    cols_a_out.send()
+    cols_b_out.send()
+    rows_a_out.send(0, lines + 16)
+    rows_b_out.send(0, lines + 16)
 
 
 SCALE = 1.0 / 12.0
@@ -744,22 +747,7 @@
 
 
 def swaps(first):
-    out = []
-    for i in range(16):
-        j = i + 1 if (i - first) % 2 == 0 else i - 1
-        out.append((i, j if 0 <= j < 16 else i))
-    return out
-
-
-def corner_swaps(first, side):
-    out = []
-    for i in range(16):
-        for j in range(16):
-            step = 1 if (i - first) % 2 == 0 else -1
-            row, col = i + step, j + side * step
-            there = 0 <= row < 16 and 0 <= col < 16
-            out.append((16 * i + j, 16 * row + col if there else 16 * i + j))
-    return out
+    return [(i, (i + 1 if (i - first) % 2 == 0 else i - 1) % 16) for i in range(16)]
 
 
 def shards(
@@ -780,28 +768,29 @@
     place = jnp.stack([lax.axis_index(TROW), lax.axis_index(TCOL)]).astype(jnp.int32)
     lines = 8 * depth + 8 * ((depth + 1) // 2)
     columns = (depth // LEVELS, 16, 128)
-    corners = staged(corners_kernel, (surface_cot, bottom), [(16, 128)] * 4, place=place)
-    corners = [
-        lax.ppermute(x, ALL, corner_swaps(first, side))
-        for x, (first, side) in zip(corners, ((0, 1), (1, 1), (0, -1), (1, -1)))
-    ]
     a, c, w, inv, ratio, rows_a, rows_b, cols_a, cols_b = staged(
         columns_kernel,
         (land_mask, kappa, bottom, theta_cot, salt_cot, theta, salt, velocity_x, velocity_y, surface_cot),
-        [whole] * 4 + [kappa.shape, (lines + 16, 256), (lines + 16, 256), columns, columns],
+        [whole] * 4 + [kappa.shape, (lines + 24, 256), (lines + 24, 256), columns, columns],
         place=place,
         flops=100 * theta.size,
         lead=(0, LEVELS),
         sends=32,
     )
-    rows_a, rows_b, cols_a, cols_b, *corners = lax.optimization_barrier((rows_a, rows_b, cols_a, cols_b, *corners))
+    cols_a = lax.ppermute(cols_a, TCOL, swaps(0))
+    cols_b = lax.ppermute(cols_b, TCOL, swaps(1))
+    rows_a, rows_b = staged(
+        ends_kernel,
+        ((cols_a, 0, 2), (cols_b, 0, 2)),
+        [rows_a.shape, rows_b.shape],
+        place=place,
+        into=((rows_a, (lines + 16, 8)), (rows_b, (lines + 16, 8))),
+    )
     rows_a = lax.ppermute(rows_a, TROW, swaps(0))
     rows_b = lax.ppermute(rows_b, TROW, swaps(1))
-    cols_a = lax.ppermute(cols_a, TCOL, swaps(0))
-    cols_b = lax.ppermute(cols_b, TCOL, swaps(1))
     own, sums = staged(
         krylov_kernel,
-        (surface_cot, bottom, (rows_a, lines, 16), (rows_b, lines, 16), (cols_a, 0, 2), (cols_b, 0, 2), *corners),
+        (surface_cot, bottom, (rows_a, lines, 24), (rows_b, lines, 24), (cols_a, 0, 2), (cols_b, 0, 2)),
         [(128, 384), (256, 128)],
         place=place,
     )

time: 75.5 us -> 68.1 us (0.902)
  starting transfers between devices: 38.2 us -> 22.2 us
  waiting for transfers between devices: 9.32 us -> 17.5 us
    ppermute x4 -> x0, starting transfers between devices: 12.5 us -> none  [shards(): lax.ppermute(x, ALL, corner_swaps(first, side))]
    ppermute x1, starting transfers between devices: 1.42 us -> 7.3 us  [shards(): cols_b = lax.ppermute(cols_b, TCOL, swaps(1))]
    ppermute x1, waiting for transfers between devices: 3.26 us -> 8.92 us  [shards(): rows_b = lax.ppermute(rows_b, TROW, swaps(1))]
    all_to_all x1, starting transfers between devices: 15.7 us -> 10.1 us  [shards(): sums = lax.all_to_all(sums, ALL, 0, 0, tiled=True)]
    ppermute x1, starting transfers between devices: 5.59 us -> 0.38 us  [shards(): rows_b = lax.ppermute(rows_b, TROW, swaps(1))]
    ppermute x1, starting transfers between devices: 0.09 us -> 1.91 us  [shards(): rows_a = lax.ppermute(rows_a, TROW, swaps(0))]
    ppermute x1, waiting for transfers between devices: 0.01 us -> 1.59 us  [shards(): cols_b = lax.ppermute(cols_b, TCOL, swaps(1))]
    ppermute x1, waiting for transfers between devices: 0.01 us -> 1.1 us  [shards(): rows_a = lax.ppermute(rows_a, TROW, swaps(0))]
  transfers between devices with their start and end apart: 9 -> 5, of which waited for: 3 -> 4; matrix products, arithmetic and copies ran while one was open for 0% -> 0% of each run, Pallas kernels for 16% -> 10%
where the time goes in v7:
time: 68.1 us; the launch traced here: 67.6 us
  Pallas kernels  24.5 us (36%)
  starting transfers between devices  22.2 us (33%)
  waiting for transfers between devices  17.5 us (26%)
  local copies, waits for them, and re-layouts  2.02 us (3%)
  between operations  0.69 us (1%)
    pallas_call x5, Pallas kernels, staged(): pl.pallas_call(body, out_shape=[jax.ShapeDtypeStruct(s, F32) for s in out...  24.5 us
    all_to_all x1, starting transfers between devices, shards(): sums = lax.all_to_all(sums, ALL, 0, 0, tiled=True)  10.1 us
    ppermute x1, waiting for transfers between devices, shards(): rows_b = lax.ppermute(rows_b, TROW, swaps(1))  8.92 us
    ppermute x1, starting transfers between devices, shards(): cols_b = lax.ppermute(cols_b, TCOL, swaps(1))  7.3 us
    all_to_all x1, waiting for transfers between devices, shards(): sums = lax.all_to_all(sums, ALL, 0, 0, tiled=True)  5.87 us
    ppermute x1, starting transfers between devices, shards(): cols_a = lax.ppermute(cols_a, TCOL, swaps(0))  2.55 us
    unnamed x10, local copies, waits for them, and re-layouts  2.02 us
    ppermute x1, starting transfers between devices, shards(): rows_a = lax.ppermute(rows_a, TROW, swaps(0))  1.91 us
  transfers between devices with their start and end apart: 5, of which 4 were waited for; matrix products, arithmetic and copies ran while one was open for 0% of the time, Pallas kernels for 10%

profile of v7, /device:TPU:1, one launch (start us, length us, event | category | flops | bytes accessed | tf_op | source)
XLA Modules:
  0.0 67.6 jit_solution(14548029556376992439)
XLA Ops:
  0.6 0.6 pad_add_fusion.refs_0_
  1.2 5.3 %shard_map.156 = (f32[25,16,256]{2,1,0:T(8,128)}, f32[25,16,256]{2,1,0:T(8,128)}, f32[25,16,256]{2,1,0:T(8,128)}, f32[25,16,256]{2,1,0:T(8,128)}, f32[24,16,256]...) custom-call(s32[2]{0:T(128)} %pad_add_fusion.refs_0_, ...), custom_call_target="tpu_custom_call" | custom-call | flops 10240000 | bytes 6078464 | tf_op jit(solution)/shard_map/pallas_call | solution.py:155
  6.5 2.6 %collective-permute-start = (f32[5,16,128]{2,1,0:T(8,128)}, f32[5,16,128]{2,1,0:T(8,128)S(1)}, u32[]{:S(2)}, u32[]{:S(2)}) collective-permute-start(f32[5,16,128]{2,1,0:T(8,128)} %get-tuple-element.21), channel_id=1, source_target_pairs={{0,1},{1,0},{2,3},{3,2},{4,5},{5,4},{6,7},{7,6},{8,9},{9,8},{10,11... | collective-permute-start | bytes 122888 | tf_op jit(solution)/shard_map/ppermute | solution.py:780
  9.1 7.3 %collective-permute-start.1 = (f32[5,16,128]{2,1,0:T(8,128)}, f32[5,16,128]{2,1,0:T(8,128)S(1)}, u32[]{:S(2)}, u32[]{:S(2)}) collective-permute-start(f32[5,16,128]{2,1,0:T(8,128)} %get-tuple-element.22), channel_id=1, source_target_pairs={{0,15},{1,2},{2,1},{3,4},{4,3},{5,6},{6,5},{7,8},{8,7},{9,10},{10,... | collective-permute-start | bytes 122888 | tf_op jit(solution)/shard_map/ppermute | solution.py:781
  16.4 0.0 collective-permute-done.refs_1_.refs_5_.refs_7_
  16.4 0.0 copy-start.2
  16.4 1.6 %collective-permute-done.1.refs_2_.refs_6_.refs_8_ = f32[5,16,128]{2,1,0:T(8,128)S(1)} collective-permute-done((f32[5,16,128]{2,1,0:T(8,128)}, f32[5,16,128]{2,1,0:T(8,128)S(1)}, u32[]{:S(2)}, u32[]{:S(2)}) %collective-permute-start.1) | collective-permute-done | bytes 40992 | tf_op jit(solution)/shard_map/ppermute | solution.py:781
  18.0 0.0 copy-start.3
  18.0 0.0 copy-done.2
  18.0 0.6 copy-done.3
  18.6 2.1 %shard_map.157 = (f32[328,256]{1,0:T(8,128)}, f32[328,256]{1,0:T(8,128)}) custom-call(s32[2]{0:T(128)} %pad_add_fusion.refs_0_, f32[5,16,128]{2,1,0:T(8,128)} %copy-done.2, f32[5,16,128]{2,1,0:T(8,128)} %copy-done.3, f32[328,256]{1,0:T(8,128)} %get-tuple-element.23.refs_3_, ...), custom_call_target="tpu_custom_call", output_to_operand_aliasing={{0}: (3, {}), {1}: (4, {})} | custom-call | bytes 753664 | tf_op jit(solution)/shard_map/pallas_call | solution.py:155
  20.7 1.9 %collective-permute-start.2 = (f32[328,256]{1,0:T(8,128)}, f32[328,256]{1,0:T(8,128)S(1)}, u32[]{:S(2)}, u32[]{:S(2)}) collective-permute-start(f32[328,256]{1,0:T(8,128)} %get-tuple-element.25), channel_id=1, source_target_pairs={{0,16},{16,0},{32,48},{48,32},{64,80},{80,64},{96,112},{112,96},{1... | collective-permute-start | bytes 1007624 | tf_op jit(solution)/shard_map/ppermute | solution.py:789
  22.6 0.4 collective-permute-start.3
  23.0 1.1 %collective-permute-done.2.refs_3_.refs_5_ = f32[328,256]{1,0:T(8,128)S(1)} collective-permute-done((f32[328,256]{1,0:T(8,128)}, f32[328,256]{1,0:T(8,128)S(1)}, u32[]{:S(2)}, u32[]{:S(2)}) %collective-permute-start.2) | collective-permute-done | bytes 335904 | tf_op jit(solution)/shard_map/ppermute | solution.py:789
  24.1 0.0 copy-start
  24.1 8.9 %collective-permute-done.3.refs_4_.refs_6_ = f32[328,256]{1,0:T(8,128)S(1)} collective-permute-done((f32[328,256]{1,0:T(8,128)}, f32[328,256]{1,0:T(8,128)S(1)}, u32[]{:S(2)}, u32[]{:S(2)}) %collective-permute-start.3) | collective-permute-done | bytes 335904 | tf_op jit(solution)/shard_map/ppermute | solution.py:790
  33.0 0.0 copy-done
  33.0 0.0 copy-start.1
  33.0 0.7 %copy-done.1 = f32[328,256]{1,0:T(8,128)} copy-done((f32[328,256]{1,0:T(8,128)}, f32[328,256]{1,0:T(8,128)S(1)}, u32[]{:S(2)}) %copy-start.1) | copy-done | bytes 335896
  33.8 3.3 %shard_map.158 = (f32[128,384]{1,0:T(8,128)}, f32[256,128]{1,0:T(8,128)}) custom-call(s32[2]{0:T(128)} %pad_add_fusion.refs_0_, f32[16,256]{1,0:T(8,128)} %refs_1_.4, s32[16,256]{1,0:T(8,128)} %refs_4_.3, f32[328,256]{1,0:T(8,128)} %copy-done, f32[328,256]{1,0:T(8,128)} %copy-done.1, f32[5,16,128]{2,1,0:T(8,128)} %copy-done.2, f32[5,16,128]{2,1,0:T(8,128)} %copy-done.3), custom_call_target="tpu_custom_call" | custom-call | bytes 1114112 | tf_op jit(solution)/shard_map/pallas_call | solution.py:155
  37.1 10.1 %all-to-all-start = ((f32[256,1,128]{2,1,0:T(1,128)}), f32[256,1,128]{2,1,0:T(1,128)S(1)}, u32[]{:S(2)}, u32[]{:S(2)}) async-start(f32[256,1,128]{2,1,0:T(1,128)} %bitcast.7), calls=%async_computation | async-start | bytes 262144 | tf_op jit(solution)/shard_map/all_to_all | solution.py:808
  47.2 7.0 %shard_map.159 = (f32[25,24,256]{2,1,0:T(8,128)}, f32[25,16,384]{2,1,0:T(8,128)}, f32[24,16,256]{2,1,0:T(8,128)}, f32[24,16,256]{2,1,0:T(8,128)}) custom-call(s32[2]{0:T(128)} %pad_add_fusion.refs_0_, s32[25,16,256]{2,1,0:T(8,128)} %refs_3_.3, s32[16,256]{1,0:T(8,128)} %refs_4_.3, f32[328,256]{1,0:T(8,128)} %copy-done, f32[328,256]{1,0:T(8,128)} %copy-done.1, ...), custom_call_target="tpu_custom_call" | custom-call | flops 20480000 | bytes 7225344 | tf_op jit(solution)/shard_map/pallas_call | solution.py:155
  54.2 5.9 %all-to-all-done = f32[256,1,128]{2,1,0:T(1,128)S(1)} async-done(((f32[256,1,128]{2,1,0:T(1,128)}), f32[256,1,128]{2,1,0:T(1,128)S(1)}, u32[]{:S(2)}, u32[]{:S(2)}) %all-to-all-start) | async-done | bytes 131104 | tf_op jit(solution)/shard_map/all_to_all | solution.py:808
  60.0 0.0 copy-start.4
  60.0 0.6 copy-done.4
  60.7 6.9 %shard_map.160 = (f32[25,16,256]{2,1,0:T(8,128)}, f32[25,16,256]{2,1,0:T(8,128)}, f32[24,16,256]{2,1,0:T(8,128)}, f32[16,256]{1,0:T(8,128)}) custom-call(s32[2]{0:T(128)} %pad_add_fusion.refs_0_, f32[256,128]{1,0:T(8,128)} %bitcast.6, f32[128,384]{1,0:T(8,128)} %get-tuple-element.28.refs_2_, s32[25,16,256]{2,1,0:T(8,128)} %refs_3_.3, s32[16,256]{1,0:T(8,128)} %refs_4_.3, ...), custom_call_target="tpu_custom_call" | custom-call | bytes 6766592 | tf_op jit(solution)/shard_map/pallas_call | solution.py:155
Async XLA Ops:
  6.5 9.9 %collective-permute-start = (f32[5,16,128]{2,1,0:T(8,128)}, f32[5,16,128]{2,1,0:T(8,128)S(1)}, u32[]{:S(2)}, u32[]{:S(2)}) collective-permute-start(f32[5,16,128]{2,1,0:T(8,128)} %get-tuple-element.21), channel_id=1, source_target_pairs={{0,1},{1,0},{2,3},{3,2},{4,5},{5,4},{6,7},{7,6},{8,9},{9,8},{10,11... | collective-permute-start | bytes 122888 | tf_op jit(solution)/shard_map/ppermute | solution.py:780
  9.1 8.9 %collective-permute-start.1 = (f32[5,16,128]{2,1,0:T(8,128)}, f32[5,16,128]{2,1,0:T(8,128)S(1)}, u32[]{:S(2)}, u32[]{:S(2)}) collective-permute-start(f32[5,16,128]{2,1,0:T(8,128)} %get-tuple-element.22), channel_id=1, source_target_pairs={{0,15},{1,2},{2,1},{3,4},{4,3},{5,6},{6,5},{7,8},{8,7},{9,10},{10,... | collective-permute-start | bytes 122888 | tf_op jit(solution)/shard_map/ppermute | solution.py:781
  16.4 1.6 %copy-start.2 = (f32[5,16,128]{2,1,0:T(8,128)}, f32[5,16,128]{2,1,0:T(8,128)S(1)}, u32[]{:S(2)}) copy-start(f32[5,16,128]{2,1,0:T(8,128)S(1)} %collective-permute-done.refs_1_.refs_5_.refs_7_) | copy-start | bytes 122884
  18.0 0.6 copy-start.3
  20.7 3.4 %collective-permute-start.2 = (f32[328,256]{1,0:T(8,128)}, f32[328,256]{1,0:T(8,128)S(1)}, u32[]{:S(2)}, u32[]{:S(2)}) collective-permute-start(f32[328,256]{1,0:T(8,128)} %get-tuple-element.25), channel_id=1, source_target_pairs={{0,16},{16,0},{32,48},{48,32},{64,80},{80,64},{96,112},{112,96},{1... | collective-permute-start | bytes 1007624 | tf_op jit(solution)/shard_map/ppermute | solution.py:789
  22.6 10.4 %collective-permute-start.3 = (f32[328,256]{1,0:T(8,128)}, f32[328,256]{1,0:T(8,128)S(1)}, u32[]{:S(2)}, u32[]{:S(2)}) collective-permute-start(f32[328,256]{1,0:T(8,128)} %get-tuple-element.26), channel_id=1, source_target_pairs={{0,240},{16,32},{32,16},{48,64},{64,48},{80,96},{96,80},{112,128},... | collective-permute-start | bytes 1007624 | tf_op jit(solution)/shard_map/ppermute | solution.py:790
  24.1 8.9 %copy-start = (f32[328,256]{1,0:T(8,128)}, f32[328,256]{1,0:T(8,128)S(1)}, u32[]{:S(2)}) copy-start(f32[328,256]{1,0:T(8,128)S(1)} %collective-permute-done.2.refs_3_.refs_5_) | copy-start | bytes 1007620
  33.0 0.8 %copy-start.1 = (f32[328,256]{1,0:T(8,128)}, f32[328,256]{1,0:T(8,128)S(1)}, u32[]{:S(2)}) copy-start(f32[328,256]{1,0:T(8,128)S(1)} %collective-permute-done.3.refs_4_.refs_6_) | copy-start | bytes 1007620
  37.1 23.0 %all-to-all-start = ((f32[256,1,128]{2,1,0:T(1,128)}), f32[256,1,128]{2,1,0:T(1,128)S(1)}, u32[]{:S(2)}, u32[]{:S(2)}) async-start(f32[256,1,128]{2,1,0:T(1,128)} %bitcast.7), calls=%async_computation | async-start | bytes 262144 | tf_op jit(solution)/shard_map/all_to_all | solution.py:808
  60.0 0.7 copy-start.4

commit v8 on v5

--- a/solution.py
+++ b/solution.py
@@ -182,30 +182,32 @@
 
 
 def krylov_kernel(ins, outs, place_ref):
-    cot_ref, bottom_ref, rows_ref, cols_ref, corner_ref = [x.get() for x in ins]
-    up_out, left_out, own_out, diag_out, sums_out = outs
-    up_ref, left_ref, own_ref, diag_ref, sums_ref = [x.ref for x in outs]
+    cot_in, bottom_in, rows_in, west_in, east_in, left_in, right_in = ins
+    near_out, own_out, sums_out = outs
+    near_ref, own_ref, sums_ref = [x.ref for x in outs]
     r = place_ref[0]
     c = place_ref[1]
     shape = (24, 384)
     row = iota(shape, 0)
     lane = iota(shape, 1)
-
-    def window(main, at):
-        top = jnp.concatenate([corner_ref[8 * at : 8 * at + 8], rows_ref[8 * at : 8 * at + 8]], axis=1)
-        side = jnp.where(iota((16, 128), 1) >= 120, pltpu.roll(cols_ref[at], 2, 1), 0.0)
-        rest = jnp.concatenate([side, main], axis=1)
-        return jnp.concatenate([top, rest], axis=0)
-
-    inside = ((row >= 8) | (r > 0)) & ((lane >= 128) | (c > 0))
-    start = jnp.where(inside, window(cot_ref[...], 0), 0.0)
-    bottom = window(bottom_ref[...].astype(F32), 1)
+    edge = iota((16, 128), 1)
+    inside = ((row >= 8) | (r > 0)) & ((lane < 256) | ((lane < 264) & (c < 15)) | ((lane >= 376) & (c > 0)))
+    rows, west, east, left, right = [x.get() for x in ins[2:]]
+
+    def window(main, n):
+        at = slice(8 * n, 8 * n + 8)
+        ends = jnp.where(edge[0:8] < 64, right[at], left[at])
+        sides = jnp.where(edge < 64, pltpu.roll(east[n], 10, 1), pltpu.roll(west[n], 2, 1))
+        top = jnp.concatenate([rows[at], ends], axis=1)
+        return jnp.concatenate([top, jnp.concatenate([main, sides], axis=1)], axis=0)
+
+    start = jnp.where(inside, window(cot_in.get()[...], 0), 0.0)
+    bottom = window(bottom_in.get()[...].astype(F32), 1)
     shifted = (4.2 + bottom / 25.0) - CENTRE
 
     def apply_shifted(v):
         below = jnp.where(row == 23, 0.0, pltpu.roll(v, 23, 0))
-        right = jnp.where(lane == 383, 0.0, pltpu.roll(v, 383, 1))
-        beside = below + pltpu.roll(v, 1, 0) + right + pltpu.roll(v, 1, 1)
+        beside = below + pltpu.roll(v, 1, 0) + pltpu.roll(v, 383, 1) + pltpu.roll(v, 1, 1)
         return jnp.where(inside, shifted * v - beside, 0.0)
 
     vectors = [start]
@@ -220,30 +222,23 @@
 
     for k, v in enumerate(vectors):
         own_ref[24 * k : 24 * k + 24] = v
-        near = pltpu.roll(v[0:16], 12, 0)[0:8]
-        up_ref[8 * k : 8 * k + 8] = near
-        left_ref[24 * k : 24 * k + 24] = pltpu.roll(v[:, 0:256], 192, 1)[:, 0:128]
-        diag_ref[8 * k : 8 * k + 8] = pltpu.roll(near[:, 0:256], 192, 1)[:, 0:128]
-    for out in (up_out, left_out, diag_out, own_out):
-        out.send()
-
-    domain = (
-        (row >= 4)
-        & (row < jnp.where(r == 15, 24, 20))
-        & (lane >= 124)
-        & (lane < jnp.where(c == 15, 384, 380))
-    )
-    cut = [jnp.where(domain, v, 0.0) for v in vectors]
+        near_ref[8 * k : 8 * k + 8] = pltpu.roll(v[0:16], 12, 0)[0:8]
+    near_out.send()
+    own_out.send()
+
+    domain = (row >= 4) & (row < jnp.where(r == 15, 24, 20))
+    cut = [jnp.where(domain, v, 0.0)[:, 0:256] for v in vectors]
+    images = [w[:, 0:256] for w in images]
     cut_parts = [halves(v) for v in cut]
     image_parts = [halves(w) for w in images]
 
     def tile(x, at):
-        i, j = divmod(at, 3)
+        i, j = divmod(at, 2)
         return x[8 * i : 8 * i + 8, 128 * j : 128 * j + 128]
 
     def dot(x, x_parts, y, y_parts):
         total = None
-        for at in range(9):
+        for at in range(6):
             p, e = two_prod(
                 tile(x, at),
                 tile(y, at),
@@ -258,8 +253,7 @@
         return total
 
     dots = [dot(cut[i], cut_parts[i], images[j], image_parts[j]) for i, j in PAIRS]
-    start_parts = halves(start)
-    dots += [dot(cut[i], cut_parts[i], start, start_parts) for i in range(KRYLOV)]
+    dots += [dot(cut[i], cut_parts[i], cut[0], cut_parts[0]) for i in range(KRYLOV)]
     zero = jnp.zeros((8, 128), F32)
     dots += [(zero, zero)] * (16 - len(dots))
     packed = []
@@ -317,16 +311,18 @@
 def columns_kernel(ins, outs):
     depth = ins[0].ref.shape[0]
     land_in, kappa_in, bottom_in, tcot_in, scot_in, theta_in, salt_in, ux_in, uy_in, surface_in = ins
-    a_out, c_out, w_out, inv_out, ratio_out, down_out, up_out, right_out, left_out, corner_out = outs
-    a_ref, c_ref, w_ref, inv_ref, ratio_ref, down_ref, up_ref, right_ref, left_ref, corner_ref = [x.ref for x in outs]
+    a_out, c_out, w_out, inv_out, ratio_out, down_out, up_out, right_out, left_out, corner_out, cross_out = outs
+    a_ref, c_ref, w_ref, inv_ref, ratio_ref, down_ref, up_ref, right_ref, left_ref, corner_ref, cross_ref = [x.ref for x in outs]
     bottom = bottom_in.get()[...]
     lines = 8 * depth + 8 * ((depth + 1) // 2)
     spare = []
     for n, field in enumerate((surface_in.get()[...], bottom.astype(F32))):
         down_ref[lines + 8 * n : lines + 8 * n + 8] = field[8:16]
-        spare.append(pltpu.roll(field[:, 128:256], 126, 1))
+        spare.append((pltpu.roll(field[:, 128:256], 126, 1), pltpu.roll(field[:, 0:128], 118, 1)))
         corner_ref[8 * n : 8 * n + 8] = field[8:16, 128:256]
+        cross_ref[8 * n : 8 * n + 8] = field[8:16, 0:128]
     corner_out.send()
+    cross_out.send()
     early = (land_in, kappa_in, tcot_in, scot_in)
     land_ref, kappa_ref, tcot_ref, scot_ref = [x.first() for x in early]
 
@@ -403,9 +399,8 @@
         first_parts = first + first_parts
         if k % LEVELS == 0:
             g = k // LEVELS
-            filler = spare[g % 2]
-            right_ref[g] = packed_cols(last_parts, filler)
-            left_ref[g] = packed_cols(first_parts, filler)
+            right_ref[g] = packed_cols(last_parts, spare[g % 2][0])
+            left_ref[g] = packed_cols(first_parts, spare[g % 2][1])
             last_parts, first_parts = [], []
             for out in (a_out, c_out, w_out):
                 out.send(k, LEVELS)
@@ -588,8 +583,6 @@
         sums_in,
         own_in,
         near_in,
-        side_in,
-        corner_in,
         land_in,
         bottom_in,
         above_in,
@@ -609,11 +602,8 @@
     theta_grad_ref, salt_grad_ref, kappa_grad_ref, forcing_grad_ref = [x.ref for x in outs]
     depth = w_in.ref.shape[0]
     r = place_ref[0]
-    c = place_ref[1]
     has_down = jnp.where(r < 15, 1.0, 0.0)
-    sums_ref, own_ref, from_below_ref, from_right_ref, from_corner_ref = [
-        x.get() for x in (sums_in, own_in, near_in, side_in, corner_in)
-    ]
+    sums_ref, own_ref, near_ref = [x.get() for x in (sums_in, own_in, near_in)]
 
     small = (8, 128)
     small_row = iota(small, 0)
@@ -673,18 +663,13 @@
         middle = jnp.where((row8 >= 5) & (r < 15), turned, upper[16:24])
         return jnp.concatenate([upper[0:16], middle, turned * has_down], axis=0)
 
-    joined = rows_joined(combined(own_ref, 24), combined(from_below_ref, 8))
-    beside = pltpu.roll(rows_joined(combined(from_right_ref, 24), combined(from_corner_ref, 8)), 64, 1)
-    lane_wide = iota((32, 128), 1)
-    ending = jnp.where((lane_wide >= 125) & (c < 15), beside, joined[:, 256:384])
-    surface = jnp.concatenate([joined[:, 128:256], ending], axis=1)
-    zeta = surface[8:24]
-
+    surface = rows_joined(combined(own_ref, 24), combined(near_ref, 8))
+    zeta = surface[8:24, 0:256]
     bottom = bottom_in.get()[...]
     land_ref = land_in.first()
     edges = Edges(place_ref, depth, *[x.get() for x in (above_in, below_in, west_in, east_in)])
-    zeta_rows = jnp.where(edges.row8 < 4, surface[24:32], surface[0:8])
-    zeta_cols = jnp.where(edges.lane16 < 64, beside[8:24], joined[8:24, 0:128])
+    zeta_rows = jnp.where(edges.row8 < 4, surface[24:32, 0:256], surface[0:8, 0:256])
+    zeta_cols = surface[8:24, 256:384]
 
     def wet_at(k):
         return jnp.where(k < bottom, land_ref[k].astype(F32), 0.0)
@@ -734,9 +719,9 @@
     return [(i, (i + step) % count) for i in range(count)]
 
 
-def across(step):
+def across(down, right):
     return [
-        (16 * i + j, 16 * ((i + step) % 16) + (j + step) % 16) for i in range(16) for j in range(16)
+        (16 * i + j, 16 * ((i + down) % 16) + (j + right) % 16) for i in range(16) for j in range(16)
     ]
 
 
@@ -758,30 +743,29 @@
     place = jnp.stack([lax.axis_index(TROW), lax.axis_index(TCOL)]).astype(jnp.int32)
     lines = 8 * depth + 8 * ((depth + 1) // 2)
     columns = (depth // LEVELS, 16, 128)
-    a, c, w, inv, ratio, down, up, right, left, corner = staged(
+    a, c, w, inv, ratio, down, up, right, left, corner, cross = staged(
         columns_kernel,
         (land_mask, kappa, bottom, theta_cot, salt_cot, theta, salt, velocity_x, velocity_y, surface_cot),
         [whole] * 4
-        + [kappa.shape, (lines + 16, 256), (lines, 256), columns, columns, (16, 128)],
+        + [kappa.shape, (lines + 16, 256), (lines, 256), columns, columns, (16, 128), (16, 128)],
         flops=100 * theta.size,
         lead=(0, LEVELS),
         sends=32,
     )
     above = lax.ppermute(down, TROW, around(16, 1))
     west = lax.ppermute(right, TCOL, around(16, 1))
-    corner = lax.ppermute(corner, ALL, across(1))
+    corner = lax.ppermute(corner, ALL, across(1, 1))
+    cross = lax.ppermute(cross, ALL, across(1, -1))
     below = lax.ppermute(up, TROW, around(16, -1))
     east = lax.ppermute(left, TCOL, around(16, -1))
-    near, side, own, tip, sums = staged(
+    near, own, sums = staged(
         krylov_kernel,
-        (surface_cot, bottom, (above, lines, 16), (west, 0, 2), corner),
-        [(32, 384), (96, 128), (96, 384), (32, 128), (256, 128)],
+        (surface_cot, bottom, (above, lines, 16), (west, 0, 2), (east, 0, 2), corner, cross),
+        [(32, 384), (96, 384), (256, 128)],
         place=place,
-        after=(below, east),
+        after=(),
     )
     near = lax.ppermute(near, TROW, around(16, -1))
-    side = lax.ppermute(side, TCOL, around(16, -1))
-    tip = lax.ppermute(tip, ALL, across(-1))
     x_open, y_open, theta_drop, salt_drop = staged(
         forward_kernel,
         (land_mask, bottom, above, below, west, east, velocity_x, velocity_y, theta, salt)
@@ -797,7 +781,7 @@
     return tuple(
         staged(
             backward_kernel,
-            (sums, own, near, side, tip, land_mask, bottom, above, below, west, east, w, a, c)
+            (sums, own, near, land_mask, bottom, above, below, west, east, w, a, c)
             + (theta_drop, salt_drop, x_open, y_open, stencil(((-2, -1), (-1, 7), (0, 7), (1, -1)), 256)),
             [whole, whole, kappa.shape, forcing.shape],
             place=place,

time: 63 us -> 60 us (0.952)
  starting transfers between devices: 33.3 us -> 31 us
  waiting for transfers between devices: 3.85 us -> 2.75 us
    ppermute x3 -> x2, starting transfers between devices: 11.8 us -> 6.91 us  [the longest x1 5.46 us: shards(): cross = lax.ppermute(cross, ALL, across(1, -1))]
    ppermute x3 -> x2, waiting for transfers between devices: 3.83 us -> 0.01 us  [the longest x1 0.01 us: shards(): corner = lax.ppermute(corner, ALL, across(1, 1))]
    all_to_all x1, waiting for transfers between devices: 0.01 us -> 2.73 us  [shards(): sums = lax.all_to_all(sums, ALL, 0, 0, tiled=True)]
    ppermute x1, starting transfers between devices: 1.64 us -> 0.01 us  [shards(): west = lax.ppermute(right, TCOL, around(16, 1))]
    ppermute x1, starting transfers between devices: 3.44 us -> 5.08 us  [shards(): east = lax.ppermute(left, TCOL, around(16, -1))]
    ppermute x1, starting transfers between devices: 0.64 us -> 1.96 us  [shards(): below = lax.ppermute(up, TROW, around(16, -1))]
    all_to_all x1, starting transfers between devices: 10.8 us -> 11.8 us  [shards(): sums = lax.all_to_all(sums, ALL, 0, 0, tiled=True)]
    unnamed x24 -> x18, local copies, waits for them, and re-layouts: 2.1 us -> 2.69 us
  transfers between devices with their start and end apart: 9 -> 8, of which waited for: 1 -> 1; matrix products, arithmetic and copies ran while one was open for 1% -> 1% of each run, Pallas kernels for 11% -> 17%
where the time goes in v8:
time: 60 us; the launch traced here: 59.7 us
  starting transfers between devices  31 us (52%)
  Pallas kernels  21.8 us (36%)
  waiting for transfers between devices  2.75 us (5%)
  local copies, waits for them, and re-layouts  2.69 us (4%)
  between operations  0.91 us (2%)
  other arithmetic  0.6 us (1%)
    pallas_call x4, Pallas kernels, staged(): pl.pallas_call(body, out_shape=[jax.ShapeDtypeStruct(s, F32) for s in out...  21.8 us
    all_to_all x1, starting transfers between devices, shards(): sums = lax.all_to_all(sums, ALL, 0, 0, tiled=True)  11.8 us
    ppermute x1, starting transfers between devices, shards(): cross = lax.ppermute(cross, ALL, across(1, -1))  5.46 us
    ppermute x1, starting transfers between devices, shards(): east = lax.ppermute(left, TCOL, around(16, -1))  5.08 us
    ppermute x1, starting transfers between devices, shards(): above = lax.ppermute(down, TROW, around(16, 1))  2.76 us
    all_to_all x1, waiting for transfers between devices, shards(): sums = lax.all_to_all(sums, ALL, 0, 0, tiled=True)  2.73 us
    unnamed x18, local copies, waits for them, and re-layouts  2.69 us
    ppermute x1, starting transfers between devices, shards(): near = lax.ppermute(near, TROW, around(16, -1))  2.4 us
  transfers between devices with their start and end apart: 8, of which 1 were waited for; matrix products, arithmetic and copies ran while one was open for 1% of the time, Pallas kernels for 17%

profile of v8, /device:TPU:1, one launch (start us, length us, event | category | flops | bytes accessed | tf_op | source)
XLA Modules:
  0.0 59.7 jit_solution(13959000156984103967)
XLA Ops:
  0.6 4.6 %shard_map.156 = (f32[25,16,256]{2,1,0:T(8,128)}, f32[25,16,256]{2,1,0:T(8,128)}, f32[25,16,256]{2,1,0:T(8,128)}, f32[25,16,256]{2,1,0:T(8,128)}, f32[24,16,256]...) custom-call(s32[25,16,256]{2,1,0:T(8,128)} %refs_4_.3, ...), custom_call_target="tpu_custom_call" | custom-call | flops 10240000 | bytes 6062080 | tf_op jit(solution)/shard_map/pallas_call | solution.py:152
  5.3 2.8 %collective-permute-start = (f32[320,256]{1,0:T(8,128)}, f32[320,256]{1,0:T(8,128)S(1)}, u32[]{:S(2)}, u32[]{:S(2)}) collective-permute-start(f32[320,256]{1,0:T(8,128)} %get-tuple-element.22), channel_id=1, source_target_pairs={{0,16},{16,32},{32,48},{48,64},{64,80},{80,96},{96,112},{112,128},... | collective-permute-start | bytes 983048 | tf_op jit(solution)/shard_map/ppermute | solution.py:755
  8.0 1.4 %collective-permute-start.3 = (f32[16,128]{1,0:T(8,128)}, f32[16,128]{1,0:T(8,128)S(1)}, u32[]{:S(2)}, u32[]{:S(2)}) collective-permute-start(f32[16,128]{1,0:T(8,128)} %get-tuple-element.25), channel_id=1, source_target_pairs={{0,17},{1,18},{2,19},{3,20},{4,21},{5,22},{6,23},{7,24},{8,25},{9,... | collective-permute-start | bytes 24584 | tf_op jit(solution)/shard_map/ppermute | solution.py:757
  9.5 5.5 %collective-permute-start.4 = (f32[16,128]{1,0:T(8,128)}, f32[16,128]{1,0:T(8,128)S(1)}, u32[]{:S(2)}, u32[]{:S(2)}) collective-permute-start(f32[16,128]{1,0:T(8,128)} %get-tuple-element.26), channel_id=1, source_target_pairs={{0,31},{1,16},{2,17},{3,18},{4,19},{5,20},{6,21},{7,22},{8,23},{9,... | collective-permute-start | bytes 24584 | tf_op jit(solution)/shard_map/ppermute | solution.py:758
  14.9 0.0 collective-permute-start.1
  14.9 5.1 %collective-permute-start.2 = (f32[5,16,128]{2,1,0:T(8,128)}, f32[5,16,128]{2,1,0:T(8,128)S(1)}, u32[]{:S(2)}, u32[]{:S(2)}) collective-permute-start(f32[5,16,128]{2,1,0:T(8,128)} %get-tuple-element.24), channel_id=1, source_target_pairs={{0,15},{1,0},{2,1},{3,2},{4,3},{5,4},{6,5},{7,6},{8,7},{9,8},{10,9... | collective-permute-start | bytes 122888 | tf_op jit(solution)/shard_map/ppermute | solution.py:760
  20.0 0.0 collective-permute-done.3.refs_6_
  20.0 2.0 %collective-permute-start.6 = (f32[304,256]{1,0:T(8,128)}, f32[304,256]{1,0:T(8,128)S(1)}, u32[]{:S(2)}, u32[]{:S(2)}) collective-permute-start(f32[304,256]{1,0:T(8,128)} %get-tuple-element.30), channel_id=1, source_target_pairs={{0,240},{16,0},{32,16},{48,32},{64,48},{80,64},{96,80},{112,96},{1... | collective-permute-start | bytes 933896 | tf_op jit(solution)/shard_map/ppermute | solution.py:759
  22.0 0.6 %pad_add_fusion.refs_0_ = s32[2]{0:T(128)} fusion(s32[1]{0:T(128)} %bitcast.1, s32[1]{0:T(128)} %bitcast), kind=kLoop, calls=%fused_computation | loop fusion | flops 2 | bytes 16 | tf_op jit(solution)/shard_map/stack | solution.py:743
  22.6 0.0 collective-permute-done.4.refs_7_
  22.6 0.0 collective-permute-done.1.refs_4_.refs_5_.refs_8_
  22.6 0.0 copy-start.3
  22.6 0.0 collective-permute-done.2.refs_5_.refs_6_.refs_9_
  22.6 0.0 copy-start.4
  22.6 0.0 collective-permute-done.refs_3_.refs_6_
  22.6 0.0 copy-done.6
  22.6 0.5 copy-done.7
  23.2 0.0 copy-done.3
  23.2 0.0 copy-done.4
  23.2 0.7 %copy-done = f32[320,256]{1,0:T(8,128)} copy-done((f32[320,256]{1,0:T(8,128)}, f32[320,256]{1,0:T(8,128)S(1)}, u32[]{:S(2)}) %copy-start) | copy-done | bytes 327704
  23.9 3.3 %shard_map.157 = (f32[32,384]{1,0:T(8,128)}, f32[96,384]{1,0:T(8,128)}, f32[256,128]{1,0:T(8,128)}) custom-call(s32[2]{0:T(128)} %pad_add_fusion.refs_0_, f32[16,256]{1,0:T(8,128)} %refs_1_.4, s32[16,256]{1,0:T(8,128)} %refs_5_.3, f32[320,256]{1,0:T(8,128)} %copy-done, f32[5,16,128]{2,1,0:T(8,128)} %copy-done.3, f32[5,16,128]{2,1,0:T(8,128)} %copy-done.4, ...), custom_call_target="tpu_custom_call" | custom-call | bytes 786432 | tf_op jit(solution)/shard_map/pallas_call | solution.py:152
  27.3 0.0 copy-start.8
  27.3 11.8 %all-to-all-start = ((f32[256,1,128]{2,1,0:T(1,128)}), f32[256,1,128]{2,1,0:T(1,128)S(1)}, u32[]{:S(2)}, u32[]{:S(2)}) async-start(f32[256,1,128]{2,1,0:T(1,128)} %bitcast.7), calls=%async_computation | async-start | bytes 262144 | tf_op jit(solution)/shard_map/all_to_all | solution.py:780
  39.2 2.4 %collective-permute-start.5 = (f32[32,384]{1,0:T(8,128)S(1)}, f32[32,384]{1,0:T(8,128)S(1)}, u32[]{:S(2)}, u32[]{:S(2)}) collective-permute-start(f32[32,384]{1,0:T(8,128)S(1)} %copy-done.8), channel_id=1, source_target_pairs={{0,240},{16,0},{32,16},{48,32},{64,48},{80,64},{96,80},{112,96},{1... | collective-permute-start | bytes 147464 | tf_op jit(solution)/shard_map/ppermute | solution.py:768
  41.6 0.0 collective-permute-done.6.refs_4_.refs_7_
  41.6 0.7 %copy-done.1 = f32[304,256]{1,0:T(8,128)} copy-done((f32[304,256]{1,0:T(8,128)}, f32[304,256]{1,0:T(8,128)S(1)}, u32[]{:S(2)}) %copy-start.1) | copy-done | bytes 311320
  42.3 7.0 %shard_map.158 = (f32[25,24,256]{2,1,0:T(8,128)}, f32[25,16,384]{2,1,0:T(8,128)}, f32[24,16,256]{2,1,0:T(8,128)}, f32[24,16,256]{2,1,0:T(8,128)}) custom-call(s32[2]{0:T(128)} %pad_add_fusion.refs_0_, s32[25,16,256]{2,1,0:T(8,128)} %refs_4_.3, s32[16,256]{1,0:T(8,128)} %refs_5_.3, f32[320,256]{1,0:T(8,128)} %copy-done, f32[304,256]{1,0:T(8,128)} %copy-done.1, ...), custom_call_target="tpu_custom_call" | custom-call | flops 20480000 | bytes 7192576 | tf_op jit(solution)/shard_map/pallas_call | solution.py:152
  49.3 0.0 collective-permute-done.5.refs_3_
  49.3 2.7 %all-to-all-done = f32[256,1,128]{2,1,0:T(1,128)S(1)} async-done(((f32[256,1,128]{2,1,0:T(1,128)}), f32[256,1,128]{2,1,0:T(1,128)S(1)}, u32[]{:S(2)}, u32[]{:S(2)}) %all-to-all-start) | async-done | bytes 131104 | tf_op jit(solution)/shard_map/all_to_all | solution.py:780
  52.0 0.0 copy-done.5
  52.0 0.6 %copy-done.2 = f32[256,1,128]{2,1,0:T(1,128)} copy-done((f32[256,1,128]{2,1,0:T(1,128)}, f32[256,1,128]{2,1,0:T(1,128)S(1)}, u32[]{:S(2)}) %copy-start.2) | copy-done | bytes 131096
  52.7 6.9 %shard_map.159 = (f32[25,16,256]{2,1,0:T(8,128)}, f32[25,16,256]{2,1,0:T(8,128)}, f32[24,16,256]{2,1,0:T(8,128)}, f32[16,256]{1,0:T(8,128)}) custom-call(s32[2]{0:T(128)} %pad_add_fusion.refs_0_, f32[256,128]{1,0:T(8,128)} %bitcast.6, f32[96,384]{1,0:T(8,128)} %get-tuple-element.28.refs_2_, f32[32,384]{1,0:T(8,128)} %copy-done.5, s32[25,16,256]{2,1,0:T(8,128)} %refs_4_.3, ...), custom_call_target="tpu_custom_call" | custom-call | bytes 6733824 | tf_op jit(solution)/shard_map/pallas_call | solution.py:152
  (7 shorter events, 0.0 us)
Async XLA Ops:
  5.3 17.4 %collective-permute-start = (f32[320,256]{1,0:T(8,128)}, f32[320,256]{1,0:T(8,128)S(1)}, u32[]{:S(2)}, u32[]{:S(2)}) collective-permute-start(f32[320,256]{1,0:T(8,128)} %get-tuple-element.22), channel_id=1, source_target_pairs={{0,16},{16,32},{32,48},{48,64},{64,80},{80,96},{96,112},{112,128},... | collective-permute-start | bytes 983048 | tf_op jit(solution)/shard_map/ppermute | solution.py:755
  8.0 12.0 %collective-permute-start.3 = (f32[16,128]{1,0:T(8,128)}, f32[16,128]{1,0:T(8,128)S(1)}, u32[]{:S(2)}, u32[]{:S(2)}) collective-permute-start(f32[16,128]{1,0:T(8,128)} %get-tuple-element.25), channel_id=1, source_target_pairs={{0,17},{1,18},{2,19},{3,20},{4,21},{5,22},{6,23},{7,24},{8,25},{9,... | collective-permute-start | bytes 24584 | tf_op jit(solution)/shard_map/ppermute | solution.py:757
  9.5 13.1 %collective-permute-start.4 = (f32[16,128]{1,0:T(8,128)}, f32[16,128]{1,0:T(8,128)S(1)}, u32[]{:S(2)}, u32[]{:S(2)}) collective-permute-start(f32[16,128]{1,0:T(8,128)} %get-tuple-element.26), channel_id=1, source_target_pairs={{0,31},{1,16},{2,17},{3,18},{4,19},{5,20},{6,21},{7,22},{8,23},{9,... | collective-permute-start | bytes 24584 | tf_op jit(solution)/shard_map/ppermute | solution.py:758
  14.9 7.7 %collective-permute-start.1 = (f32[5,16,128]{2,1,0:T(8,128)}, f32[5,16,128]{2,1,0:T(8,128)S(1)}, u32[]{:S(2)}, u32[]{:S(2)}) collective-permute-start(f32[5,16,128]{2,1,0:T(8,128)} %get-tuple-element.23), channel_id=1, source_target_pairs={{0,1},{1,2},{2,3},{3,4},{4,5},{5,6},{6,7},{7,8},{8,9},{9,10},{10,1... | collective-permute-start | bytes 122888 | tf_op jit(solution)/shard_map/ppermute | solution.py:756
  14.9 7.7 %collective-permute-start.2 = (f32[5,16,128]{2,1,0:T(8,128)}, f32[5,16,128]{2,1,0:T(8,128)S(1)}, u32[]{:S(2)}, u32[]{:S(2)}) collective-permute-start(f32[5,16,128]{2,1,0:T(8,128)} %get-tuple-element.24), channel_id=1, source_target_pairs={{0,15},{1,0},{2,1},{3,2},{4,3},{5,4},{6,5},{7,6},{8,7},{9,8},{10,9... | collective-permute-start | bytes 122888 | tf_op jit(solution)/shard_map/ppermute | solution.py:760
  20.0 2.6 %copy-start.6 = (f32[16,128]{1,0:T(8,128)}, f32[16,128]{1,0:T(8,128)S(1)}, u32[]{:S(2)}) copy-start(f32[16,128]{1,0:T(8,128)S(1)} %collective-permute-done.3.refs_6_) | copy-start | bytes 24580
  20.0 21.5 %collective-permute-start.6 = (f32[304,256]{1,0:T(8,128)}, f32[304,256]{1,0:T(8,128)S(1)}, u32[]{:S(2)}, u32[]{:S(2)}) collective-permute-start(f32[304,256]{1,0:T(8,128)} %get-tuple-element.30), channel_id=1, source_target_pairs={{0,240},{16,0},{32,16},{48,32},{64,48},{80,64},{96,80},{112,96},{1... | collective-permute-start | bytes 933896 | tf_op jit(solution)/shard_map/ppermute | solution.py:759
  22.6 0.6 copy-start.7
  22.6 0.6 %copy-start.3 = (f32[5,16,128]{2,1,0:T(8,128)}, f32[5,16,128]{2,1,0:T(8,128)S(1)}, u32[]{:S(2)}) copy-start(f32[5,16,128]{2,1,0:T(8,128)S(1)} %collective-permute-done.1.refs_4_.refs_5_.refs_8_) | copy-start | bytes 122884
  22.6 0.6 %copy-start.4 = (f32[5,16,128]{2,1,0:T(8,128)}, f32[5,16,128]{2,1,0:T(8,128)S(1)}, u32[]{:S(2)}) copy-start(f32[5,16,128]{2,1,0:T(8,128)S(1)} %collective-permute-done.2.refs_5_.refs_6_.refs_9_) | copy-start | bytes 122884
  23.2 0.7 %copy-start = (f32[320,256]{1,0:T(8,128)}, f32[320,256]{1,0:T(8,128)S(1)}, u32[]{:S(2)}) copy-start(f32[320,256]{1,0:T(8,128)S(1)} %collective-permute-done.refs_3_.refs_6_) | copy-start | bytes 983044
  27.3 11.9 %copy-start.8 = (f32[32,384]{1,0:T(8,128)S(1)}, f32[32,384]{1,0:T(8,128)}, u32[]{:S(2)}) copy-start(f32[32,384]{1,0:T(8,128)} %get-tuple-element.29) | copy-start | bytes 147460
  27.3 24.7 %all-to-all-start = ((f32[256,1,128]{2,1,0:T(1,128)}), f32[256,1,128]{2,1,0:T(1,128)S(1)}, u32[]{:S(2)}, u32[]{:S(2)}) async-start(f32[256,1,128]{2,1,0:T(1,128)} %bitcast.7), calls=%async_computation | async-start | bytes 262144 | tf_op jit(solution)/shard_map/all_to_all | solution.py:780
  39.2 10.1 %collective-permute-start.5 = (f32[32,384]{1,0:T(8,128)S(1)}, f32[32,384]{1,0:T(8,128)S(1)}, u32[]{:S(2)}, u32[]{:S(2)}) collective-permute-start(f32[32,384]{1,0:T(8,128)S(1)} %copy-done.8), channel_id=1, source_target_pairs={{0,240},{16,0},{32,16},{48,32},{64,48},{80,64},{96,80},{112,96},{1... | collective-permute-start | bytes 147464 | tf_op jit(solution)/shard_map/ppermute | solution.py:768
  41.6 0.7 %copy-start.1 = (f32[304,256]{1,0:T(8,128)}, f32[304,256]{1,0:T(8,128)S(1)}, u32[]{:S(2)}) copy-start(f32[304,256]{1,0:T(8,128)S(1)} %collective-permute-done.6.refs_4_.refs_7_) | copy-start | bytes 933892
  49.3 2.7 %copy-start.5 = (f32[32,384]{1,0:T(8,128)}, f32[32,384]{1,0:T(8,128)S(1)}, u32[]{:S(2)}) copy-start(f32[32,384]{1,0:T(8,128)S(1)} %collective-permute-done.5.refs_3_) | copy-start | bytes 147460
  52.0 0.7 %copy-start.2 = (f32[256,1,128]{2,1,0:T(1,128)}, f32[256,1,128]{2,1,0:T(1,128)S(1)}, u32[]{:S(2)}) copy-start(f32[256,1,128]{2,1,0:T(1,128)S(1)} %all-to-all-done) | copy-start | bytes 393220

commit v9 on v8

--- a/solution.py
+++ b/solution.py
@@ -311,8 +311,8 @@
 def columns_kernel(ins, outs):
     depth = ins[0].ref.shape[0]
     land_in, kappa_in, bottom_in, tcot_in, scot_in, theta_in, salt_in, ux_in, uy_in, surface_in = ins
-    a_out, c_out, w_out, inv_out, ratio_out, down_out, up_out, right_out, left_out, corner_out, cross_out = outs
-    a_ref, c_ref, w_ref, inv_ref, ratio_ref, down_ref, up_ref, right_ref, left_ref, corner_ref, cross_ref = [x.ref for x in outs]
+    a_out, c_out, w_out, inv_out, ratio_out, down_out, up_out, right_out, left_out, corner_out = outs
+    a_ref, c_ref, w_ref, inv_ref, ratio_ref, down_ref, up_ref, right_ref, left_ref, corner_ref = [x.ref for x in outs]
     bottom = bottom_in.get()[...]
     lines = 8 * depth + 8 * ((depth + 1) // 2)
     spare = []
@@ -320,9 +320,7 @@
         down_ref[lines + 8 * n : lines + 8 * n + 8] = field[8:16]
         spare.append((pltpu.roll(field[:, 128:256], 126, 1), pltpu.roll(field[:, 0:128], 118, 1)))
         corner_ref[8 * n : 8 * n + 8] = field[8:16, 128:256]
-        cross_ref[8 * n : 8 * n + 8] = field[8:16, 0:128]
     corner_out.send()
-    cross_out.send()
     early = (land_in, kappa_in, tcot_in, scot_in)
     land_ref, kappa_ref, tcot_ref, scot_ref = [x.first() for x in early]
 
@@ -607,10 +605,14 @@
 
     small = (8, 128)
     small_row = iota(small, 0)
-    total = (sums_ref[0:8], jnp.zeros(small, F32))
-    for at in range(1, 32):
-        s, e = two_sum(total[0], sums_ref[8 * at : 8 * at + 8])
-        total = (s, total[1] + e)
+    terms = [(sums_ref[8 * at : 8 * at + 8], None) for at in range(32)]
+    while len(terms) > 1:
+        joined = []
+        for x, y in zip(terms[::2], terms[1::2]):
+            s, e = two_sum(x[0], y[0])
+            joined.append((s, e if x[1] is None else (x[1] + y[1]) + e))
+        terms = joined
+    total = terms[0]
     for step in (4, 2, 1):
         s, e = two_sum(total[0], pltpu.roll(total[0], step, 0))
         total = (s, (total[1] + pltpu.roll(total[1], step, 0)) + e)
@@ -743,19 +745,21 @@
     place = jnp.stack([lax.axis_index(TROW), lax.axis_index(TCOL)]).astype(jnp.int32)
     lines = 8 * depth + 8 * ((depth + 1) // 2)
     columns = (depth // LEVELS, 16, 128)
-    a, c, w, inv, ratio, down, up, right, left, corner, cross = staged(
+    cross = jnp.concatenate([surface_cot[8:16, 0:128], bottom[8:16, 0:128].astype(F32)])
+    cross = lax.ppermute(cross, ALL, across(1, -1))
+    a, c, w, inv, ratio, down, up, right, left, corner = staged(
         columns_kernel,
         (land_mask, kappa, bottom, theta_cot, salt_cot, theta, salt, velocity_x, velocity_y, surface_cot),
         [whole] * 4
-        + [kappa.shape, (lines + 16, 256), (lines, 256), columns, columns, (16, 128), (16, 128)],
+        + [kappa.shape, (lines + 16, 256), (lines, 256), columns, columns, (16, 128)],
         flops=100 * theta.size,
         lead=(0, LEVELS),
         sends=32,
     )
+    down, up, right, left, corner, cross = lax.optimization_barrier((down, up, right, left, corner, cross))
     above = lax.ppermute(down, TROW, around(16, 1))
     west = lax.ppermute(right, TCOL, around(16, 1))
     corner = lax.ppermute(corner, ALL, across(1, 1))
-    cross = lax.ppermute(cross, ALL, across(1, -1))
     below = lax.ppermute(up, TROW, around(16, -1))
     east = lax.ppermute(left, TCOL, around(16, -1))
     near, own, sums = staged(

time: 60 us -> 61.6 us (1.027)
  local copies, waits for them, and re-layouts: 2.69 us -> 4.3 us
  starting transfers between devices: 31 us -> 29.8 us
  other arithmetic: 0.6 us -> 1.27 us
    ppermute x1, starting transfers between devices: 5.46 us -> 9.42 us  [shards(): cross = lax.ppermute(cross, ALL, across(1, -1))]
    ppermute x1, starting transfers between devices: 2.76 us -> 0.37 us  [shards(): above = lax.ppermute(down, TROW, around(16, 1))]
    ppermute x1, starting transfers between devices: 1.44 us -> 0.01 us  [shards(): corner = lax.ppermute(corner, ALL, across(1, 1))]
    ppermute x1, starting transfers between devices: 1.96 us -> 0.64 us  [shards(): below = lax.ppermute(up, TROW, around(16, -1))]
    unnamed x18 -> x22, local copies, waits for them, and re-layouts: 2.69 us -> 3.6 us
    slice x0 -> x1, local copies, waits for them, and re-layouts: none -> 0.69 us  [shards(): surface_cot[8:16, 0:128]]
    convert_element_type x0 -> x1, other arithmetic: none -> 0.69 us  [shards(): bottom[8:16, 0:128].astype(F32)]
  transfers between devices with their start and end apart: 8 -> 8, of which waited for: 1 -> 2; matrix products, arithmetic and copies ran while one was open for 1% -> 1% of each run, Pallas kernels for 17% -> 24%
where the time goes in v9:
time: 61.6 us; the launch traced here: 61.3 us
  starting transfers between devices  29.8 us (48%)
  Pallas kernels  21.8 us (35%)
  local copies, waits for them, and re-layouts  4.3 us (7%)
  waiting for transfers between devices  3.2 us (5%)
  other arithmetic  1.27 us (2%)
  between operations  0.9 us (1%)
    pallas_call x4, Pallas kernels, staged(): pl.pallas_call(body, out_shape=[jax.ShapeDtypeStruct(s, F32) for s in out...  21.8 us
    all_to_all x1, starting transfers between devices, shards(): sums = lax.all_to_all(sums, ALL, 0, 0, tiled=True)  11.9 us
    ppermute x1, starting transfers between devices, shards(): cross = lax.ppermute(cross, ALL, across(1, -1))  9.42 us
    ppermute x1, starting transfers between devices, shards(): east = lax.ppermute(left, TCOL, around(16, -1))  5.1 us
    unnamed x22, local copies, waits for them, and re-layouts  3.6 us
    all_to_all x1, waiting for transfers between devices, shards(): sums = lax.all_to_all(sums, ALL, 0, 0, tiled=True)  2.73 us
    ppermute x1, starting transfers between devices, shards(): near = lax.ppermute(near, TROW, around(16, -1))  2.4 us
  transfers between devices with their start and end apart: 8, of which 2 were waited for; matrix products, arithmetic and copies ran while one was open for 1% of the time, Pallas kernels for 24%

profile of v9, /device:TPU:1, one launch (start us, length us, event | category | flops | bytes accessed | tf_op | source)
XLA Modules:
  0.0 61.3 jit_solution(8890383012372189709)
XLA Ops:
  0.6 0.7 %slice.6 = f32[8,128]{1,0:T(8,128)S(1)} slice(f32[16,256]{1,0:T(8,128)} %refs_1_.4), slice={[8:16], [0:128]} | slice | bytes 8192 | tf_op jit(solution)/shard_map/slice | solution.py:748
  1.3 0.7 %slice_convert_fusion = f32[8,128]{1,0:T(8,128)S(1)} fusion(s32[16,256]{1,0:T(8,128)} %refs_5_.3), kind=kLoop, calls=%fused_computation.1 | loop fusion | flops 1024 | bytes 8192 | tf_op jit(solution)/shard_map/convert_element_type | solution.py:748
  2.0 9.4 %collective-permute-start = (f32[16,128]{1,0:T(8,128)S(1)}, f32[16,128]{1,0:T(8,128)S(1)}, u32[]{:S(2)}, u32[]{:S(2)}) collective-permute-start(f32[16,128]{1,0:T(8,128)S(1)} %pad_maximum_fusion), channel_id=1, source_target_pairs={{0,31},{1,16},{2,17},{3,18},{4,19},{5,20},{6,21},{7,22},{8,23},{9,... | collective-permute-start | bytes 24584 | tf_op jit(solution)/shard_map/ppermute | solution.py:749
  11.4 4.6 %shard_map.156 = (f32[25,16,256]{2,1,0:T(8,128)}, f32[25,16,256]{2,1,0:T(8,128)}, f32[25,16,256]{2,1,0:T(8,128)}, f32[25,16,256]{2,1,0:T(8,128)}, f32[24,16,256]...) custom-call(s32[25,16,256]{2,1,0:T(8,128)} %refs_4_.3, ...), custom_call_target="tpu_custom_call" | custom-call | flops 10240000 | bytes 6053888 | tf_op jit(solution)/shard_map/pallas_call | solution.py:152
  16.1 0.0 copy-start.9
  16.1 0.0 collective-permute-done.refs_7_
  16.1 0.4 collective-permute-start.1
  16.5 0.2 copy-done.6
  16.7 0.7 %copy-done.10 = f32[16,128]{1,0:T(8,128)S(1)} copy-done((f32[16,128]{1,0:T(8,128)S(1)}, f32[16,128]{1,0:T(8,128)}, u32[]{:S(2)}) %copy-start.10) | copy-done | bytes 8216
  17.4 0.0 collective-permute-start.4
  17.4 0.0 collective-permute-start.2
  17.4 5.1 %collective-permute-start.3 = (f32[5,16,128]{2,1,0:T(8,128)S(1)}, f32[5,16,128]{2,1,0:T(8,128)S(1)}, u32[]{:S(2)}, u32[]{:S(2)}) collective-permute-start(f32[5,16,128]{2,1,0:T(8,128)S(1)} %copy-done.9), channel_id=1, source_target_pairs={{0,15},{1,0},{2,1},{3,2},{4,3},{5,4},{6,5},{7,6},{8,7},{9,8},{10,9... | collective-permute-start | bytes 122888 | tf_op jit(solution)/shard_map/ppermute | solution.py:764
  22.5 0.6 %collective-permute-start.6 = (f32[304,256]{1,0:T(8,128)}, f32[304,256]{1,0:T(8,128)S(1)}, u32[]{:S(2)}, u32[]{:S(2)}) collective-permute-start(f32[304,256]{1,0:T(8,128)} %get-tuple-element.40), channel_id=1, source_target_pairs={{0,240},{16,0},{32,16},{48,32},{64,48},{80,64},{96,80},{112,96},{1... | collective-permute-start | bytes 933896 | tf_op jit(solution)/shard_map/ppermute | solution.py:763
  23.1 0.6 pad_add_fusion.refs_0_
  23.7 0.4 collective-permute-done.4.refs_6_
  24.1 0.0 collective-permute-done.2.refs_4_.refs_5_.refs_8_
  24.2 0.0 collective-permute-done.3.refs_5_.refs_6_.refs_9_
  24.2 0.0 collective-permute-done.1.refs_3_.refs_6_
  24.2 0.6 copy-done.7
  24.7 0.0 copy-done.3
  24.8 0.0 copy-done.4
  24.8 0.7 %copy-done = f32[320,256]{1,0:T(8,128)} copy-done((f32[320,256]{1,0:T(8,128)}, f32[320,256]{1,0:T(8,128)S(1)}, u32[]{:S(2)}) %copy-start) | copy-done | bytes 327704
  25.5 3.3 %shard_map.157 = (f32[32,384]{1,0:T(8,128)}, f32[96,384]{1,0:T(8,128)}, f32[256,128]{1,0:T(8,128)}) custom-call(s32[2]{0:T(128)} %pad_add_fusion.refs_0_, f32[16,256]{1,0:T(8,128)} %refs_1_.4, s32[16,256]{1,0:T(8,128)} %refs_5_.3, f32[320,256]{1,0:T(8,128)} %copy-done, f32[5,16,128]{2,1,0:T(8,128)} %copy-done.3, f32[5,16,128]{2,1,0:T(8,128)} %copy-done.4, ...), custom_call_target="tpu_custom_call" | custom-call | bytes 786432 | tf_op jit(solution)/shard_map/pallas_call | solution.py:152
  28.9 11.9 %all-to-all-start = ((f32[256,1,128]{2,1,0:T(1,128)}), f32[256,1,128]{2,1,0:T(1,128)S(1)}, u32[]{:S(2)}, u32[]{:S(2)}) async-start(f32[256,1,128]{2,1,0:T(1,128)} %bitcast.7), calls=%async_computation | async-start | bytes 262144 | tf_op jit(solution)/shard_map/all_to_all | solution.py:784
  40.7 2.4 %collective-permute-start.5 = (f32[32,384]{1,0:T(8,128)S(1)}, f32[32,384]{1,0:T(8,128)S(1)}, u32[]{:S(2)}, u32[]{:S(2)}) collective-permute-start(f32[32,384]{1,0:T(8,128)S(1)} %copy-done.8), channel_id=1, source_target_pairs={{0,240},{16,0},{32,16},{48,32},{64,48},{80,64},{96,80},{112,96},{1... | collective-permute-start | bytes 147464 | tf_op jit(solution)/shard_map/ppermute | solution.py:772
  43.1 0.0 collective-permute-done.6.refs_4_.refs_7_
  43.2 0.7 %copy-done.1 = f32[304,256]{1,0:T(8,128)} copy-done((f32[304,256]{1,0:T(8,128)}, f32[304,256]{1,0:T(8,128)S(1)}, u32[]{:S(2)}) %copy-start.1) | copy-done | bytes 311320
  43.9 7.0 %shard_map.158 = (f32[25,24,256]{2,1,0:T(8,128)}, f32[25,16,384]{2,1,0:T(8,128)}, f32[24,16,256]{2,1,0:T(8,128)}, f32[24,16,256]{2,1,0:T(8,128)}) custom-call(s32[2]{0:T(128)} %pad_add_fusion.refs_0_, s32[25,16,256]{2,1,0:T(8,128)} %refs_4_.3, s32[16,256]{1,0:T(8,128)} %refs_5_.3, f32[320,256]{1,0:T(8,128)} %copy-done, f32[304,256]{1,0:T(8,128)} %copy-done.1, ...), custom_call_target="tpu_custom_call" | custom-call | flops 20480000 | bytes 7192576 | tf_op jit(solution)/shard_map/pallas_call | solution.py:152
  50.8 0.0 collective-permute-done.5.refs_3_
  50.9 2.7 %all-to-all-done = f32[256,1,128]{2,1,0:T(1,128)S(1)} async-done(((f32[256,1,128]{2,1,0:T(1,128)}), f32[256,1,128]{2,1,0:T(1,128)S(1)}, u32[]{:S(2)}, u32[]{:S(2)}) %all-to-all-start) | async-done | bytes 131104 | tf_op jit(solution)/shard_map/all_to_all | solution.py:784
  53.6 0.6 %copy-done.2 = f32[256,1,128]{2,1,0:T(1,128)} copy-done((f32[256,1,128]{2,1,0:T(1,128)}, f32[256,1,128]{2,1,0:T(1,128)S(1)}, u32[]{:S(2)}) %copy-start.2) | copy-done | bytes 131096
  54.2 6.9 %shard_map.159 = (f32[25,16,256]{2,1,0:T(8,128)}, f32[25,16,256]{2,1,0:T(8,128)}, f32[24,16,256]{2,1,0:T(8,128)}, f32[16,256]{1,0:T(8,128)}) custom-call(s32[2]{0:T(128)} %pad_add_fusion.refs_0_, f32[256,128]{1,0:T(8,128)} %bitcast.6, f32[96,384]{1,0:T(8,128)} %get-tuple-element.38.refs_2_, f32[32,384]{1,0:T(8,128)} %copy-done.5, s32[25,16,256]{2,1,0:T(8,128)} %refs_4_.3, ...), custom_call_target="tpu_custom_call" | custom-call | bytes 6733824 | tf_op jit(solution)/shard_map/pallas_call | solution.py:152
  (14 shorter events, 0.0 us)
Async XLA Ops:
  2.0 14.0 %collective-permute-start = (f32[16,128]{1,0:T(8,128)S(1)}, f32[16,128]{1,0:T(8,128)S(1)}, u32[]{:S(2)}, u32[]{:S(2)}) collective-permute-start(f32[16,128]{1,0:T(8,128)S(1)} %pad_maximum_fusion), channel_id=1, source_target_pairs={{0,31},{1,16},{2,17},{3,18},{4,19},{5,20},{6,21},{7,22},{8,23},{9,... | collective-permute-start | bytes 24584 | tf_op jit(solution)/shard_map/ppermute | solution.py:749
  16.1 1.3 %copy-start.9 = (f32[5,16,128]{2,1,0:T(8,128)S(1)}, f32[5,16,128]{2,1,0:T(8,128)}, u32[]{:S(2)}) copy-start(f32[5,16,128]{2,1,0:T(8,128)} %get-tuple-element.34) | copy-start | bytes 122884
  16.1 0.6 copy-start.6
  16.1 8.1 %collective-permute-start.1 = (f32[320,256]{1,0:T(8,128)}, f32[320,256]{1,0:T(8,128)S(1)}, u32[]{:S(2)}, u32[]{:S(2)}) collective-permute-start(f32[320,256]{1,0:T(8,128)} %get-tuple-element.32), channel_id=1, source_target_pairs={{0,16},{16,32},{32,48},{48,64},{64,80},{80,96},{96,112},{112,128},... | collective-permute-start | bytes 983048 | tf_op jit(solution)/shard_map/ppermute | solution.py:760
  16.7 0.7 %copy-start.10 = (f32[16,128]{1,0:T(8,128)S(1)}, f32[16,128]{1,0:T(8,128)}, u32[]{:S(2)}) copy-start(f32[16,128]{1,0:T(8,128)} %get-tuple-element.35) | copy-start | bytes 24580
  17.4 6.8 %collective-permute-start.4 = (f32[16,128]{1,0:T(8,128)S(1)}, f32[16,128]{1,0:T(8,128)S(1)}, u32[]{:S(2)}, u32[]{:S(2)}) collective-permute-start(f32[16,128]{1,0:T(8,128)S(1)} %copy-done.10), channel_id=1, source_target_pairs={{0,17},{1,18},{2,19},{3,20},{4,21},{5,22},{6,23},{7,24},{8,25},{9,... | collective-permute-start | bytes 24584 | tf_op jit(solution)/shard_map/ppermute | solution.py:762
  17.4 6.8 %collective-permute-start.2 = (f32[5,16,128]{2,1,0:T(8,128)}, f32[5,16,128]{2,1,0:T(8,128)S(1)}, u32[]{:S(2)}, u32[]{:S(2)}) collective-permute-start(f32[5,16,128]{2,1,0:T(8,128)} %get-tuple-element.33), channel_id=1, source_target_pairs={{0,1},{1,2},{2,3},{3,4},{4,5},{5,6},{6,7},{7,8},{8,9},{9,10},{10,1... | collective-permute-start | bytes 122888 | tf_op jit(solution)/shard_map/ppermute | solution.py:761
  17.4 6.8 %collective-permute-start.3 = (f32[5,16,128]{2,1,0:T(8,128)S(1)}, f32[5,16,128]{2,1,0:T(8,128)S(1)}, u32[]{:S(2)}, u32[]{:S(2)}) collective-permute-start(f32[5,16,128]{2,1,0:T(8,128)S(1)} %copy-done.9), channel_id=1, source_target_pairs={{0,15},{1,0},{2,1},{3,2},{4,3},{5,4},{6,5},{7,6},{8,7},{9,8},{10,9... | collective-permute-start | bytes 122888 | tf_op jit(solution)/shard_map/ppermute | solution.py:764
  22.5 20.7 %collective-permute-start.6 = (f32[304,256]{1,0:T(8,128)}, f32[304,256]{1,0:T(8,128)S(1)}, u32[]{:S(2)}, u32[]{:S(2)}) collective-permute-start(f32[304,256]{1,0:T(8,128)} %get-tuple-element.40), channel_id=1, source_target_pairs={{0,240},{16,0},{32,16},{48,32},{64,48},{80,64},{96,80},{112,96},{1... | collective-permute-start | bytes 933896 | tf_op jit(solution)/shard_map/ppermute | solution.py:763
  24.1 0.6 copy-start.7
  24.2 0.6 %copy-start.3 = (f32[5,16,128]{2,1,0:T(8,128)}, f32[5,16,128]{2,1,0:T(8,128)S(1)}, u32[]{:S(2)}) copy-start(f32[5,16,128]{2,1,0:T(8,128)S(1)} %collective-permute-done.2.refs_4_.refs_5_.refs_8_) | copy-start | bytes 122884
  24.2 0.6 %copy-start.4 = (f32[5,16,128]{2,1,0:T(8,128)}, f32[5,16,128]{2,1,0:T(8,128)S(1)}, u32[]{:S(2)}) copy-start(f32[5,16,128]{2,1,0:T(8,128)S(1)} %collective-permute-done.3.refs_5_.refs_6_.refs_9_) | copy-start | bytes 122884
  24.8 0.7 %copy-start = (f32[320,256]{1,0:T(8,128)}, f32[320,256]{1,0:T(8,128)S(1)}, u32[]{:S(2)}) copy-start(f32[320,256]{1,0:T(8,128)S(1)} %collective-permute-done.1.refs_3_.refs_6_) | copy-start | bytes 983044
  28.8 11.9 %copy-start.8 = (f32[32,384]{1,0:T(8,128)S(1)}, f32[32,384]{1,0:T(8,128)}, u32[]{:S(2)}) copy-start(f32[32,384]{1,0:T(8,128)} %get-tuple-element.39) | copy-start | bytes 147460
  28.9 24.7 %all-to-all-start = ((f32[256,1,128]{2,1,0:T(1,128)}), f32[256,1,128]{2,1,0:T(1,128)S(1)}, u32[]{:S(2)}, u32[]{:S(2)}) async-start(f32[256,1,128]{2,1,0:T(1,128)} %bitcast.7), calls=%async_computation | async-start | bytes 262144 | tf_op jit(solution)/shard_map/all_to_all | solution.py:784
  40.7 10.1 %collective-permute-start.5 = (f32[32,384]{1,0:T(8,128)S(1)}, f32[32,384]{1,0:T(8,128)S(1)}, u32[]{:S(2)}, u32[]{:S(2)}) collective-permute-start(f32[32,384]{1,0:T(8,128)S(1)} %copy-done.8), channel_id=1, source_target_pairs={{0,240},{16,0},{32,16},{48,32},{64,48},{80,64},{96,80},{112,96},{1... | collective-permute-start | bytes 147464 | tf_op jit(solution)/shard_map/ppermute | solution.py:772
  43.2 0.7 %copy-start.1 = (f32[304,256]{1,0:T(8,128)}, f32[304,256]{1,0:T(8,128)S(1)}, u32[]{:S(2)}) copy-start(f32[304,256]{1,0:T(8,128)S(1)} %collective-permute-done.6.refs_4_.refs_7_) | copy-start | bytes 933892
  50.9 2.7 %copy-start.5 = (f32[32,384]{1,0:T(8,128)}, f32[32,384]{1,0:T(8,128)S(1)}, u32[]{:S(2)}) copy-start(f32[32,384]{1,0:T(8,128)S(1)} %collective-permute-done.5.refs_3_) | copy-start | bytes 147460
  53.6 0.6 %copy-start.2 = (f32[256,1,128]{2,1,0:T(1,128)}, f32[256,1,128]{2,1,0:T(1,128)S(1)}, u32[]{:S(2)}) copy-start(f32[256,1,128]{2,1,0:T(1,128)S(1)} %all-to-all-done) | copy-start | bytes 393220

commit v10 on v9

--- a/solution.py
+++ b/solution.py
@@ -182,7 +182,7 @@
 
 
 def krylov_kernel(ins, outs, place_ref):
-    cot_in, bottom_in, rows_in, west_in, east_in, left_in, right_in = ins
+    cot_in, bottom_in = ins[:2]
     near_out, own_out, sums_out = outs
     near_ref, own_ref, sums_ref = [x.ref for x in outs]
     r = place_ref[0]
@@ -192,7 +192,7 @@
     lane = iota(shape, 1)
     edge = iota((16, 128), 1)
     inside = ((row >= 8) | (r > 0)) & ((lane < 256) | ((lane < 264) & (c < 15)) | ((lane >= 376) & (c > 0)))
-    rows, west, east, left, right = [x.get() for x in ins[2:]]
+    rows, left, west, right, east = [x.get() for x in ins[2:]]
 
     def window(main, n):
         at = slice(8 * n, 8 * n + 8)
@@ -311,8 +311,8 @@
 def columns_kernel(ins, outs):
     depth = ins[0].ref.shape[0]
     land_in, kappa_in, bottom_in, tcot_in, scot_in, theta_in, salt_in, ux_in, uy_in, surface_in = ins
-    a_out, c_out, w_out, inv_out, ratio_out, down_out, up_out, right_out, left_out, corner_out = outs
-    a_ref, c_ref, w_ref, inv_ref, ratio_ref, down_ref, up_ref, right_ref, left_ref, corner_ref = [x.ref for x in outs]
+    a_out, c_out, w_out, inv_out, ratio_out, down_out, up_out, right_out, left_out, corner_out, cross_out = outs
+    a_ref, c_ref, w_ref, inv_ref, ratio_ref, down_ref, up_ref, right_ref, left_ref, corner_ref, cross_ref = [x.ref for x in outs]
     bottom = bottom_in.get()[...]
     lines = 8 * depth + 8 * ((depth + 1) // 2)
     spare = []
@@ -320,7 +320,10 @@
         down_ref[lines + 8 * n : lines + 8 * n + 8] = field[8:16]
         spare.append((pltpu.roll(field[:, 128:256], 126, 1), pltpu.roll(field[:, 0:128], 118, 1)))
         corner_ref[8 * n : 8 * n + 8] = field[8:16, 128:256]
+        cross_ref[8 * n : 8 * n + 8] = field[8:16, 0:128]
+    cross_ref[16:80] = jnp.zeros((64, 128), F32)
     corner_out.send()
+    cross_out.send()
     early = (land_in, kappa_in, tcot_in, scot_in)
     land_ref, kappa_ref, tcot_ref, scot_ref = [x.first() for x in early]
 
@@ -745,26 +748,24 @@
     place = jnp.stack([lax.axis_index(TROW), lax.axis_index(TCOL)]).astype(jnp.int32)
     lines = 8 * depth + 8 * ((depth + 1) // 2)
     columns = (depth // LEVELS, 16, 128)
-    cross = jnp.concatenate([surface_cot[8:16, 0:128], bottom[8:16, 0:128].astype(F32)])
-    cross = lax.ppermute(cross, ALL, across(1, -1))
-    a, c, w, inv, ratio, down, up, right, left, corner = staged(
+    a, c, w, inv, ratio, down, up, right, left, corner, cross = staged(
         columns_kernel,
         (land_mask, kappa, bottom, theta_cot, salt_cot, theta, salt, velocity_x, velocity_y, surface_cot),
         [whole] * 4
-        + [kappa.shape, (lines + 16, 256), (lines, 256), columns, columns, (16, 128)],
+        + [kappa.shape, (lines + 16, 256), (lines, 256), columns, columns, (16, 128), (80, 128)],
         flops=100 * theta.size,
         lead=(0, LEVELS),
         sends=32,
     )
-    down, up, right, left, corner, cross = lax.optimization_barrier((down, up, right, left, corner, cross))
+    corner = lax.ppermute(corner, ALL, across(1, 1))
+    west = lax.ppermute(right, TCOL, around(16, 1))
+    cross = lax.ppermute(cross, ALL, across(1, -1))
+    east = lax.ppermute(left, TCOL, around(16, -1))
     above = lax.ppermute(down, TROW, around(16, 1))
-    west = lax.ppermute(right, TCOL, around(16, 1))
-    corner = lax.ppermute(corner, ALL, across(1, 1))
     below = lax.ppermute(up, TROW, around(16, -1))
-    east = lax.ppermute(left, TCOL, around(16, -1))
     near, own, sums = staged(
         krylov_kernel,
-        (surface_cot, bottom, (above, lines, 16), (west, 0, 2), (east, 0, 2), corner, cross),
+        (surface_cot, bottom, (above, lines, 16), corner, (west, 0, 2), (cross, 0, 16), (east, 0, 2)),
         [(32, 384), (96, 384), (256, 128)],
         place=place,
         after=(),

time: 61.6 us -> 56.7 us (0.920)
  starting transfers between devices: 29.8 us -> 27.4 us
  local copies, waits for them, and re-layouts: 4.3 us -> 2.7 us
  other arithmetic: 1.27 us -> 0.6 us
    ppermute x1, starting transfers between devices: 9.42 us -> 4.72 us  [shards(): cross = lax.ppermute(cross, ALL, across(1, -1))]
    ppermute x1, starting transfers between devices: 0.37 us -> 2.76 us  [shards(): above = lax.ppermute(down, TROW, around(16, 1))]
    ppermute x1, starting transfers between devices: 5.1 us -> 2.97 us  [shards(): east = lax.ppermute(left, TCOL, around(16, -1))]
    ppermute x1, starting transfers between devices: 0.01 us -> 1.64 us  [shards(): west = lax.ppermute(right, TCOL, around(16, 1))]
    ppermute x1, starting transfers between devices: 0.01 us -> 1.44 us  [shards(): corner = lax.ppermute(corner, ALL, across(1, 1))]
    all_to_all x1, starting transfers between devices: 11.9 us -> 11 us  [shards(): sums = lax.all_to_all(sums, ALL, 0, 0, tiled=True)]
    unnamed x22 -> x18, local copies, waits for them, and re-layouts: 3.6 us -> 2.7 us
    slice x1 -> x0, local copies, waits for them, and re-layouts: 0.69 us -> none  [shards(): surface_cot[8:16, 0:128]]
  transfers between devices with their start and end apart: 8 -> 8, of which waited for: 2 -> 2; matrix products, arithmetic and copies ran while one was open for 1% -> 1% of each run, Pallas kernels for 24% -> 18%
where the time goes in v10:
time: 56.7 us; the launch traced here: 56.4 us
  starting transfers between devices  27.4 us (48%)
  Pallas kernels  21.8 us (38%)
  waiting for transfers between devices  2.99 us (5%)
  local copies, waits for them, and re-layouts  2.7 us (5%)
  between operations  0.88 us (2%)
  other arithmetic  0.6 us (1%)
    pallas_call x4, Pallas kernels, staged(): pl.pallas_call(body, out_shape=[jax.ShapeDtypeStruct(s, F32) for s in out...  21.8 us
    all_to_all x1, starting transfers between devices, shards(): sums = lax.all_to_all(sums, ALL, 0, 0, tiled=True)  11 us
    ppermute x1, starting transfers between devices, shards(): cross = lax.ppermute(cross, ALL, across(1, -1))  4.72 us
    ppermute x1, starting transfers between devices, shards(): east = lax.ppermute(left, TCOL, around(16, -1))  2.97 us
    ppermute x1, starting transfers between devices, shards(): above = lax.ppermute(down, TROW, around(16, 1))  2.76 us
    all_to_all x1, waiting for transfers between devices, shards(): sums = lax.all_to_all(sums, ALL, 0, 0, tiled=True)  2.73 us
    unnamed x18, local copies, waits for them, and re-layouts  2.7 us
    ppermute x1, starting transfers between devices, shards(): near = lax.ppermute(near, TROW, around(16, -1))  2.4 us
  transfers between devices with their start and end apart: 8, of which 2 were waited for; matrix products, arithmetic and copies ran while one was open for 1% of the time, Pallas kernels for 18%

profile of v10, /device:TPU:1, one launch (start us, length us, event | category | flops | bytes accessed | tf_op | source)
XLA Modules:
  0.0 56.4 jit_solution(15358446345013545473)
XLA Ops:
  0.6 4.6 %shard_map.156 = (f32[25,16,256]{2,1,0:T(8,128)}, f32[25,16,256]{2,1,0:T(8,128)}, f32[25,16,256]{2,1,0:T(8,128)}, f32[25,16,256]{2,1,0:T(8,128)}, f32[24,16,256]...) custom-call(s32[25,16,256]{2,1,0:T(8,128)} %refs_4_.3, ...), custom_call_target="tpu_custom_call" | custom-call | flops 10240000 | bytes 6094848 | tf_op jit(solution)/shard_map/pallas_call | solution.py:152
  5.3 2.8 %collective-permute-start = (f32[320,256]{1,0:T(8,128)}, f32[320,256]{1,0:T(8,128)S(1)}, u32[]{:S(2)}, u32[]{:S(2)}) collective-permute-start(f32[320,256]{1,0:T(8,128)} %get-tuple-element.22), channel_id=1, source_target_pairs={{0,16},{16,32},{32,48},{48,64},{64,80},{80,96},{96,112},{112,128},... | collective-permute-start | bytes 983048 | tf_op jit(solution)/shard_map/ppermute | solution.py:764
  8.0 1.4 %collective-permute-start.1 = (f32[16,128]{1,0:T(8,128)}, f32[16,128]{1,0:T(8,128)S(1)}, u32[]{:S(2)}, u32[]{:S(2)}) collective-permute-start(f32[16,128]{1,0:T(8,128)} %get-tuple-element.23), channel_id=1, source_target_pairs={{0,17},{1,18},{2,19},{3,20},{4,21},{5,22},{6,23},{7,24},{8,25},{9,... | collective-permute-start | bytes 24584 | tf_op jit(solution)/shard_map/ppermute | solution.py:760
  9.5 1.6 %collective-permute-start.2 = (f32[5,16,128]{2,1,0:T(8,128)}, f32[5,16,128]{2,1,0:T(8,128)S(1)}, u32[]{:S(2)}, u32[]{:S(2)}) collective-permute-start(f32[5,16,128]{2,1,0:T(8,128)} %get-tuple-element.24), channel_id=1, source_target_pairs={{0,1},{1,2},{2,3},{3,4},{4,5},{5,6},{6,7},{7,8},{8,9},{9,10},{10,1... | collective-permute-start | bytes 122888 | tf_op jit(solution)/shard_map/ppermute | solution.py:761
  11.1 4.7 %collective-permute-start.3 = (f32[80,128]{1,0:T(8,128)}, f32[80,128]{1,0:T(8,128)S(1)}, u32[]{:S(2)}, u32[]{:S(2)}) collective-permute-start(f32[80,128]{1,0:T(8,128)} %get-tuple-element.25), channel_id=1, source_target_pairs={{0,31},{1,16},{2,17},{3,18},{4,19},{5,20},{6,21},{7,22},{8,23},{9,... | collective-permute-start | bytes 122888 | tf_op jit(solution)/shard_map/ppermute | solution.py:762
  15.8 3.0 %collective-permute-start.4 = (f32[5,16,128]{2,1,0:T(8,128)}, f32[5,16,128]{2,1,0:T(8,128)S(1)}, u32[]{:S(2)}, u32[]{:S(2)}) collective-permute-start(f32[5,16,128]{2,1,0:T(8,128)} %get-tuple-element.26), channel_id=1, source_target_pairs={{0,15},{1,0},{2,1},{3,2},{4,3},{5,4},{6,5},{7,6},{8,7},{9,8},{10,9... | collective-permute-start | bytes 122888 | tf_op jit(solution)/shard_map/ppermute | solution.py:763
  18.8 0.0 collective-permute-done.1.refs_4_
  18.8 0.5 collective-permute-start.6
  19.3 0.6 %pad_add_fusion.refs_0_ = s32[2]{0:T(128)} fusion(s32[1]{0:T(128)} %bitcast.1, s32[1]{0:T(128)} %bitcast), kind=kLoop, calls=%fused_computation | loop fusion | flops 2 | bytes 16 | tf_op jit(solution)/shard_map/stack | solution.py:748
  20.0 0.0 collective-permute-done.2.refs_5_.refs_8_
  20.0 0.0 collective-permute-done.3.refs_6_
  20.0 0.0 copy-start.6
  20.0 0.2 collective-permute-done.4.refs_7_.refs_6_.refs_9_
  20.2 0.0 collective-permute-done.refs_3_.refs_6_
  20.2 0.0 copy-done.7
  20.2 0.3 copy-done.3
  20.6 0.0 copy-done.6
  20.6 0.2 copy-done.4
  20.8 0.7 %copy-done = f32[320,256]{1,0:T(8,128)} copy-done((f32[320,256]{1,0:T(8,128)}, f32[320,256]{1,0:T(8,128)S(1)}, u32[]{:S(2)}) %copy-start) | copy-done | bytes 327704
  21.5 3.3 %shard_map.157 = (f32[32,384]{1,0:T(8,128)}, f32[96,384]{1,0:T(8,128)}, f32[256,128]{1,0:T(8,128)}) custom-call(s32[2]{0:T(128)} %pad_add_fusion.refs_0_, f32[16,256]{1,0:T(8,128)} %refs_1_.4, s32[16,256]{1,0:T(8,128)} %refs_5_.3, f32[320,256]{1,0:T(8,128)} %copy-done, f32[16,128]{1,0:T(8,128)} %copy-done.7, f32[5,16,128]{2,1,0:T(8,128)} %copy-done.3, ...), custom_call_target="tpu_custom_call" | custom-call | bytes 819200 | tf_op jit(solution)/shard_map/pallas_call | solution.py:152
  24.9 0.0 copy-start.8
  24.9 11.0 %all-to-all-start = ((f32[256,1,128]{2,1,0:T(1,128)}), f32[256,1,128]{2,1,0:T(1,128)S(1)}, u32[]{:S(2)}, u32[]{:S(2)}) async-start(f32[256,1,128]{2,1,0:T(1,128)} %bitcast.7), calls=%async_computation | async-start | bytes 262144 | tf_op jit(solution)/shard_map/all_to_all | solution.py:785
  35.9 0.0 copy-done.8
  35.9 2.4 %collective-permute-start.5 = (f32[32,384]{1,0:T(8,128)S(1)}, f32[32,384]{1,0:T(8,128)S(1)}, u32[]{:S(2)}, u32[]{:S(2)}) collective-permute-start(f32[32,384]{1,0:T(8,128)S(1)} %copy-done.8), channel_id=1, source_target_pairs={{0,240},{16,0},{32,16},{48,32},{64,48},{80,64},{96,80},{112,96},{1... | collective-permute-start | bytes 147464 | tf_op jit(solution)/shard_map/ppermute | solution.py:773
  38.3 0.0 collective-permute-done.6.refs_4_.refs_7_
  38.3 0.7 %copy-done.1 = f32[304,256]{1,0:T(8,128)} copy-done((f32[304,256]{1,0:T(8,128)}, f32[304,256]{1,0:T(8,128)S(1)}, u32[]{:S(2)}) %copy-start.1) | copy-done | bytes 311320
  39.0 7.0 %shard_map.158 = (f32[25,24,256]{2,1,0:T(8,128)}, f32[25,16,384]{2,1,0:T(8,128)}, f32[24,16,256]{2,1,0:T(8,128)}, f32[24,16,256]{2,1,0:T(8,128)}) custom-call(s32[2]{0:T(128)} %pad_add_fusion.refs_0_, s32[25,16,256]{2,1,0:T(8,128)} %refs_4_.3, s32[16,256]{1,0:T(8,128)} %refs_5_.3, f32[320,256]{1,0:T(8,128)} %copy-done, f32[304,256]{1,0:T(8,128)} %copy-done.1, ...), custom_call_target="tpu_custom_call" | custom-call | flops 20480000 | bytes 7192576 | tf_op jit(solution)/shard_map/pallas_call | solution.py:152
  46.0 0.0 collective-permute-done.5.refs_3_
  46.0 0.0 copy-start.5
  46.0 2.7 %all-to-all-done = f32[256,1,128]{2,1,0:T(1,128)S(1)} async-done(((f32[256,1,128]{2,1,0:T(1,128)}), f32[256,1,128]{2,1,0:T(1,128)S(1)}, u32[]{:S(2)}, u32[]{:S(2)}) %all-to-all-start) | async-done | bytes 131104 | tf_op jit(solution)/shard_map/all_to_all | solution.py:785
  48.7 0.6 %copy-done.2 = f32[256,1,128]{2,1,0:T(1,128)} copy-done((f32[256,1,128]{2,1,0:T(1,128)}, f32[256,1,128]{2,1,0:T(1,128)S(1)}, u32[]{:S(2)}) %copy-start.2) | copy-done | bytes 131096
  49.4 6.9 %shard_map.159 = (f32[25,16,256]{2,1,0:T(8,128)}, f32[25,16,256]{2,1,0:T(8,128)}, f32[24,16,256]{2,1,0:T(8,128)}, f32[16,256]{1,0:T(8,128)}) custom-call(s32[2]{0:T(128)} %pad_add_fusion.refs_0_, f32[256,128]{1,0:T(8,128)} %bitcast.6, f32[96,384]{1,0:T(8,128)} %get-tuple-element.28.refs_2_, f32[32,384]{1,0:T(8,128)} %copy-done.5, s32[25,16,256]{2,1,0:T(8,128)} %refs_4_.3, ...), custom_call_target="tpu_custom_call" | custom-call | bytes 6733824 | tf_op jit(solution)/shard_map/pallas_call | solution.py:152
  (7 shorter events, 0.0 us)
Async XLA Ops:
  5.3 15.0 %collective-permute-start = (f32[320,256]{1,0:T(8,128)}, f32[320,256]{1,0:T(8,128)S(1)}, u32[]{:S(2)}, u32[]{:S(2)}) collective-permute-start(f32[320,256]{1,0:T(8,128)} %get-tuple-element.22), channel_id=1, source_target_pairs={{0,16},{16,32},{32,48},{48,64},{64,80},{80,96},{96,112},{112,128},... | collective-permute-start | bytes 983048 | tf_op jit(solution)/shard_map/ppermute | solution.py:764
  8.0 10.8 %collective-permute-start.1 = (f32[16,128]{1,0:T(8,128)}, f32[16,128]{1,0:T(8,128)S(1)}, u32[]{:S(2)}, u32[]{:S(2)}) collective-permute-start(f32[16,128]{1,0:T(8,128)} %get-tuple-element.23), channel_id=1, source_target_pairs={{0,17},{1,18},{2,19},{3,20},{4,21},{5,22},{6,23},{7,24},{8,25},{9,... | collective-permute-start | bytes 24584 | tf_op jit(solution)/shard_map/ppermute | solution.py:760
  9.5 10.5 %collective-permute-start.2 = (f32[5,16,128]{2,1,0:T(8,128)}, f32[5,16,128]{2,1,0:T(8,128)S(1)}, u32[]{:S(2)}, u32[]{:S(2)}) collective-permute-start(f32[5,16,128]{2,1,0:T(8,128)} %get-tuple-element.24), channel_id=1, source_target_pairs={{0,1},{1,2},{2,3},{3,4},{4,5},{5,6},{6,7},{7,8},{8,9},{9,10},{10,1... | collective-permute-start | bytes 122888 | tf_op jit(solution)/shard_map/ppermute | solution.py:761
  11.1 8.9 %collective-permute-start.3 = (f32[80,128]{1,0:T(8,128)}, f32[80,128]{1,0:T(8,128)S(1)}, u32[]{:S(2)}, u32[]{:S(2)}) collective-permute-start(f32[80,128]{1,0:T(8,128)} %get-tuple-element.25), channel_id=1, source_target_pairs={{0,31},{1,16},{2,17},{3,18},{4,19},{5,20},{6,21},{7,22},{8,23},{9,... | collective-permute-start | bytes 122888 | tf_op jit(solution)/shard_map/ppermute | solution.py:762
  15.8 4.4 %collective-permute-start.4 = (f32[5,16,128]{2,1,0:T(8,128)}, f32[5,16,128]{2,1,0:T(8,128)S(1)}, u32[]{:S(2)}, u32[]{:S(2)}) collective-permute-start(f32[5,16,128]{2,1,0:T(8,128)} %get-tuple-element.26), channel_id=1, source_target_pairs={{0,15},{1,0},{2,1},{3,2},{4,3},{5,4},{6,5},{7,6},{8,7},{9,8},{10,9... | collective-permute-start | bytes 122888 | tf_op jit(solution)/shard_map/ppermute | solution.py:763
  18.8 1.4 %copy-start.7 = (f32[16,128]{1,0:T(8,128)}, f32[16,128]{1,0:T(8,128)S(1)}, u32[]{:S(2)}) copy-start(f32[16,128]{1,0:T(8,128)S(1)} %collective-permute-done.1.refs_4_) | copy-start | bytes 24580
  18.8 19.5 %collective-permute-start.6 = (f32[304,256]{1,0:T(8,128)}, f32[304,256]{1,0:T(8,128)S(1)}, u32[]{:S(2)}, u32[]{:S(2)}) collective-permute-start(f32[304,256]{1,0:T(8,128)} %get-tuple-element.30), channel_id=1, source_target_pairs={{0,240},{16,0},{32,16},{48,32},{64,48},{80,64},{96,80},{112,96},{1... | collective-permute-start | bytes 933896 | tf_op jit(solution)/shard_map/ppermute | solution.py:765
  20.0 0.6 %copy-start.3 = (f32[5,16,128]{2,1,0:T(8,128)}, f32[5,16,128]{2,1,0:T(8,128)S(1)}, u32[]{:S(2)}) copy-start(f32[5,16,128]{2,1,0:T(8,128)S(1)} %collective-permute-done.2.refs_5_.refs_8_) | copy-start | bytes 122884
  20.0 0.6 %copy-start.6 = (f32[80,128]{1,0:T(8,128)}, f32[80,128]{1,0:T(8,128)S(1)}, u32[]{:S(2)}) copy-start(f32[80,128]{1,0:T(8,128)S(1)} %collective-permute-done.3.refs_6_) | copy-start | bytes 122884
  20.2 0.6 %copy-start.4 = (f32[5,16,128]{2,1,0:T(8,128)}, f32[5,16,128]{2,1,0:T(8,128)S(1)}, u32[]{:S(2)}) copy-start(f32[5,16,128]{2,1,0:T(8,128)S(1)} %collective-permute-done.4.refs_7_.refs_6_.refs_9_) | copy-start | bytes 122884
  20.8 0.7 %copy-start = (f32[320,256]{1,0:T(8,128)}, f32[320,256]{1,0:T(8,128)S(1)}, u32[]{:S(2)}) copy-start(f32[320,256]{1,0:T(8,128)S(1)} %collective-permute-done.refs_3_.refs_6_) | copy-start | bytes 983044
  24.9 11.0 %copy-start.8 = (f32[32,384]{1,0:T(8,128)S(1)}, f32[32,384]{1,0:T(8,128)}, u32[]{:S(2)}) copy-start(f32[32,384]{1,0:T(8,128)} %get-tuple-element.29) | copy-start | bytes 147460
  24.9 23.8 %all-to-all-start = ((f32[256,1,128]{2,1,0:T(1,128)}), f32[256,1,128]{2,1,0:T(1,128)S(1)}, u32[]{:S(2)}, u32[]{:S(2)}) async-start(f32[256,1,128]{2,1,0:T(1,128)} %bitcast.7), calls=%async_computation | async-start | bytes 262144 | tf_op jit(solution)/shard_map/all_to_all | solution.py:785
  35.9 10.1 %collective-permute-start.5 = (f32[32,384]{1,0:T(8,128)S(1)}, f32[32,384]{1,0:T(8,128)S(1)}, u32[]{:S(2)}, u32[]{:S(2)}) collective-permute-start(f32[32,384]{1,0:T(8,128)S(1)} %copy-done.8), channel_id=1, source_target_pairs={{0,240},{16,0},{32,16},{48,32},{64,48},{80,64},{96,80},{112,96},{1... | collective-permute-start | bytes 147464 | tf_op jit(solution)/shard_map/ppermute | solution.py:773
  38.3 0.7 %copy-start.1 = (f32[304,256]{1,0:T(8,128)}, f32[304,256]{1,0:T(8,128)S(1)}, u32[]{:S(2)}) copy-start(f32[304,256]{1,0:T(8,128)S(1)} %collective-permute-done.6.refs_4_.refs_7_) | copy-start | bytes 933892
  46.0 2.7 %copy-start.5 = (f32[32,384]{1,0:T(8,128)}, f32[32,384]{1,0:T(8,128)S(1)}, u32[]{:S(2)}) copy-start(f32[32,384]{1,0:T(8,128)S(1)} %collective-permute-done.5.refs_3_) | copy-start | bytes 147460
  48.7 0.7 %copy-start.2 = (f32[256,1,128]{2,1,0:T(1,128)}, f32[256,1,128]{2,1,0:T(1,128)S(1)}, u32[]{:S(2)}) copy-start(f32[256,1,128]{2,1,0:T(1,128)S(1)} %all-to-all-done) | copy-start | bytes 393220

commit v11 on v10

--- a/solution.py
+++ b/solution.py
@@ -17,7 +17,6 @@
 PAIRS = [(i, j) for i in range(KRYLOV) for j in range(i, KRYLOV)]
 F32 = jnp.float32
 VM = pl.BlockSpec(memory_space=pltpu.VMEM)
-SM = pl.BlockSpec(memory_space=pltpu.SMEM)
 HB = pl.BlockSpec(memory_space=pltpu.HBM)
 PARAMS = pltpu.CompilerParams(vmem_limit_bytes=58 * 1024 * 1024)
 
@@ -107,9 +106,7 @@
         self.pending.append(copy)
 
 
-def staged(kernel, args, outs, place=None, scratch=(), sends=None, after=(), flops=0, lead=None):
-    smem = [] if place is None else [place]
-
+def staged(kernel, args, outs, place=False, scratch=(), sends=None, after=(), flops=0, lead=None):
     def parts_of(shape):
         if lead is None or len(shape) < 3 or shape[0] < 24:
             return [None]
@@ -125,7 +122,7 @@
 
     def body(*refs):
         refs = list(refs)
-        places = [refs.pop(0) for _ in smem]
+        places = [(lax.axis_index(TROW), lax.axis_index(TCOL))] if place else []
         sources = [refs.pop(0) for _ in range(n_in)]
         sources = [s if cut is None else s.at[pl.ds(*cut)] for s, cut in zip(sources, cuts)]
         for _ in after:
@@ -152,7 +149,7 @@
     return pl.pallas_call(
         body,
         out_shape=[jax.ShapeDtypeStruct(s, F32) for s in outs],
-        in_specs=[SM] * len(smem) + [HB] * (n_in + len(after)),
+        in_specs=[HB] * (n_in + len(after)),
         out_specs=[HB] * n_out,
         scratch_shapes=staging
         + [pltpu.VMEM(s, t) for s, t in scratch]
@@ -161,7 +158,7 @@
             flops=flops, bytes_accessed=4 * (sum(a.size for a in args) + sum(map(math.prod, outs))), transcendentals=0
         ),
         compiler_params=PARAMS,
-    )(*smem, *args, *after)
+    )(*args, *after)
 
 
 def merge_rows(a, b, step):
@@ -745,7 +742,6 @@
 ):
     depth = theta.shape[0]
     whole = theta.shape
-    place = jnp.stack([lax.axis_index(TROW), lax.axis_index(TCOL)]).astype(jnp.int32)
     lines = 8 * depth + 8 * ((depth + 1) // 2)
     columns = (depth // LEVELS, 16, 128)
     a, c, w, inv, ratio, down, up, right, left, corner, cross = staged(
@@ -767,7 +763,7 @@
         krylov_kernel,
         (surface_cot, bottom, (above, lines, 16), corner, (west, 0, 2), (cross, 0, 16), (east, 0, 2)),
         [(32, 384), (96, 384), (256, 128)],
-        place=place,
+        place=True,
         after=(),
     )
     near = lax.ppermute(near, TROW, around(16, -1))
@@ -776,7 +772,7 @@
         (land_mask, bottom, above, below, west, east, velocity_x, velocity_y, theta, salt)
         + (stencil(((-1, -1), (0, 7), (1, 7), (2, -1)), 384), forcing, kappa, inv, ratio),
         [(depth, 24, 256), (depth, 16, 384), kappa.shape, kappa.shape],
-        place=place,
+        place=True,
         flops=200 * theta.size,
         lead=(0, LEVELS),
         sends=16,
@@ -789,7 +785,7 @@
             (sums, own, near, land_mask, bottom, above, below, west, east, w, a, c)
             + (theta_drop, salt_drop, x_open, y_open, stencil(((-2, -1), (-1, 7), (0, 7), (1, -1)), 256)),
             [whole, whole, kappa.shape, forcing.shape],
-            place=place,
+            place=True,
             scratch=[((32 * depth, 768), BF16), ((32 * depth, 256), F32)],
             sends=12,
             lead=(depth - LEVELS, LEVELS),

time: 56.7 us -> 59.5 us (1.049)
  waiting for transfers between devices: 2.99 us -> 9.84 us
  Pallas kernels: 21.8 us -> 19.8 us
  starting transfers between devices: 27.4 us -> 26 us
  other arithmetic: 0.6 us -> 0 us
    ppermute x1, waiting for transfers between devices: 0.01 us -> 4.12 us  [shards(): corner = lax.ppermute(corner, ALL, across(1, 1))]
    ppermute x1, starting transfers between devices: 2.97 us -> 0.73 us  [shards(): east = lax.ppermute(left, TCOL, around(16, -1))]
    ppermute x1, waiting for transfers between devices: 0.24 us -> 2.31 us  [shards(): east = lax.ppermute(left, TCOL, around(16, -1))]
    pallas_call x4, Pallas kernels: 21.8 us -> 19.8 us  [staged(): pl.pallas_call(body, out_shape=[jax.ShapeDtypeStruct(s, F32) for s in out...]
    ppermute x1, starting transfers between devices: 1.44 us -> 2.46 us  [shards(): corner = lax.ppermute(corner, ALL, across(1, 1))]
    ppermute x1, starting transfers between devices: 4.72 us -> 3.74 us  [shards(): cross = lax.ppermute(cross, ALL, across(1, -1))]
    all_to_all x1, waiting for transfers between devices: 2.73 us -> 3.39 us  [shards(): sums = lax.all_to_all(sums, ALL, 0, 0, tiled=True)]
    all_to_all x1, starting transfers between devices: 11 us -> 11.6 us  [shards(): sums = lax.all_to_all(sums, ALL, 0, 0, tiled=True)]
  transfers between devices with their start and end apart: 8 -> 8, of which waited for: 2 -> 3; matrix products, arithmetic and copies ran while one was open for 1% -> 0% of each run, Pallas kernels for 18% -> 15%
where the time goes in v11:
time: 59.5 us; the launch traced here: 59.2 us
  starting transfers between devices  26 us (44%)
  Pallas kernels  19.8 us (33%)
  waiting for transfers between devices  9.84 us (17%)
  local copies, waits for them, and re-layouts  2.68 us (5%)
  between operations  0.9 us (2%)
    pallas_call x4, Pallas kernels, staged(): pl.pallas_call(body, out_shape=[jax.ShapeDtypeStruct(s, F32) for s in out...  19.8 us
    all_to_all x1, starting transfers between devices, shards(): sums = lax.all_to_all(sums, ALL, 0, 0, tiled=True)  11.6 us
    ppermute x1, waiting for transfers between devices, shards(): corner = lax.ppermute(corner, ALL, across(1, 1))  4.12 us
    ppermute x1, starting transfers between devices, shards(): cross = lax.ppermute(cross, ALL, across(1, -1))  3.74 us
    all_to_all x1, waiting for transfers between devices, shards(): sums = lax.all_to_all(sums, ALL, 0, 0, tiled=True)  3.39 us
    ppermute x1, starting transfers between devices, shards(): above = lax.ppermute(down, TROW, around(16, 1))  2.76 us
    unnamed x18, local copies, waits for them, and re-layouts  2.68 us
    ppermute x1, starting transfers between devices, shards(): corner = lax.ppermute(corner, ALL, across(1, 1))  2.46 us
  transfers between devices with their start and end apart: 8, of which 3 were waited for; matrix products, arithmetic and copies ran while one was open for 0% of the time, Pallas kernels for 15%

profile of v11, /device:TPU:1, one launch (start us, length us, event | category | flops | bytes accessed | tf_op | source)
XLA Modules:
  0.0 59.2 jit_solution(3145986043231525192)
XLA Ops:
  0.6 4.6 %shard_map.156 = (f32[25,16,256]{2,1,0:T(8,128)}, f32[25,16,256]{2,1,0:T(8,128)}, f32[25,16,256]{2,1,0:T(8,128)}, f32[25,16,256]{2,1,0:T(8,128)}, f32[24,16,256]...) custom-call(s32[25,16,256]{2,1,0:T(8,128)} %refs_3_.3, ...), custom_call_target="tpu_custom_call" | custom-call | flops 10240000 | bytes 6094848 | tf_op jit(solution)/shard_map/pallas_call | solution.py:149
  5.3 2.8 %collective-permute-start = (f32[320,256]{1,0:T(8,128)}, f32[320,256]{1,0:T(8,128)S(1)}, u32[]{:S(2)}, u32[]{:S(2)}) collective-permute-start(f32[320,256]{1,0:T(8,128)} %get-tuple-element.22), channel_id=1, source_target_pairs={{0,16},{16,32},{32,48},{48,64},{64,80},{80,96},{96,112},{112,128},... | collective-permute-start | bytes 983048 | tf_op jit(solution)/shard_map/ppermute | solution.py:760
  8.0 0.6 %collective-permute-start.6 = (f32[304,256]{1,0:T(8,128)}, f32[304,256]{1,0:T(8,128)S(1)}, u32[]{:S(2)}, u32[]{:S(2)}) collective-permute-start(f32[304,256]{1,0:T(8,128)} %get-tuple-element.30), channel_id=1, source_target_pairs={{0,240},{16,0},{32,16},{48,32},{64,48},{80,64},{96,80},{112,96},{1... | collective-permute-start | bytes 933896 | tf_op jit(solution)/shard_map/ppermute | solution.py:761
  8.7 2.5 %collective-permute-start.1 = (f32[16,128]{1,0:T(8,128)}, f32[16,128]{1,0:T(8,128)S(1)}, u32[]{:S(2)}, u32[]{:S(2)}) collective-permute-start(f32[16,128]{1,0:T(8,128)} %get-tuple-element.23), channel_id=1, source_target_pairs={{0,17},{1,18},{2,19},{3,20},{4,21},{5,22},{6,23},{7,24},{8,25},{9,... | collective-permute-start | bytes 24584 | tf_op jit(solution)/shard_map/ppermute | solution.py:756
  11.1 1.6 %collective-permute-start.2 = (f32[5,16,128]{2,1,0:T(8,128)}, f32[5,16,128]{2,1,0:T(8,128)S(1)}, u32[]{:S(2)}, u32[]{:S(2)}) collective-permute-start(f32[5,16,128]{2,1,0:T(8,128)} %get-tuple-element.24), channel_id=1, source_target_pairs={{0,1},{1,2},{2,3},{3,4},{4,5},{5,6},{6,7},{7,8},{8,9},{9,10},{10,1... | collective-permute-start | bytes 122888 | tf_op jit(solution)/shard_map/ppermute | solution.py:757
  12.8 3.7 %collective-permute-start.3 = (f32[80,128]{1,0:T(8,128)}, f32[80,128]{1,0:T(8,128)S(1)}, u32[]{:S(2)}, u32[]{:S(2)}) collective-permute-start(f32[80,128]{1,0:T(8,128)} %get-tuple-element.25), channel_id=1, source_target_pairs={{0,31},{1,16},{2,17},{3,18},{4,19},{5,20},{6,21},{7,22},{8,23},{9,... | collective-permute-start | bytes 122888 | tf_op jit(solution)/shard_map/ppermute | solution.py:758
  16.5 4.1 %collective-permute-done.1.refs_3_ = f32[16,128]{1,0:T(8,128)S(1)} collective-permute-done((f32[16,128]{1,0:T(8,128)}, f32[16,128]{1,0:T(8,128)S(1)}, u32[]{:S(2)}, u32[]{:S(2)}) %collective-permute-start.1) | collective-permute-done | bytes 8224 | tf_op jit(solution)/shard_map/ppermute | solution.py:756
  20.6 0.7 %collective-permute-start.4 = (f32[5,16,128]{2,1,0:T(8,128)}, f32[5,16,128]{2,1,0:T(8,128)S(1)}, u32[]{:S(2)}, u32[]{:S(2)}) collective-permute-start(f32[5,16,128]{2,1,0:T(8,128)} %get-tuple-element.26), channel_id=1, source_target_pairs={{0,15},{1,0},{2,1},{3,2},{4,3},{5,4},{6,5},{7,6},{8,7},{9,8},{10,9... | collective-permute-start | bytes 122888 | tf_op jit(solution)/shard_map/ppermute | solution.py:759
  21.4 0.0 collective-permute-done.2.refs_4_.refs_7_
  21.4 0.0 collective-permute-done.3.refs_5_
  21.4 0.0 copy-start.6
  21.4 2.3 %collective-permute-done.4.refs_6_.refs_5_.refs_8_ = f32[5,16,128]{2,1,0:T(8,128)S(1)} collective-permute-done((f32[5,16,128]{2,1,0:T(8,128)}, f32[5,16,128]{2,1,0:T(8,128)S(1)}, u32[]{:S(2)}, u32[]{:S(2)}) %collective-permute-start.4) | collective-permute-done | bytes 40992 | tf_op jit(solution)/shard_map/ppermute | solution.py:759
  23.7 0.0 collective-permute-done.refs_2_.refs_5_
  23.7 0.0 copy-done.7
  23.7 0.0 copy-done.3
  23.7 0.0 copy-done.6
  23.7 0.6 copy-done.4
  24.3 0.7 %copy-done = f32[320,256]{1,0:T(8,128)} copy-done((f32[320,256]{1,0:T(8,128)}, f32[320,256]{1,0:T(8,128)S(1)}, u32[]{:S(2)}) %copy-start) | copy-done | bytes 327704
  25.0 2.7 %shard_map.157 = (f32[32,384]{1,0:T(8,128)}, f32[96,384]{1,0:T(8,128)}, f32[256,128]{1,0:T(8,128)}) custom-call(f32[16,256]{1,0:T(8,128)} %refs_0_.4, s32[16,256]{1,0:T(8,128)} %refs_4_.3, f32[320,256]{1,0:T(8,128)} %copy-done, f32[16,128]{1,0:T(8,128)} %copy-done.7, f32[5,16,128]{2,1,0:T(8,128)} %copy-done.3, f32[80,128]{1,0:T(8,128)} %copy-done.6, ...), custom_call_target="tpu_custom_call" | custom-call | bytes 819200 | tf_op jit(solution)/shard_map/pallas_call | solution.py:149
  27.7 0.0 copy-start.8
  27.7 11.6 %all-to-all-start = ((f32[256,1,128]{2,1,0:T(1,128)}), f32[256,1,128]{2,1,0:T(1,128)S(1)}, u32[]{:S(2)}, u32[]{:S(2)}) async-start(f32[256,1,128]{2,1,0:T(1,128)} %bitcast.5), calls=%async_computation | async-start | bytes 262144 | tf_op jit(solution)/shard_map/all_to_all | solution.py:781
  39.3 0.0 copy-done.8
  39.3 2.4 %collective-permute-start.5 = (f32[32,384]{1,0:T(8,128)S(1)}, f32[32,384]{1,0:T(8,128)S(1)}, u32[]{:S(2)}, u32[]{:S(2)}) collective-permute-start(f32[32,384]{1,0:T(8,128)S(1)} %copy-done.8), channel_id=1, source_target_pairs={{0,240},{16,0},{32,16},{48,32},{64,48},{80,64},{96,80},{112,96},{1... | collective-permute-start | bytes 147464 | tf_op jit(solution)/shard_map/ppermute | solution.py:769
  41.8 0.0 collective-permute-done.6.refs_3_.refs_6_
  41.8 0.7 %copy-done.1 = f32[304,256]{1,0:T(8,128)} copy-done((f32[304,256]{1,0:T(8,128)}, f32[304,256]{1,0:T(8,128)S(1)}, u32[]{:S(2)}) %copy-start.1) | copy-done | bytes 311320
  42.5 6.3 %shard_map.158 = (f32[25,24,256]{2,1,0:T(8,128)}, f32[25,16,384]{2,1,0:T(8,128)}, f32[24,16,256]{2,1,0:T(8,128)}, f32[24,16,256]{2,1,0:T(8,128)}) custom-call(s32[25,16,256]{2,1,0:T(8,128)} %refs_3_.3, s32[16,256]{1,0:T(8,128)} %refs_4_.3, f32[320,256]{1,0:T(8,128)} %copy-done, f32[304,256]{1,0:T(8,128)} %copy-done.1, f32[5,16,128]{2,1,0:T(8,128)} %copy-done.3, ...), custom_call_target="tpu_custom_call" | custom-call | flops 20480000 | bytes 7192576 | tf_op jit(solution)/shard_map/pallas_call | solution.py:149
  48.8 0.0 collective-permute-done.5.refs_2_
  48.8 0.0 copy-start.5
  48.8 3.4 %all-to-all-done = f32[256,1,128]{2,1,0:T(1,128)S(1)} async-done(((f32[256,1,128]{2,1,0:T(1,128)}), f32[256,1,128]{2,1,0:T(1,128)S(1)}, u32[]{:S(2)}, u32[]{:S(2)}) %all-to-all-start) | async-done | bytes 131104 | tf_op jit(solution)/shard_map/all_to_all | solution.py:781
  52.2 0.0 copy-done.5
  52.2 0.6 %copy-done.2 = f32[256,1,128]{2,1,0:T(1,128)} copy-done((f32[256,1,128]{2,1,0:T(1,128)}, f32[256,1,128]{2,1,0:T(1,128)S(1)}, u32[]{:S(2)}) %copy-start.2) | copy-done | bytes 131096
  52.9 6.2 %shard_map.159 = (f32[25,16,256]{2,1,0:T(8,128)}, f32[25,16,256]{2,1,0:T(8,128)}, f32[24,16,256]{2,1,0:T(8,128)}, f32[16,256]{1,0:T(8,128)}) custom-call(f32[256,128]{1,0:T(8,128)} %bitcast.4, f32[96,384]{1,0:T(8,128)} %get-tuple-element.28.refs_1_, f32[32,384]{1,0:T(8,128)} %copy-done.5, s32[25,16,256]{2,1,0:T(8,128)} %refs_3_.3, s32[16,256]{1,0:T(8,128)} %refs_4_.3, ...), custom_call_target="tpu_custom_call" | custom-call | bytes 6733824 | tf_op jit(solution)/shard_map/pallas_call | solution.py:149
  (6 shorter events, 0.0 us)
Async XLA Ops:
  5.3 18.4 %collective-permute-start = (f32[320,256]{1,0:T(8,128)}, f32[320,256]{1,0:T(8,128)S(1)}, u32[]{:S(2)}, u32[]{:S(2)}) collective-permute-start(f32[320,256]{1,0:T(8,128)} %get-tuple-element.22), channel_id=1, source_target_pairs={{0,16},{16,32},{32,48},{48,64},{64,80},{80,96},{96,112},{112,128},... | collective-permute-start | bytes 983048 | tf_op jit(solution)/shard_map/ppermute | solution.py:760
  8.0 33.7 %collective-permute-start.6 = (f32[304,256]{1,0:T(8,128)}, f32[304,256]{1,0:T(8,128)S(1)}, u32[]{:S(2)}, u32[]{:S(2)}) collective-permute-start(f32[304,256]{1,0:T(8,128)} %get-tuple-element.30), channel_id=1, source_target_pairs={{0,240},{16,0},{32,16},{48,32},{64,48},{80,64},{96,80},{112,96},{1... | collective-permute-start | bytes 933896 | tf_op jit(solution)/shard_map/ppermute | solution.py:761
  8.7 12.0 %collective-permute-start.1 = (f32[16,128]{1,0:T(8,128)}, f32[16,128]{1,0:T(8,128)S(1)}, u32[]{:S(2)}, u32[]{:S(2)}) collective-permute-start(f32[16,128]{1,0:T(8,128)} %get-tuple-element.23), channel_id=1, source_target_pairs={{0,17},{1,18},{2,19},{3,20},{4,21},{5,22},{6,23},{7,24},{8,25},{9,... | collective-permute-start | bytes 24584 | tf_op jit(solution)/shard_map/ppermute | solution.py:756
  11.1 10.2 %collective-permute-start.2 = (f32[5,16,128]{2,1,0:T(8,128)}, f32[5,16,128]{2,1,0:T(8,128)S(1)}, u32[]{:S(2)}, u32[]{:S(2)}) collective-permute-start(f32[5,16,128]{2,1,0:T(8,128)} %get-tuple-element.24), channel_id=1, source_target_pairs={{0,1},{1,2},{2,3},{3,4},{4,5},{5,6},{6,7},{7,8},{8,9},{9,10},{10,1... | collective-permute-start | bytes 122888 | tf_op jit(solution)/shard_map/ppermute | solution.py:757
  12.8 8.6 %collective-permute-start.3 = (f32[80,128]{1,0:T(8,128)}, f32[80,128]{1,0:T(8,128)S(1)}, u32[]{:S(2)}, u32[]{:S(2)}) collective-permute-start(f32[80,128]{1,0:T(8,128)} %get-tuple-element.25), channel_id=1, source_target_pairs={{0,31},{1,16},{2,17},{3,18},{4,19},{5,20},{6,21},{7,22},{8,23},{9,... | collective-permute-start | bytes 122888 | tf_op jit(solution)/shard_map/ppermute | solution.py:758
  20.6 3.1 %copy-start.7 = (f32[16,128]{1,0:T(8,128)}, f32[16,128]{1,0:T(8,128)S(1)}, u32[]{:S(2)}) copy-start(f32[16,128]{1,0:T(8,128)S(1)} %collective-permute-done.1.refs_3_) | copy-start | bytes 24580
  20.6 3.1 %collective-permute-start.4 = (f32[5,16,128]{2,1,0:T(8,128)}, f32[5,16,128]{2,1,0:T(8,128)S(1)}, u32[]{:S(2)}, u32[]{:S(2)}) collective-permute-start(f32[5,16,128]{2,1,0:T(8,128)} %get-tuple-element.26), channel_id=1, source_target_pairs={{0,15},{1,0},{2,1},{3,2},{4,3},{5,4},{6,5},{7,6},{8,7},{9,8},{10,9... | collective-permute-start | bytes 122888 | tf_op jit(solution)/shard_map/ppermute | solution.py:759
  21.4 2.3 %copy-start.3 = (f32[5,16,128]{2,1,0:T(8,128)}, f32[5,16,128]{2,1,0:T(8,128)S(1)}, u32[]{:S(2)}) copy-start(f32[5,16,128]{2,1,0:T(8,128)S(1)} %collective-permute-done.2.refs_4_.refs_7_) | copy-start | bytes 122884
  21.4 2.3 %copy-start.6 = (f32[80,128]{1,0:T(8,128)}, f32[80,128]{1,0:T(8,128)S(1)}, u32[]{:S(2)}) copy-start(f32[80,128]{1,0:T(8,128)S(1)} %collective-permute-done.3.refs_5_) | copy-start | bytes 122884
  23.7 0.6 %copy-start.4 = (f32[5,16,128]{2,1,0:T(8,128)}, f32[5,16,128]{2,1,0:T(8,128)S(1)}, u32[]{:S(2)}) copy-start(f32[5,16,128]{2,1,0:T(8,128)S(1)} %collective-permute-done.4.refs_6_.refs_5_.refs_8_) | copy-start | bytes 122884
  24.3 0.7 %copy-start = (f32[320,256]{1,0:T(8,128)}, f32[320,256]{1,0:T(8,128)S(1)}, u32[]{:S(2)}) copy-start(f32[320,256]{1,0:T(8,128)S(1)} %collective-permute-done.refs_2_.refs_5_) | copy-start | bytes 983044
  27.7 11.6 %copy-start.8 = (f32[32,384]{1,0:T(8,128)S(1)}, f32[32,384]{1,0:T(8,128)}, u32[]{:S(2)}) copy-start(f32[32,384]{1,0:T(8,128)} %get-tuple-element.29) | copy-start | bytes 147460
  27.7 24.5 %all-to-all-start = ((f32[256,1,128]{2,1,0:T(1,128)}), f32[256,1,128]{2,1,0:T(1,128)S(1)}, u32[]{:S(2)}, u32[]{:S(2)}) async-start(f32[256,1,128]{2,1,0:T(1,128)} %bitcast.5), calls=%async_computation | async-start | bytes 262144 | tf_op jit(solution)/shard_map/all_to_all | solution.py:781
  39.3 9.4 %collective-permute-start.5 = (f32[32,384]{1,0:T(8,128)S(1)}, f32[32,384]{1,0:T(8,128)S(1)}, u32[]{:S(2)}, u32[]{:S(2)}) collective-permute-start(f32[32,384]{1,0:T(8,128)S(1)} %copy-done.8), channel_id=1, source_target_pairs={{0,240},{16,0},{32,16},{48,32},{64,48},{80,64},{96,80},{112,96},{1... | collective-permute-start | bytes 147464 | tf_op jit(solution)/shard_map/ppermute | solution.py:769
  41.8 0.7 %copy-start.1 = (f32[304,256]{1,0:T(8,128)}, f32[304,256]{1,0:T(8,128)S(1)}, u32[]{:S(2)}) copy-start(f32[304,256]{1,0:T(8,128)S(1)} %collective-permute-done.6.refs_3_.refs_6_) | copy-start | bytes 933892
  48.8 3.4 %copy-start.5 = (f32[32,384]{1,0:T(8,128)}, f32[32,384]{1,0:T(8,128)S(1)}, u32[]{:S(2)}) copy-start(f32[32,384]{1,0:T(8,128)S(1)} %collective-permute-done.5.refs_2_) | copy-start | bytes 147460
  52.2 0.7 %copy-start.2 = (f32[256,1,128]{2,1,0:T(1,128)}, f32[256,1,128]{2,1,0:T(1,128)S(1)}, u32[]{:S(2)}) copy-start(f32[256,1,128]{2,1,0:T(1,128)S(1)} %all-to-all-done) | copy-start | bytes 393220
